TPU v7x, 32 devices: a whole 2x2x4 slice. The times are simulated.
32 devices in a mesh: frame: 4 (over x, core), height: 4 (over z), width: 2 (over y).
Axes of the slice: x: 2, y: 2, z: 4, core: 2. Of those that a mesh axis runs over, the one named last changes fastest.
Arguments:
- queries: bfloat16 [16, 24, 16, 128], P('frame', 'height', 'width'), may hold values from -8 to 8
- key_vectors: bfloat16 [16, 24, 16, 128], P('frame', 'height', 'width'), may hold values from -8 to 8
- value_vectors: bfloat16 [16, 24, 16, 128], P('frame', 'height', 'width'), may hold values from -24 to 24
- out_weight: bfloat16 [128, 3072], replicated, may hold values from -0.5 to 0.5
- projected_grad: bfloat16 [16, 24, 16, 3072], P('frame', 'height', 'width'), may hold values from -6 to 6
Outputs:
- projected: bfloat16 [16, 24, 16, 3072], P('frame', 'height', 'width')
- grad_query: bfloat16 [16, 24, 16, 128], P('frame', 'height', 'width')
- grad_key: bfloat16 [16, 24, 16, 128], P('frame', 'height', 'width')
- grad_value: bfloat16 [16, 24, 16, 128], P('frame', 'height', 'width')
- grad_out_weight: float32 [128, 3072], replicated
All inputs are finite; a program needn't handle non-finite values.
Results may differ from a plain program's by a relative error of at most 0.023.
Values may be sent and summed in bfloat16 or wider, within the bound.
No kernel may reach another device: no remote copies, remote signals or barrier semaphores. Data moves between devices by JAX's collectives and lax.ppermute only.
A program may use at most 128 MiB of HBM per device.

v0:
```python
import math

import jax
import jax.numpy as jnp
from jax import lax
from jax.sharding import PartitionSpec as P


def shifted(block, axis, distance):
    devices = range(lax.axis_size(axis))
    route = [(i - distance, i) for i in devices if i - distance in devices]
    return lax.ppermute(block, axis, route)


def window_start(position, extent):
    return jnp.maximum(jnp.minimum(position - 1, extent - 3), 0)


def near_tiles(source, axis_dim, position, extent, sender):
    tile_len = source.shape[axis_dim]
    strides = (2, 1, -1, -2) if extent >= 3 else (1, -1)
    arrived = {stride: sender(source, stride) for stride in strides}
    blanks = jnp.zeros_like(source)
    ordered = [
        source if stride == 0 else arrived.get(stride, blanks) for stride in (2, 1, 0, -1, -2)
    ]
    joined = jnp.concatenate(ordered, axis=axis_dim)
    offset = (window_start(position, extent) - position + 2) * tile_len
    return lax.dynamic_slice_in_dim(joined, offset, min(3, extent) * tile_len, axis_dim)


def place_window(window_grads, axis_dim, start_tile, tile_len, total_tiles):
    grid_shape = list(window_grads.shape)
    grid_shape[axis_dim] = total_tiles * tile_len
    blanks = jnp.zeros(tuple(grid_shape), jnp.float32)
    return lax.dynamic_update_slice_in_dim(blanks, window_grads, start_tile * tile_len, axis_dim)


def return_near(window_grads, axis_dim, position, extent, tile_len, sender):
    placed = place_window(
        window_grads, axis_dim, window_start(position, extent) - position + 2, tile_len, 5
    )
    summed = lax.slice_in_dim(placed, 2 * tile_len, 3 * tile_len, axis=axis_dim)
    strides = (-2, -1, 1, 2) if extent >= 3 else (-1, 1)
    for stride in strides:
        piece_out = lax.slice_in_dim(
            placed, (stride + 2) * tile_len, (stride + 3) * tile_len, axis=axis_dim
        )
        summed = summed + sender(piece_out, stride)
    return summed


def fetch_frame(stacked):
    extent = lax.axis_size("frame")
    position = lax.axis_index("frame")
    return near_tiles(
        stacked, 1, position, extent, lambda incoming, stride: shifted(incoming, "frame", stride)
    )


def fetch_height(stacked):
    extent = lax.axis_size("height")
    position = lax.axis_index("height")
    return near_tiles(
        stacked, 2, position, extent, lambda incoming, stride: shifted(incoming, "height", stride)
    )


def fetch_width(stacked):
    extent = lax.axis_size("width")
    position = lax.axis_index("width")
    return near_tiles(
        stacked, 3, position, extent, lambda incoming, stride: shifted(incoming, "width", stride)
    )


def return_frame(window_grads, tile_len):
    extent = lax.axis_size("frame")
    position = lax.axis_index("frame")
    return return_near(
        window_grads,
        1,
        position,
        extent,
        tile_len,
        lambda outgoing, stride: shifted(outgoing.astype(jnp.bfloat16), "frame", stride).astype(
            outgoing.dtype
        ),
    )


def return_height(window_grads, tile_len):
    extent = lax.axis_size("height")
    position = lax.axis_index("height")
    return return_near(
        window_grads,
        2,
        position,
        extent,
        tile_len,
        lambda outgoing, stride: shifted(outgoing.astype(jnp.bfloat16), "height", stride).astype(
            outgoing.dtype
        ),
    )


def return_width(window_grads, tile_len):
    extent = lax.axis_size("width")
    position = lax.axis_index("width")
    return return_near(
        window_grads,
        3,
        position,
        extent,
        tile_len,
        lambda outgoing, stride: shifted(outgoing.astype(jnp.bfloat16), "width", stride).astype(
            outgoing.dtype
        ),
    )


def gradient_block(
    probability, prob_bf, attended_grad, row_dot, query_rows, key_rows, value_rows, inv_root
):
    prob_grad = jnp.einsum(
        "qd,kd->qk", attended_grad, value_rows, preferred_element_type=jnp.float32
    )
    score_grad = (probability * (prob_grad - row_dot)).astype(jnp.bfloat16)
    query_part = jnp.dot(score_grad, key_rows, preferred_element_type=jnp.float32)
    key_part = (
        jnp.einsum("qk,qd->kd", score_grad, query_rows, preferred_element_type=jnp.float32)
        * inv_root
    )
    value_part = jnp.einsum("qk,qd->kd", prob_bf, attended_grad, preferred_element_type=jnp.float32)
    return (query_part, key_part, value_part)


def body(queries, key_vectors, value_vectors, out_weight, projected_grad):
    frame_len, height_len, width_len, head_dim = queries.shape
    model_dim = out_weight.shape[1]
    inv_root = 1.0 / math.sqrt(head_dim)
    stacked = jnp.stack((key_vectors, value_vectors))
    window = fetch_width(fetch_height(fetch_frame(stacked)))
    key_rows = window[0].reshape(-1, head_dim)
    value_rows = window[1].reshape(-1, head_dim)
    query_rows = queries.reshape(-1, head_dim)
    grad_rows = projected_grad.reshape(-1, model_dim)
    scores = (
        jnp.einsum("qd,kd->qk", query_rows, key_rows, preferred_element_type=jnp.float32) * inv_root
    )
    row_max = jnp.max(scores, axis=1, keepdims=True)
    row_sum = jnp.sum(jnp.exp(scores - row_max), axis=1, keepdims=True)
    probability = jnp.exp(scores - row_max) / row_sum
    prob_bf = probability.astype(jnp.bfloat16)
    attended = jnp.dot(prob_bf, value_rows, preferred_element_type=jnp.float32).astype(jnp.bfloat16)
    projected = (
        jnp.dot(attended, out_weight, preferred_element_type=jnp.float32)
        .astype(jnp.bfloat16)
        .reshape(projected_grad.shape)
    )
    attended_grad = jnp.einsum(
        "tm,dm->td", grad_rows, out_weight, preferred_element_type=jnp.float32
    ).astype(jnp.bfloat16)
    weight_term = jnp.einsum("td,tm->dm", attended, grad_rows, preferred_element_type=jnp.float32)
    tile_count = lax.axis_size("frame") * lax.axis_size("height") * lax.axis_size("width")
    grad_out_weight = lax.psum(weight_term, ("frame", "height", "width")) / float(tile_count)
    row_dot = jnp.sum(
        attended_grad.astype(jnp.float32) * attended.astype(jnp.float32), axis=1, keepdims=True
    )
    slab_rows = frame_len * window.shape[2] * window.shape[3]
    query_grad = jnp.zeros((query_rows.shape[0], head_dim), jnp.float32)
    key_parts = []
    value_parts = []
    for slab_index in range(window.shape[1] // frame_len):
        key_block = key_rows[slab_index * slab_rows : (slab_index + 1) * slab_rows]
        value_block = value_rows[slab_index * slab_rows : (slab_index + 1) * slab_rows]
        block_scores = (
            jnp.einsum("qd,kd->qk", query_rows, key_block, preferred_element_type=jnp.float32)
            * inv_root
        )
        block_prob = jnp.exp(block_scores - row_max) / row_sum
        piece_query, piece_key, piece_value = gradient_block(
            block_prob,
            block_prob.astype(jnp.bfloat16),
            attended_grad,
            row_dot,
            query_rows,
            key_block,
            value_block,
            inv_root,
        )
        query_grad = query_grad + piece_query
        key_parts.append(piece_key)
        value_parts.append(piece_value)
    key_grad = jnp.concatenate(key_parts, axis=0)
    value_grad = jnp.concatenate(value_parts, axis=0)
    grad_query = (query_grad * inv_root).astype(jnp.bfloat16).reshape(queries.shape)
    window_grads = jnp.stack((key_grad, value_grad)).reshape(window.shape)
    returned = return_frame(
        return_height(return_width(window_grads, width_len), height_len), frame_len
    )
    grad_key = returned[0].astype(jnp.bfloat16)
    grad_value = returned[1].astype(jnp.bfloat16)
    return (projected, grad_query, grad_key, grad_value, grad_out_weight)


def solution(mesh):
    in_specs = (
        P("frame", "height", "width", None),
        P("frame", "height", "width", None),
        P("frame", "height", "width", None),
        P(),
        P("frame", "height", "width", None),
    )
    out_specs = (
        P("frame", "height", "width", None),
        P("frame", "height", "width", None),
        P("frame", "height", "width", None),
        P("frame", "height", "width", None),
        P(),
    )
    return jax.shard_map(body, mesh=mesh, in_specs=in_specs, out_specs=out_specs, check_vma=False)
```

profile of v0, /device:TPU:0, one launch (start us, length us, event | category | flops | bytes accessed | tf_op | source)
XLA Modules:
  0.0 281.3 jit_solution(2343856774046282273)
XLA Ops:
  7.2 0.9 pad_maximum_fusion.2
  8.1 4.8 %collective-permute-start = (bf16[2,4,6,8,128]{4,3,2,1,0:T(8,128)(2,1)S(1)}, bf16[2,4,6,8,128]{4,3,2,1,0:T(8,128)(2,1)S(1)}, u32[]{:S(2)}, u32[]{:S(2)}) collective-permute-start(bf16[2,4,6,8,128]{4,3,2,1,0:T(8,128)(2,1)S(1)} %pad_maximum_fusion.2), channel_id=1, source_target_pairs={{0,16},{8,24},{1,17},{9,25},{2,18},{10,26},{3,19},{11,27},{4,20},{... | collective-permute-start | bytes 294920 | tf_op jit(solution)/shard_map/ppermute | solution.py:12
  13.0 1.5 collective-permute-start.1
  14.5 1.3 collective-permute-start.2
  15.8 1.3 collective-permute-start.3
  17.2 0.8 constant_dynamic-update-slice_fusion.2
  18.0 5.2 %collective-permute-done.3 = bf16[2,4,6,8,128]{4,3,2,1,0:T(8,128)(2,1)S(1)} collective-permute-done((bf16[2,4,6,8,128]{4,3,2,1,0:T(8,128)(2,1)S(1)}, bf16[2,4,6,8,128]{4,3,2,1,0:T(8,128)(2,1)S(1)}, u32[]{:S(2)}, u32[]{:S(2)}) %collective-permute-start.3) | collective-permute-done | bytes 98336 | tf_op jit(solution)/shard_map/ppermute | solution.py:12
  23.2 4.5 %collective-permute-start.4 = (bf16[2,12,6,8,128]{4,3,2,1,0:T(8,128)(2,1)S(1)}, bf16[2,12,6,8,128]{4,3,2,1,0:T(8,128)(2,1)S(1)}, u32[]{:S(2)}, u32[]{:S(2)}) collective-permute-start(bf16[2,12,6,8,128]{4,3,2,1,0:T(8,128)(2,1)S(1)} %constant_dynamic-slice_fusion.9), channel_id=1, source_target_pairs={{0,4},{2,6},{1,5},{3,7},{8,12},{10,14},{9,13},{11,15},{16,20},{18,... | collective-permute-start | bytes 884744 | tf_op jit(solution)/shard_map/ppermute | solution.py:12
  27.8 3.5 %collective-permute-start.5 = (bf16[2,12,6,8,128]{4,3,2,1,0:T(8,128)(2,1)S(1)}, bf16[2,12,6,8,128]{4,3,2,1,0:T(8,128)(2,1)S(1)}, u32[]{:S(2)}, u32[]{:S(2)}) collective-permute-start(bf16[2,12,6,8,128]{4,3,2,1,0:T(8,128)(2,1)S(1)} %constant_dynamic-slice_fusion.9), channel_id=1, source_target_pairs={{0,2},{2,4},{4,6},{1,3},{3,5},{5,7},{8,10},{10,12},{12,14},{9,11},... | collective-permute-start | bytes 884744 | tf_op jit(solution)/shard_map/ppermute | solution.py:12
  31.3 1.3 collective-permute-start.6
  32.6 1.3 collective-permute-start.7
  33.9 1.3 collective-permute-done.4
  35.2 5.5 %collective-permute-done.5 = bf16[2,12,6,8,128]{4,3,2,1,0:T(8,128)(2,1)S(1)} collective-permute-done((bf16[2,12,6,8,128]{4,3,2,1,0:T(8,128)(2,1)S(1)}, bf16[2,12,6,8,128]{4,3,2,1,0:T(8,128)(2,1)S(1)}, u32[]{:S(2)}, u32[]{:S(2)}) %collective-permute-start.5) | collective-permute-done | bytes 294944 | tf_op jit(solution)/shard_map/ppermute | solution.py:12
  40.7 1.2 collective-permute-done.6
  42.0 12.0 %collective-permute-done.7 = bf16[2,12,6,8,128]{4,3,2,1,0:T(8,128)(2,1)S(1)} collective-permute-done((bf16[2,12,6,8,128]{4,3,2,1,0:T(8,128)(2,1)S(1)}, bf16[2,12,6,8,128]{4,3,2,1,0:T(8,128)(2,1)S(1)}, u32[]{:S(2)}, u32[]{:S(2)}) %collective-permute-start.7) | collective-permute-done | bytes 294944 | tf_op jit(solution)/shard_map/ppermute | solution.py:12
  54.0 1.1 copy-done.4
  55.2 1.0 constant_dynamic-slice_fusion.8
  56.1 4.3 %collective-permute-start.8 = (bf16[2,12,18,8,128]{4,3,2,1,0:T(8,128)(2,1)}, bf16[2,12,18,8,128]{4,3,2,1,0:T(8,128)(2,1)}, u32[]{:S(2)}, u32[]{:S(2)}) collective-permute-start(bf16[2,12,18,8,128]{4,3,2,1,0:T(8,128)(2,1)} %constant_dynamic-slice_fusion.8), channel_id=1, source_target_pairs={{0,1},{2,3},{4,5},{6,7},{8,9},{10,11},{12,13},{14,15},{16,17},{18,... | collective-permute-start | bytes 2654216 | tf_op jit(solution)/shard_map/ppermute | solution.py:12
  60.5 1.3 collective-permute-start.9
  61.9 0.5 convolution_convert_fusion.1
  62.4 15.5 %collective-permute-done.8 = bf16[2,12,18,8,128]{4,3,2,1,0:T(8,128)(2,1)} collective-permute-done((bf16[2,12,18,8,128]{4,3,2,1,0:T(8,128)(2,1)}, bf16[2,12,18,8,128]{4,3,2,1,0:T(8,128)(2,1)}, u32[]{:S(2)}, u32[]{:S(2)}) %collective-permute-start.8) | collective-permute-done | bytes 884768 | tf_op jit(solution)/shard_map/ppermute | solution.py:12
  77.9 1.4 constant_dynamic-update-slice_fusion.12
  79.5 3.3 %collective-permute-done.9 = bf16[2,12,18,8,128]{4,3,2,1,0:T(8,128)(2,1)S(1)} collective-permute-done((bf16[2,12,18,8,128]{4,3,2,1,0:T(8,128)(2,1)}, bf16[2,12,18,8,128]{4,3,2,1,0:T(8,128)(2,1)S(1)}, u32[]{:S(2)}, u32[]{:S(2)}) %collective-permute-start.9) | collective-permute-done | bytes 884768 | tf_op jit(solution)/shard_map/ppermute | solution.py:12
  83.6 0.5 copy-done.6
  84.1 0.6 fusion.42
  84.7 0.5 fusion.18
  85.6 0.3 fusion.12
  85.9 0.8 multiply_reduce_fusion
  86.7 0.4 fusion.29
  87.4 0.4 convolution_multiply_fusion.4
  87.8 0.3 fusion.14
  88.1 0.4 fusion.33
  88.8 0.4 convolution_multiply_fusion.6
  89.1 0.3 fusion.13
  89.5 0.4 fusion.31
  90.1 0.4 convolution_multiply_fusion.5
  90.8 0.6 broadcast_in_dim.18
  91.3 0.4 maximum_dynamic-update-slice_fusion
  91.7 0.6 convert.24
  92.3 2.8 %copy-done.1 = f32[2,12,18,40,128]{4,3,2,1,0:T(8,128)} copy-done((f32[2,12,18,40,128]{4,3,2,1,0:T(8,128)}, f32[2,12,18,40,128]{4,3,2,1,0:T(8,128)S(1)}, u32[]{:S(2)}) %copy-start.1) | copy-done | bytes 8847384
  95.2 1.5 fusion.39
  96.7 1.3 collective-permute-start.10
  98.0 6.4 %collective-permute-start.11 = (bf16[2,12,18,8,128]{4,3,2,1,0:T(8,128)(2,1)}, bf16[2,12,18,8,128]{4,3,2,1,0:T(8,128)(2,1)}, u32[]{:S(2)}, u32[]{:S(2)}) collective-permute-start(bf16[2,12,18,8,128]{4,3,2,1,0:T(8,128)(2,1)} %get-tuple-element.6), channel_id=1, source_target_pairs={{0,1},{2,3},{4,5},{6,7},{8,9},{10,11},{12,13},{14,15},{16,17},{18,... | collective-permute-start | bytes 2654216 | tf_op jit(solution)/shard_map/ppermute | solution.py:12
  104.9 1.6 fusion.44
  106.5 11.8 %collective-permute-done.10 = bf16[2,12,18,8,128]{4,3,2,1,0:T(8,128)(2,1)} collective-permute-done((bf16[2,12,18,8,128]{4,3,2,1,0:T(8,128)(2,1)}, bf16[2,12,18,8,128]{4,3,2,1,0:T(8,128)(2,1)}, u32[]{:S(2)}, u32[]{:S(2)}) %collective-permute-start.10) | collective-permute-done | bytes 884768 | tf_op jit(solution)/shard_map/ppermute | solution.py:12
  118.2 2.1 collective-permute-done.11
  120.5 2.3 fusion.20
  123.0 1.4 copy-done.2
  124.4 1.1 fusion.40
  125.5 1.3 collective-permute-start.12
  126.8 1.3 collective-permute-start.13
  128.1 5.3 %collective-permute-start.14 = (bf16[2,12,6,8,128]{4,3,2,1,0:T(8,128)(2,1)}, bf16[2,12,6,8,128]{4,3,2,1,0:T(8,128)(2,1)}, u32[]{:S(2)}, u32[]{:S(2)}) collective-permute-start(bf16[2,12,6,8,128]{4,3,2,1,0:T(8,128)(2,1)} %get-tuple-element.17), channel_id=1, source_target_pairs={{0,2},{2,4},{4,6},{1,3},{3,5},{5,7},{8,10},{10,12},{12,14},{9,11},... | collective-permute-start | bytes 884744 | tf_op jit(solution)/shard_map/ppermute | solution.py:12
  133.3 5.5 %collective-permute-start.15 = (bf16[2,12,6,8,128]{4,3,2,1,0:T(8,128)(2,1)}, bf16[2,12,6,8,128]{4,3,2,1,0:T(8,128)(2,1)}, u32[]{:S(2)}, u32[]{:S(2)}) collective-permute-start(bf16[2,12,6,8,128]{4,3,2,1,0:T(8,128)(2,1)} %get-tuple-element.16), channel_id=1, source_target_pairs={{0,4},{2,6},{1,5},{3,7},{8,12},{10,14},{9,13},{11,15},{16,20},{18,... | collective-permute-start | bytes 884744 | tf_op jit(solution)/shard_map/ppermute | solution.py:12
  138.8 0.9 fusion.23
  139.7 1.5 convolution_convert_fusion
  141.2 2.3 collective-permute-done.15
  143.6 1.4 fusion.28
  145.1 1.3 collective-permute-start.16
  146.4 1.3 collective-permute-start.17
  147.7 3.0 %collective-permute-start.18 = (bf16[2,4,6,8,128]{4,3,2,1,0:T(8,128)(2,1)S(1)}, bf16[2,4,6,8,128]{4,3,2,1,0:T(8,128)(2,1)S(1)}, u32[]{:S(2)}, u32[]{:S(2)}) collective-permute-start(bf16[2,4,6,8,128]{4,3,2,1,0:T(8,128)(2,1)S(1)} %get-tuple-element.21), channel_id=1, source_target_pairs={{0,8},{8,16},{16,24},{1,9},{9,17},{17,25},{2,10},{10,18},{18,26},{... | collective-permute-start | bytes 294920 | tf_op jit(solution)/shard_map/ppermute | solution.py:12
  150.8 4.6 %collective-permute-start.19 = (bf16[2,4,6,8,128]{4,3,2,1,0:T(8,128)(2,1)S(1)}, bf16[2,4,6,8,128]{4,3,2,1,0:T(8,128)(2,1)S(1)}, u32[]{:S(2)}, u32[]{:S(2)}) collective-permute-start(bf16[2,4,6,8,128]{4,3,2,1,0:T(8,128)(2,1)S(1)} %get-tuple-element.20), channel_id=1, source_target_pairs={{0,16},{8,24},{1,17},{9,25},{2,18},{10,26},{3,19},{11,27},{4,20},{... | collective-permute-start | bytes 294920 | tf_op jit(solution)/shard_map/ppermute | solution.py:12
  155.3 115.6 %all-reduce.2.cloned.1.call-done = f32[128,3072]{1,0:T(8,128)} async-done(((f32[128,3072]{1,0:T(8,128)}), f32[128,3072]{1,0:T(8,128)}) %all-reduce.2.cloned.1.call-update) | async-done | bytes 1572880 | tf_op jit(solution)/shard_map/psum | solution.py:166
  271.0 2.7 broadcast_multiply_fusion
  273.8 0.6 slice_bitcast_fusion
  (51 shorter events, 4.0 us)
Async XLA Ops:
  7.2 54.7 %copy-start = (bf16[4,6,8,3072]{3,2,1,0:T(8,128)(2,1)S(1)}, bf16[4,6,8,3072]{3,2,1,0:T(8,128)(2,1)}, u32[]{:S(2)}) copy-start(bf16[4,6,8,3072]{3,2,1,0:T(8,128)(2,1)} %param.9) | copy-start | bytes 3538948
  7.2 263.8 %all-reduce.2.cloned.1.call-start = ((), (), s32[]{:S(2)}) async-start(), calls=%async_computation | async-start | bytes 3145728 | tf_op jit(solution)/shard_map/psum | solution.py:166
  8.1 8.9 %collective-permute-start = (bf16[2,4,6,8,128]{4,3,2,1,0:T(8,128)(2,1)S(1)}, bf16[2,4,6,8,128]{4,3,2,1,0:T(8,128)(2,1)S(1)}, u32[]{:S(2)}, u32[]{:S(2)}) collective-permute-start(bf16[2,4,6,8,128]{4,3,2,1,0:T(8,128)(2,1)S(1)} %pad_maximum_fusion.2), channel_id=1, source_target_pairs={{0,16},{8,24},{1,17},{9,25},{2,18},{10,26},{3,19},{11,27},{4,20},{... | collective-permute-start | bytes 294920 | tf_op jit(solution)/shard_map/ppermute | solution.py:12
  13.0 4.1 %collective-permute-start.1 = (bf16[2,4,6,8,128]{4,3,2,1,0:T(8,128)(2,1)S(1)}, bf16[2,4,6,8,128]{4,3,2,1,0:T(8,128)(2,1)S(1)}, u32[]{:S(2)}, u32[]{:S(2)}) collective-permute-start(bf16[2,4,6,8,128]{4,3,2,1,0:T(8,128)(2,1)S(1)} %pad_maximum_fusion.2), channel_id=1, source_target_pairs={{0,8},{8,16},{16,24},{1,9},{9,17},{17,25},{2,10},{10,18},{18,26},{... | collective-permute-start | bytes 294920 | tf_op jit(solution)/shard_map/ppermute | solution.py:12
  14.5 3.5 %collective-permute-start.2 = (bf16[2,4,6,8,128]{4,3,2,1,0:T(8,128)(2,1)S(1)}, bf16[2,4,6,8,128]{4,3,2,1,0:T(8,128)(2,1)S(1)}, u32[]{:S(2)}, u32[]{:S(2)}) collective-permute-start(bf16[2,4,6,8,128]{4,3,2,1,0:T(8,128)(2,1)S(1)} %pad_maximum_fusion.2), channel_id=1, source_target_pairs={{8,0},{16,8},{24,16},{9,1},{17,9},{25,17},{10,2},{18,10},{26,18},{... | collective-permute-start | bytes 294920 | tf_op jit(solution)/shard_map/ppermute | solution.py:12
  15.8 7.4 %collective-permute-start.3 = (bf16[2,4,6,8,128]{4,3,2,1,0:T(8,128)(2,1)S(1)}, bf16[2,4,6,8,128]{4,3,2,1,0:T(8,128)(2,1)S(1)}, u32[]{:S(2)}, u32[]{:S(2)}) collective-permute-start(bf16[2,4,6,8,128]{4,3,2,1,0:T(8,128)(2,1)S(1)} %pad_maximum_fusion.2), channel_id=1, source_target_pairs={{16,0},{24,8},{17,1},{25,9},{18,2},{26,10},{19,3},{27,11},{20,4},{... | collective-permute-start | bytes 294920 | tf_op jit(solution)/shard_map/ppermute | solution.py:12
  23.2 11.9 %collective-permute-start.4 = (bf16[2,12,6,8,128]{4,3,2,1,0:T(8,128)(2,1)S(1)}, bf16[2,12,6,8,128]{4,3,2,1,0:T(8,128)(2,1)S(1)}, u32[]{:S(2)}, u32[]{:S(2)}) collective-permute-start(bf16[2,12,6,8,128]{4,3,2,1,0:T(8,128)(2,1)S(1)} %constant_dynamic-slice_fusion.9), channel_id=1, source_target_pairs={{0,4},{2,6},{1,5},{3,7},{8,12},{10,14},{9,13},{11,15},{16,20},{18,... | collective-permute-start | bytes 884744 | tf_op jit(solution)/shard_map/ppermute | solution.py:12
  27.8 12.9 %collective-permute-start.5 = (bf16[2,12,6,8,128]{4,3,2,1,0:T(8,128)(2,1)S(1)}, bf16[2,12,6,8,128]{4,3,2,1,0:T(8,128)(2,1)S(1)}, u32[]{:S(2)}, u32[]{:S(2)}) collective-permute-start(bf16[2,12,6,8,128]{4,3,2,1,0:T(8,128)(2,1)S(1)} %constant_dynamic-slice_fusion.9), channel_id=1, source_target_pairs={{0,2},{2,4},{4,6},{1,3},{3,5},{5,7},{8,10},{10,12},{12,14},{9,11},... | collective-permute-start | bytes 884744 | tf_op jit(solution)/shard_map/ppermute | solution.py:12
  31.3 10.6 %collective-permute-start.6 = (bf16[2,12,6,8,128]{4,3,2,1,0:T(8,128)(2,1)S(1)}, bf16[2,12,6,8,128]{4,3,2,1,0:T(8,128)(2,1)S(1)}, u32[]{:S(2)}, u32[]{:S(2)}) collective-permute-start(bf16[2,12,6,8,128]{4,3,2,1,0:T(8,128)(2,1)S(1)} %constant_dynamic-slice_fusion.9), channel_id=1, source_target_pairs={{2,0},{4,2},{6,4},{3,1},{5,3},{7,5},{10,8},{12,10},{14,12},{11,9},... | collective-permute-start | bytes 884744 | tf_op jit(solution)/shard_map/ppermute | solution.py:12
  32.6 21.4 %collective-permute-start.7 = (bf16[2,12,6,8,128]{4,3,2,1,0:T(8,128)(2,1)S(1)}, bf16[2,12,6,8,128]{4,3,2,1,0:T(8,128)(2,1)S(1)}, u32[]{:S(2)}, u32[]{:S(2)}) collective-permute-start(bf16[2,12,6,8,128]{4,3,2,1,0:T(8,128)(2,1)S(1)} %constant_dynamic-slice_fusion.9), channel_id=1, source_target_pairs={{4,0},{6,2},{5,1},{7,3},{12,8},{14,10},{13,9},{15,11},{20,16},{22,... | collective-permute-start | bytes 884744 | tf_op jit(solution)/shard_map/ppermute | solution.py:12
  42.0 19.9 %copy-start.3 = (bf16[128,3072]{1,0:T(8,128)(2,1)S(1)}, bf16[128,3072]{1,0:T(8,128)(2,1)}, u32[]{:S(2)}) copy-start(bf16[128,3072]{1,0:T(8,128)(2,1)} %param.8) | copy-start | bytes 2359300
  54.0 1.1 copy-start.4
  56.1 21.8 %collective-permute-start.8 = (bf16[2,12,18,8,128]{4,3,2,1,0:T(8,128)(2,1)}, bf16[2,12,18,8,128]{4,3,2,1,0:T(8,128)(2,1)}, u32[]{:S(2)}, u32[]{:S(2)}) collective-permute-start(bf16[2,12,18,8,128]{4,3,2,1,0:T(8,128)(2,1)} %constant_dynamic-slice_fusion.8), channel_id=1, source_target_pairs={{0,1},{2,3},{4,5},{6,7},{8,9},{10,11},{12,13},{14,15},{16,17},{18,... | collective-permute-start | bytes 2654216 | tf_op jit(solution)/shard_map/ppermute | solution.py:12
  60.5 22.3 %collective-permute-start.9 = (bf16[2,12,18,8,128]{4,3,2,1,0:T(8,128)(2,1)}, bf16[2,12,18,8,128]{4,3,2,1,0:T(8,128)(2,1)S(1)}, u32[]{:S(2)}, u32[]{:S(2)}) collective-permute-start(bf16[2,12,18,8,128]{4,3,2,1,0:T(8,128)(2,1)} %constant_dynamic-slice_fusion.8), channel_id=1, source_target_pairs={{1,0},{3,2},{5,4},{7,6},{9,8},{11,10},{13,12},{15,14},{17,16},{19,... | collective-permute-start | bytes 2654216 | tf_op jit(solution)/shard_map/ppermute | solution.py:12
  61.9 17.4 %copy-start.5 = (bf16[2,12,30,8,128]{4,3,2,1,0:T(8,128)(2,1)S(1)}, bf16[2,12,30,8,128]{4,3,2,1,0:T(8,128)(2,1)}, u32[]{:S(2)}) copy-start(bf16[2,12,30,8,128]{4,3,2,1,0:T(8,128)(2,1)} %copy-done.4) | copy-start | bytes 4423684
  83.3 0.8 copy-start.6
  91.7 3.4 %copy-start.1 = (f32[2,12,18,40,128]{4,3,2,1,0:T(8,128)}, f32[2,12,18,40,128]{4,3,2,1,0:T(8,128)S(1)}, u32[]{:S(2)}) copy-start(f32[2,12,18,40,128]{4,3,2,1,0:T(8,128)S(1)} %maximum_dynamic-update-slice_fusion) | copy-start | bytes 26542084
  96.7 21.5 %collective-permute-start.10 = (bf16[2,12,18,8,128]{4,3,2,1,0:T(8,128)(2,1)}, bf16[2,12,18,8,128]{4,3,2,1,0:T(8,128)(2,1)}, u32[]{:S(2)}, u32[]{:S(2)}) collective-permute-start(bf16[2,12,18,8,128]{4,3,2,1,0:T(8,128)(2,1)} %get-tuple-element.5), channel_id=1, source_target_pairs={{1,0},{3,2},{5,4},{7,6},{9,8},{11,10},{13,12},{15,14},{17,16},{19,... | collective-permute-start | bytes 2654216 | tf_op jit(solution)/shard_map/ppermute | solution.py:12
  98.0 22.4 %collective-permute-start.11 = (bf16[2,12,18,8,128]{4,3,2,1,0:T(8,128)(2,1)}, bf16[2,12,18,8,128]{4,3,2,1,0:T(8,128)(2,1)}, u32[]{:S(2)}, u32[]{:S(2)}) collective-permute-start(bf16[2,12,18,8,128]{4,3,2,1,0:T(8,128)(2,1)} %get-tuple-element.6), channel_id=1, source_target_pairs={{0,1},{2,3},{4,5},{6,7},{8,9},{10,11},{12,13},{14,15},{16,17},{18,... | collective-permute-start | bytes 2654216 | tf_op jit(solution)/shard_map/ppermute | solution.py:12
  122.8 1.6 copy-start.2
  125.5 15.7 %collective-permute-start.12 = (bf16[2,12,6,8,128]{4,3,2,1,0:T(8,128)(2,1)}, bf16[2,12,6,8,128]{4,3,2,1,0:T(8,128)(2,1)S(1)}, u32[]{:S(2)}, u32[]{:S(2)}) collective-permute-start(bf16[2,12,6,8,128]{4,3,2,1,0:T(8,128)(2,1)} %get-tuple-element.15), channel_id=1, source_target_pairs={{4,0},{6,2},{5,1},{7,3},{12,8},{14,10},{13,9},{15,11},{20,16},{22,... | collective-permute-start | bytes 884744 | tf_op jit(solution)/shard_map/ppermute | solution.py:12
  126.8 14.5 %collective-permute-start.13 = (bf16[2,12,6,8,128]{4,3,2,1,0:T(8,128)(2,1)}, bf16[2,12,6,8,128]{4,3,2,1,0:T(8,128)(2,1)S(1)}, u32[]{:S(2)}, u32[]{:S(2)}) collective-permute-start(bf16[2,12,6,8,128]{4,3,2,1,0:T(8,128)(2,1)} %get-tuple-element.18), channel_id=1, source_target_pairs={{2,0},{4,2},{6,4},{3,1},{5,3},{7,5},{10,8},{12,10},{14,12},{11,9},... | collective-permute-start | bytes 884744 | tf_op jit(solution)/shard_map/ppermute | solution.py:12
  128.1 13.2 %collective-permute-start.14 = (bf16[2,12,6,8,128]{4,3,2,1,0:T(8,128)(2,1)}, bf16[2,12,6,8,128]{4,3,2,1,0:T(8,128)(2,1)}, u32[]{:S(2)}, u32[]{:S(2)}) collective-permute-start(bf16[2,12,6,8,128]{4,3,2,1,0:T(8,128)(2,1)} %get-tuple-element.17), channel_id=1, source_target_pairs={{0,2},{2,4},{4,6},{1,3},{3,5},{5,7},{8,10},{10,12},{12,14},{9,11},... | collective-permute-start | bytes 884744 | tf_op jit(solution)/shard_map/ppermute | solution.py:12
  133.3 10.2 %collective-permute-start.15 = (bf16[2,12,6,8,128]{4,3,2,1,0:T(8,128)(2,1)}, bf16[2,12,6,8,128]{4,3,2,1,0:T(8,128)(2,1)}, u32[]{:S(2)}, u32[]{:S(2)}) collective-permute-start(bf16[2,12,6,8,128]{4,3,2,1,0:T(8,128)(2,1)} %get-tuple-element.16), channel_id=1, source_target_pairs={{0,4},{2,6},{1,5},{3,7},{8,12},{10,14},{9,13},{11,15},{16,20},{18,... | collective-permute-start | bytes 884744 | tf_op jit(solution)/shard_map/ppermute | solution.py:12
  145.1 128.5 %collective-permute-start.16 = (bf16[2,4,6,8,128]{4,3,2,1,0:T(8,128)(2,1)S(1)}, bf16[2,4,6,8,128]{4,3,2,1,0:T(8,128)(2,1)S(1)}, u32[]{:S(2)}, u32[]{:S(2)}) collective-permute-start(bf16[2,4,6,8,128]{4,3,2,1,0:T(8,128)(2,1)S(1)} %get-tuple-element.19), channel_id=1, source_target_pairs={{16,0},{24,8},{17,1},{25,9},{18,2},{26,10},{19,3},{27,11},{20,4},{... | collective-permute-start | bytes 294920 | tf_op jit(solution)/shard_map/ppermute | solution.py:12
  146.4 127.3 %collective-permute-start.17 = (bf16[2,4,6,8,128]{4,3,2,1,0:T(8,128)(2,1)S(1)}, bf16[2,4,6,8,128]{4,3,2,1,0:T(8,128)(2,1)S(1)}, u32[]{:S(2)}, u32[]{:S(2)}) collective-permute-start(bf16[2,4,6,8,128]{4,3,2,1,0:T(8,128)(2,1)S(1)} %get-tuple-element.22), channel_id=1, source_target_pairs={{8,0},{16,8},{24,16},{9,1},{17,9},{25,17},{10,2},{18,10},{26,18},{... | collective-permute-start | bytes 294920 | tf_op jit(solution)/shard_map/ppermute | solution.py:12
  147.7 126.0 %collective-permute-start.18 = (bf16[2,4,6,8,128]{4,3,2,1,0:T(8,128)(2,1)S(1)}, bf16[2,4,6,8,128]{4,3,2,1,0:T(8,128)(2,1)S(1)}, u32[]{:S(2)}, u32[]{:S(2)}) collective-permute-start(bf16[2,4,6,8,128]{4,3,2,1,0:T(8,128)(2,1)S(1)} %get-tuple-element.21), channel_id=1, source_target_pairs={{0,8},{8,16},{16,24},{1,9},{9,17},{17,25},{2,10},{10,18},{18,26},{... | collective-permute-start | bytes 294920 | tf_op jit(solution)/shard_map/ppermute | solution.py:12
  150.8 122.9 %collective-permute-start.19 = (bf16[2,4,6,8,128]{4,3,2,1,0:T(8,128)(2,1)S(1)}, bf16[2,4,6,8,128]{4,3,2,1,0:T(8,128)(2,1)S(1)}, u32[]{:S(2)}, u32[]{:S(2)}) collective-permute-start(bf16[2,4,6,8,128]{4,3,2,1,0:T(8,128)(2,1)S(1)} %get-tuple-element.20), channel_id=1, source_target_pairs={{0,16},{8,24},{1,17},{9,25},{2,18},{10,26},{3,19},{11,27},{4,20},{... | collective-permute-start | bytes 294920 | tf_op jit(solution)/shard_map/ppermute | solution.py:12
Sparse Core Ops, SparseCore 0:
  139.9 131.0 all-reduce.1
where the time goes:
time: 282 us; the launch traced here: 281 us
  waiting for transfers between devices  176 us (62%)
  starting transfers between devices  56.3 us (20%)
  between operations  14.6 us (5%)
  local copies, waits for them, and re-layouts  14 us (5%)
  matrix products  10.4 us (4%)
  other arithmetic  10.2 us (4%)
    psum x1, waiting for transfers between devices, body(): lax.psum(weight_term, ('frame', 'height', 'width')) / float(tile_count)  116 us
    ppermute x20, waiting for transfers between devices, shifted(): return lax.ppermute(block, axis, route)  60.1 us
    ppermute x20, starting transfers between devices, shifted(): return lax.ppermute(block, axis, route)  56.3 us
    unnamed x25, local copies, waits for them, and re-layouts  7.92 us
  transfers between devices with their start and end apart: 21, of which 11 were waited for; matrix products, arithmetic and copies ran while one was open for 4% of the time, Pallas kernels for 0%

commit v1 on v0

v1 whole, which is shorter than its diff:
```python
import math

import jax
import jax.numpy as jnp
from jax import lax
from jax.sharding import PartitionSpec as P

AXES = ("frame", "height", "width")


def window_of(position, extent):
    span = min(3, extent)
    start = max(0, min(position - 1, extent - 3))
    return range(start, start + span)


def routes_of(extent):
    first = [(p ^ 1, p) for p in range(extent) if (p ^ 1) in window_of(p, extent)]
    if extent > 4:
        first = [(p + 1, p) for p in range(extent - 1)]
    wanted = [(s, p) for p in range(extent) for s in window_of(p, extent) if s != p]
    routes = [first]
    for pair in wanted:
        if pair in first:
            continue
        for route in routes[1:]:
            if all(pair[0] != s and pair[1] != p for s, p in route):
                route.append(pair)
                break
        else:
            routes.append([pair])
    return [route for route in routes if route]


def slots_of(extent):
    routes = routes_of(extent)
    arrivals = [[c for c, r in enumerate(routes) if any(q == p for _, q in r)] for p in range(extent)]
    return [[arrivals[p][k] for p in range(extent)] for k in range(min(3, extent) - 1)]


def chosen(options, choice, axis):
    value = options[choice[0]]
    for option in sorted(set(choice)):
        if option != choice[0]:
            here = jnp.array([c == option for c in choice])[lax.axis_index(axis)]
            value = jnp.where(here, options[option], value)
    return value


def give_back(pieces, axis):
    extent = lax.axis_size(axis)
    slots = slots_of(extent)
    summed = pieces[0]
    for c, route in enumerate(routes_of(extent)):
        holders = [next((k for k in range(len(slots)) if slots[k][p] == c), None) for p in range(extent)]
        used = sorted({k for k in holders if k is not None})
        choice = [k if k is not None else used[0] for k in holders]
        outgoing = chosen({k: pieces[k + 1] for k in used}, choice, axis).astype(jnp.bfloat16)
        back = lax.ppermute(outgoing, axis, [(p, s) for s, p in route])
        summed = summed + back.astype(jnp.float32)
    return summed


def sum_everywhere(term):
    rows, columns = term.shape
    plane = lax.axis_size("frame") * lax.axis_size("width")
    column = lax.axis_size("height")
    part = term.astype(jnp.bfloat16).reshape(plane, rows // plane, columns)
    part = lax.all_to_all(part, ("frame", "width"), 0, 0)
    part = jnp.sum(part.astype(jnp.float32), axis=0).astype(jnp.bfloat16)
    part = part.reshape(rows // plane, column, columns // column).transpose(1, 0, 2)
    part = lax.all_to_all(part, "height", 0, 0)
    part = jnp.sum(part.astype(jnp.float32), axis=0).astype(jnp.bfloat16)
    whole = lax.all_gather(part, ("frame", "width", "height"))
    whole = whole.reshape(plane, column, rows // plane, columns // column)
    return whole.transpose(0, 2, 1, 3).reshape(rows, columns).astype(jnp.float32)


def body(queries, key_vectors, value_vectors, out_weight, projected_grad):
    head_dim = queries.shape[-1]
    model_dim = out_weight.shape[1]
    inv_root = 1.0 / math.sqrt(head_dim)
    extents = tuple(lax.axis_size(axis) for axis in AXES)
    spans = tuple(min(3, extent) for extent in extents)
    query_rows = queries.reshape(-1, head_dim)
    grad_rows = projected_grad.reshape(-1, model_dim)
    tile = query_rows.shape[0]
    own = jnp.stack((key_vectors.reshape(tile, head_dim), value_vectors.reshape(tile, head_dim)))
    everything = lax.all_gather(own, AXES).reshape(extents + (2, tile, head_dim))
    starts = [
        jnp.maximum(jnp.minimum(lax.axis_index(axis) - 1, lax.axis_size(axis) - 3), 0) for axis in AXES
    ]
    window = lax.dynamic_slice(everything, (*starts, 0, 0, 0), spans + (2, tile, head_dim))
    key_rows = window[:, :, :, 0].reshape(-1, head_dim)
    value_rows = window[:, :, :, 1].reshape(-1, head_dim)
    attended_grad = jnp.einsum(
        "tm,dm->td", grad_rows, out_weight, preferred_element_type=jnp.float32
    ).astype(jnp.bfloat16)
    scores = (
        jnp.einsum("qd,kd->qk", query_rows, key_rows, preferred_element_type=jnp.float32) * inv_root
    )
    row_max = jnp.max(scores, axis=1, keepdims=True)
    weights = jnp.exp(scores - row_max)
    probability = weights / jnp.sum(weights, axis=1, keepdims=True)
    prob_bf = probability.astype(jnp.bfloat16)
    attended = jnp.dot(prob_bf, value_rows, preferred_element_type=jnp.float32).astype(jnp.bfloat16)
    weight_term = jnp.einsum("td,tm->dm", attended, grad_rows, preferred_element_type=jnp.float32)
    tile_count = math.prod(extents)
    grad_out_weight = sum_everywhere(weight_term * (1.0 / float(tile_count)))
    projected = (
        jnp.dot(attended, out_weight, preferred_element_type=jnp.float32)
        .astype(jnp.bfloat16)
        .reshape(projected_grad.shape)
    )
    row_dot = jnp.sum(
        attended_grad.astype(jnp.float32) * attended.astype(jnp.float32), axis=1, keepdims=True
    )
    prob_grad = jnp.einsum(
        "qd,kd->qk", attended_grad, value_rows, preferred_element_type=jnp.float32
    )
    score_grad = (probability * (prob_grad - row_dot)).astype(jnp.bfloat16)
    query_grad = jnp.dot(score_grad, key_rows, preferred_element_type=jnp.float32)
    grad_query = (query_grad * inv_root).astype(jnp.bfloat16).reshape(queries.shape)
    key_grad = (
        jnp.einsum("qk,qd->kd", score_grad, query_rows, preferred_element_type=jnp.float32)
        * inv_root
    )
    value_grad = jnp.einsum("qk,qd->kd", prob_bf, attended_grad, preferred_element_type=jnp.float32)
    grads = jnp.stack((key_grad, value_grad)).reshape((2,) + spans + (tile, head_dim))
    for dim, axis in ((3, "width"), (2, "height"), (1, "frame")):
        extent = lax.axis_size(axis)
        position = lax.axis_index(axis)
        slots = slots_of(extent)
        routes = routes_of(extent)
        orders = [[list(window_of(p, extent)).index(p) for p in range(extent)]]
        for slot in slots:
            senders = [next(s for s, q in routes[slot[p]] if q == p) for p in range(extent)]
            orders.append([list(window_of(p, extent)).index(senders[p]) for p in range(extent)])
        pieces = [
            lax.dynamic_index_in_dim(grads, jnp.array(order)[position], dim, keepdims=False)
            for order in orders
        ]
        grads = give_back(pieces, axis)
    grad_key = grads[0].astype(jnp.bfloat16).reshape(key_vectors.shape)
    grad_value = grads[1].astype(jnp.bfloat16).reshape(value_vectors.shape)
    return (projected, grad_query, grad_key, grad_value, grad_out_weight)


def solution(mesh):
    tokens = P("frame", "height", "width", None)
    return jax.shard_map(
        body,
        mesh=mesh,
        in_specs=(tokens, tokens, tokens, P(), tokens),
        out_specs=(tokens, tokens, tokens, tokens, P()),
        check_vma=False,
    )
```

time: 282 us -> 222 us (0.79)
  waiting for transfers between devices: 176 us -> 62.9 us
  blocking collectives: 0 us -> 80 us
  starting transfers between devices: 56.3 us -> 20.1 us
  between operations: 14.6 us -> 27.9 us
  local copies, waits for them, and re-layouts: 14 us -> 8.39 us
    psum x1 -> x0, waiting for transfers between devices: 116 us -> none  [body(): lax.psum(weight_term, ('frame', 'height', 'width')) / float(tile_count)]
    all_gather x0 -> x1, blocking collectives: none -> 80 us  [sum_everywhere(): whole = lax.all_gather(part, ('frame', 'width', 'height'))]
    ppermute x20 -> x7, waiting for transfers between devices: 60.1 us -> 0.02 us  [give_back(): back = lax.ppermute(outgoing, axis, [(p, s) for s, p in route])]
    all_gather x0 -> x1, waiting for transfers between devices: none -> 59.7 us  [body(): lax.all_gather(own, AXES).reshape(extents + (2, tile, head_dim))]
    ppermute x20 -> x7, starting transfers between devices: 56.3 us -> 12.4 us  [give_back(): back = lax.ppermute(outgoing, axis, [(p, s) for s, p in route])]
    all_to_all x0 -> x2, starting transfers between devices: none -> 7.66 us  [the longest x1 4.23 us: sum_everywhere(): part = lax.all_to_all(part, ('frame', 'width'), 0, 0)]
    unnamed x25 -> x15, local copies, waits for them, and re-layouts: 7.92 us -> 1.74 us
    dynamic_update_slice x3 -> x0, other arithmetic: 4.08 us -> none  [place_window(): lax.dynamic_update_slice_in_dim(blanks, window_grads, start_tile * tile_l...]
  transfers between devices with their start and end apart: 21 -> 10, of which waited for: 11 -> 2; matrix products, arithmetic and copies ran while one was open for 4% -> 7% of each run, Pallas kernels for 0% -> 0%
where the time goes in v1:
time: 222 us; the launch traced here: 220 us
  blocking collectives  80 us (36%)
  waiting for transfers between devices  62.9 us (28%)
  between operations  27.9 us (13%)
  starting transfers between devices  20.1 us (9%)
  matrix products  13.2 us (6%)
  local copies, waits for them, and re-layouts  8.39 us (4%)
  other arithmetic  7.52 us (3%)
    all_gather x1, blocking collectives, sum_everywhere(): whole = lax.all_gather(part, ('frame', 'width', 'height'))  80 us
    all_gather x1, waiting for transfers between devices, body(): lax.all_gather(own, AXES).reshape(extents + (2, tile, head_dim))  59.7 us
    ppermute x7, starting transfers between devices, give_back(): back = lax.ppermute(outgoing, axis, [(p, s) for s, p in route])  12.4 us
  transfers between devices with their start and end apart: 10, of which 2 were waited for; matrix products, arithmetic and copies ran while one was open for 7% of the time, Pallas kernels for 0%

profile of v1, /device:TPU:0, one launch (start us, length us, event | category | flops | bytes accessed | tf_op | source)
XLA Modules:
  0.0 220.1 jit_solution(14337104214083219339)
XLA Ops:
  7.2 0.0 copy-start
  7.2 0.0 all-gather.4.cloned.1.call-start
  7.2 1.6 pad_maximum_fusion
  8.8 0.0 all-gather.4.cloned.1.call-update
  8.8 1.2 dynamic_slice.58
  12.0 0.0 copy-done
  12.0 1.6 convolution_convert_fusion.1
  13.6 59.7 %all-gather.4.cloned.1.call-done = bf16[64,192,128]{2,1,0:T(8,128)(2,1)} async-done(((bf16[2,192,128]{2,1,0:T(8,128)(2,1)}), bf16[64,192,128]{2,1,0:T(8,128)(2,1)}) %all-gather.4.cloned.1.call-update) | async-done | bytes 3145744 | tf_op jit(solution)/shard_map/all_gather | solution.py:89
  73.3 0.0 copy-start.3
  73.3 1.6 constant_dynamic-slice_fusion
  74.9 0.0 copy-start.1
  74.9 0.0 copy-done.3
  74.9 0.6 fusion.28
  75.5 0.3 copy-done.1
  75.8 0.5 fusion.4
  76.3 2.1 fusion.12
  78.5 0.8 multiply_reduce_fusion
  79.3 0.8 fusion.1
  80.1 0.0 copy-start.2
  80.1 0.7 convolution_multiply_fusion.1
  80.8 1.3 fusion.2
  82.1 0.0 copy-done.2
  82.1 4.2 %all-to-all-start = ((bf16[8,16,3072]{2,1,0:T(8,128)(2,1)}), bf16[8,16,3072]{2,1,0:T(8,128)(2,1)}, u32[]{:S(2)}, u32[]{:S(2)}) async-start(bf16[8,16,3072]{2,1,0:T(8,128)(2,1)} %bitcast.97), calls=%async_computation | async-start | bytes 1572864 | tf_op jit(solution)/shard_map/all_to_all | solution.py:69
  86.3 0.0 copy-start.5
  86.3 0.0 copy-start.6
  86.3 0.0 copy-start.4
  86.3 2.2 %fusion.11 = bf16[2,3,3,192,128]{4,3,2,1,0:T(8,128)(2,1)} fusion(s32[]{:T(128)S(6)} %select_n.46, f32[1,3,3,2,192,128]{5,4,3,2,1,0:T(8,128)} %bitcast.94, f32[1,3,3,2,192,128]{5,4,3,2,1,0:T(8,128)S(1)} %bitcast.90), kind=kLoop, calls=%fused_computation.26 | loop fusion | flops 442368 | bytes 4423684 | tf_op jit(solution)/shard_map/convert_element_type | solution.py:58
  88.6 1.9 collective-permute-start
  90.4 0.0 copy-done.5
  90.4 0.0 copy-done.6
  90.4 0.7 fusion.25
  92.4 0.0 copy-done.4
  92.4 0.7 fusion.27
  103.5 2.7 %fusion.10 = bf16[192,128]{1,0:T(8,128)(2,1)} fusion(bf16[192,3456]{1,0:T(8,128)(2,1)} %copy-done.2, bf16[3456,128]{1,0:T(8,128)(2,1)} %bitcast.93), kind=kOutput, calls=%fused_computation.25 | convolution fusion | flops 169918464 | bytes 2260992 | tf_op jit(solution)/shard_map/dot_general | solution.py:122
  106.2 0.0 all-to-all-done
  106.2 1.2 reduce_sum.44
  107.5 0.7 copy.30
  108.2 3.4 %all-to-all-start.1 = ((bf16[4,16,768]{2,1,0:T(8,128)(2,1)}), bf16[4,16,768]{2,1,0:T(8,128)(2,1)S(1)}, u32[]{:S(2)}, u32[]{:S(2)}) async-start(bf16[4,16,768]{2,1,0:T(8,128)(2,1)} %copy.30), calls=%async_computation.1 | async-start | bytes 196608 | tf_op jit(solution)/shard_map/all_to_all | solution.py:72
  111.6 2.6 %convolution_convert_fusion = bf16[192,3072]{1,0:T(8,128)(2,1)} fusion(bf16[192,128]{1,0:T(8,128)(2,1)S(1)} %get-tuple-element.22, bf16[128,3072]{1,0:T(8,128)(2,1)} %param.16), kind=kOutput, calls=%fused_computation.9 | convolution fusion | flops 151584768 | bytes 2015232 | tf_op jit(solution)/shard_map/dot_general | solution.py:111
  114.2 3.2 %all-to-all-done.1 = bf16[4,16,768]{2,1,0:T(8,128)(2,1)S(1)} async-done(((bf16[4,16,768]{2,1,0:T(8,128)(2,1)}), bf16[4,16,768]{2,1,0:T(8,128)(2,1)S(1)}, u32[]{:S(2)}, u32[]{:S(2)}) %all-to-all-start.1) | async-done | bytes 98336 | tf_op jit(solution)/shard_map/all_to_all | solution.py:72
  117.4 0.0 collective-permute-done
  117.5 1.6 fusion.9
  119.1 0.1 fusion.16
  119.2 0.7 collective-permute-start.3
  119.9 3.4 %collective-permute-start.2 = (bf16[2,3,192,128]{3,2,1,0:T(8,128)(2,1)S(1)}, bf16[2,3,192,128]{3,2,1,0:T(8,128)(2,1)S(1)}, u32[]{:S(2)}, u32[]{:S(2)}) collective-permute-start(bf16[2,3,192,128]{3,2,1,0:T(8,128)(2,1)S(1)} %get-tuple-element.8), channel_id=1, source_target_pairs={{0,4},{4,2},{1,5},{5,3},{8,12},{12,10},{9,13},{13,11},{16,20},{20,... | collective-permute-start | bytes 884744 | tf_op jit(solution)/shard_map/ppermute | solution.py:59
  123.2 0.6 collective-permute-start.1
  123.9 80.0 %all-gather.1 = bf16[512,768]{1,0:T(8,128)(2,1)S(1)} all-gather(bf16[16,768]{1,0:T(8,128)(2,1)S(1)} %reduce_sum.45), channel_id=3, replica_groups=mesh['frame'=4,'height'=4,'width'=2] {'frame','width','height'}, dimensions={0}, use_global_device_ids=true | all-gather | bytes 811008 | tf_op jit(solution)/shard_map/all_gather | solution.py:74
  203.8 0.0 collective-permute-done.3
  203.8 0.0 collective-permute-done.2
  203.8 0.0 collective-permute-done.1
  203.9 0.1 fusion.14
  204.0 0.7 collective-permute-start.6
  204.7 5.0 %collective-permute-start.5 = (bf16[2,192,128]{2,1,0:T(8,128)(2,1)S(1)}, bf16[2,192,128]{2,1,0:T(8,128)(2,1)S(1)}, u32[]{:S(2)}, u32[]{:S(2)}) collective-permute-start(bf16[2,192,128]{2,1,0:T(8,128)(2,1)S(1)} %get-tuple-element.10), channel_id=1, source_target_pairs={{0,16},{16,8},{1,17},{17,9},{2,18},{18,10},{3,19},{19,11},{4,20},{... | collective-permute-start | bytes 294920 | tf_op jit(solution)/shard_map/ppermute | solution.py:59
  209.7 0.2 collective-permute-start.4
  209.9 0.2 convert_bitcast_fusion
  210.1 1.0 copy.31
  211.1 1.4 copy.34
  212.5 0.0 collective-permute-done.6
  212.5 0.0 collective-permute-done.5
  212.5 0.0 collective-permute-done.4
  212.5 0.1 fusion.19
  212.6 0.6 fusion.24
  (3 shorter events, 0.1 us)
Async XLA Ops:
  7.2 4.9 %copy-start = (bf16[4,6,8,3072]{3,2,1,0:T(8,128)(2,1)S(1)}, bf16[4,6,8,3072]{3,2,1,0:T(8,128)(2,1)}, u32[]{:S(2)}) copy-start(bf16[4,6,8,3072]{3,2,1,0:T(8,128)(2,1)} %param.17) | copy-start | bytes 3538948
  7.2 66.1 %all-gather.4.cloned.1.call-start = ((), (), s32[]{:S(2)}) async-start(), calls=%async_computation.2 | async-start | bytes 3244032 | tf_op jit(solution)/shard_map/all_gather | solution.py:89
  73.3 1.6 copy-start.3
  74.9 0.9 copy-start.1
  80.1 2.0 copy-start.2
  82.1 24.1 %all-to-all-start = ((bf16[8,16,3072]{2,1,0:T(8,128)(2,1)}), bf16[8,16,3072]{2,1,0:T(8,128)(2,1)}, u32[]{:S(2)}, u32[]{:S(2)}) async-start(bf16[8,16,3072]{2,1,0:T(8,128)(2,1)} %bitcast.97), calls=%async_computation | async-start | bytes 1572864 | tf_op jit(solution)/shard_map/all_to_all | solution.py:69
  86.3 4.1 %copy-start.5 = (s32[4]{0:T(128)S(1)}, s32[4]{0:T(128)}, u32[]{:S(2)}) copy-start(s32[4]{0:T(128)} %constant.74.clone) | copy-start | bytes 52
  86.3 4.1 %copy-start.6 = (s32[4]{0:T(128)S(1)}, s32[4]{0:T(128)}, u32[]{:S(2)}) copy-start(s32[4]{0:T(128)} %constant.75.clone) | copy-start | bytes 52
  86.3 6.1 %copy-start.4 = (s32[4]{0:T(128)S(1)}, s32[4]{0:T(128)}, u32[]{:S(2)}) copy-start(s32[4]{0:T(128)} %constant.76.clone) | copy-start | bytes 52
  88.6 28.9 %collective-permute-start = (bf16[2,3,3,192,128]{4,3,2,1,0:T(8,128)(2,1)}, bf16[2,3,3,192,128]{4,3,2,1,0:T(8,128)(2,1)}, u32[]{:S(2)}, u32[]{:S(2)}) collective-permute-start(bf16[2,3,3,192,128]{4,3,2,1,0:T(8,128)(2,1)} %fusion.11), channel_id=1, source_target_pairs={{0,1},{1,0},{2,3},{3,2},{4,5},{5,4},{6,7},{7,6},{8,9},{9,8},{10,11... | collective-permute-start | bytes 2654216 | tf_op jit(solution)/shard_map/ppermute | solution.py:59
  108.2 9.3 %all-to-all-start.1 = ((bf16[4,16,768]{2,1,0:T(8,128)(2,1)}), bf16[4,16,768]{2,1,0:T(8,128)(2,1)S(1)}, u32[]{:S(2)}, u32[]{:S(2)}) async-start(bf16[4,16,768]{2,1,0:T(8,128)(2,1)} %copy.30), calls=%async_computation.1 | async-start | bytes 196608 | tf_op jit(solution)/shard_map/all_to_all | solution.py:72
  119.2 84.7 %collective-permute-start.3 = (bf16[2,3,192,128]{3,2,1,0:T(8,128)(2,1)S(1)}, bf16[2,3,192,128]{3,2,1,0:T(8,128)(2,1)S(1)}, u32[]{:S(2)}, u32[]{:S(2)}) collective-permute-start(bf16[2,3,192,128]{3,2,1,0:T(8,128)(2,1)S(1)} %get-tuple-element.8), channel_id=1, source_target_pairs={{2,4},{6,2},{3,5},{7,3},{10,12},{14,10},{11,13},{15,11},{18,20},{2... | collective-permute-start | bytes 884744 | tf_op jit(solution)/shard_map/ppermute | solution.py:59
  119.9 84.0 %collective-permute-start.2 = (bf16[2,3,192,128]{3,2,1,0:T(8,128)(2,1)S(1)}, bf16[2,3,192,128]{3,2,1,0:T(8,128)(2,1)S(1)}, u32[]{:S(2)}, u32[]{:S(2)}) collective-permute-start(bf16[2,3,192,128]{3,2,1,0:T(8,128)(2,1)S(1)} %get-tuple-element.8), channel_id=1, source_target_pairs={{0,4},{4,2},{1,5},{5,3},{8,12},{12,10},{9,13},{13,11},{16,20},{20,... | collective-permute-start | bytes 884744 | tf_op jit(solution)/shard_map/ppermute | solution.py:59
  123.2 80.6 %collective-permute-start.1 = (bf16[2,3,192,128]{3,2,1,0:T(8,128)(2,1)S(1)}, bf16[2,3,192,128]{3,2,1,0:T(8,128)(2,1)S(1)}, u32[]{:S(2)}, u32[]{:S(2)}) collective-permute-start(bf16[2,3,192,128]{3,2,1,0:T(8,128)(2,1)S(1)} %get-tuple-element.7), channel_id=1, source_target_pairs={{0,2},{2,0},{4,6},{6,4},{1,3},{3,1},{5,7},{7,5},{8,10},{10,8},{12,... | collective-permute-start | bytes 884744 | tf_op jit(solution)/shard_map/ppermute | solution.py:59
  204.0 8.5 %collective-permute-start.6 = (bf16[2,192,128]{2,1,0:T(8,128)(2,1)S(1)}, bf16[2,192,128]{2,1,0:T(8,128)(2,1)S(1)}, u32[]{:S(2)}, u32[]{:S(2)}) collective-permute-start(bf16[2,192,128]{2,1,0:T(8,128)(2,1)S(1)} %get-tuple-element.10), channel_id=1, source_target_pairs={{8,16},{24,8},{9,17},{25,9},{10,18},{26,10},{11,19},{27,11},{12,20... | collective-permute-start | bytes 294920 | tf_op jit(solution)/shard_map/ppermute | solution.py:59
  204.7 7.8 %collective-permute-start.5 = (bf16[2,192,128]{2,1,0:T(8,128)(2,1)S(1)}, bf16[2,192,128]{2,1,0:T(8,128)(2,1)S(1)}, u32[]{:S(2)}, u32[]{:S(2)}) collective-permute-start(bf16[2,192,128]{2,1,0:T(8,128)(2,1)S(1)} %get-tuple-element.10), channel_id=1, source_target_pairs={{0,16},{16,8},{1,17},{17,9},{2,18},{18,10},{3,19},{19,11},{4,20},{... | collective-permute-start | bytes 294920 | tf_op jit(solution)/shard_map/ppermute | solution.py:59
  209.7 2.8 %collective-permute-start.4 = (bf16[2,192,128]{2,1,0:T(8,128)(2,1)S(1)}, bf16[2,192,128]{2,1,0:T(8,128)(2,1)S(1)}, u32[]{:S(2)}, u32[]{:S(2)}) collective-permute-start(bf16[2,192,128]{2,1,0:T(8,128)(2,1)S(1)} %get-tuple-element.9), channel_id=1, source_target_pairs={{0,8},{8,0},{16,24},{24,16},{1,9},{9,1},{17,25},{25,17},{2,10},{10... | collective-permute-start | bytes 294920 | tf_op jit(solution)/shard_map/ppermute | solution.py:59
Sparse Core Ops, SparseCore 0:
  11.5 61.7 all-gather.3

commit v2 on v1

v2 whole, which is shorter than its diff:
```python
import functools
import math

import jax
import jax.numpy as jnp
from jax import lax
from jax.experimental import pallas as pl
from jax.experimental.pallas import tpu as pltpu
from jax.sharding import PartitionSpec as P

AXES = ("frame", "height", "width")
VMEM = pl.BlockSpec(memory_space=pltpu.VMEM)
SMEM = pl.BlockSpec(memory_space=pltpu.SMEM)
PARAMS = pltpu.CompilerParams(vmem_limit_bytes=24 * 1024 * 1024)
STAT_ROWS = 8


def window_of(position, extent):
    span = min(3, extent)
    start = max(0, min(position - 1, extent - 3))
    return range(start, start + span)


def routes_of(extent):
    first = [(p ^ 1, p) for p in range(extent) if (p ^ 1) in window_of(p, extent)]
    if extent > 4:
        first = [(p + 1, p) for p in range(extent - 1)]
    wanted = [(s, p) for p in range(extent) for s in window_of(p, extent) if s != p]
    wanted.sort(key=lambda pair: (pair[0] ^ pair[1], pair))
    routes = [first]
    for pair in wanted:
        if pair in first:
            continue
        for route in routes[1:]:
            if all(pair[0] != s and pair[1] != p for s, p in route):
                route.append(pair)
                break
        else:
            routes.append([pair])
    return [route for route in routes if route]


def slots_of(extent):
    routes = routes_of(extent)
    arrivals = [[c for c, r in enumerate(routes) if any(q == p for _, q in r)] for p in range(extent)]
    return [[arrivals[p][k] for p in range(extent)] for k in range(min(3, extent) - 1)]


def chosen(options, choice, axis):
    value = options[choice[0]]
    position = lax.axis_index(axis)
    for option in sorted(set(choice)):
        if option != choice[0]:
            here = functools.reduce(
                jnp.logical_or, [position == p for p, c in enumerate(choice) if c == option]
            )
            value = jnp.where(here, options[option], value)
    return value


def fetch(block, axis):
    extent = lax.axis_size(axis)
    routes = routes_of(extent)
    arrived = [lax.ppermute(block, axis, route) for route in routes]
    tiles = []
    for slot in slots_of(extent):
        used = sorted(set(slot))
        reached = sum(len(routes[c]) for c in used)
        if reached == extent:
            tiles.append(functools.reduce(jnp.add, [arrived[c] for c in used]))
        else:
            tiles.append(chosen(arrived, slot, axis))
    return tiles


def give_back(pieces, axis):
    extent = lax.axis_size(axis)
    slots = slots_of(extent)
    summed = pieces[0]
    for c, route in enumerate(routes_of(extent)):
        holders = [next((k for k in range(len(slots)) if slots[k][p] == c), None) for p in range(extent)]
        used = sorted({k for k in holders if k is not None})
        choice = [k if k is not None else used[0] for k in holders]
        outgoing = chosen({k: pieces[k + 1] for k in used}, choice, axis).astype(jnp.bfloat16)
        back = lax.ppermute(outgoing, axis, [(p, s) for s, p in route])
        summed = summed + back.astype(jnp.float32)
    return summed


def flip(block, axes, bits):
    sizes = [lax.axis_size(axis) for axis in axes]
    route = []
    for flat in range(math.prod(sizes)):
        rest, target, scale = flat, 0, 1
        for size, bit in zip(reversed(sizes), reversed(bits)):
            target += ((rest % size) ^ bit) * scale
            rest //= size
            scale *= size
        route.append((flat, target))
    return lax.ppermute(block, axes, route)


def rows_of(refs, part):
    block = refs[0][:, part]
    for ref in refs[1:]:
        block = block + ref[:, part]
    return block.reshape(-1, block.shape[-1])


def token_kernel(
    place, queries, queries_other, grads, weight, payload, grads_half, grad_rows, both_queries
):
    half = grads_half.shape[1]
    product = lax.dot_general(
        grads[...], weight[...], (((1,), (1,)), ((), ())), preferred_element_type=jnp.float32
    ).astype(jnp.bfloat16)
    grad_rows[...] = product
    payload[:, half:] = product
    payload[:, :half] = grads[:, pl.ds(pl.multiple_of((1 - place[0]) * half, half), half)]
    grads_half[...] = grads[:, pl.ds(pl.multiple_of(place[0] * half, half), half)]
    both_tiles(place, queries[...], queries_other[...], both_queries)


def both_tiles(place, mine, theirs, both):
    tile = mine.shape[0]
    both[pl.ds(pl.multiple_of(place[0] * tile, tile), tile), :] = mine
    both[pl.ds(pl.multiple_of((1 - place[0]) * tile, tile), tile), :] = theirs


def forward_kernel(inv_root, layout, place, both_queries, *refs):
    groups, rest = split_groups(layout, refs)
    partial, scores = rest
    dim = both_queries.shape[1]
    query_rows = both_queries[...]
    top = None
    start = 0
    spans = []
    for group in groups:
        keys = rows_of(group, 0)
        piece = lax.dot_general(
            keys, query_rows, (((1,), (1,)), ((), ())), preferred_element_type=jnp.float32
        )
        scores[start : start + keys.shape[0], :] = piece
        spans.append((start, keys.shape[0]))
        start += keys.shape[0]
        piece_top = jnp.max(piece, axis=0, keepdims=True)
        top = piece_top if top is None else jnp.maximum(top, piece_top)
    total = jnp.zeros_like(top)
    mixed = jnp.zeros((dim, query_rows.shape[0]), jnp.float32)
    for group, (start, count) in zip(groups, spans):
        weights = jnp.exp((scores[start : start + count, :] - top) * inv_root)
        total = total + jnp.sum(weights, axis=0, keepdims=True)
        mixed = mixed + lax.dot_general(
            rows_of(group, 1),
            weights.astype(jnp.bfloat16),
            (((0,), (0,)), ((), ())),
            preferred_element_type=jnp.float32,
        )
    partial[:dim, :] = mixed
    row = lax.broadcasted_iota(jnp.int32, (STAT_ROWS, query_rows.shape[0]), 0)
    partial[dim:, :] = jnp.where(row == 0, top * inv_root, total)


def merge_kernel(scale, plane, place, mine, theirs, payload, grads_half, grad_rows, *refs):
    stats, attended_own, terms, both_grads, both_attended, term_rows = (
        refs[0],
        refs[1],
        refs[2:-3],
        refs[-3],
        refs[-2],
        refs[-1],
    )
    tile, dim = grad_rows.shape
    half = grads_half.shape[1]
    top_a, top_b = mine[dim : dim + 1, :], theirs[dim : dim + 1, :]
    sum_a, sum_b = mine[dim + 1 : dim + 2, :], theirs[dim + 1 : dim + 2, :]
    top = jnp.maximum(top_a, top_b)
    share_a, share_b = jnp.exp(top_a - top), jnp.exp(top_b - top)
    total = share_a * sum_a + share_b * sum_b
    mixed = mine[:dim, :] * (share_a / total) + theirs[:dim, :] * (share_b / total)
    attended_t = mixed.astype(jnp.bfloat16).astype(jnp.float32)
    both_tiles(place, grad_rows[...], payload[:, half:], both_grads)
    row_dot = jnp.sum(both_grads[...].astype(jnp.float32).T * attended_t, axis=0, keepdims=True)
    row = lax.broadcasted_iota(jnp.int32, (STAT_ROWS, mixed.shape[1]), 0)
    stats[...] = jnp.where(row == 0, top + jnp.log(total), row_dot)
    both_attended[...] = attended_t.T.astype(jnp.bfloat16)
    rows_mine = both_attended[pl.ds(pl.multiple_of(place[0] * tile, tile), tile), :]
    rows_theirs = both_attended[pl.ds(pl.multiple_of((1 - place[0]) * tile, tile), tile), :]
    attended_own[...] = rows_mine
    if not terms:
        return
    contract = (((0,), (0,)), ((), ()))
    term = lax.dot_general(
        rows_mine, grads_half[...], contract, preferred_element_type=jnp.float32
    )
    term = term + lax.dot_general(
        rows_theirs, payload[:, :half], contract, preferred_element_type=jnp.float32
    )
    term_rows[...] = term * scale
    count = dim // plane
    for order, out in enumerate(terms):
        chunk = place[1] ^ order
        out[...] = term_rows[pl.ds(pl.multiple_of(chunk * count, count), count), :].astype(jnp.bfloat16)


def split_groups(layout, refs):
    groups, start = [], 0
    for count in layout:
        groups.append(refs[start : start + count])
        start += count
    return groups, refs[start:]


def backward_kernel(
    inv_root, layout, targets, place, stats, both_queries, payload, grad_rows, *refs
):
    groups, rest = split_groups(layout, refs)
    count = 1 + max(out for out, _ in targets)
    outs, (query_own, query_other, both_grads, both_out) = rest[:count], rest[count:]
    tile, dim = grad_rows.shape
    columns = payload.shape[1]
    both_tiles(place, grad_rows[...], payload[:, columns - dim :], both_grads)
    query_rows, out_grads = both_queries[...], both_grads[...]
    level, row_dot = stats[0:1, :], stats[1:2, :]
    along = (((1,), (1,)), ((), ()))
    query_grad = jnp.zeros((dim, 2 * tile), jnp.float32)
    for group, (target, first) in zip(groups, targets):
        out, tiles = outs[target], group[0].shape[0]
        keys, values = rows_of(group, 0), rows_of(group, 1)
        scores = lax.dot_general(keys, query_rows, along, preferred_element_type=jnp.float32)
        probability = jnp.exp(scores * inv_root - level)
        prob_grad = lax.dot_general(values, out_grads, along, preferred_element_type=jnp.float32)
        score_grad = (probability * (prob_grad - row_dot)).astype(jnp.bfloat16)
        shape = (tiles,) + out.shape[2:]
        key_grad = jnp.dot(score_grad, query_rows, preferred_element_type=jnp.float32) * inv_root
        value_grad = jnp.dot(
            probability.astype(jnp.bfloat16), out_grads, preferred_element_type=jnp.float32
        )
        out[first : first + tiles, 0] = key_grad.reshape(shape).astype(out.dtype)
        out[first : first + tiles, 1] = value_grad.reshape(shape).astype(out.dtype)
        query_grad = query_grad + lax.dot_general(
            keys, score_grad, (((0,), (0,)), ((), ())), preferred_element_type=jnp.float32
        )
    both_out[...] = query_grad.T * inv_root
    query_own[...] = both_out[pl.ds(pl.multiple_of(place[0] * tile, tile), tile), :]
    other = both_out[pl.ds(pl.multiple_of((1 - place[0]) * tile, tile), tile), :]
    other = other.astype(jnp.bfloat16)
    rows = query_other.shape[0]
    for block in range(tile // rows):
        query_other[:, block * dim : (block + 1) * dim] = other[block * rows : (block + 1) * rows]


def assemble_kernel(flipped, rows, place, part, *refs):
    whole, rows_ref, done = refs[-3 - flipped], refs[-2], refs[-1]
    count, width = rows_ref.shape
    for order in range(count // rows):
        row = pl.multiple_of((place[1] ^ order) * rows, rows)
        rows_ref[pl.ds(row, rows), :] = part[order * rows : (order + 1) * rows, :].astype(jnp.float32)
    core = 1 - place[0] if flipped else place[0]
    columns = pl.ds(pl.multiple_of(core * width, width), width)
    copy = pltpu.make_async_copy(rows_ref, whole.at[:, columns], done)
    copy.start()
    if flipped:
        query_own, grad_query = refs[0], refs[-3]
        dim, step = grad_query.shape[1], part.shape[0] - count
        for block in range(width // dim):
            piece = part[count:, block * dim : (block + 1) * dim].astype(jnp.float32)
            span = slice(block * step, (block + 1) * step)
            grad_query[span, :] = (query_own[span, :] + piece).astype(jnp.bfloat16)
    copy.wait()


def assemble(flipped, place, part, rows, shape, whole=None, query_own=None):
    anywhere = pl.BlockSpec(memory_space=pl.ANY)
    outs, out_specs, operands, in_specs = shape, anywhere, (place, part), [SMEM, VMEM]
    if flipped:
        outs, out_specs = (shape, shaped(*query_own.shape)), (anywhere, VMEM)
        operands, in_specs = operands + (query_own, whole), in_specs + [VMEM, anywhere]
    return pl.pallas_call(
        functools.partial(assemble_kernel, flipped, rows),
        out_shape=outs,
        in_specs=in_specs,
        out_specs=out_specs,
        scratch_shapes=[
            pltpu.VMEM((shape.shape[0], part.shape[1]), jnp.float32),
            pltpu.SemaphoreType.DMA,
        ],
        input_output_aliases={3: 0} if flipped else {},
        compiler_params=PARAMS,
    )(*operands)


def pack_kernel(*refs):
    start = 0
    for piece in refs[:-1]:
        refs[-1][start : start + piece.shape[0], :] = piece[...]
        start += piece.shape[0]


def combine_kernel(column, *refs):
    arrived, pieces = refs[: -column.shape[0]], refs[-column.shape[0] :]
    for k, piece in enumerate(pieces):
        total = column[k]
        for block in arrived:
            total = total + block[k].astype(jnp.float32)
        piece[...] = total.astype(piece.dtype)


def shaped(*shape, kind=jnp.bfloat16):
    return jax.ShapeDtypeStruct(shape, kind)


def kernel_call(kernel, operands, outs, scratch=(), cost=None):
    many = isinstance(outs, (list, tuple))
    return pl.pallas_call(
        kernel,
        out_shape=outs,
        in_specs=[SMEM] + [VMEM] * (len(operands) - 1),
        out_specs=[VMEM] * len(outs) if many else VMEM,
        scratch_shapes=list(scratch),
        compiler_params=PARAMS,
        cost_estimate=cost,
    )(*operands)


def cost_of(flops, moved):
    return pl.CostEstimate(flops=int(flops), bytes_accessed=int(moved), transcendentals=0)


PLANE_BITS = ((0, 0), (0, 1), (2, 0), (2, 1))


def sum_over_plane(terms):
    summed = terms[0].astype(jnp.float32)
    for term, bit in zip(terms[1:], PLANE_BITS[1:]):
        summed = summed + flip(term, ("frame", "width"), bit).astype(jnp.float32)
    return summed.astype(jnp.bfloat16)


def join_sum(part, query_own, query_other, place):
    plane = len(part)
    pieces = part + [query_other]
    part = pl.pallas_call(
        pack_kernel,
        out_shape=shaped(sum(p.shape[0] for p in pieces), pieces[0].shape[1]),
        in_specs=[VMEM] * len(pieces),
        out_specs=VMEM,
        compiler_params=PARAMS,
    )(*pieces)
    other = flip(part, ("frame",), (1,))
    rows = (part.shape[0] - query_other.shape[0]) // plane
    shape = shaped(plane * rows, 2 * part.shape[1], kind=jnp.float32)
    whole = assemble(False, place, part, rows, shape)
    return assemble(True, place, other, rows, shape, whole, query_own)


def body(queries, key_vectors, value_vectors, out_weight, projected_grad):
    head_dim = queries.shape[-1]
    model_dim = out_weight.shape[1]
    half = model_dim // 2
    inv_root = 1.0 / math.sqrt(head_dim)
    extents = tuple(lax.axis_size(axis) for axis in AXES)
    assert extents[0] == 4
    small = extents[1:] == (4, 2)
    frame, height, width = (lax.axis_index(axis) for axis in AXES)
    core = frame % 2
    place = jnp.stack([core, (frame // 2) * 2 + width, height]).astype(jnp.int32)
    query_rows = queries.reshape(-1, head_dim)
    grads = projected_grad.reshape(-1, model_dim)
    tile = query_rows.shape[0]

    own = jnp.stack((key_vectors.reshape(tile, head_dim), value_vectors.reshape(tile, head_dim)))
    cross = [(2 * s + y, 2 * p + 1 - y) for s, p in ((2, 1), (1, 2)) for y in (0, 1)]

    if small:
        swap = [(0, 1), (1, 0)]
        tiles = fetch(own, "height")
        own_beside = lax.ppermute(own[None], "width", swap)
        others = jnp.stack(tiles)
        column = jnp.stack([own] + tiles)
        others, column, own_beside, query_rows_late = lax.optimization_barrier(
            (others, column, own_beside, query_rows)
        )
        others_beside = lax.ppermute(others, "width", swap)
        far = [
            lax.ppermute(column, "frame", [(2, 0), (1, 3)]),
            lax.ppermute(column, ("frame", "width"), cross),
        ]
        blocks = [column, own_beside, others_beside, *far]
        layout = (1, 1, 1, 2)
        targets = ((0, 0), (1, 0), (1, 1), (2, 0))
        column_tiles, kinds = 1 + others.shape[0], 3
    else:
        query_rows_late = query_rows
        column = jnp.stack([own] + fetch(own, "height"))
        beside = fetch(column, "width")
        everything = jnp.concatenate([column] + beside, axis=0)
        far = [
            lax.ppermute(everything[:, :, : tile // 2], "frame", [(2, 0), (1, 3)]),
            lax.ppermute(everything[:, :, tile // 2 :], "frame", [(2, 1), (1, 2)]),
        ]
        blocks = [column] + beside + far
        layout = (1,) * (1 + len(beside)) + (2,)
        targets = tuple((k, 0) for k in range(len(layout)))
        column_tiles, kinds = column.shape[0], len(layout)
    queries_other = flip(query_rows_late, ("frame",), (1,))
    payload, grads_half, grad_rows, both_queries = kernel_call(
        token_kernel,
        (place, query_rows, queries_other, grads, out_weight),
        (
            shaped(tile, half + head_dim),
            shaped(tile, half),
            shaped(tile, head_dim),
            shaped(2 * tile, head_dim),
        ),
        cost=cost_of(2 * tile * head_dim * model_dim, 4 * tile * model_dim),
    )
    payload, grad_rows, *blocks = lax.optimization_barrier((payload, grad_rows, *blocks))
    payload = flip(payload, ("frame",), (1,))
    grad_shapes = [(column_tiles, 2, tile, head_dim)] * (kinds - 1)
    grad_shapes.append((column_tiles, 2, tile, head_dim) if small else far[0].shape)
    key_count = sum(shape[0] * shape[2] for shape in grad_shapes)
    product = 2 * key_count * 2 * tile * head_dim
    moved = sum(b.size * 2 for b in blocks)

    partial = kernel_call(
        functools.partial(forward_kernel, inv_root, layout),
        (place, both_queries, *blocks),
        shaped(head_dim + STAT_ROWS, 2 * tile, kind=jnp.float32),
        scratch=(pltpu.VMEM((key_count, 2 * tile), jnp.float32),),
        cost=cost_of(2 * product, moved),
    )
    partial_other = flip(partial, ("frame",), (1,))
    plane = 4
    chunks = plane if small else 0
    merged = kernel_call(
        functools.partial(merge_kernel, 1.0 / float(math.prod(extents)), plane),
        (place, partial, partial_other, payload, grads_half, grad_rows),
        (
            shaped(STAT_ROWS, 2 * tile, kind=jnp.float32),
            shaped(tile, head_dim),
            *[shaped(head_dim // plane, half)] * chunks,
        ),
        scratch=(
            pltpu.VMEM((2 * tile, head_dim), jnp.bfloat16),
            pltpu.VMEM((2 * tile, head_dim), jnp.bfloat16),
            pltpu.VMEM((head_dim, half), jnp.float32),
        ),
        cost=cost_of(4 * tile * head_dim * half, 4 * tile * model_dim),
    )
    stats, attended, *terms = merged
    back = kernel_call(
        functools.partial(backward_kernel, inv_root, layout, targets),
        (place, stats, both_queries, payload, grad_rows, *blocks),
        (
            shaped(*grad_shapes[0], kind=jnp.float32),
            *[shaped(*shape) for shape in grad_shapes[1:]],
            shaped(tile, head_dim, kind=jnp.float32),
            shaped(tile * head_dim // half, half),
        ),
        scratch=(
            pltpu.VMEM((2 * tile, head_dim), jnp.bfloat16),
            pltpu.VMEM((2 * tile, head_dim), jnp.float32),
        ),
        cost=cost_of(5 * product, 2 * moved),
    )
    if small:
        terms[0], *back = lax.optimization_barrier((terms[0], *back))
        part = sum_over_plane(terms)
        other = flip(part, ("height",), (1,))
        part = (part.astype(jnp.float32) + other.astype(jnp.float32)).astype(jnp.bfloat16)
        part, attended = lax.optimization_barrier((part, attended))
        other = flip(part, ("height",), (2,))
    else:
        weight_term = jnp.einsum("td,tm->dm", attended, grads, preferred_element_type=jnp.float32)
        grad_out_weight = lax.psum(weight_term, AXES) / float(math.prod(extents))
    projected = (
        jnp.dot(attended, out_weight, preferred_element_type=jnp.float32)
        .astype(jnp.bfloat16)
        .reshape(projected_grad.shape)
    )
    column_grad, *beside_grads, far_grad, query_own, query_other = back
    if small:
        arrived = [
            lax.ppermute(beside_grads[0], "width", [(0, 1), (1, 0)]),
            lax.ppermute(far_grad, "frame", [(0, 2), (3, 1)]),
            lax.ppermute(far_grad, ("frame", "width"), [(p, s) for s, p in cross]),
        ]
        other, projected = lax.optimization_barrier((other, projected))
        part = (part.astype(jnp.float32) + other.astype(jnp.float32)).astype(jnp.bfloat16)
        part, column_grad = lax.optimization_barrier((part, column_grad))
        part = [part] + [flip(part, ("frame", "width"), bit) for bit in PLANE_BITS[1:]]
        shape = column_grad.shape[1:]
        pieces = pl.pallas_call(
            combine_kernel,
            out_shape=[shaped(*shape, kind=jnp.float32)] + [shaped(*shape)] * (column_tiles - 1),
            in_specs=[VMEM] * 4,
            out_specs=[VMEM] * column_tiles,
            compiler_params=PARAMS,
        )(column_grad, *arrived)
    else:
        arrived = jnp.concatenate(
            (
                lax.ppermute(far_grad, "frame", [(0, 2), (3, 1)]),
                lax.ppermute(far_grad, "frame", [(1, 2), (2, 1)]),
            ),
            axis=2,
        ).astype(jnp.float32)
        pieces = [column_grad] + [b.astype(jnp.float32) for b in beside_grads]
        span = column_tiles
        pieces = [p + arrived[i * span : (i + 1) * span] for i, p in enumerate(pieces)]
        column_grad = give_back(pieces, "width")
        pieces = [column_grad[k] for k in range(column_tiles)]
    if small:
        grad_out_weight, grad_query = join_sum(part, query_own, query_other, place)
    else:
        query_other = flip(query_other, ("frame",), (1,)).reshape(-1, half // head_dim, head_dim)
        query_other = query_other.transpose(1, 0, 2).reshape(tile, head_dim)
        grad_query = (query_own + query_other.astype(jnp.float32)).astype(jnp.bfloat16)
    own_grad = give_back(pieces, "height")
    grad_key = own_grad[0].astype(jnp.bfloat16).reshape(key_vectors.shape)
    grad_value = own_grad[1].astype(jnp.bfloat16).reshape(value_vectors.shape)
    grad_query = grad_query.reshape(queries.shape)
    return (projected, grad_query, grad_key, grad_value, grad_out_weight)


def solution(mesh):
    tokens = P("frame", "height", "width", None)
    return jax.shard_map(
        body,
        mesh=mesh,
        in_specs=(tokens, tokens, tokens, P(), tokens),
        out_specs=(tokens, tokens, tokens, tokens, P()),
        check_vma=False,
    )
```

time: 222 us -> 70.3 us (0.32)
  blocking collectives: 80 us -> 0 us
  waiting for transfers between devices: 62.9 us -> 15.3 us
  between operations: 27.9 us -> 0.87 us
  starting transfers between devices: 20.1 us -> 38.6 us
  matrix products: 13.2 us -> 1.48 us
  Pallas kernels: 0 us -> 10.6 us
  local copies, waits for them, and re-layouts: 8.39 us -> 1.92 us
  other arithmetic: 7.52 us -> 1.23 us
    all_gather x1 -> x0, blocking collectives: 80 us -> none  [sum_everywhere(): whole = lax.all_gather(part, ('frame', 'width', 'height'))]
    all_gather x1 -> x0, waiting for transfers between devices: 59.7 us -> none  [body(): lax.all_gather(own, AXES).reshape(extents + (2, tile, head_dim))]
    ppermute x0 -> x22, starting transfers between devices: none -> 31.2 us  [the longest x12 11.9 us: flip(): return lax.ppermute(block, axes, route)]
    ppermute x0 -> x22, waiting for transfers between devices: none -> 14.8 us  [the longest x12 8.45 us: flip(): return lax.ppermute(block, axes, route)]
    dot_general x8 -> x0, matrix products: 10.6 us -> none  [the longest x1 2.7 us: body(): jnp.dot(score_grad, key_rows, preferred_element_type=jnp.float32)]
    pallas_call x0 -> x8, Pallas kernels: none -> 10.6 us  [the longest x4 6.83 us: kernel_call(): pl.pallas_call(kernel, out_shape=outs, in_specs=[SMEM] + [VMEM] * (len(op...]
    all_to_all x2 -> x0, starting transfers between devices: 7.66 us -> none  [the longest x1 4.23 us: sum_everywhere(): part = lax.all_to_all(part, ('frame', 'width'), 0, 0)]
    ppermute x7 -> x3, starting transfers between devices: 12.4 us -> 7.36 us  [give_back(): back = lax.ppermute(outgoing, axis, [(p, s) for s, p in route])]
  transfers between devices with their start and end apart: 10 -> 25, of which waited for: 2 -> 10; matrix products, arithmetic and copies ran while one was open for 7% -> 3% of each run, Pallas kernels for 0% -> 10%
where the time goes in v2:
time: 70.3 us; the launch traced here: 70 us
  starting transfers between devices  38.6 us (55%)
  waiting for transfers between devices  15.3 us (22%)
  Pallas kernels  10.6 us (15%)
  local copies, waits for them, and re-layouts  1.92 us (3%)
  matrix products  1.48 us (2%)
  other arithmetic  1.23 us (2%)
  between operations  0.87 us (1%)
    ppermute x12, starting transfers between devices, flip(): return lax.ppermute(block, axes, route)  11.9 us
    ppermute x12, waiting for transfers between devices, flip(): return lax.ppermute(block, axes, route)  8.45 us
    ppermute x3, starting transfers between devices, fetch(): arrived = [lax.ppermute(block, axis, route) for route in routes]  8.25 us
    ppermute x3, starting transfers between devices, give_back(): back = lax.ppermute(outgoing, axis, [(p, s) for s, p in route])  7.36 us
    pallas_call x4, Pallas kernels, kernel_call(): pl.pallas_call(kernel, out_shape=outs, in_specs=[SMEM] + [VMEM] * (len(op...  6.83 us
    ppermute x1, starting transfers between devices, body(): lax.ppermute(far_grad, 'frame', [(0, 2), (3, 1)])  4.94 us
    pallas_call x2, Pallas kernels, assemble(): pl.pallas_call(functools.partial(assemble_kernel, flipped, rows), out_sha...  3.59 us
    ppermute x1, waiting for transfers between devices, body(): others_beside = lax.ppermute(others, 'width', swap)  3.29 us
  transfers between devices with their start and end apart: 25, of which 10 were waited for; matrix products, arithmetic and copies ran while one was open for 3% of the time, Pallas kernels for 10%

profile of v2, /device:TPU:0, one launch (start us, length us, event | category | flops | bytes accessed | tf_op | source)
XLA Modules:
  0.0 70.0 jit_solution(15168967230233083993)
XLA Ops:
  0.7 0.9 %fusion = (bf16[1,2,192,128]{3,2,1,0:T(8,128)(2,1)S(1)}, bf16[2,192,128]{2,1,0:T(8,128)(2,1)S(1)}) fusion(bf16[1,192,128]{2,1,0:T(8,128)(2,1)} %bitcast.24, bf16[1,192,128]{2,1,0:T(8,128)(2,1)} %bitcast.25), kind=kLoop, calls=%fused_computation.10 | loop fusion | flops 49152 | bytes 294912 | tf_op jit(solution)/shard_map/stack | solution.py:380
  1.6 0.7 collective-permute-start.2
  2.2 1.3 %collective-permute-start.1 = (bf16[2,192,128]{2,1,0:T(8,128)(2,1)S(1)}, bf16[2,192,128]{2,1,0:T(8,128)(2,1)S(1)}, u32[]{:S(2)}, u32[]{:S(2)}) collective-permute-start(bf16[2,192,128]{2,1,0:T(8,128)(2,1)S(1)} %get-tuple-element.94), channel_id=1, source_target_pairs={{2,6},{4,0},{3,7},{5,1},{10,14},{12,8},{11,15},{13,9},{18,22},{20,... | collective-permute-start | bytes 294920 | tf_op jit(solution)/shard_map/ppermute | solution.py:64
  3.5 6.3 %collective-permute-start = (bf16[2,192,128]{2,1,0:T(8,128)(2,1)S(1)}, bf16[2,192,128]{2,1,0:T(8,128)(2,1)S(1)}, u32[]{:S(2)}, u32[]{:S(2)}) collective-permute-start(bf16[2,192,128]{2,1,0:T(8,128)(2,1)S(1)} %get-tuple-element.94), channel_id=1, source_target_pairs={{2,0},{0,2},{6,4},{4,6},{3,1},{1,3},{7,5},{5,7},{10,8},{8,10},{14,... | collective-permute-start | bytes 294920 | tf_op jit(solution)/shard_map/ppermute | solution.py:64
  9.8 1.5 %collective-permute-start.3 = (bf16[1,2,192,128]{3,2,1,0:T(8,128)(2,1)S(1)}, bf16[1,2,192,128]{3,2,1,0:T(8,128)(2,1)S(1)}, u32[]{:S(2)}, u32[]{:S(2)}) collective-permute-start(bf16[1,2,192,128]{3,2,1,0:T(8,128)(2,1)S(1)} %get-tuple-element.93), channel_id=1, source_target_pairs={{0,1},{1,0},{2,3},{3,2},{4,5},{5,4},{6,7},{7,6},{8,9},{9,8},{10,11... | collective-permute-start | bytes 294920 | tf_op jit(solution)/shard_map/ppermute | solution.py:378
  11.4 0.0 collective-permute-done.2
  11.4 1.4 %collective-permute-done.1 = bf16[2,192,128]{2,1,0:T(8,128)(2,1)S(1)} collective-permute-done((bf16[2,192,128]{2,1,0:T(8,128)(2,1)S(1)}, bf16[2,192,128]{2,1,0:T(8,128)(2,1)S(1)}, u32[]{:S(2)}, u32[]{:S(2)}) %collective-permute-start.1) | collective-permute-done | bytes 98336 | tf_op jit(solution)/shard_map/ppermute | solution.py:64
  12.8 1.4 %collective-permute-done = bf16[2,192,128]{2,1,0:T(8,128)(2,1)S(1)} collective-permute-done((bf16[2,192,128]{2,1,0:T(8,128)(2,1)S(1)}, bf16[2,192,128]{2,1,0:T(8,128)(2,1)S(1)}, u32[]{:S(2)}, u32[]{:S(2)}) %collective-permute-start) | collective-permute-done | bytes 98336 | tf_op jit(solution)/shard_map/ppermute | solution.py:64
  14.2 0.2 collective-permute-done.3.refs_1_
  14.5 0.7 collective-permute-start.7
  15.1 1.3 %collective-permute-start.6 = (bf16[3,2,192,128]{3,2,1,0:T(8,128)(2,1)S(1)}, bf16[3,2,192,128]{3,2,1,0:T(8,128)(2,1)S(1)}, u32[]{:S(2)}, u32[]{:S(2)}) collective-permute-start(bf16[3,2,192,128]{3,2,1,0:T(8,128)(2,1)S(1)} %pad_maximum_fusion.refs_0_), channel_id=1, source_target_pairs={{16,0},{8,24},{17,1},{9,25},{18,2},{10,26},{19,3},{11,27},{20,4},{... | collective-permute-start | bytes 884744 | tf_op jit(solution)/shard_map/ppermute | solution.py:386
  16.4 1.6 %collective-permute-start.5 = (bf16[2,2,192,128]{3,2,1,0:T(8,128)(2,1)S(1)}, bf16[2,2,192,128]{3,2,1,0:T(8,128)(2,1)S(1)}, u32[]{:S(2)}, u32[]{:S(2)}) collective-permute-start(bf16[2,2,192,128]{3,2,1,0:T(8,128)(2,1)S(1)} %pad_maximum_fusion.1), channel_id=1, source_target_pairs={{0,1},{1,0},{2,3},{3,2},{4,5},{5,4},{6,7},{7,6},{8,9},{9,8},{10,11... | collective-permute-start | bytes 589832 | tf_op jit(solution)/shard_map/ppermute | solution.py:384
  18.0 2.5 %collective-permute-start.4 = (bf16[192,128]{1,0:T(8,128)(2,1)S(1)}, bf16[192,128]{1,0:T(8,128)(2,1)S(1)}, u32[]{:S(2)}, u32[]{:S(2)}) collective-permute-start(bf16[192,128]{1,0:T(8,128)(2,1)S(1)} %bitcast.19), channel_id=1, source_target_pairs={{0,8},{8,0},{16,24},{24,16},{1,9},{9,1},{17,25},{25,17},{2,10},{10... | collective-permute-start | bytes 147464 | tf_op jit(solution)/shard_map/ppermute | solution.py:100
  20.5 0.1 pad_add_fusion.place
  20.6 0.8 %collective-permute-done.4.queries_other = bf16[192,128]{1,0:T(8,128)(2,1)S(1)} collective-permute-done((bf16[192,128]{1,0:T(8,128)(2,1)S(1)}, bf16[192,128]{1,0:T(8,128)(2,1)S(1)}, u32[]{:S(2)}, u32[]{:S(2)}) %collective-permute-start.4) | collective-permute-done | bytes 49184 | tf_op jit(solution)/shard_map/ppermute | solution.py:100
  21.4 1.3 %copy-done.1 = bf16[4,6,8,3072]{3,2,1,0:T(8,128)(2,1)S(1)} copy-done((bf16[4,6,8,3072]{3,2,1,0:T(8,128)(2,1)S(1)}, bf16[4,6,8,3072]{3,2,1,0:T(8,128)(2,1)}, u32[]{:S(2)}) %copy-start.1) | copy-done | bytes 1179672
  22.7 1.0 %shard_map.92 = (bf16[192,1664]{1,0:T(8,128)(2,1)S(1)}, bf16[192,1536]{1,0:T(8,128)(2,1)S(1)}, bf16[192,128]{1,0:T(8,128)(2,1)S(1)}, bf16[384,128]{1,0:T(8,128)(2,1)S(1)}) custom-call(s32[3]{0:T(128)S(1)} %pad_add_fusion.place, bf16[192,128]{1,0:T(8,128)(2,1)S(1)} %bitcast.20, bf16[192,128]{1,0:T(8,128)(2,1)S(1)} %collective-permute-done.4.queries_other, ...), custom_call_target="tpu_custom_call" | custom-call | flops 150994944 | bytes 2359296 | tf_op jit(solution)/shard_map/pallas_call | solution.py:315
  23.7 3.3 %collective-permute-done.5.refs_2_ = bf16[2,2,192,128]{3,2,1,0:T(8,128)(2,1)S(1)} collective-permute-done((bf16[2,2,192,128]{3,2,1,0:T(8,128)(2,1)S(1)}, bf16[2,2,192,128]{3,2,1,0:T(8,128)(2,1)S(1)}, u32[]{:S(2)}, u32[]{:S(2)}) %collective-permute-start.5) | collective-permute-done | bytes 196640 | tf_op jit(solution)/shard_map/ppermute | solution.py:384
  27.0 0.0 collective-permute-done.7.refs_4_
  27.0 0.0 collective-permute-done.6.refs_3_
  27.0 0.3 collective-permute-start.9
  27.3 2.0 %shard_map.93.mine = f32[136,384]{1,0:T(8,128)S(1)} custom-call(s32[3]{0:T(128)S(1)} %pad_add_fusion.place, bf16[384,128]{1,0:T(8,128)(2,1)S(1)} %get-tuple-element.49.both_queries, bf16[3,2,192,128]{3,2,1,0:T(8,128)(2,1)S(1)} %pad_maximum_fusion.refs_0_, bf16[1,2,192,128]{3,2,1,0:T(8,128)(2,1)S(1)} %collective-permute-done.3.refs_1_, ...), custom_call_target="tpu_custom_call" | custom-call | flops 339738624 | bytes 1179648 | tf_op jit(solution)/shard_map/pallas_call | solution.py:315
  29.2 0.3 collective-permute-start.8
  29.6 1.2 %collective-permute-done.8.theirs = f32[136,384]{1,0:T(8,128)S(1)} collective-permute-done((f32[136,384]{1,0:T(8,128)S(1)}, f32[136,384]{1,0:T(8,128)S(1)}, u32[]{:S(2)}, u32[]{:S(2)}) %collective-permute-start.8) | collective-permute-done | bytes 208928 | tf_op jit(solution)/shard_map/ppermute | solution.py:100
  30.8 0.0 collective-permute-done.9.payload
  30.8 1.1 %shard_map.94 = (f32[8,384]{1,0:T(8,128)S(1)}, bf16[192,128]{1,0:T(8,128)(2,1)S(1)}, bf16[32,1536]{1,0:T(8,128)(2,1)S(1)}, bf16[32,1536]{1,0:T(8,128)(2,1)S(1)},...) custom-call(s32[3]{0:T(128)S(1)} %pad_add_fusion.place, f32[136,384]{1,0:T(8,128)S(1)} %shard_map.93.mine, ...), custom_call_target="tpu_custom_call" | custom-call | flops 150994944 | bytes 2359296 | tf_op jit(solution)/shard_map/pallas_call | solution.py:315
  31.9 1.5 %collective-permute-start.10 = (bf16[32,1536]{1,0:T(8,128)(2,1)S(1)}, bf16[32,1536]{1,0:T(8,128)(2,1)S(1)}, u32[]{:S(2)}, u32[]{:S(2)}) collective-permute-start(bf16[32,1536]{1,0:T(8,128)(2,1)S(1)} %get-tuple-element.71), channel_id=1, source_target_pairs={{0,1},{1,0},{8,9},{9,8},{16,17},{17,16},{24,25},{25,24},{2,3},{3,2... | collective-permute-start | bytes 294920 | tf_op jit(solution)/shard_map/ppermute | solution.py:100
  33.4 0.3 collective-permute-start.11
  33.7 1.8 %collective-permute-start.12 = (bf16[32,1536]{1,0:T(8,128)(2,1)S(1)}, bf16[32,1536]{1,0:T(8,128)(2,1)S(1)}, u32[]{:S(2)}, u32[]{:S(2)}) collective-permute-start(bf16[32,1536]{1,0:T(8,128)(2,1)S(1)} %get-tuple-element.73), channel_id=1, source_target_pairs={{0,17},{1,16},{8,25},{9,24},{16,1},{17,0},{24,9},{25,8},{2,19},{3,... | collective-permute-start | bytes 294920 | tf_op jit(solution)/shard_map/ppermute | solution.py:100
  35.5 2.7 %shard_map.95 = (f32[3,2,192,128]{3,2,1,0:T(8,128)S(1)}, bf16[3,2,192,128]{3,2,1,0:T(8,128)(2,1)S(1)}, bf16[3,2,192,128]{3,2,1,0:T(8,128)(2,1)S(1)}, f32[192,128]{1,0:T(8,128)S(1)}, bf16[16,1536]{1,0:T(8,128)(2,1)S(1)}) custom-call(s32[3]{0:T(128)S(1)} %pad_add_fusion.place, f32[8,384]{1,0:T(8,128)S(1)} %get-tuple-element.64.stats, ...), custom_call_target="tpu_custom_call" | custom-call | flops 849346560 | bytes 2359296 | tf_op jit(solution)/shard_map/pallas_call | solution.py:315
  38.2 0.0 collective-permute-done.10
  38.2 0.8 %collective-permute-done.11 = bf16[32,1536]{1,0:T(8,128)(2,1)S(1)} collective-permute-done((bf16[32,1536]{1,0:T(8,128)(2,1)S(1)}, bf16[32,1536]{1,0:T(8,128)(2,1)S(1)}, u32[]{:S(2)}, u32[]{:S(2)}) %collective-permute-start.11) | collective-permute-done | bytes 98336 | tf_op jit(solution)/shard_map/ppermute | solution.py:100
  39.0 1.2 %collective-permute-done.12 = bf16[32,1536]{1,0:T(8,128)(2,1)S(1)} collective-permute-done((bf16[32,1536]{1,0:T(8,128)(2,1)S(1)}, bf16[32,1536]{1,0:T(8,128)(2,1)S(1)}, u32[]{:S(2)}, u32[]{:S(2)}) %collective-permute-start.12) | collective-permute-done | bytes 98336 | tf_op jit(solution)/shard_map/ppermute | solution.py:100
  40.2 0.1 add_convert_fusion.3
  40.3 0.1 collective-permute-start.13
  40.4 0.7 collective-permute-start.21
  41.1 4.9 %collective-permute-start.20 = (bf16[3,2,192,128]{3,2,1,0:T(8,128)(2,1)S(1)}, bf16[3,2,192,128]{3,2,1,0:T(8,128)(2,1)S(1)}, u32[]{:S(2)}, u32[]{:S(2)}) collective-permute-start(bf16[3,2,192,128]{3,2,1,0:T(8,128)(2,1)S(1)} %get-tuple-element.86), channel_id=1, source_target_pairs={{0,16},{24,8},{1,17},{25,9},{2,18},{26,10},{3,19},{27,11},{4,20},{... | collective-permute-start | bytes 884744 | tf_op jit(solution)/shard_map/ppermute | solution.py:486
  46.0 0.4 collective-permute-start.19
  46.5 0.0 collective-permute-done.13
  46.5 1.4 %collective-permute-start.14 = (bf16[32,1536]{1,0:T(8,128)(2,1)S(1)}, bf16[32,1536]{1,0:T(8,128)(2,1)S(1)}, u32[]{:S(2)}, u32[]{:S(2)}) collective-permute-start(bf16[32,1536]{1,0:T(8,128)(2,1)S(1)} %add_convert_fusion.2), channel_id=1, source_target_pairs={{0,4},{2,6},{4,0},{6,2},{1,5},{3,7},{5,1},{7,3},{8,12},{10,14},{12... | collective-permute-start | bytes 294920 | tf_op jit(solution)/shard_map/ppermute | solution.py:100
  47.9 1.5 %convolution_convert_fusion = bf16[192,3072]{1,0:T(8,128)(2,1)} fusion(bf16[192,128]{1,0:T(8,128)(2,1)S(1)} %get-tuple-element.76, bf16[128,3072]{1,0:T(8,128)(2,1)S(1)} %copy-done), kind=kOutput, calls=%fused_computation | convolution fusion | flops 151584768 | bytes 2015232 | tf_op jit(solution)/shard_map/dot_general | solution.py:478
  49.4 4.4 %collective-permute-done.14 = bf16[32,1536]{1,0:T(8,128)(2,1)S(1)} collective-permute-done((bf16[32,1536]{1,0:T(8,128)(2,1)S(1)}, bf16[32,1536]{1,0:T(8,128)(2,1)S(1)}, u32[]{:S(2)}, u32[]{:S(2)}) %collective-permute-start.14) | collective-permute-done | bytes 98336 | tf_op jit(solution)/shard_map/ppermute | solution.py:100
  53.9 1.3 %collective-permute-start.17 = (bf16[32,1536]{1,0:T(8,128)(2,1)S(1)}, bf16[32,1536]{1,0:T(8,128)(2,1)S(1)}, u32[]{:S(2)}, u32[]{:S(2)}) collective-permute-start(bf16[32,1536]{1,0:T(8,128)(2,1)S(1)} %add_convert_fusion.1.refs_0_), channel_id=1, source_target_pairs={{0,17},{1,16},{8,25},{9,24},{16,1},{17,0},{24,9},{25,8},{2,19},{3,... | collective-permute-start | bytes 294920 | tf_op jit(solution)/shard_map/ppermute | solution.py:100
  55.2 0.2 collective-permute-start.16
  55.5 0.0 collective-permute-done.19.refs_0_
  55.5 2.0 %collective-permute-start.15 = (bf16[32,1536]{1,0:T(8,128)(2,1)S(1)}, bf16[32,1536]{1,0:T(8,128)(2,1)S(1)}, u32[]{:S(2)}, u32[]{:S(2)}) collective-permute-start(bf16[32,1536]{1,0:T(8,128)(2,1)S(1)} %add_convert_fusion.1.refs_0_), channel_id=1, source_target_pairs={{0,1},{1,0},{8,9},{9,8},{16,17},{17,16},{24,25},{25,24},{2,3},{3,2... | collective-permute-start | bytes 294920 | tf_op jit(solution)/shard_map/ppermute | solution.py:100
  57.4 0.0 collective-permute-done.21.refs_2_
  57.4 0.0 collective-permute-done.20.refs_1_
  57.4 0.1 shard_map.99
  57.6 2.0 %collective-permute-start.22 = (bf16[2,192,128]{2,1,0:T(8,128)(2,1)S(1)}, bf16[2,192,128]{2,1,0:T(8,128)(2,1)S(1)}, u32[]{:S(2)}, u32[]{:S(2)}) collective-permute-start(bf16[2,192,128]{2,1,0:T(8,128)(2,1)S(1)} %get-tuple-element.88), channel_id=1, source_target_pairs={{0,2},{2,0},{4,6},{6,4},{1,3},{3,1},{5,7},{7,5},{8,10},{10,8},{12,... | collective-permute-start | bytes 294920 | tf_op jit(solution)/shard_map/ppermute | solution.py:85
  59.5 0.7 collective-permute-start.24
  60.2 0.0 collective-permute-done.17.refs_3_
  60.2 4.7 %collective-permute-start.23 = (bf16[2,192,128]{2,1,0:T(8,128)(2,1)S(1)}, bf16[2,192,128]{2,1,0:T(8,128)(2,1)S(1)}, u32[]{:S(2)}, u32[]{:S(2)}) collective-permute-start(bf16[2,192,128]{2,1,0:T(8,128)(2,1)S(1)} %get-tuple-element.89), channel_id=1, source_target_pairs={{6,2},{0,4},{7,3},{1,5},{14,10},{8,12},{15,11},{9,13},{22,18},{16,... | collective-permute-start | bytes 294920 | tf_op jit(solution)/shard_map/ppermute | solution.py:85
  65.0 0.0 collective-permute-done.16.refs_2_
  65.0 0.0 collective-permute-done.15.refs_1_
  65.0 0.1 collective-permute-start.18
  65.1 1.5 %shard_map.97.refs_1_ = f32[128,3072]{1,0:T(8,128)} custom-call(s32[3]{0:T(128)S(1)} %pad_add_fusion.place, bf16[144,1536]{1,0:T(8,128)(2,1)S(1)} %shard_map.96.part), custom_call_target="tpu_custom_call" | custom-call | tf_op jit(solution)/shard_map/pallas_call | solution.py:279
  66.6 0.0 collective-permute-done.22
  66.6 0.0 collective-permute-done.24
  66.6 0.5 collective-permute-done.23
  67.1 0.1 add_convert_fusion
  67.2 0.6 fusion.1
  67.8 0.0 collective-permute-done.18.part
  67.8 2.1 %shard_map.98 = (f32[128,3072]{1,0:T(8,128)}, bf16[192,128]{1,0:T(8,128)(2,1)}) custom-call(s32[3]{0:T(128)S(1)} %pad_add_fusion.place, bf16[144,1536]{1,0:T(8,128)(2,1)S(1)} %collective-permute-done.18.part, f32[192,128]{1,0:T(8,128)S(1)} %get-tuple-element.82.refs_0_, f32[128,3072]{1,0:T(8,128)} %shard_map.97.refs_1_), custom_call_target="tpu_custom_call", output_to_operand_aliasing={{0}: (3, {})} | custom-call | tf_op jit(solution)/shard_map/pallas_call | solution.py:279
  (11 shorter events, 0.2 us)
Async XLA Ops:
  0.6 17.4 %copy-start.2 = (bf16[4,6,8,128]{3,2,1,0:T(8,128)(2,1)S(1)}, bf16[4,6,8,128]{3,2,1,0:T(8,128)(2,1)}, u32[]{:S(2)}) copy-start(bf16[4,6,8,128]{3,2,1,0:T(8,128)(2,1)} %param.5) | copy-start | bytes 147460
  0.6 20.8 %copy-start = (bf16[128,3072]{1,0:T(8,128)(2,1)S(1)}, bf16[128,3072]{1,0:T(8,128)(2,1)}, u32[]{:S(2)}) copy-start(bf16[128,3072]{1,0:T(8,128)(2,1)} %weight.1) | copy-start | bytes 2359300
  1.6 9.8 %collective-permute-start.2 = (bf16[2,192,128]{2,1,0:T(8,128)(2,1)S(1)}, bf16[2,192,128]{2,1,0:T(8,128)(2,1)S(1)}, u32[]{:S(2)}, u32[]{:S(2)}) collective-permute-start(bf16[2,192,128]{2,1,0:T(8,128)(2,1)S(1)} %get-tuple-element.94), channel_id=1, source_target_pairs={{2,4},{4,2},{3,5},{5,3},{10,12},{12,10},{11,13},{13,11},{18,20},{2... | collective-permute-start | bytes 294920 | tf_op jit(solution)/shard_map/ppermute | solution.py:64
  2.2 10.5 %collective-permute-start.1 = (bf16[2,192,128]{2,1,0:T(8,128)(2,1)S(1)}, bf16[2,192,128]{2,1,0:T(8,128)(2,1)S(1)}, u32[]{:S(2)}, u32[]{:S(2)}) collective-permute-start(bf16[2,192,128]{2,1,0:T(8,128)(2,1)S(1)} %get-tuple-element.94), channel_id=1, source_target_pairs={{2,6},{4,0},{3,7},{5,1},{10,14},{12,8},{11,15},{13,9},{18,22},{20,... | collective-permute-start | bytes 294920 | tf_op jit(solution)/shard_map/ppermute | solution.py:64
  3.5 10.6 %collective-permute-start = (bf16[2,192,128]{2,1,0:T(8,128)(2,1)S(1)}, bf16[2,192,128]{2,1,0:T(8,128)(2,1)S(1)}, u32[]{:S(2)}, u32[]{:S(2)}) collective-permute-start(bf16[2,192,128]{2,1,0:T(8,128)(2,1)S(1)} %get-tuple-element.94), channel_id=1, source_target_pairs={{2,0},{0,2},{6,4},{4,6},{3,1},{1,3},{7,5},{5,7},{10,8},{8,10},{14,... | collective-permute-start | bytes 294920 | tf_op jit(solution)/shard_map/ppermute | solution.py:64
  9.8 4.6 %collective-permute-start.3 = (bf16[1,2,192,128]{3,2,1,0:T(8,128)(2,1)S(1)}, bf16[1,2,192,128]{3,2,1,0:T(8,128)(2,1)S(1)}, u32[]{:S(2)}, u32[]{:S(2)}) collective-permute-start(bf16[1,2,192,128]{3,2,1,0:T(8,128)(2,1)S(1)} %get-tuple-element.93), channel_id=1, source_target_pairs={{0,1},{1,0},{2,3},{3,2},{4,5},{5,4},{6,7},{7,6},{8,9},{9,8},{10,11... | collective-permute-start | bytes 294920 | tf_op jit(solution)/shard_map/ppermute | solution.py:378
  14.5 12.5 %collective-permute-start.7 = (bf16[3,2,192,128]{3,2,1,0:T(8,128)(2,1)S(1)}, bf16[3,2,192,128]{3,2,1,0:T(8,128)(2,1)S(1)}, u32[]{:S(2)}, u32[]{:S(2)}) collective-permute-start(bf16[3,2,192,128]{3,2,1,0:T(8,128)(2,1)S(1)} %pad_maximum_fusion.refs_0_), channel_id=1, source_target_pairs={{16,9},{17,8},{8,17},{9,16},{18,11},{19,10},{10,19},{11,18},{20,13... | collective-permute-start | bytes 884744 | tf_op jit(solution)/shard_map/ppermute | solution.py:387
  15.1 11.9 %collective-permute-start.6 = (bf16[3,2,192,128]{3,2,1,0:T(8,128)(2,1)S(1)}, bf16[3,2,192,128]{3,2,1,0:T(8,128)(2,1)S(1)}, u32[]{:S(2)}, u32[]{:S(2)}) collective-permute-start(bf16[3,2,192,128]{3,2,1,0:T(8,128)(2,1)S(1)} %pad_maximum_fusion.refs_0_), channel_id=1, source_target_pairs={{16,0},{8,24},{17,1},{9,25},{18,2},{10,26},{19,3},{11,27},{20,4},{... | collective-permute-start | bytes 884744 | tf_op jit(solution)/shard_map/ppermute | solution.py:386
  16.4 10.6 %collective-permute-start.5 = (bf16[2,2,192,128]{3,2,1,0:T(8,128)(2,1)S(1)}, bf16[2,2,192,128]{3,2,1,0:T(8,128)(2,1)S(1)}, u32[]{:S(2)}, u32[]{:S(2)}) collective-permute-start(bf16[2,2,192,128]{3,2,1,0:T(8,128)(2,1)S(1)} %pad_maximum_fusion.1), channel_id=1, source_target_pairs={{0,1},{1,0},{2,3},{3,2},{4,5},{5,4},{6,7},{7,6},{8,9},{9,8},{10,11... | collective-permute-start | bytes 589832 | tf_op jit(solution)/shard_map/ppermute | solution.py:384
  18.0 3.4 %collective-permute-start.4 = (bf16[192,128]{1,0:T(8,128)(2,1)S(1)}, bf16[192,128]{1,0:T(8,128)(2,1)S(1)}, u32[]{:S(2)}, u32[]{:S(2)}) collective-permute-start(bf16[192,128]{1,0:T(8,128)(2,1)S(1)} %bitcast.19), channel_id=1, source_target_pairs={{0,8},{8,0},{16,24},{24,16},{1,9},{9,1},{17,25},{25,17},{2,10},{10... | collective-permute-start | bytes 147464 | tf_op jit(solution)/shard_map/ppermute | solution.py:100
  21.4 1.3 %copy-start.1 = (bf16[4,6,8,3072]{3,2,1,0:T(8,128)(2,1)S(1)}, bf16[4,6,8,3072]{3,2,1,0:T(8,128)(2,1)}, u32[]{:S(2)}) copy-start(bf16[4,6,8,3072]{3,2,1,0:T(8,128)(2,1)} %param.9) | copy-start | bytes 3538948
  27.0 3.8 %collective-permute-start.9 = (bf16[192,1664]{1,0:T(8,128)(2,1)S(1)}, bf16[192,1664]{1,0:T(8,128)(2,1)S(1)}, u32[]{:S(2)}, u32[]{:S(2)}) collective-permute-start(bf16[192,1664]{1,0:T(8,128)(2,1)S(1)} %get-tuple-element.60), channel_id=1, source_target_pairs={{0,8},{8,0},{16,24},{24,16},{1,9},{9,1},{17,25},{25,17},{2,10},{10... | collective-permute-start | bytes 1916936 | tf_op jit(solution)/shard_map/ppermute | solution.py:100
  29.2 1.5 %collective-permute-start.8 = (f32[136,384]{1,0:T(8,128)S(1)}, f32[136,384]{1,0:T(8,128)S(1)}, u32[]{:S(2)}, u32[]{:S(2)}) collective-permute-start(f32[136,384]{1,0:T(8,128)S(1)} %shard_map.93.mine), channel_id=1, source_target_pairs={{0,8},{8,0},{16,24},{24,16},{1,9},{9,1},{17,25},{25,17},{2,10},{10... | collective-permute-start | bytes 626696 | tf_op jit(solution)/shard_map/ppermute | solution.py:100
  31.9 6.3 %collective-permute-start.10 = (bf16[32,1536]{1,0:T(8,128)(2,1)S(1)}, bf16[32,1536]{1,0:T(8,128)(2,1)S(1)}, u32[]{:S(2)}, u32[]{:S(2)}) collective-permute-start(bf16[32,1536]{1,0:T(8,128)(2,1)S(1)} %get-tuple-element.71), channel_id=1, source_target_pairs={{0,1},{1,0},{8,9},{9,8},{16,17},{17,16},{24,25},{25,24},{2,3},{3,2... | collective-permute-start | bytes 294920 | tf_op jit(solution)/shard_map/ppermute | solution.py:100
  33.4 5.6 %collective-permute-start.11 = (bf16[32,1536]{1,0:T(8,128)(2,1)S(1)}, bf16[32,1536]{1,0:T(8,128)(2,1)S(1)}, u32[]{:S(2)}, u32[]{:S(2)}) collective-permute-start(bf16[32,1536]{1,0:T(8,128)(2,1)S(1)} %get-tuple-element.72), channel_id=1, source_target_pairs={{0,16},{1,17},{8,24},{9,25},{16,0},{17,1},{24,8},{25,9},{2,18},{3,... | collective-permute-start | bytes 294920 | tf_op jit(solution)/shard_map/ppermute | solution.py:100
  33.7 6.5 %collective-permute-start.12 = (bf16[32,1536]{1,0:T(8,128)(2,1)S(1)}, bf16[32,1536]{1,0:T(8,128)(2,1)S(1)}, u32[]{:S(2)}, u32[]{:S(2)}) collective-permute-start(bf16[32,1536]{1,0:T(8,128)(2,1)S(1)} %get-tuple-element.73), channel_id=1, source_target_pairs={{0,17},{1,16},{8,25},{9,24},{16,1},{17,0},{24,9},{25,8},{2,19},{3,... | collective-permute-start | bytes 294920 | tf_op jit(solution)/shard_map/ppermute | solution.py:100
  40.3 6.2 %collective-permute-start.13 = (bf16[32,1536]{1,0:T(8,128)(2,1)S(1)}, bf16[32,1536]{1,0:T(8,128)(2,1)S(1)}, u32[]{:S(2)}, u32[]{:S(2)}) collective-permute-start(bf16[32,1536]{1,0:T(8,128)(2,1)S(1)} %add_convert_fusion.3), channel_id=1, source_target_pairs={{0,2},{2,0},{4,6},{6,4},{1,3},{3,1},{5,7},{7,5},{8,10},{10,8},{12,... | collective-permute-start | bytes 294920 | tf_op jit(solution)/shard_map/ppermute | solution.py:100
  40.4 17.0 %collective-permute-start.21 = (bf16[3,2,192,128]{3,2,1,0:T(8,128)(2,1)S(1)}, bf16[3,2,192,128]{3,2,1,0:T(8,128)(2,1)S(1)}, u32[]{:S(2)}, u32[]{:S(2)}) collective-permute-start(bf16[3,2,192,128]{3,2,1,0:T(8,128)(2,1)S(1)} %get-tuple-element.86), channel_id=1, source_target_pairs={{9,16},{8,17},{17,8},{16,9},{11,18},{10,19},{19,10},{18,11},{13,20... | collective-permute-start | bytes 884744 | tf_op jit(solution)/shard_map/ppermute | solution.py:487
  41.1 16.3 %collective-permute-start.20 = (bf16[3,2,192,128]{3,2,1,0:T(8,128)(2,1)S(1)}, bf16[3,2,192,128]{3,2,1,0:T(8,128)(2,1)S(1)}, u32[]{:S(2)}, u32[]{:S(2)}) collective-permute-start(bf16[3,2,192,128]{3,2,1,0:T(8,128)(2,1)S(1)} %get-tuple-element.86), channel_id=1, source_target_pairs={{0,16},{24,8},{1,17},{25,9},{2,18},{26,10},{3,19},{27,11},{4,20},{... | collective-permute-start | bytes 884744 | tf_op jit(solution)/shard_map/ppermute | solution.py:486
  46.0 9.4 %collective-permute-start.19 = (bf16[3,2,192,128]{3,2,1,0:T(8,128)(2,1)S(1)}, bf16[3,2,192,128]{3,2,1,0:T(8,128)(2,1)S(1)}, u32[]{:S(2)}, u32[]{:S(2)}) collective-permute-start(bf16[3,2,192,128]{3,2,1,0:T(8,128)(2,1)S(1)} %get-tuple-element.85), channel_id=1, source_target_pairs={{0,1},{1,0},{2,3},{3,2},{4,5},{5,4},{6,7},{7,6},{8,9},{9,8},{10,11... | collective-permute-start | bytes 884744 | tf_op jit(solution)/shard_map/ppermute | solution.py:485
  46.5 7.3 %collective-permute-start.14 = (bf16[32,1536]{1,0:T(8,128)(2,1)S(1)}, bf16[32,1536]{1,0:T(8,128)(2,1)S(1)}, u32[]{:S(2)}, u32[]{:S(2)}) collective-permute-start(bf16[32,1536]{1,0:T(8,128)(2,1)S(1)} %add_convert_fusion.2), channel_id=1, source_target_pairs={{0,4},{2,6},{4,0},{6,2},{1,5},{3,7},{5,1},{7,3},{8,12},{10,14},{12... | collective-permute-start | bytes 294920 | tf_op jit(solution)/shard_map/ppermute | solution.py:100
  53.9 6.3 %collective-permute-start.17 = (bf16[32,1536]{1,0:T(8,128)(2,1)S(1)}, bf16[32,1536]{1,0:T(8,128)(2,1)S(1)}, u32[]{:S(2)}, u32[]{:S(2)}) collective-permute-start(bf16[32,1536]{1,0:T(8,128)(2,1)S(1)} %add_convert_fusion.1.refs_0_), channel_id=1, source_target_pairs={{0,17},{1,16},{8,25},{9,24},{16,1},{17,0},{24,9},{25,8},{2,19},{3,... | collective-permute-start | bytes 294920 | tf_op jit(solution)/shard_map/ppermute | solution.py:100
  55.2 9.8 %collective-permute-start.16 = (bf16[32,1536]{1,0:T(8,128)(2,1)S(1)}, bf16[32,1536]{1,0:T(8,128)(2,1)S(1)}, u32[]{:S(2)}, u32[]{:S(2)}) collective-permute-start(bf16[32,1536]{1,0:T(8,128)(2,1)S(1)} %add_convert_fusion.1.refs_0_), channel_id=1, source_target_pairs={{0,16},{1,17},{8,24},{9,25},{16,0},{17,1},{24,8},{25,9},{2,18},{3,... | collective-permute-start | bytes 294920 | tf_op jit(solution)/shard_map/ppermute | solution.py:100
  55.5 9.5 %collective-permute-start.15 = (bf16[32,1536]{1,0:T(8,128)(2,1)S(1)}, bf16[32,1536]{1,0:T(8,128)(2,1)S(1)}, u32[]{:S(2)}, u32[]{:S(2)}) collective-permute-start(bf16[32,1536]{1,0:T(8,128)(2,1)S(1)} %add_convert_fusion.1.refs_0_), channel_id=1, source_target_pairs={{0,1},{1,0},{8,9},{9,8},{16,17},{17,16},{24,25},{25,24},{2,3},{3,2... | collective-permute-start | bytes 294920 | tf_op jit(solution)/shard_map/ppermute | solution.py:100
  57.6 9.0 %collective-permute-start.22 = (bf16[2,192,128]{2,1,0:T(8,128)(2,1)S(1)}, bf16[2,192,128]{2,1,0:T(8,128)(2,1)S(1)}, u32[]{:S(2)}, u32[]{:S(2)}) collective-permute-start(bf16[2,192,128]{2,1,0:T(8,128)(2,1)S(1)} %get-tuple-element.88), channel_id=1, source_target_pairs={{0,2},{2,0},{4,6},{6,4},{1,3},{3,1},{5,7},{7,5},{8,10},{10,8},{12,... | collective-permute-start | bytes 294920 | tf_op jit(solution)/shard_map/ppermute | solution.py:85
  59.5 7.1 %collective-permute-start.24 = (bf16[2,192,128]{2,1,0:T(8,128)(2,1)S(1)}, bf16[2,192,128]{2,1,0:T(8,128)(2,1)S(1)}, u32[]{:S(2)}, u32[]{:S(2)}) collective-permute-start(bf16[2,192,128]{2,1,0:T(8,128)(2,1)S(1)} %get-tuple-element.89), channel_id=1, source_target_pairs={{4,2},{2,4},{5,3},{3,5},{12,10},{10,12},{13,11},{11,13},{20,18},{1... | collective-permute-start | bytes 294920 | tf_op jit(solution)/shard_map/ppermute | solution.py:85
  60.2 6.9 %collective-permute-start.23 = (bf16[2,192,128]{2,1,0:T(8,128)(2,1)S(1)}, bf16[2,192,128]{2,1,0:T(8,128)(2,1)S(1)}, u32[]{:S(2)}, u32[]{:S(2)}) collective-permute-start(bf16[2,192,128]{2,1,0:T(8,128)(2,1)S(1)} %get-tuple-element.89), channel_id=1, source_target_pairs={{6,2},{0,4},{7,3},{1,5},{14,10},{8,12},{15,11},{9,13},{22,18},{16,... | collective-permute-start | bytes 294920 | tf_op jit(solution)/shard_map/ppermute | solution.py:85
  65.0 2.8 %collective-permute-start.18 = (bf16[144,1536]{1,0:T(8,128)(2,1)S(1)}, bf16[144,1536]{1,0:T(8,128)(2,1)S(1)}, u32[]{:S(2)}, u32[]{:S(2)}) collective-permute-start(bf16[144,1536]{1,0:T(8,128)(2,1)S(1)} %shard_map.96.part), channel_id=1, source_target_pairs={{0,8},{8,0},{16,24},{24,16},{1,9},{9,1},{17,25},{25,17},{2,10},{10... | collective-permute-start | bytes 1327112 | tf_op jit(solution)/shard_map/ppermute | solution.py:100

commit v3 on v2

--- a/solution.py
+++ b/solution.py
@@ -77,7 +77,7 @@
     extent = lax.axis_size(axis)
     slots = slots_of(extent)
     summed = pieces[0]
-    for c, route in enumerate(routes_of(extent)):
+    for c, route in reversed(list(enumerate(routes_of(extent)))):
         holders = [next((k for k in range(len(slots)) if slots[k][p] == c), None) for p in range(extent)]
         used = sorted({k for k in holders if k is not None})
         choice = [k if k is not None else used[0] for k in holders]
@@ -127,14 +127,14 @@
     both[pl.ds(pl.multiple_of((1 - place[0]) * tile, tile), tile), :] = theirs
 
 
-def forward_kernel(inv_root, layout, place, both_queries, *refs):
+def forward_kernel(inv_root, layout, carried, both_queries, *refs):
     groups, rest = split_groups(layout, refs)
-    partial, scores = rest
+    partial, scores = rest[-2:]
     dim = both_queries.shape[1]
     query_rows = both_queries[...]
-    top = None
-    start = 0
-    spans = []
+    top, start, spans = None, 0, []
+    if carried:
+        top = rest[0][dim : dim + 1, :]
     for group in groups:
         keys = rows_of(group, 0)
         piece = lax.dot_general(
@@ -143,12 +143,17 @@
         scores[start : start + keys.shape[0], :] = piece
         spans.append((start, keys.shape[0]))
         start += keys.shape[0]
-        piece_top = jnp.max(piece, axis=0, keepdims=True)
+        piece_top = jnp.max(piece, axis=0, keepdims=True) * inv_root
         top = piece_top if top is None else jnp.maximum(top, piece_top)
-    total = jnp.zeros_like(top)
-    mixed = jnp.zeros((dim, query_rows.shape[0]), jnp.float32)
+    if carried:
+        share = jnp.exp(rest[0][dim : dim + 1, :] - top)
+        total = rest[0][dim + 1 : dim + 2, :] * share
+        mixed = rest[0][:dim, :] * share
+    else:
+        total = jnp.zeros_like(top)
+        mixed = jnp.zeros((dim, query_rows.shape[0]), jnp.float32)
     for group, (start, count) in zip(groups, spans):
-        weights = jnp.exp((scores[start : start + count, :] - top) * inv_root)
+        weights = jnp.exp(scores[start : start + count, :] * inv_root - top)
         total = total + jnp.sum(weights, axis=0, keepdims=True)
         mixed = mixed + lax.dot_general(
             rows_of(group, 1),
@@ -158,7 +163,7 @@
         )
     partial[:dim, :] = mixed
     row = lax.broadcasted_iota(jnp.int32, (STAT_ROWS, query_rows.shape[0]), 0)
-    partial[dim:, :] = jnp.where(row == 0, top * inv_root, total)
+    partial[dim:, :] = jnp.where(row == 0, top, total)
 
 
 def merge_kernel(scale, plane, place, mine, theirs, payload, grads_half, grad_rows, *refs):
@@ -253,13 +258,16 @@
 def assemble_kernel(flipped, rows, place, part, *refs):
     whole, rows_ref, done = refs[-3 - flipped], refs[-2], refs[-1]
     count, width = rows_ref.shape
-    for order in range(count // rows):
-        row = pl.multiple_of((place[1] ^ order) * rows, rows)
-        rows_ref[pl.ds(row, rows), :] = part[order * rows : (order + 1) * rows, :].astype(jnp.float32)
     core = 1 - place[0] if flipped else place[0]
     columns = pl.ds(pl.multiple_of(core * width, width), width)
-    copy = pltpu.make_async_copy(rows_ref, whole.at[:, columns], done)
-    copy.start()
+    copies = []
+    for order in range(count // rows):
+        span = pl.ds(pl.multiple_of((place[1] ^ order) * rows, rows), rows)
+        rows_ref[span, :] = part[order * rows : (order + 1) * rows, :].astype(jnp.float32)
+        copies.append(
+            pltpu.make_async_copy(rows_ref.at[span, :], whole.at[span, columns], done.at[order])
+        )
+        copies[-1].start()
     if flipped:
         query_own, grad_query = refs[0], refs[-3]
         dim, step = grad_query.shape[1], part.shape[0] - count
@@ -267,7 +275,8 @@
             piece = part[count:, block * dim : (block + 1) * dim].astype(jnp.float32)
             span = slice(block * step, (block + 1) * step)
             grad_query[span, :] = (query_own[span, :] + piece).astype(jnp.bfloat16)
-    copy.wait()
+    for copy in copies:
+        copy.wait()
 
 
 def assemble(flipped, place, part, rows, shape, whole=None, query_own=None):
@@ -283,7 +292,7 @@
         out_specs=out_specs,
         scratch_shapes=[
             pltpu.VMEM((shape.shape[0], part.shape[1]), jnp.float32),
-            pltpu.SemaphoreType.DMA,
+            pltpu.SemaphoreType.DMA((shape.shape[0] // rows,)),
         ],
         input_output_aliases={3: 0} if flipped else {},
         compiler_params=PARAMS,
@@ -415,21 +424,33 @@
         ),
         cost=cost_of(2 * tile * head_dim * model_dim, 4 * tile * model_dim),
     )
-    payload, grad_rows, *blocks = lax.optimization_barrier((payload, grad_rows, *blocks))
-    payload = flip(payload, ("frame",), (1,))
     grad_shapes = [(column_tiles, 2, tile, head_dim)] * (kinds - 1)
     grad_shapes.append((column_tiles, 2, tile, head_dim) if small else far[0].shape)
     key_count = sum(shape[0] * shape[2] for shape in grad_shapes)
     product = 2 * key_count * 2 * tile * head_dim
     moved = sum(b.size * 2 for b in blocks)
 
-    partial = kernel_call(
-        functools.partial(forward_kernel, inv_root, layout),
-        (place, both_queries, *blocks),
-        shaped(head_dim + STAT_ROWS, 2 * tile, kind=jnp.float32),
-        scratch=(pltpu.VMEM((key_count, 2 * tile), jnp.float32),),
-        cost=cost_of(2 * product, moved),
-    )
+    def forward(operands, groups, carried):
+        keys, start = 0, 0
+        for count in groups:
+            keys += operands[start].shape[0] * operands[start].shape[2]
+            start += count
+        return pl.pallas_call(
+            functools.partial(forward_kernel, inv_root, groups, bool(carried)),
+            out_shape=shaped(head_dim + STAT_ROWS, 2 * tile, kind=jnp.float32),
+            in_specs=[VMEM] * (1 + len(operands) + len(carried)),
+            out_specs=VMEM,
+            scratch_shapes=[pltpu.VMEM((keys, 2 * tile), jnp.float32)],
+            compiler_params=PARAMS,
+            cost_estimate=cost_of(8 * keys * tile * head_dim, moved * keys // key_count),
+        )(both_queries, *operands, *carried)
+
+    partial = forward([blocks[0]] + far, (1, 2), ())
+    beside = blocks[1 : -len(far)]
+    payload, partial, *beside = lax.optimization_barrier((payload, partial, *beside))
+    payload = flip(payload, ("frame",), (1,))
+    partial = forward(beside, (1,) * len(beside), (partial,))
+    blocks = [blocks[0]] + beside + far
     partial_other = flip(partial, ("frame",), (1,))
     plane = 4
     chunks = plane if small else 0

time: 70.3 us -> 68.7 us (0.977)
  the two profiles are of different devices: /device:TPU:0 before, /device:TPU:11 now
where the time goes in v3:
time: 68.7 us; the launch traced here: 68.4 us
  starting transfers between devices  32 us (47%)
  waiting for transfers between devices  20.4 us (30%)
  Pallas kernels  10.5 us (15%)
  local copies, waits for them, and re-layouts  1.92 us (3%)
  matrix products  1.47 us (2%)
  other arithmetic  1.23 us (2%)
  between operations  0.93 us (1%)
    ppermute x12, starting transfers between devices, flip(): return lax.ppermute(block, axes, route)  10.7 us
    ppermute x1, starting transfers between devices, body(): lax.ppermute(far_grad, 'frame', [(0, 2), (3, 1)])  6.82 us
    ppermute x12, waiting for transfers between devices, flip(): return lax.ppermute(block, axes, route)  6.17 us
    ppermute x3, starting transfers between devices, fetch(): arrived = [lax.ppermute(block, axis, route) for route in routes]  4.96 us
    pallas_call x3, Pallas kernels, kernel_call(): pl.pallas_call(kernel, out_shape=outs, in_specs=[SMEM] + [VMEM] * (len(op...  4.86 us
    ppermute x1, waiting for transfers between devices, body(): lax.ppermute(beside_grads[0], 'width', [(0, 1), (1, 0)])  4.26 us
    ppermute x3, waiting for transfers between devices, give_back(): back = lax.ppermute(outgoing, axis, [(p, s) for s, p in route])  3.96 us
    pallas_call x2, Pallas kernels, assemble(): pl.pallas_call(functools.partial(assemble_kernel, flipped, rows), out_sha...  3.54 us
  transfers between devices with their start and end apart: 25, of which 10 were waited for; matrix products, arithmetic and copies ran while one was open for 3% of the time, Pallas kernels for 11%

profile of v3, /device:TPU:11, one launch (start us, length us, event | category | flops | bytes accessed | tf_op | source)
XLA Modules:
  0.0 68.4 jit_solution(13752950234095695556)
XLA Ops:
  0.7 0.9 %fusion = (bf16[1,2,192,128]{3,2,1,0:T(8,128)(2,1)S(1)}, bf16[2,192,128]{2,1,0:T(8,128)(2,1)S(1)}) fusion(bf16[1,192,128]{2,1,0:T(8,128)(2,1)} %bitcast.24, bf16[1,192,128]{2,1,0:T(8,128)(2,1)} %bitcast.25), kind=kLoop, calls=%fused_computation.10 | loop fusion | flops 49152 | bytes 294912 | tf_op jit(solution)/shard_map/stack | solution.py:389
  1.6 3.2 %collective-permute-start.2 = (bf16[2,192,128]{2,1,0:T(8,128)(2,1)S(1)}, bf16[2,192,128]{2,1,0:T(8,128)(2,1)S(1)}, u32[]{:S(2)}, u32[]{:S(2)}) collective-permute-start(bf16[2,192,128]{2,1,0:T(8,128)(2,1)S(1)} %get-tuple-element.88), channel_id=1, source_target_pairs={{2,4},{4,2},{3,5},{5,3},{10,12},{12,10},{11,13},{13,11},{18,20},{2... | collective-permute-start | bytes 294920 | tf_op jit(solution)/shard_map/ppermute | solution.py:64
  4.8 1.7 %collective-permute-start.1 = (bf16[2,192,128]{2,1,0:T(8,128)(2,1)S(1)}, bf16[2,192,128]{2,1,0:T(8,128)(2,1)S(1)}, u32[]{:S(2)}, u32[]{:S(2)}) collective-permute-start(bf16[2,192,128]{2,1,0:T(8,128)(2,1)S(1)} %get-tuple-element.88), channel_id=1, source_target_pairs={{2,6},{4,0},{3,7},{5,1},{10,14},{12,8},{11,15},{13,9},{18,22},{20,... | collective-permute-start | bytes 294920 | tf_op jit(solution)/shard_map/ppermute | solution.py:64
  6.5 0.1 collective-permute-start
  6.5 1.3 %collective-permute-start.3 = (bf16[1,2,192,128]{3,2,1,0:T(8,128)(2,1)S(1)}, bf16[1,2,192,128]{3,2,1,0:T(8,128)(2,1)S(1)}, u32[]{:S(2)}, u32[]{:S(2)}) collective-permute-start(bf16[1,2,192,128]{3,2,1,0:T(8,128)(2,1)S(1)} %get-tuple-element.87), channel_id=1, source_target_pairs={{0,1},{1,0},{2,3},{3,2},{4,5},{5,4},{6,7},{7,6},{8,9},{9,8},{10,11... | collective-permute-start | bytes 294920 | tf_op jit(solution)/shard_map/ppermute | solution.py:387
  7.9 0.0 collective-permute-done.2
  7.9 1.1 %collective-permute-done.1 = bf16[2,192,128]{2,1,0:T(8,128)(2,1)S(1)} collective-permute-done((bf16[2,192,128]{2,1,0:T(8,128)(2,1)S(1)}, bf16[2,192,128]{2,1,0:T(8,128)(2,1)S(1)}, u32[]{:S(2)}, u32[]{:S(2)}) %collective-permute-start.1) | collective-permute-done | bytes 98336 | tf_op jit(solution)/shard_map/ppermute | solution.py:64
  8.9 1.5 %collective-permute-done = bf16[2,192,128]{2,1,0:T(8,128)(2,1)S(1)} collective-permute-done((bf16[2,192,128]{2,1,0:T(8,128)(2,1)S(1)}, bf16[2,192,128]{2,1,0:T(8,128)(2,1)S(1)}, u32[]{:S(2)}, u32[]{:S(2)}) %collective-permute-start) | collective-permute-done | bytes 98336 | tf_op jit(solution)/shard_map/ppermute | solution.py:64
  10.4 0.0 collective-permute-done.3.refs_0_.refs_1_
  10.5 0.7 collective-permute-start.6
  11.1 1.3 %collective-permute-start.5 = (bf16[3,2,192,128]{3,2,1,0:T(8,128)(2,1)S(1)}, bf16[3,2,192,128]{3,2,1,0:T(8,128)(2,1)S(1)}, u32[]{:S(2)}, u32[]{:S(2)}) collective-permute-start(bf16[3,2,192,128]{3,2,1,0:T(8,128)(2,1)S(1)} %pad_maximum_fusion.refs_0_), channel_id=1, source_target_pairs={{16,0},{8,24},{17,1},{9,25},{18,2},{10,26},{19,3},{11,27},{20,4},{... | collective-permute-start | bytes 884744 | tf_op jit(solution)/shard_map/ppermute | solution.py:395
  12.4 1.3 %collective-permute-start.7 = (bf16[2,2,192,128]{3,2,1,0:T(8,128)(2,1)S(1)}, bf16[2,2,192,128]{3,2,1,0:T(8,128)(2,1)S(1)}, u32[]{:S(2)}, u32[]{:S(2)}) collective-permute-start(bf16[2,2,192,128]{3,2,1,0:T(8,128)(2,1)S(1)} %pad_maximum_fusion.1), channel_id=1, source_target_pairs={{0,1},{1,0},{2,3},{3,2},{4,5},{5,4},{6,7},{7,6},{8,9},{9,8},{10,11... | collective-permute-start | bytes 589832 | tf_op jit(solution)/shard_map/ppermute | solution.py:393
  13.8 3.3 %collective-permute-start.4 = (bf16[192,128]{1,0:T(8,128)(2,1)S(1)}, bf16[192,128]{1,0:T(8,128)(2,1)S(1)}, u32[]{:S(2)}, u32[]{:S(2)}) collective-permute-start(bf16[192,128]{1,0:T(8,128)(2,1)S(1)} %bitcast.19), channel_id=1, source_target_pairs={{0,8},{8,0},{16,24},{24,16},{1,9},{9,1},{17,25},{25,17},{2,10},{10... | collective-permute-start | bytes 147464 | tf_op jit(solution)/shard_map/ppermute | solution.py:100
  17.0 0.1 pad_add_fusion.place
  17.1 0.8 %collective-permute-done.4.queries_other = bf16[192,128]{1,0:T(8,128)(2,1)S(1)} collective-permute-done((bf16[192,128]{1,0:T(8,128)(2,1)S(1)}, bf16[192,128]{1,0:T(8,128)(2,1)S(1)}, u32[]{:S(2)}, u32[]{:S(2)}) %collective-permute-start.4) | collective-permute-done | bytes 49184 | tf_op jit(solution)/shard_map/ppermute | solution.py:100
  17.9 1.3 %copy-done.1 = bf16[4,6,8,3072]{3,2,1,0:T(8,128)(2,1)S(1)} copy-done((bf16[4,6,8,3072]{3,2,1,0:T(8,128)(2,1)S(1)}, bf16[4,6,8,3072]{3,2,1,0:T(8,128)(2,1)}, u32[]{:S(2)}) %copy-start.1) | copy-done | bytes 1179672
  19.2 1.0 %shard_map.92 = (bf16[192,1664]{1,0:T(8,128)(2,1)S(1)}, bf16[192,1536]{1,0:T(8,128)(2,1)S(1)}, bf16[192,128]{1,0:T(8,128)(2,1)S(1)}, bf16[384,128]{1,0:T(8,128)(2,1)S(1)}) custom-call(s32[3]{0:T(128)S(1)} %pad_add_fusion.place, bf16[192,128]{1,0:T(8,128)(2,1)S(1)} %bitcast.20, bf16[192,128]{1,0:T(8,128)(2,1)S(1)} %collective-permute-done.4.queries_other, ...), custom_call_target="tpu_custom_call" | custom-call | flops 150994944 | bytes 2359296 | tf_op jit(solution)/shard_map/pallas_call | solution.py:324
  20.2 0.0 collective-permute-done.6.refs_2_.refs_4_
  20.2 3.5 %collective-permute-done.5.refs_1_.refs_3_ = bf16[3,2,192,128]{3,2,1,0:T(8,128)(2,1)S(1)} collective-permute-done((bf16[3,2,192,128]{3,2,1,0:T(8,128)(2,1)S(1)}, bf16[3,2,192,128]{3,2,1,0:T(8,128)(2,1)S(1)}, u32[]{:S(2)}, u32[]{:S(2)}) %collective-permute-start.5) | collective-permute-done | bytes 294944 | tf_op jit(solution)/shard_map/ppermute | solution.py:395
  23.7 1.2 %shard_map.93.refs_2_ = f32[136,384]{1,0:T(8,128)S(1)} custom-call(bf16[384,128]{1,0:T(8,128)(2,1)S(1)} %get-tuple-element.46.both_queries, bf16[3,2,192,128]{3,2,1,0:T(8,128)(2,1)S(1)} %pad_maximum_fusion.refs_0_, bf16[3,2,192,128]{3,2,1,0:T(8,128)(2,1)S(1)} %collective-permute-done.5.refs_1_.refs_3_, ...), custom_call_target="tpu_custom_call" | custom-call | flops 226492416 | bytes 786432 | tf_op jit(solution)/shard_map/pallas_call | solution.py:438
  24.9 0.0 collective-permute-done.7.refs_1_.refs_2_
  24.9 0.1 collective-permute-start.9
  24.9 0.8 %shard_map.94.mine = f32[136,384]{1,0:T(8,128)S(1)} custom-call(bf16[384,128]{1,0:T(8,128)(2,1)S(1)} %get-tuple-element.46.both_queries, bf16[1,2,192,128]{3,2,1,0:T(8,128)(2,1)S(1)} %collective-permute-done.3.refs_0_.refs_1_, bf16[2,2,192,128]{3,2,1,0:T(8,128)(2,1)S(1)} %collective-permute-done.7.refs_1_.refs_2_, f32[136,384]{1,0:T(8,128)S(1)} %shard_map.93.refs_2_), custom_call_target="tpu_custom_call" | custom-call | flops 113246208 | bytes 393216 | tf_op jit(solution)/shard_map/pallas_call | solution.py:438
  25.7 0.6 collective-permute-start.8
  26.3 1.1 %collective-permute-done.8.theirs = f32[136,384]{1,0:T(8,128)S(1)} collective-permute-done((f32[136,384]{1,0:T(8,128)S(1)}, f32[136,384]{1,0:T(8,128)S(1)}, u32[]{:S(2)}, u32[]{:S(2)}) %collective-permute-start.8) | collective-permute-done | bytes 208928 | tf_op jit(solution)/shard_map/ppermute | solution.py:100
  27.4 0.0 collective-permute-done.9.payload
  27.4 1.1 %shard_map.95 = (f32[8,384]{1,0:T(8,128)S(1)}, bf16[192,128]{1,0:T(8,128)(2,1)S(1)}, bf16[32,1536]{1,0:T(8,128)(2,1)S(1)}, bf16[32,1536]{1,0:T(8,128)(2,1)S(1)},...) custom-call(s32[3]{0:T(128)S(1)} %pad_add_fusion.place, f32[136,384]{1,0:T(8,128)S(1)} %shard_map.94.mine, ...), custom_call_target="tpu_custom_call" | custom-call | flops 150994944 | bytes 2359296 | tf_op jit(solution)/shard_map/pallas_call | solution.py:324
  28.5 0.5 collective-permute-start.10
  29.0 0.7 %collective-permute-start.11 = (bf16[32,1536]{1,0:T(8,128)(2,1)S(1)}, bf16[32,1536]{1,0:T(8,128)(2,1)S(1)}, u32[]{:S(2)}, u32[]{:S(2)}) collective-permute-start(bf16[32,1536]{1,0:T(8,128)(2,1)S(1)} %get-tuple-element.66), channel_id=1, source_target_pairs={{0,16},{1,17},{8,24},{9,25},{16,0},{17,1},{24,8},{25,9},{2,18},{3,... | collective-permute-start | bytes 294920 | tf_op jit(solution)/shard_map/ppermute | solution.py:100
  29.7 1.5 %collective-permute-start.12 = (bf16[32,1536]{1,0:T(8,128)(2,1)S(1)}, bf16[32,1536]{1,0:T(8,128)(2,1)S(1)}, u32[]{:S(2)}, u32[]{:S(2)}) collective-permute-start(bf16[32,1536]{1,0:T(8,128)(2,1)S(1)} %get-tuple-element.67), channel_id=1, source_target_pairs={{0,17},{1,16},{8,25},{9,24},{16,1},{17,0},{24,9},{25,8},{2,19},{3,... | collective-permute-start | bytes 294920 | tf_op jit(solution)/shard_map/ppermute | solution.py:100
  31.2 2.7 %shard_map.96 = (f32[3,2,192,128]{3,2,1,0:T(8,128)S(1)}, bf16[3,2,192,128]{3,2,1,0:T(8,128)(2,1)S(1)}, bf16[3,2,192,128]{3,2,1,0:T(8,128)(2,1)S(1)}, f32[192,128]{1,0:T(8,128)S(1)}, bf16[16,1536]{1,0:T(8,128)(2,1)S(1)}) custom-call(s32[3]{0:T(128)S(1)} %pad_add_fusion.place, f32[8,384]{1,0:T(8,128)S(1)} %get-tuple-element.58.stats, ...), custom_call_target="tpu_custom_call" | custom-call | flops 849346560 | bytes 2359296 | tf_op jit(solution)/shard_map/pallas_call | solution.py:324
  33.9 0.0 collective-permute-done.10
  34.0 0.0 collective-permute-done.11
  34.0 1.3 %collective-permute-done.12 = bf16[32,1536]{1,0:T(8,128)(2,1)S(1)} collective-permute-done((bf16[32,1536]{1,0:T(8,128)(2,1)S(1)}, bf16[32,1536]{1,0:T(8,128)(2,1)S(1)}, u32[]{:S(2)}, u32[]{:S(2)}) %collective-permute-start.12) | collective-permute-done | bytes 98336 | tf_op jit(solution)/shard_map/ppermute | solution.py:100
  35.2 0.1 add_convert_fusion.3
  35.3 1.7 %collective-permute-start.13 = (bf16[32,1536]{1,0:T(8,128)(2,1)S(1)}, bf16[32,1536]{1,0:T(8,128)(2,1)S(1)}, u32[]{:S(2)}, u32[]{:S(2)}) collective-permute-start(bf16[32,1536]{1,0:T(8,128)(2,1)S(1)} %add_convert_fusion.3), channel_id=1, source_target_pairs={{0,2},{2,0},{4,6},{6,4},{1,3},{3,1},{5,7},{7,5},{8,10},{10,8},{12,... | collective-permute-start | bytes 294920 | tf_op jit(solution)/shard_map/ppermute | solution.py:100
  37.0 0.7 collective-permute-start.21
  37.7 6.8 %collective-permute-start.20 = (bf16[3,2,192,128]{3,2,1,0:T(8,128)(2,1)S(1)}, bf16[3,2,192,128]{3,2,1,0:T(8,128)(2,1)S(1)}, u32[]{:S(2)}, u32[]{:S(2)}) collective-permute-start(bf16[3,2,192,128]{3,2,1,0:T(8,128)(2,1)S(1)} %get-tuple-element.80), channel_id=1, source_target_pairs={{0,16},{24,8},{1,17},{25,9},{2,18},{26,10},{3,19},{27,11},{4,20},{... | collective-permute-start | bytes 884744 | tf_op jit(solution)/shard_map/ppermute | solution.py:507
  44.5 1.0 %collective-permute-start.19 = (bf16[3,2,192,128]{3,2,1,0:T(8,128)(2,1)S(1)}, bf16[3,2,192,128]{3,2,1,0:T(8,128)(2,1)S(1)}, u32[]{:S(2)}, u32[]{:S(2)}) collective-permute-start(bf16[3,2,192,128]{3,2,1,0:T(8,128)(2,1)S(1)} %get-tuple-element.79), channel_id=1, source_target_pairs={{0,1},{1,0},{2,3},{3,2},{4,5},{5,4},{6,7},{7,6},{8,9},{9,8},{10,11... | collective-permute-start | bytes 884744 | tf_op jit(solution)/shard_map/ppermute | solution.py:506
  45.6 0.0 collective-permute-done.13
  45.6 0.1 collective-permute-start.14
  45.7 1.5 %convolution_convert_fusion = bf16[192,3072]{1,0:T(8,128)(2,1)} fusion(bf16[192,128]{1,0:T(8,128)(2,1)S(1)} %get-tuple-element.70, bf16[128,3072]{1,0:T(8,128)(2,1)S(1)} %copy-done), kind=kOutput, calls=%fused_computation | convolution fusion | flops 151584768 | bytes 2015232 | tf_op jit(solution)/shard_map/dot_general | solution.py:499
  47.1 3.0 %collective-permute-done.14 = bf16[32,1536]{1,0:T(8,128)(2,1)S(1)} collective-permute-done((bf16[32,1536]{1,0:T(8,128)(2,1)S(1)}, bf16[32,1536]{1,0:T(8,128)(2,1)S(1)}, u32[]{:S(2)}, u32[]{:S(2)}) %collective-permute-start.14) | collective-permute-done | bytes 98336 | tf_op jit(solution)/shard_map/ppermute | solution.py:100
  50.2 0.1 collective-permute-start.17
  50.2 1.6 %collective-permute-start.16 = (bf16[32,1536]{1,0:T(8,128)(2,1)S(1)}, bf16[32,1536]{1,0:T(8,128)(2,1)S(1)}, u32[]{:S(2)}, u32[]{:S(2)}) collective-permute-start(bf16[32,1536]{1,0:T(8,128)(2,1)S(1)} %add_convert_fusion.1.refs_0_), channel_id=1, source_target_pairs={{0,16},{1,17},{8,24},{9,25},{16,0},{17,1},{24,8},{25,9},{2,18},{3,... | collective-permute-start | bytes 294920 | tf_op jit(solution)/shard_map/ppermute | solution.py:100
  51.8 4.3 %collective-permute-done.19.refs_0_ = bf16[3,2,192,128]{3,2,1,0:T(8,128)(2,1)S(1)} collective-permute-done((bf16[3,2,192,128]{3,2,1,0:T(8,128)(2,1)S(1)}, bf16[3,2,192,128]{3,2,1,0:T(8,128)(2,1)S(1)}, u32[]{:S(2)}, u32[]{:S(2)}) %collective-permute-start.19) | collective-permute-done | bytes 294944 | tf_op jit(solution)/shard_map/ppermute | solution.py:506
  56.1 0.5 collective-permute-start.15
  56.6 0.0 collective-permute-done.21.refs_2_
  56.6 0.0 collective-permute-done.20.refs_1_
  56.6 0.1 shard_map.100
  56.7 0.1 collective-permute-start.24
  56.8 1.3 %collective-permute-start.23 = (bf16[2,192,128]{2,1,0:T(8,128)(2,1)S(1)}, bf16[2,192,128]{2,1,0:T(8,128)(2,1)S(1)}, u32[]{:S(2)}, u32[]{:S(2)}) collective-permute-start(bf16[2,192,128]{2,1,0:T(8,128)(2,1)S(1)} %get-tuple-element.82), channel_id=1, source_target_pairs={{6,2},{0,4},{7,3},{1,5},{14,10},{8,12},{15,11},{9,13},{22,18},{16,... | collective-permute-start | bytes 294920 | tf_op jit(solution)/shard_map/ppermute | solution.py:85
  58.1 0.0 collective-permute-done.17.refs_3_
  58.1 1.9 %collective-permute-start.22 = (bf16[2,192,128]{2,1,0:T(8,128)(2,1)S(1)}, bf16[2,192,128]{2,1,0:T(8,128)(2,1)S(1)}, u32[]{:S(2)}, u32[]{:S(2)}) collective-permute-start(bf16[2,192,128]{2,1,0:T(8,128)(2,1)S(1)} %get-tuple-element.82), channel_id=1, source_target_pairs={{4,2},{2,4},{5,3},{3,5},{12,10},{10,12},{13,11},{11,13},{20,18},{1... | collective-permute-start | bytes 294920 | tf_op jit(solution)/shard_map/ppermute | solution.py:85
  60.1 0.0 collective-permute-done.15.refs_1_
  60.1 0.1 collective-permute-start.18
  60.2 1.5 %shard_map.98.refs_1_ = f32[128,3072]{1,0:T(8,128)} custom-call(s32[3]{0:T(128)S(1)} %pad_add_fusion.place, bf16[144,1536]{1,0:T(8,128)(2,1)S(1)} %shard_map.97.part), custom_call_target="tpu_custom_call" | custom-call | tf_op jit(solution)/shard_map/pallas_call | solution.py:288
  61.7 0.0 collective-permute-done.24
  61.7 1.7 %collective-permute-done.23 = bf16[2,192,128]{2,1,0:T(8,128)(2,1)S(1)} collective-permute-done((bf16[2,192,128]{2,1,0:T(8,128)(2,1)S(1)}, bf16[2,192,128]{2,1,0:T(8,128)(2,1)S(1)}, u32[]{:S(2)}, u32[]{:S(2)}) %collective-permute-start.23) | collective-permute-done | bytes 98336 | tf_op jit(solution)/shard_map/ppermute | solution.py:85
  63.4 2.2 %collective-permute-done.22 = bf16[2,192,128]{2,1,0:T(8,128)(2,1)S(1)} collective-permute-done((bf16[2,192,128]{2,1,0:T(8,128)(2,1)S(1)}, bf16[2,192,128]{2,1,0:T(8,128)(2,1)S(1)}, u32[]{:S(2)}, u32[]{:S(2)}) %collective-permute-start.22) | collective-permute-done | bytes 98336 | tf_op jit(solution)/shard_map/ppermute | solution.py:85
  65.6 0.1 add_convert_fusion
  65.7 0.6 fusion.1
  66.3 0.0 collective-permute-done.18.part
  66.3 2.1 %shard_map.99 = (f32[128,3072]{1,0:T(8,128)}, bf16[192,128]{1,0:T(8,128)(2,1)}) custom-call(s32[3]{0:T(128)S(1)} %pad_add_fusion.place, bf16[144,1536]{1,0:T(8,128)(2,1)S(1)} %collective-permute-done.18.part, f32[192,128]{1,0:T(8,128)S(1)} %get-tuple-element.76.refs_0_, f32[128,3072]{1,0:T(8,128)} %shard_map.98.refs_1_), custom_call_target="tpu_custom_call", output_to_operand_aliasing={{0}: (3, {})} | custom-call | tf_op jit(solution)/shard_map/pallas_call | solution.py:288
  (12 shorter events, 0.2 us)
Async XLA Ops:
  0.6 13.1 %copy-start.2 = (bf16[4,6,8,128]{3,2,1,0:T(8,128)(2,1)S(1)}, bf16[4,6,8,128]{3,2,1,0:T(8,128)(2,1)}, u32[]{:S(2)}) copy-start(bf16[4,6,8,128]{3,2,1,0:T(8,128)(2,1)} %param.5) | copy-start | bytes 147460
  0.6 17.3 %copy-start = (bf16[128,3072]{1,0:T(8,128)(2,1)S(1)}, bf16[128,3072]{1,0:T(8,128)(2,1)}, u32[]{:S(2)}) copy-start(bf16[128,3072]{1,0:T(8,128)(2,1)} %weight.1) | copy-start | bytes 2359300
  1.6 6.3 %collective-permute-start.2 = (bf16[2,192,128]{2,1,0:T(8,128)(2,1)S(1)}, bf16[2,192,128]{2,1,0:T(8,128)(2,1)S(1)}, u32[]{:S(2)}, u32[]{:S(2)}) collective-permute-start(bf16[2,192,128]{2,1,0:T(8,128)(2,1)S(1)} %get-tuple-element.88), channel_id=1, source_target_pairs={{2,4},{4,2},{3,5},{5,3},{10,12},{12,10},{11,13},{13,11},{18,20},{2... | collective-permute-start | bytes 294920 | tf_op jit(solution)/shard_map/ppermute | solution.py:64
  4.8 4.1 %collective-permute-start.1 = (bf16[2,192,128]{2,1,0:T(8,128)(2,1)S(1)}, bf16[2,192,128]{2,1,0:T(8,128)(2,1)S(1)}, u32[]{:S(2)}, u32[]{:S(2)}) collective-permute-start(bf16[2,192,128]{2,1,0:T(8,128)(2,1)S(1)} %get-tuple-element.88), channel_id=1, source_target_pairs={{2,6},{4,0},{3,7},{5,1},{10,14},{12,8},{11,15},{13,9},{18,22},{20,... | collective-permute-start | bytes 294920 | tf_op jit(solution)/shard_map/ppermute | solution.py:64
  6.5 3.9 %collective-permute-start = (bf16[2,192,128]{2,1,0:T(8,128)(2,1)S(1)}, bf16[2,192,128]{2,1,0:T(8,128)(2,1)S(1)}, u32[]{:S(2)}, u32[]{:S(2)}) collective-permute-start(bf16[2,192,128]{2,1,0:T(8,128)(2,1)S(1)} %get-tuple-element.88), channel_id=1, source_target_pairs={{2,0},{0,2},{6,4},{4,6},{3,1},{1,3},{7,5},{5,7},{10,8},{8,10},{14,... | collective-permute-start | bytes 294920 | tf_op jit(solution)/shard_map/ppermute | solution.py:64
  6.5 3.9 %collective-permute-start.3 = (bf16[1,2,192,128]{3,2,1,0:T(8,128)(2,1)S(1)}, bf16[1,2,192,128]{3,2,1,0:T(8,128)(2,1)S(1)}, u32[]{:S(2)}, u32[]{:S(2)}) collective-permute-start(bf16[1,2,192,128]{3,2,1,0:T(8,128)(2,1)S(1)} %get-tuple-element.87), channel_id=1, source_target_pairs={{0,1},{1,0},{2,3},{3,2},{4,5},{5,4},{6,7},{7,6},{8,9},{9,8},{10,11... | collective-permute-start | bytes 294920 | tf_op jit(solution)/shard_map/ppermute | solution.py:387
  10.5 9.7 %collective-permute-start.6 = (bf16[3,2,192,128]{3,2,1,0:T(8,128)(2,1)S(1)}, bf16[3,2,192,128]{3,2,1,0:T(8,128)(2,1)S(1)}, u32[]{:S(2)}, u32[]{:S(2)}) collective-permute-start(bf16[3,2,192,128]{3,2,1,0:T(8,128)(2,1)S(1)} %pad_maximum_fusion.refs_0_), channel_id=1, source_target_pairs={{16,9},{17,8},{8,17},{9,16},{18,11},{19,10},{10,19},{11,18},{20,13... | collective-permute-start | bytes 884744 | tf_op jit(solution)/shard_map/ppermute | solution.py:396
  11.1 12.6 %collective-permute-start.5 = (bf16[3,2,192,128]{3,2,1,0:T(8,128)(2,1)S(1)}, bf16[3,2,192,128]{3,2,1,0:T(8,128)(2,1)S(1)}, u32[]{:S(2)}, u32[]{:S(2)}) collective-permute-start(bf16[3,2,192,128]{3,2,1,0:T(8,128)(2,1)S(1)} %pad_maximum_fusion.refs_0_), channel_id=1, source_target_pairs={{16,0},{8,24},{17,1},{9,25},{18,2},{10,26},{19,3},{11,27},{20,4},{... | collective-permute-start | bytes 884744 | tf_op jit(solution)/shard_map/ppermute | solution.py:395
  12.4 12.4 %collective-permute-start.7 = (bf16[2,2,192,128]{3,2,1,0:T(8,128)(2,1)S(1)}, bf16[2,2,192,128]{3,2,1,0:T(8,128)(2,1)S(1)}, u32[]{:S(2)}, u32[]{:S(2)}) collective-permute-start(bf16[2,2,192,128]{3,2,1,0:T(8,128)(2,1)S(1)} %pad_maximum_fusion.1), channel_id=1, source_target_pairs={{0,1},{1,0},{2,3},{3,2},{4,5},{5,4},{6,7},{7,6},{8,9},{9,8},{10,11... | collective-permute-start | bytes 589832 | tf_op jit(solution)/shard_map/ppermute | solution.py:393
  13.8 4.1 %collective-permute-start.4 = (bf16[192,128]{1,0:T(8,128)(2,1)S(1)}, bf16[192,128]{1,0:T(8,128)(2,1)S(1)}, u32[]{:S(2)}, u32[]{:S(2)}) collective-permute-start(bf16[192,128]{1,0:T(8,128)(2,1)S(1)} %bitcast.19), channel_id=1, source_target_pairs={{0,8},{8,0},{16,24},{24,16},{1,9},{9,1},{17,25},{25,17},{2,10},{10... | collective-permute-start | bytes 147464 | tf_op jit(solution)/shard_map/ppermute | solution.py:100
  17.9 1.3 %copy-start.1 = (bf16[4,6,8,3072]{3,2,1,0:T(8,128)(2,1)S(1)}, bf16[4,6,8,3072]{3,2,1,0:T(8,128)(2,1)}, u32[]{:S(2)}) copy-start(bf16[4,6,8,3072]{3,2,1,0:T(8,128)(2,1)} %param.9) | copy-start | bytes 3538948
  24.9 2.5 %collective-permute-start.9 = (bf16[192,1664]{1,0:T(8,128)(2,1)S(1)}, bf16[192,1664]{1,0:T(8,128)(2,1)S(1)}, u32[]{:S(2)}, u32[]{:S(2)}) collective-permute-start(bf16[192,1664]{1,0:T(8,128)(2,1)S(1)} %get-tuple-element.54), channel_id=1, source_target_pairs={{0,8},{8,0},{16,24},{24,16},{1,9},{9,1},{17,25},{25,17},{2,10},{10... | collective-permute-start | bytes 1916936 | tf_op jit(solution)/shard_map/ppermute | solution.py:100
  25.7 1.6 %collective-permute-start.8 = (f32[136,384]{1,0:T(8,128)S(1)}, f32[136,384]{1,0:T(8,128)S(1)}, u32[]{:S(2)}, u32[]{:S(2)}) collective-permute-start(f32[136,384]{1,0:T(8,128)S(1)} %shard_map.94.mine), channel_id=1, source_target_pairs={{0,8},{8,0},{16,24},{24,16},{1,9},{9,1},{17,25},{25,17},{2,10},{10... | collective-permute-start | bytes 626696 | tf_op jit(solution)/shard_map/ppermute | solution.py:100
  28.5 5.5 %collective-permute-start.10 = (bf16[32,1536]{1,0:T(8,128)(2,1)S(1)}, bf16[32,1536]{1,0:T(8,128)(2,1)S(1)}, u32[]{:S(2)}, u32[]{:S(2)}) collective-permute-start(bf16[32,1536]{1,0:T(8,128)(2,1)S(1)} %get-tuple-element.65), channel_id=1, source_target_pairs={{0,1},{1,0},{8,9},{9,8},{16,17},{17,16},{24,25},{25,24},{2,3},{3,2... | collective-permute-start | bytes 294920 | tf_op jit(solution)/shard_map/ppermute | solution.py:100
  29.0 5.0 %collective-permute-start.11 = (bf16[32,1536]{1,0:T(8,128)(2,1)S(1)}, bf16[32,1536]{1,0:T(8,128)(2,1)S(1)}, u32[]{:S(2)}, u32[]{:S(2)}) collective-permute-start(bf16[32,1536]{1,0:T(8,128)(2,1)S(1)} %get-tuple-element.66), channel_id=1, source_target_pairs={{0,16},{1,17},{8,24},{9,25},{16,0},{17,1},{24,8},{25,9},{2,18},{3,... | collective-permute-start | bytes 294920 | tf_op jit(solution)/shard_map/ppermute | solution.py:100
  29.7 5.5 %collective-permute-start.12 = (bf16[32,1536]{1,0:T(8,128)(2,1)S(1)}, bf16[32,1536]{1,0:T(8,128)(2,1)S(1)}, u32[]{:S(2)}, u32[]{:S(2)}) collective-permute-start(bf16[32,1536]{1,0:T(8,128)(2,1)S(1)} %get-tuple-element.67), channel_id=1, source_target_pairs={{0,17},{1,16},{8,25},{9,24},{16,1},{17,0},{24,9},{25,8},{2,19},{3,... | collective-permute-start | bytes 294920 | tf_op jit(solution)/shard_map/ppermute | solution.py:100
  35.3 10.3 %collective-permute-start.13 = (bf16[32,1536]{1,0:T(8,128)(2,1)S(1)}, bf16[32,1536]{1,0:T(8,128)(2,1)S(1)}, u32[]{:S(2)}, u32[]{:S(2)}) collective-permute-start(bf16[32,1536]{1,0:T(8,128)(2,1)S(1)} %add_convert_fusion.3), channel_id=1, source_target_pairs={{0,2},{2,0},{4,6},{6,4},{1,3},{3,1},{5,7},{7,5},{8,10},{10,8},{12,... | collective-permute-start | bytes 294920 | tf_op jit(solution)/shard_map/ppermute | solution.py:100
  37.0 19.6 %collective-permute-start.21 = (bf16[3,2,192,128]{3,2,1,0:T(8,128)(2,1)S(1)}, bf16[3,2,192,128]{3,2,1,0:T(8,128)(2,1)S(1)}, u32[]{:S(2)}, u32[]{:S(2)}) collective-permute-start(bf16[3,2,192,128]{3,2,1,0:T(8,128)(2,1)S(1)} %get-tuple-element.80), channel_id=1, source_target_pairs={{9,16},{8,17},{17,8},{16,9},{11,18},{10,19},{19,10},{18,11},{13,20... | collective-permute-start | bytes 884744 | tf_op jit(solution)/shard_map/ppermute | solution.py:508
  37.7 18.9 %collective-permute-start.20 = (bf16[3,2,192,128]{3,2,1,0:T(8,128)(2,1)S(1)}, bf16[3,2,192,128]{3,2,1,0:T(8,128)(2,1)S(1)}, u32[]{:S(2)}, u32[]{:S(2)}) collective-permute-start(bf16[3,2,192,128]{3,2,1,0:T(8,128)(2,1)S(1)} %get-tuple-element.80), channel_id=1, source_target_pairs={{0,16},{24,8},{1,17},{25,9},{2,18},{26,10},{3,19},{27,11},{4,20},{... | collective-permute-start | bytes 884744 | tf_op jit(solution)/shard_map/ppermute | solution.py:507
  44.5 11.5 %collective-permute-start.19 = (bf16[3,2,192,128]{3,2,1,0:T(8,128)(2,1)S(1)}, bf16[3,2,192,128]{3,2,1,0:T(8,128)(2,1)S(1)}, u32[]{:S(2)}, u32[]{:S(2)}) collective-permute-start(bf16[3,2,192,128]{3,2,1,0:T(8,128)(2,1)S(1)} %get-tuple-element.79), channel_id=1, source_target_pairs={{0,1},{1,0},{2,3},{3,2},{4,5},{5,4},{6,7},{7,6},{8,9},{9,8},{10,11... | collective-permute-start | bytes 884744 | tf_op jit(solution)/shard_map/ppermute | solution.py:506
  45.6 4.5 %collective-permute-start.14 = (bf16[32,1536]{1,0:T(8,128)(2,1)S(1)}, bf16[32,1536]{1,0:T(8,128)(2,1)S(1)}, u32[]{:S(2)}, u32[]{:S(2)}) collective-permute-start(bf16[32,1536]{1,0:T(8,128)(2,1)S(1)} %add_convert_fusion.2), channel_id=1, source_target_pairs={{0,4},{2,6},{4,0},{6,2},{1,5},{3,7},{5,1},{7,3},{8,12},{10,14},{12... | collective-permute-start | bytes 294920 | tf_op jit(solution)/shard_map/ppermute | solution.py:100
  50.2 8.0 %collective-permute-start.17 = (bf16[32,1536]{1,0:T(8,128)(2,1)S(1)}, bf16[32,1536]{1,0:T(8,128)(2,1)S(1)}, u32[]{:S(2)}, u32[]{:S(2)}) collective-permute-start(bf16[32,1536]{1,0:T(8,128)(2,1)S(1)} %add_convert_fusion.1.refs_0_), channel_id=1, source_target_pairs={{0,17},{1,16},{8,25},{9,24},{16,1},{17,0},{24,9},{25,8},{2,19},{3,... | collective-permute-start | bytes 294920 | tf_op jit(solution)/shard_map/ppermute | solution.py:100
  50.2 9.8 %collective-permute-start.16 = (bf16[32,1536]{1,0:T(8,128)(2,1)S(1)}, bf16[32,1536]{1,0:T(8,128)(2,1)S(1)}, u32[]{:S(2)}, u32[]{:S(2)}) collective-permute-start(bf16[32,1536]{1,0:T(8,128)(2,1)S(1)} %add_convert_fusion.1.refs_0_), channel_id=1, source_target_pairs={{0,16},{1,17},{8,24},{9,25},{16,0},{17,1},{24,8},{25,9},{2,18},{3,... | collective-permute-start | bytes 294920 | tf_op jit(solution)/shard_map/ppermute | solution.py:100
  56.1 4.0 %collective-permute-start.15 = (bf16[32,1536]{1,0:T(8,128)(2,1)S(1)}, bf16[32,1536]{1,0:T(8,128)(2,1)S(1)}, u32[]{:S(2)}, u32[]{:S(2)}) collective-permute-start(bf16[32,1536]{1,0:T(8,128)(2,1)S(1)} %add_convert_fusion.1.refs_0_), channel_id=1, source_target_pairs={{0,1},{1,0},{8,9},{9,8},{16,17},{17,16},{24,25},{25,24},{2,3},{3,2... | collective-permute-start | bytes 294920 | tf_op jit(solution)/shard_map/ppermute | solution.py:100
  56.7 4.9 %collective-permute-start.24 = (bf16[2,192,128]{2,1,0:T(8,128)(2,1)S(1)}, bf16[2,192,128]{2,1,0:T(8,128)(2,1)S(1)}, u32[]{:S(2)}, u32[]{:S(2)}) collective-permute-start(bf16[2,192,128]{2,1,0:T(8,128)(2,1)S(1)} %get-tuple-element.83), channel_id=1, source_target_pairs={{0,2},{2,0},{4,6},{6,4},{1,3},{3,1},{5,7},{7,5},{8,10},{10,8},{12,... | collective-permute-start | bytes 294920 | tf_op jit(solution)/shard_map/ppermute | solution.py:85
  56.8 6.6 %collective-permute-start.23 = (bf16[2,192,128]{2,1,0:T(8,128)(2,1)S(1)}, bf16[2,192,128]{2,1,0:T(8,128)(2,1)S(1)}, u32[]{:S(2)}, u32[]{:S(2)}) collective-permute-start(bf16[2,192,128]{2,1,0:T(8,128)(2,1)S(1)} %get-tuple-element.82), channel_id=1, source_target_pairs={{6,2},{0,4},{7,3},{1,5},{14,10},{8,12},{15,11},{9,13},{22,18},{16,... | collective-permute-start | bytes 294920 | tf_op jit(solution)/shard_map/ppermute | solution.py:85
  58.1 7.5 %collective-permute-start.22 = (bf16[2,192,128]{2,1,0:T(8,128)(2,1)S(1)}, bf16[2,192,128]{2,1,0:T(8,128)(2,1)S(1)}, u32[]{:S(2)}, u32[]{:S(2)}) collective-permute-start(bf16[2,192,128]{2,1,0:T(8,128)(2,1)S(1)} %get-tuple-element.82), channel_id=1, source_target_pairs={{4,2},{2,4},{5,3},{3,5},{12,10},{10,12},{13,11},{11,13},{20,18},{1... | collective-permute-start | bytes 294920 | tf_op jit(solution)/shard_map/ppermute | solution.py:85
  60.1 6.2 %collective-permute-start.18 = (bf16[144,1536]{1,0:T(8,128)(2,1)S(1)}, bf16[144,1536]{1,0:T(8,128)(2,1)S(1)}, u32[]{:S(2)}, u32[]{:S(2)}) collective-permute-start(bf16[144,1536]{1,0:T(8,128)(2,1)S(1)} %shard_map.97.part), channel_id=1, source_target_pairs={{0,8},{8,0},{16,24},{24,16},{1,9},{9,1},{17,25},{25,17},{2,10},{10... | collective-permute-start | bytes 1327112 | tf_op jit(solution)/shard_map/ppermute | solution.py:100

commit v4 on v3

--- a/solution.py
+++ b/solution.py
@@ -392,8 +392,8 @@
         )
         others_beside = lax.ppermute(others, "width", swap)
         far = [
+            lax.ppermute(column, ("frame", "width"), cross),
             lax.ppermute(column, "frame", [(2, 0), (1, 3)]),
-            lax.ppermute(column, ("frame", "width"), cross),
         ]
         blocks = [column, own_beside, others_beside, *far]
         layout = (1, 1, 1, 2)
@@ -504,8 +504,8 @@
     if small:
         arrived = [
             lax.ppermute(beside_grads[0], "width", [(0, 1), (1, 0)]),
+            lax.ppermute(far_grad, ("frame", "width"), [(p, s) for s, p in cross]),
             lax.ppermute(far_grad, "frame", [(0, 2), (3, 1)]),
-            lax.ppermute(far_grad, ("frame", "width"), [(p, s) for s, p in cross]),
         ]
         other, projected = lax.optimization_barrier((other, projected))
         part = (part.astype(jnp.float32) + other.astype(jnp.float32)).astype(jnp.bfloat16)

time: 68.7 us -> 71.7 us (1.044)
  the two profiles are of different devices: /device:TPU:11 before, /device:TPU:9 now
where the time goes in v4:
time: 71.7 us; the launch traced here: 71.4 us
  starting transfers between devices  33.3 us (46%)
  waiting for transfers between devices  22.1 us (31%)
  Pallas kernels  10.5 us (15%)
  local copies, waits for them, and re-layouts  1.92 us (3%)
  matrix products  1.48 us (2%)
  other arithmetic  1.23 us (2%)
  between operations  0.89 us (1%)
    ppermute x12, starting transfers between devices, flip(): return lax.ppermute(block, axes, route)  9.05 us
    ppermute x12, waiting for transfers between devices, flip(): return lax.ppermute(block, axes, route)  8.01 us
    ppermute x1, waiting for transfers between devices, body(): lax.ppermute(beside_grads[0], 'width', [(0, 1), (1, 0)])  5.34 us
    ppermute x1, starting transfers between devices, body(): lax.ppermute(column, ('frame', 'width'), cross)  5.01 us
    ppermute x3, starting transfers between devices, fetch(): arrived = [lax.ppermute(block, axis, route) for route in routes]  4.96 us
    pallas_call x3, Pallas kernels, kernel_call(): pl.pallas_call(kernel, out_shape=outs, in_specs=[SMEM] + [VMEM] * (len(op...  4.86 us
    ppermute x1, starting transfers between devices, body(): lax.ppermute(far_grad, ('frame', 'width'), [(p, s) for s, p in cross])  4.58 us
    pallas_call x2, Pallas kernels, assemble(): pl.pallas_call(functools.partial(assemble_kernel, flipped, rows), out_sha...  3.54 us
  transfers between devices with their start and end apart: 25, of which 12 were waited for; matrix products, arithmetic and copies ran while one was open for 3% of the time, Pallas kernels for 10%

profile of v4, /device:TPU:9, one launch (start us, length us, event | category | flops | bytes accessed | tf_op | source)
XLA Modules:
  0.0 71.4 jit_solution(5039953911509415338)
XLA Ops:
  0.7 0.9 %fusion = (bf16[1,2,192,128]{3,2,1,0:T(8,128)(2,1)S(1)}, bf16[2,192,128]{2,1,0:T(8,128)(2,1)S(1)}) fusion(bf16[1,192,128]{2,1,0:T(8,128)(2,1)} %bitcast.24, bf16[1,192,128]{2,1,0:T(8,128)(2,1)} %bitcast.25), kind=kLoop, calls=%fused_computation.10 | loop fusion | flops 49152 | bytes 294912 | tf_op jit(solution)/shard_map/stack | solution.py:389
  1.6 3.2 %collective-permute-start.2 = (bf16[2,192,128]{2,1,0:T(8,128)(2,1)S(1)}, bf16[2,192,128]{2,1,0:T(8,128)(2,1)S(1)}, u32[]{:S(2)}, u32[]{:S(2)}) collective-permute-start(bf16[2,192,128]{2,1,0:T(8,128)(2,1)S(1)} %get-tuple-element.88), channel_id=1, source_target_pairs={{2,4},{4,2},{3,5},{5,3},{10,12},{12,10},{11,13},{13,11},{18,20},{2... | collective-permute-start | bytes 294920 | tf_op jit(solution)/shard_map/ppermute | solution.py:64
  4.8 1.7 %collective-permute-start.1 = (bf16[2,192,128]{2,1,0:T(8,128)(2,1)S(1)}, bf16[2,192,128]{2,1,0:T(8,128)(2,1)S(1)}, u32[]{:S(2)}, u32[]{:S(2)}) collective-permute-start(bf16[2,192,128]{2,1,0:T(8,128)(2,1)S(1)} %get-tuple-element.88), channel_id=1, source_target_pairs={{2,6},{4,0},{3,7},{5,1},{10,14},{12,8},{11,15},{13,9},{18,22},{20,... | collective-permute-start | bytes 294920 | tf_op jit(solution)/shard_map/ppermute | solution.py:64
  6.5 0.1 collective-permute-start
  6.5 1.3 %collective-permute-start.3 = (bf16[1,2,192,128]{3,2,1,0:T(8,128)(2,1)S(1)}, bf16[1,2,192,128]{3,2,1,0:T(8,128)(2,1)S(1)}, u32[]{:S(2)}, u32[]{:S(2)}) collective-permute-start(bf16[1,2,192,128]{3,2,1,0:T(8,128)(2,1)S(1)} %get-tuple-element.87), channel_id=1, source_target_pairs={{0,1},{1,0},{2,3},{3,2},{4,5},{5,4},{6,7},{7,6},{8,9},{9,8},{10,11... | collective-permute-start | bytes 294920 | tf_op jit(solution)/shard_map/ppermute | solution.py:387
  7.9 0.0 collective-permute-done.2
  7.9 1.1 %collective-permute-done.1 = bf16[2,192,128]{2,1,0:T(8,128)(2,1)S(1)} collective-permute-done((bf16[2,192,128]{2,1,0:T(8,128)(2,1)S(1)}, bf16[2,192,128]{2,1,0:T(8,128)(2,1)S(1)}, u32[]{:S(2)}, u32[]{:S(2)}) %collective-permute-start.1) | collective-permute-done | bytes 98336 | tf_op jit(solution)/shard_map/ppermute | solution.py:64
  8.9 1.5 %collective-permute-done = bf16[2,192,128]{2,1,0:T(8,128)(2,1)S(1)} collective-permute-done((bf16[2,192,128]{2,1,0:T(8,128)(2,1)S(1)}, bf16[2,192,128]{2,1,0:T(8,128)(2,1)S(1)}, u32[]{:S(2)}, u32[]{:S(2)}) %collective-permute-start) | collective-permute-done | bytes 98336 | tf_op jit(solution)/shard_map/ppermute | solution.py:64
  10.4 0.0 collective-permute-done.3.refs_0_.refs_1_
  10.5 3.1 %collective-permute-start.6 = (bf16[3,2,192,128]{3,2,1,0:T(8,128)(2,1)S(1)}, bf16[3,2,192,128]{3,2,1,0:T(8,128)(2,1)S(1)}, u32[]{:S(2)}, u32[]{:S(2)}) collective-permute-start(bf16[3,2,192,128]{3,2,1,0:T(8,128)(2,1)S(1)} %pad_maximum_fusion.refs_0_), channel_id=1, source_target_pairs={{16,0},{8,24},{17,1},{9,25},{18,2},{10,26},{19,3},{11,27},{20,4},{... | collective-permute-start | bytes 884744 | tf_op jit(solution)/shard_map/ppermute | solution.py:396
  13.6 5.0 %collective-permute-start.5 = (bf16[3,2,192,128]{3,2,1,0:T(8,128)(2,1)S(1)}, bf16[3,2,192,128]{3,2,1,0:T(8,128)(2,1)S(1)}, u32[]{:S(2)}, u32[]{:S(2)}) collective-permute-start(bf16[3,2,192,128]{3,2,1,0:T(8,128)(2,1)S(1)} %pad_maximum_fusion.refs_0_), channel_id=1, source_target_pairs={{16,9},{17,8},{8,17},{9,16},{18,11},{19,10},{10,19},{11,18},{20,13... | collective-permute-start | bytes 884744 | tf_op jit(solution)/shard_map/ppermute | solution.py:395
  18.6 0.3 collective-permute-start.7
  18.9 0.0 collective-permute-start.4
  18.9 0.1 pad_add_fusion.place
  19.0 1.2 %collective-permute-done.4.queries_other = bf16[192,128]{1,0:T(8,128)(2,1)S(1)} collective-permute-done((bf16[192,128]{1,0:T(8,128)(2,1)S(1)}, bf16[192,128]{1,0:T(8,128)(2,1)S(1)}, u32[]{:S(2)}, u32[]{:S(2)}) %collective-permute-start.4) | collective-permute-done | bytes 49184 | tf_op jit(solution)/shard_map/ppermute | solution.py:100
  20.1 1.3 %copy-done.1 = bf16[4,6,8,3072]{3,2,1,0:T(8,128)(2,1)S(1)} copy-done((bf16[4,6,8,3072]{3,2,1,0:T(8,128)(2,1)S(1)}, bf16[4,6,8,3072]{3,2,1,0:T(8,128)(2,1)}, u32[]{:S(2)}) %copy-start.1) | copy-done | bytes 1179672
  21.4 1.0 %shard_map.92 = (bf16[192,1664]{1,0:T(8,128)(2,1)S(1)}, bf16[192,1536]{1,0:T(8,128)(2,1)S(1)}, bf16[192,128]{1,0:T(8,128)(2,1)S(1)}, bf16[384,128]{1,0:T(8,128)(2,1)S(1)}) custom-call(s32[3]{0:T(128)S(1)} %pad_add_fusion.place, bf16[192,128]{1,0:T(8,128)(2,1)S(1)} %bitcast.20, bf16[192,128]{1,0:T(8,128)(2,1)S(1)} %collective-permute-done.4.queries_other, ...), custom_call_target="tpu_custom_call" | custom-call | flops 150994944 | bytes 2359296 | tf_op jit(solution)/shard_map/pallas_call | solution.py:324
  22.4 0.0 collective-permute-done.6.refs_2_.refs_4_
  22.4 1.9 %collective-permute-done.5.refs_1_.refs_3_ = bf16[3,2,192,128]{3,2,1,0:T(8,128)(2,1)S(1)} collective-permute-done((bf16[3,2,192,128]{3,2,1,0:T(8,128)(2,1)S(1)}, bf16[3,2,192,128]{3,2,1,0:T(8,128)(2,1)S(1)}, u32[]{:S(2)}, u32[]{:S(2)}) %collective-permute-start.5) | collective-permute-done | bytes 294944 | tf_op jit(solution)/shard_map/ppermute | solution.py:395
  24.3 1.2 %shard_map.93.refs_2_ = f32[136,384]{1,0:T(8,128)S(1)} custom-call(bf16[384,128]{1,0:T(8,128)(2,1)S(1)} %get-tuple-element.46.both_queries, bf16[3,2,192,128]{3,2,1,0:T(8,128)(2,1)S(1)} %pad_maximum_fusion.refs_0_, bf16[3,2,192,128]{3,2,1,0:T(8,128)(2,1)S(1)} %collective-permute-done.5.refs_1_.refs_3_, ...), custom_call_target="tpu_custom_call" | custom-call | flops 226492416 | bytes 786432 | tf_op jit(solution)/shard_map/pallas_call | solution.py:438
  25.5 0.8 %collective-permute-done.7.refs_1_.refs_2_ = bf16[2,2,192,128]{3,2,1,0:T(8,128)(2,1)S(1)} collective-permute-done((bf16[2,2,192,128]{3,2,1,0:T(8,128)(2,1)S(1)}, bf16[2,2,192,128]{3,2,1,0:T(8,128)(2,1)S(1)}, u32[]{:S(2)}, u32[]{:S(2)}) %collective-permute-start.7) | collective-permute-done | bytes 196640 | tf_op jit(solution)/shard_map/ppermute | solution.py:393
  26.3 0.0 collective-permute-start.9
  26.3 0.8 %shard_map.94.mine = f32[136,384]{1,0:T(8,128)S(1)} custom-call(bf16[384,128]{1,0:T(8,128)(2,1)S(1)} %get-tuple-element.46.both_queries, bf16[1,2,192,128]{3,2,1,0:T(8,128)(2,1)S(1)} %collective-permute-done.3.refs_0_.refs_1_, bf16[2,2,192,128]{3,2,1,0:T(8,128)(2,1)S(1)} %collective-permute-done.7.refs_1_.refs_2_, f32[136,384]{1,0:T(8,128)S(1)} %shard_map.93.refs_2_), custom_call_target="tpu_custom_call" | custom-call | flops 113246208 | bytes 393216 | tf_op jit(solution)/shard_map/pallas_call | solution.py:438
  27.1 0.6 collective-permute-start.8
  27.7 1.1 %collective-permute-done.8.theirs = f32[136,384]{1,0:T(8,128)S(1)} collective-permute-done((f32[136,384]{1,0:T(8,128)S(1)}, f32[136,384]{1,0:T(8,128)S(1)}, u32[]{:S(2)}, u32[]{:S(2)}) %collective-permute-start.8) | collective-permute-done | bytes 208928 | tf_op jit(solution)/shard_map/ppermute | solution.py:100
  28.8 0.0 collective-permute-done.9.payload
  28.8 1.1 %shard_map.95 = (f32[8,384]{1,0:T(8,128)S(1)}, bf16[192,128]{1,0:T(8,128)(2,1)S(1)}, bf16[32,1536]{1,0:T(8,128)(2,1)S(1)}, bf16[32,1536]{1,0:T(8,128)(2,1)S(1)},...) custom-call(s32[3]{0:T(128)S(1)} %pad_add_fusion.place, f32[136,384]{1,0:T(8,128)S(1)} %shard_map.94.mine, ...), custom_call_target="tpu_custom_call" | custom-call | flops 150994944 | bytes 2359296 | tf_op jit(solution)/shard_map/pallas_call | solution.py:324
  29.9 0.3 collective-permute-start.10
  30.2 1.2 %collective-permute-start.11 = (bf16[32,1536]{1,0:T(8,128)(2,1)S(1)}, bf16[32,1536]{1,0:T(8,128)(2,1)S(1)}, u32[]{:S(2)}, u32[]{:S(2)}) collective-permute-start(bf16[32,1536]{1,0:T(8,128)(2,1)S(1)} %get-tuple-element.66), channel_id=1, source_target_pairs={{0,16},{1,17},{8,24},{9,25},{16,0},{17,1},{24,8},{25,9},{2,18},{3,... | collective-permute-start | bytes 294920 | tf_op jit(solution)/shard_map/ppermute | solution.py:100
  31.4 1.2 %collective-permute-start.12 = (bf16[32,1536]{1,0:T(8,128)(2,1)S(1)}, bf16[32,1536]{1,0:T(8,128)(2,1)S(1)}, u32[]{:S(2)}, u32[]{:S(2)}) collective-permute-start(bf16[32,1536]{1,0:T(8,128)(2,1)S(1)} %get-tuple-element.67), channel_id=1, source_target_pairs={{0,17},{1,16},{8,25},{9,24},{16,1},{17,0},{24,9},{25,8},{2,19},{3,... | collective-permute-start | bytes 294920 | tf_op jit(solution)/shard_map/ppermute | solution.py:100
  32.6 2.7 %shard_map.96 = (f32[3,2,192,128]{3,2,1,0:T(8,128)S(1)}, bf16[3,2,192,128]{3,2,1,0:T(8,128)(2,1)S(1)}, bf16[3,2,192,128]{3,2,1,0:T(8,128)(2,1)S(1)}, f32[192,128]{1,0:T(8,128)S(1)}, bf16[16,1536]{1,0:T(8,128)(2,1)S(1)}) custom-call(s32[3]{0:T(128)S(1)} %pad_add_fusion.place, f32[8,384]{1,0:T(8,128)S(1)} %get-tuple-element.58.stats, ...), custom_call_target="tpu_custom_call" | custom-call | flops 849346560 | bytes 2359296 | tf_op jit(solution)/shard_map/pallas_call | solution.py:324
  35.4 0.0 collective-permute-done.10
  35.4 0.0 collective-permute-done.11
  35.4 1.7 %collective-permute-done.12 = bf16[32,1536]{1,0:T(8,128)(2,1)S(1)} collective-permute-done((bf16[32,1536]{1,0:T(8,128)(2,1)S(1)}, bf16[32,1536]{1,0:T(8,128)(2,1)S(1)}, u32[]{:S(2)}, u32[]{:S(2)}) %collective-permute-start.12) | collective-permute-done | bytes 98336 | tf_op jit(solution)/shard_map/ppermute | solution.py:100
  37.1 0.1 add_convert_fusion.3
  37.2 1.8 %collective-permute-start.13 = (bf16[32,1536]{1,0:T(8,128)(2,1)S(1)}, bf16[32,1536]{1,0:T(8,128)(2,1)S(1)}, u32[]{:S(2)}, u32[]{:S(2)}) collective-permute-start(bf16[32,1536]{1,0:T(8,128)(2,1)S(1)} %add_convert_fusion.3), channel_id=1, source_target_pairs={{0,2},{2,0},{4,6},{6,4},{1,3},{3,1},{5,7},{7,5},{8,10},{10,8},{12,... | collective-permute-start | bytes 294920 | tf_op jit(solution)/shard_map/ppermute | solution.py:100
  39.0 1.3 %collective-permute-start.21 = (bf16[3,2,192,128]{3,2,1,0:T(8,128)(2,1)S(1)}, bf16[3,2,192,128]{3,2,1,0:T(8,128)(2,1)S(1)}, u32[]{:S(2)}, u32[]{:S(2)}) collective-permute-start(bf16[3,2,192,128]{3,2,1,0:T(8,128)(2,1)S(1)} %get-tuple-element.80), channel_id=1, source_target_pairs={{0,16},{24,8},{1,17},{25,9},{2,18},{26,10},{3,19},{27,11},{4,20},{... | collective-permute-start | bytes 884744 | tf_op jit(solution)/shard_map/ppermute | solution.py:508
  40.3 4.6 %collective-permute-start.20 = (bf16[3,2,192,128]{3,2,1,0:T(8,128)(2,1)S(1)}, bf16[3,2,192,128]{3,2,1,0:T(8,128)(2,1)S(1)}, u32[]{:S(2)}, u32[]{:S(2)}) collective-permute-start(bf16[3,2,192,128]{3,2,1,0:T(8,128)(2,1)S(1)} %get-tuple-element.80), channel_id=1, source_target_pairs={{9,16},{8,17},{17,8},{16,9},{11,18},{10,19},{19,10},{18,11},{13,20... | collective-permute-start | bytes 884744 | tf_op jit(solution)/shard_map/ppermute | solution.py:507
  44.9 0.4 collective-permute-start.19
  45.3 0.0 collective-permute-done.13
  45.3 0.1 collective-permute-start.14
  45.4 1.5 %convolution_convert_fusion = bf16[192,3072]{1,0:T(8,128)(2,1)} fusion(bf16[192,128]{1,0:T(8,128)(2,1)S(1)} %get-tuple-element.70, bf16[128,3072]{1,0:T(8,128)(2,1)S(1)} %copy-done), kind=kOutput, calls=%fused_computation | convolution fusion | flops 151584768 | bytes 2015232 | tf_op jit(solution)/shard_map/dot_general | solution.py:499
  46.9 3.9 %collective-permute-done.14 = bf16[32,1536]{1,0:T(8,128)(2,1)S(1)} collective-permute-done((bf16[32,1536]{1,0:T(8,128)(2,1)S(1)}, bf16[32,1536]{1,0:T(8,128)(2,1)S(1)}, u32[]{:S(2)}, u32[]{:S(2)}) %collective-permute-start.14) | collective-permute-done | bytes 98336 | tf_op jit(solution)/shard_map/ppermute | solution.py:100
  50.8 0.1 collective-permute-start.17
  50.9 2.1 %collective-permute-start.16 = (bf16[32,1536]{1,0:T(8,128)(2,1)S(1)}, bf16[32,1536]{1,0:T(8,128)(2,1)S(1)}, u32[]{:S(2)}, u32[]{:S(2)}) collective-permute-start(bf16[32,1536]{1,0:T(8,128)(2,1)S(1)} %add_convert_fusion.1.refs_0_), channel_id=1, source_target_pairs={{0,16},{1,17},{8,24},{9,25},{16,0},{17,1},{24,8},{25,9},{2,18},{3,... | collective-permute-start | bytes 294920 | tf_op jit(solution)/shard_map/ppermute | solution.py:100
  53.0 5.3 %collective-permute-done.19.refs_0_ = bf16[3,2,192,128]{3,2,1,0:T(8,128)(2,1)S(1)} collective-permute-done((bf16[3,2,192,128]{3,2,1,0:T(8,128)(2,1)S(1)}, bf16[3,2,192,128]{3,2,1,0:T(8,128)(2,1)S(1)}, u32[]{:S(2)}, u32[]{:S(2)}) %collective-permute-start.19) | collective-permute-done | bytes 294944 | tf_op jit(solution)/shard_map/ppermute | solution.py:506
  58.4 0.5 collective-permute-start.15
  58.9 0.0 collective-permute-done.21.refs_2_
  58.9 0.0 collective-permute-done.20.refs_1_
  58.9 0.1 shard_map.100
  59.0 0.1 collective-permute-start.24
  59.1 1.3 %collective-permute-start.23 = (bf16[2,192,128]{2,1,0:T(8,128)(2,1)S(1)}, bf16[2,192,128]{2,1,0:T(8,128)(2,1)S(1)}, u32[]{:S(2)}, u32[]{:S(2)}) collective-permute-start(bf16[2,192,128]{2,1,0:T(8,128)(2,1)S(1)} %get-tuple-element.82), channel_id=1, source_target_pairs={{6,2},{0,4},{7,3},{1,5},{14,10},{8,12},{15,11},{9,13},{22,18},{16,... | collective-permute-start | bytes 294920 | tf_op jit(solution)/shard_map/ppermute | solution.py:85
  60.4 0.0 collective-permute-done.17.refs_3_
  60.4 1.9 %collective-permute-start.22 = (bf16[2,192,128]{2,1,0:T(8,128)(2,1)S(1)}, bf16[2,192,128]{2,1,0:T(8,128)(2,1)S(1)}, u32[]{:S(2)}, u32[]{:S(2)}) collective-permute-start(bf16[2,192,128]{2,1,0:T(8,128)(2,1)S(1)} %get-tuple-element.82), channel_id=1, source_target_pairs={{4,2},{2,4},{5,3},{3,5},{12,10},{10,12},{13,11},{11,13},{20,18},{1... | collective-permute-start | bytes 294920 | tf_op jit(solution)/shard_map/ppermute | solution.py:85
  62.4 0.0 collective-permute-done.16.refs_2_
  62.4 0.1 collective-permute-done.15.refs_1_
  62.5 1.1 %collective-permute-start.18 = (bf16[144,1536]{1,0:T(8,128)(2,1)S(1)}, bf16[144,1536]{1,0:T(8,128)(2,1)S(1)}, u32[]{:S(2)}, u32[]{:S(2)}) collective-permute-start(bf16[144,1536]{1,0:T(8,128)(2,1)S(1)} %shard_map.97.part), channel_id=1, source_target_pairs={{0,8},{8,0},{16,24},{24,16},{1,9},{9,1},{17,25},{25,17},{2,10},{10... | collective-permute-start | bytes 1327112 | tf_op jit(solution)/shard_map/ppermute | solution.py:100
  63.7 1.5 %shard_map.98.refs_1_ = f32[128,3072]{1,0:T(8,128)} custom-call(s32[3]{0:T(128)S(1)} %pad_add_fusion.place, bf16[144,1536]{1,0:T(8,128)(2,1)S(1)} %shard_map.97.part), custom_call_target="tpu_custom_call" | custom-call | tf_op jit(solution)/shard_map/pallas_call | solution.py:288
  65.1 0.0 collective-permute-done.24
  65.1 0.3 collective-permute-done.23
  65.4 3.2 %collective-permute-done.22 = bf16[2,192,128]{2,1,0:T(8,128)(2,1)S(1)} collective-permute-done((bf16[2,192,128]{2,1,0:T(8,128)(2,1)S(1)}, bf16[2,192,128]{2,1,0:T(8,128)(2,1)S(1)}, u32[]{:S(2)}, u32[]{:S(2)}) %collective-permute-start.22) | collective-permute-done | bytes 98336 | tf_op jit(solution)/shard_map/ppermute | solution.py:85
  68.6 0.1 add_convert_fusion
  68.7 0.6 fusion.1
  69.3 2.1 %shard_map.99 = (f32[128,3072]{1,0:T(8,128)}, bf16[192,128]{1,0:T(8,128)(2,1)}) custom-call(s32[3]{0:T(128)S(1)} %pad_add_fusion.place, bf16[144,1536]{1,0:T(8,128)(2,1)S(1)} %collective-permute-done.18.part, f32[192,128]{1,0:T(8,128)S(1)} %get-tuple-element.76.refs_0_, f32[128,3072]{1,0:T(8,128)} %shard_map.98.refs_1_), custom_call_target="tpu_custom_call", output_to_operand_aliasing={{0}: (3, {})} | custom-call | tf_op jit(solution)/shard_map/pallas_call | solution.py:288
  (12 shorter events, 0.2 us)
Async XLA Ops:
  0.6 18.3 %copy-start.2 = (bf16[4,6,8,128]{3,2,1,0:T(8,128)(2,1)S(1)}, bf16[4,6,8,128]{3,2,1,0:T(8,128)(2,1)}, u32[]{:S(2)}) copy-start(bf16[4,6,8,128]{3,2,1,0:T(8,128)(2,1)} %param.5) | copy-start | bytes 147460
  0.6 19.5 %copy-start = (bf16[128,3072]{1,0:T(8,128)(2,1)S(1)}, bf16[128,3072]{1,0:T(8,128)(2,1)}, u32[]{:S(2)}) copy-start(bf16[128,3072]{1,0:T(8,128)(2,1)} %weight.1) | copy-start | bytes 2359300
  1.6 6.3 %collective-permute-start.2 = (bf16[2,192,128]{2,1,0:T(8,128)(2,1)S(1)}, bf16[2,192,128]{2,1,0:T(8,128)(2,1)S(1)}, u32[]{:S(2)}, u32[]{:S(2)}) collective-permute-start(bf16[2,192,128]{2,1,0:T(8,128)(2,1)S(1)} %get-tuple-element.88), channel_id=1, source_target_pairs={{2,4},{4,2},{3,5},{5,3},{10,12},{12,10},{11,13},{13,11},{18,20},{2... | collective-permute-start | bytes 294920 | tf_op jit(solution)/shard_map/ppermute | solution.py:64
  4.8 4.1 %collective-permute-start.1 = (bf16[2,192,128]{2,1,0:T(8,128)(2,1)S(1)}, bf16[2,192,128]{2,1,0:T(8,128)(2,1)S(1)}, u32[]{:S(2)}, u32[]{:S(2)}) collective-permute-start(bf16[2,192,128]{2,1,0:T(8,128)(2,1)S(1)} %get-tuple-element.88), channel_id=1, source_target_pairs={{2,6},{4,0},{3,7},{5,1},{10,14},{12,8},{11,15},{13,9},{18,22},{20,... | collective-permute-start | bytes 294920 | tf_op jit(solution)/shard_map/ppermute | solution.py:64
  6.5 3.9 %collective-permute-start = (bf16[2,192,128]{2,1,0:T(8,128)(2,1)S(1)}, bf16[2,192,128]{2,1,0:T(8,128)(2,1)S(1)}, u32[]{:S(2)}, u32[]{:S(2)}) collective-permute-start(bf16[2,192,128]{2,1,0:T(8,128)(2,1)S(1)} %get-tuple-element.88), channel_id=1, source_target_pairs={{2,0},{0,2},{6,4},{4,6},{3,1},{1,3},{7,5},{5,7},{10,8},{8,10},{14,... | collective-permute-start | bytes 294920 | tf_op jit(solution)/shard_map/ppermute | solution.py:64
  6.5 3.9 %collective-permute-start.3 = (bf16[1,2,192,128]{3,2,1,0:T(8,128)(2,1)S(1)}, bf16[1,2,192,128]{3,2,1,0:T(8,128)(2,1)S(1)}, u32[]{:S(2)}, u32[]{:S(2)}) collective-permute-start(bf16[1,2,192,128]{3,2,1,0:T(8,128)(2,1)S(1)} %get-tuple-element.87), channel_id=1, source_target_pairs={{0,1},{1,0},{2,3},{3,2},{4,5},{5,4},{6,7},{7,6},{8,9},{9,8},{10,11... | collective-permute-start | bytes 294920 | tf_op jit(solution)/shard_map/ppermute | solution.py:387
  10.5 12.0 %collective-permute-start.6 = (bf16[3,2,192,128]{3,2,1,0:T(8,128)(2,1)S(1)}, bf16[3,2,192,128]{3,2,1,0:T(8,128)(2,1)S(1)}, u32[]{:S(2)}, u32[]{:S(2)}) collective-permute-start(bf16[3,2,192,128]{3,2,1,0:T(8,128)(2,1)S(1)} %pad_maximum_fusion.refs_0_), channel_id=1, source_target_pairs={{16,0},{8,24},{17,1},{9,25},{18,2},{10,26},{19,3},{11,27},{20,4},{... | collective-permute-start | bytes 884744 | tf_op jit(solution)/shard_map/ppermute | solution.py:396
  13.6 10.7 %collective-permute-start.5 = (bf16[3,2,192,128]{3,2,1,0:T(8,128)(2,1)S(1)}, bf16[3,2,192,128]{3,2,1,0:T(8,128)(2,1)S(1)}, u32[]{:S(2)}, u32[]{:S(2)}) collective-permute-start(bf16[3,2,192,128]{3,2,1,0:T(8,128)(2,1)S(1)} %pad_maximum_fusion.refs_0_), channel_id=1, source_target_pairs={{16,9},{17,8},{8,17},{9,16},{18,11},{19,10},{10,19},{11,18},{20,13... | collective-permute-start | bytes 884744 | tf_op jit(solution)/shard_map/ppermute | solution.py:395
  18.6 7.7 %collective-permute-start.7 = (bf16[2,2,192,128]{3,2,1,0:T(8,128)(2,1)S(1)}, bf16[2,2,192,128]{3,2,1,0:T(8,128)(2,1)S(1)}, u32[]{:S(2)}, u32[]{:S(2)}) collective-permute-start(bf16[2,2,192,128]{3,2,1,0:T(8,128)(2,1)S(1)} %pad_maximum_fusion.1), channel_id=1, source_target_pairs={{0,1},{1,0},{2,3},{3,2},{4,5},{5,4},{6,7},{7,6},{8,9},{9,8},{10,11... | collective-permute-start | bytes 589832 | tf_op jit(solution)/shard_map/ppermute | solution.py:393
  18.9 1.2 %collective-permute-start.4 = (bf16[192,128]{1,0:T(8,128)(2,1)S(1)}, bf16[192,128]{1,0:T(8,128)(2,1)S(1)}, u32[]{:S(2)}, u32[]{:S(2)}) collective-permute-start(bf16[192,128]{1,0:T(8,128)(2,1)S(1)} %bitcast.19), channel_id=1, source_target_pairs={{0,8},{8,0},{16,24},{24,16},{1,9},{9,1},{17,25},{25,17},{2,10},{10... | collective-permute-start | bytes 147464 | tf_op jit(solution)/shard_map/ppermute | solution.py:100
  20.1 1.3 %copy-start.1 = (bf16[4,6,8,3072]{3,2,1,0:T(8,128)(2,1)S(1)}, bf16[4,6,8,3072]{3,2,1,0:T(8,128)(2,1)}, u32[]{:S(2)}) copy-start(bf16[4,6,8,3072]{3,2,1,0:T(8,128)(2,1)} %param.9) | copy-start | bytes 3538948
  26.3 2.4 %collective-permute-start.9 = (bf16[192,1664]{1,0:T(8,128)(2,1)S(1)}, bf16[192,1664]{1,0:T(8,128)(2,1)S(1)}, u32[]{:S(2)}, u32[]{:S(2)}) collective-permute-start(bf16[192,1664]{1,0:T(8,128)(2,1)S(1)} %get-tuple-element.54), channel_id=1, source_target_pairs={{0,8},{8,0},{16,24},{24,16},{1,9},{9,1},{17,25},{25,17},{2,10},{10... | collective-permute-start | bytes 1916936 | tf_op jit(solution)/shard_map/ppermute | solution.py:100
  27.1 1.7 %collective-permute-start.8 = (f32[136,384]{1,0:T(8,128)S(1)}, f32[136,384]{1,0:T(8,128)S(1)}, u32[]{:S(2)}, u32[]{:S(2)}) collective-permute-start(f32[136,384]{1,0:T(8,128)S(1)} %shard_map.94.mine), channel_id=1, source_target_pairs={{0,8},{8,0},{16,24},{24,16},{1,9},{9,1},{17,25},{25,17},{2,10},{10... | collective-permute-start | bytes 626696 | tf_op jit(solution)/shard_map/ppermute | solution.py:100
  29.9 5.5 %collective-permute-start.10 = (bf16[32,1536]{1,0:T(8,128)(2,1)S(1)}, bf16[32,1536]{1,0:T(8,128)(2,1)S(1)}, u32[]{:S(2)}, u32[]{:S(2)}) collective-permute-start(bf16[32,1536]{1,0:T(8,128)(2,1)S(1)} %get-tuple-element.65), channel_id=1, source_target_pairs={{0,1},{1,0},{8,9},{9,8},{16,17},{17,16},{24,25},{25,24},{2,3},{3,2... | collective-permute-start | bytes 294920 | tf_op jit(solution)/shard_map/ppermute | solution.py:100
  30.2 5.2 %collective-permute-start.11 = (bf16[32,1536]{1,0:T(8,128)(2,1)S(1)}, bf16[32,1536]{1,0:T(8,128)(2,1)S(1)}, u32[]{:S(2)}, u32[]{:S(2)}) collective-permute-start(bf16[32,1536]{1,0:T(8,128)(2,1)S(1)} %get-tuple-element.66), channel_id=1, source_target_pairs={{0,16},{1,17},{8,24},{9,25},{16,0},{17,1},{24,8},{25,9},{2,18},{3,... | collective-permute-start | bytes 294920 | tf_op jit(solution)/shard_map/ppermute | solution.py:100
  31.4 5.7 %collective-permute-start.12 = (bf16[32,1536]{1,0:T(8,128)(2,1)S(1)}, bf16[32,1536]{1,0:T(8,128)(2,1)S(1)}, u32[]{:S(2)}, u32[]{:S(2)}) collective-permute-start(bf16[32,1536]{1,0:T(8,128)(2,1)S(1)} %get-tuple-element.67), channel_id=1, source_target_pairs={{0,17},{1,16},{8,25},{9,24},{16,1},{17,0},{24,9},{25,8},{2,19},{3,... | collective-permute-start | bytes 294920 | tf_op jit(solution)/shard_map/ppermute | solution.py:100
  37.2 8.1 %collective-permute-start.13 = (bf16[32,1536]{1,0:T(8,128)(2,1)S(1)}, bf16[32,1536]{1,0:T(8,128)(2,1)S(1)}, u32[]{:S(2)}, u32[]{:S(2)}) collective-permute-start(bf16[32,1536]{1,0:T(8,128)(2,1)S(1)} %add_convert_fusion.3), channel_id=1, source_target_pairs={{0,2},{2,0},{4,6},{6,4},{1,3},{3,1},{5,7},{7,5},{8,10},{10,8},{12,... | collective-permute-start | bytes 294920 | tf_op jit(solution)/shard_map/ppermute | solution.py:100
  39.0 19.9 %collective-permute-start.21 = (bf16[3,2,192,128]{3,2,1,0:T(8,128)(2,1)S(1)}, bf16[3,2,192,128]{3,2,1,0:T(8,128)(2,1)S(1)}, u32[]{:S(2)}, u32[]{:S(2)}) collective-permute-start(bf16[3,2,192,128]{3,2,1,0:T(8,128)(2,1)S(1)} %get-tuple-element.80), channel_id=1, source_target_pairs={{0,16},{24,8},{1,17},{25,9},{2,18},{26,10},{3,19},{27,11},{4,20},{... | collective-permute-start | bytes 884744 | tf_op jit(solution)/shard_map/ppermute | solution.py:508
  40.3 18.6 %collective-permute-start.20 = (bf16[3,2,192,128]{3,2,1,0:T(8,128)(2,1)S(1)}, bf16[3,2,192,128]{3,2,1,0:T(8,128)(2,1)S(1)}, u32[]{:S(2)}, u32[]{:S(2)}) collective-permute-start(bf16[3,2,192,128]{3,2,1,0:T(8,128)(2,1)S(1)} %get-tuple-element.80), channel_id=1, source_target_pairs={{9,16},{8,17},{17,8},{16,9},{11,18},{10,19},{19,10},{18,11},{13,20... | collective-permute-start | bytes 884744 | tf_op jit(solution)/shard_map/ppermute | solution.py:507
  44.9 13.5 %collective-permute-start.19 = (bf16[3,2,192,128]{3,2,1,0:T(8,128)(2,1)S(1)}, bf16[3,2,192,128]{3,2,1,0:T(8,128)(2,1)S(1)}, u32[]{:S(2)}, u32[]{:S(2)}) collective-permute-start(bf16[3,2,192,128]{3,2,1,0:T(8,128)(2,1)S(1)} %get-tuple-element.79), channel_id=1, source_target_pairs={{0,1},{1,0},{2,3},{3,2},{4,5},{5,4},{6,7},{7,6},{8,9},{9,8},{10,11... | collective-permute-start | bytes 884744 | tf_op jit(solution)/shard_map/ppermute | solution.py:506
  45.3 5.4 %collective-permute-start.14 = (bf16[32,1536]{1,0:T(8,128)(2,1)S(1)}, bf16[32,1536]{1,0:T(8,128)(2,1)S(1)}, u32[]{:S(2)}, u32[]{:S(2)}) collective-permute-start(bf16[32,1536]{1,0:T(8,128)(2,1)S(1)} %add_convert_fusion.2), channel_id=1, source_target_pairs={{0,4},{2,6},{4,0},{6,2},{1,5},{3,7},{5,1},{7,3},{8,12},{10,14},{12... | collective-permute-start | bytes 294920 | tf_op jit(solution)/shard_map/ppermute | solution.py:100
  50.8 9.6 %collective-permute-start.17 = (bf16[32,1536]{1,0:T(8,128)(2,1)S(1)}, bf16[32,1536]{1,0:T(8,128)(2,1)S(1)}, u32[]{:S(2)}, u32[]{:S(2)}) collective-permute-start(bf16[32,1536]{1,0:T(8,128)(2,1)S(1)} %add_convert_fusion.1.refs_0_), channel_id=1, source_target_pairs={{0,17},{1,16},{8,25},{9,24},{16,1},{17,0},{24,9},{25,8},{2,19},{3,... | collective-permute-start | bytes 294920 | tf_op jit(solution)/shard_map/ppermute | solution.py:100
  50.9 11.5 %collective-permute-start.16 = (bf16[32,1536]{1,0:T(8,128)(2,1)S(1)}, bf16[32,1536]{1,0:T(8,128)(2,1)S(1)}, u32[]{:S(2)}, u32[]{:S(2)}) collective-permute-start(bf16[32,1536]{1,0:T(8,128)(2,1)S(1)} %add_convert_fusion.1.refs_0_), channel_id=1, source_target_pairs={{0,16},{1,17},{8,24},{9,25},{16,0},{17,1},{24,8},{25,9},{2,18},{3,... | collective-permute-start | bytes 294920 | tf_op jit(solution)/shard_map/ppermute | solution.py:100
  58.4 4.2 %collective-permute-start.15 = (bf16[32,1536]{1,0:T(8,128)(2,1)S(1)}, bf16[32,1536]{1,0:T(8,128)(2,1)S(1)}, u32[]{:S(2)}, u32[]{:S(2)}) collective-permute-start(bf16[32,1536]{1,0:T(8,128)(2,1)S(1)} %add_convert_fusion.1.refs_0_), channel_id=1, source_target_pairs={{0,1},{1,0},{8,9},{9,8},{16,17},{17,16},{24,25},{25,24},{2,3},{3,2... | collective-permute-start | bytes 294920 | tf_op jit(solution)/shard_map/ppermute | solution.py:100
  59.0 6.1 %collective-permute-start.24 = (bf16[2,192,128]{2,1,0:T(8,128)(2,1)S(1)}, bf16[2,192,128]{2,1,0:T(8,128)(2,1)S(1)}, u32[]{:S(2)}, u32[]{:S(2)}) collective-permute-start(bf16[2,192,128]{2,1,0:T(8,128)(2,1)S(1)} %get-tuple-element.83), channel_id=1, source_target_pairs={{0,2},{2,0},{4,6},{6,4},{1,3},{3,1},{5,7},{7,5},{8,10},{10,8},{12,... | collective-permute-start | bytes 294920 | tf_op jit(solution)/shard_map/ppermute | solution.py:85
  59.1 6.3 %collective-permute-start.23 = (bf16[2,192,128]{2,1,0:T(8,128)(2,1)S(1)}, bf16[2,192,128]{2,1,0:T(8,128)(2,1)S(1)}, u32[]{:S(2)}, u32[]{:S(2)}) collective-permute-start(bf16[2,192,128]{2,1,0:T(8,128)(2,1)S(1)} %get-tuple-element.82), channel_id=1, source_target_pairs={{6,2},{0,4},{7,3},{1,5},{14,10},{8,12},{15,11},{9,13},{22,18},{16,... | collective-permute-start | bytes 294920 | tf_op jit(solution)/shard_map/ppermute | solution.py:85
  60.4 8.2 %collective-permute-start.22 = (bf16[2,192,128]{2,1,0:T(8,128)(2,1)S(1)}, bf16[2,192,128]{2,1,0:T(8,128)(2,1)S(1)}, u32[]{:S(2)}, u32[]{:S(2)}) collective-permute-start(bf16[2,192,128]{2,1,0:T(8,128)(2,1)S(1)} %get-tuple-element.82), channel_id=1, source_target_pairs={{4,2},{2,4},{5,3},{3,5},{12,10},{10,12},{13,11},{11,13},{20,18},{1... | collective-permute-start | bytes 294920 | tf_op jit(solution)/shard_map/ppermute | solution.py:85
  62.5 6.8 %collective-permute-start.18 = (bf16[144,1536]{1,0:T(8,128)(2,1)S(1)}, bf16[144,1536]{1,0:T(8,128)(2,1)S(1)}, u32[]{:S(2)}, u32[]{:S(2)}) collective-permute-start(bf16[144,1536]{1,0:T(8,128)(2,1)S(1)} %shard_map.97.part), channel_id=1, source_target_pairs={{0,8},{8,0},{16,24},{24,16},{1,9},{9,1},{17,25},{25,17},{2,10},{10... | collective-permute-start | bytes 1327112 | tf_op jit(solution)/shard_map/ppermute | solution.py:100

commit v5 on v3

--- a/solution.py
+++ b/solution.py
@@ -502,6 +502,7 @@
     )
     column_grad, *beside_grads, far_grad, query_own, query_other = back
     if small:
+        far_grad, projected = lax.optimization_barrier((far_grad, projected))
         arrived = [
             lax.ppermute(beside_grads[0], "width", [(0, 1), (1, 0)]),
             lax.ppermute(far_grad, "frame", [(0, 2), (3, 1)]),

time: 68.7 us -> 71.3 us (1.038)
  the two profiles are of different devices: /device:TPU:11 before, /device:TPU:9 now
where the time goes in v5:
time: 71.3 us; the launch traced here: 71 us
  starting transfers between devices  36.4 us (51%)
  waiting for transfers between devices  18.7 us (26%)
  Pallas kernels  10.5 us (15%)
  local copies, waits for them, and re-layouts  1.92 us (3%)
  matrix products  1.47 us (2%)
  other arithmetic  1.23 us (2%)
  between operations  0.9 us (1%)
    ppermute x12, starting transfers between devices, flip(): return lax.ppermute(block, axes, route)  9.84 us
    ppermute x1, starting transfers between devices, body(): lax.ppermute(far_grad, ('frame', 'width'), [(p, s) for s, p in cross])  6.04 us
    ppermute x1, starting transfers between devices, body(): lax.ppermute(column, ('frame', 'width'), cross)  5.69 us
    ppermute x12, waiting for transfers between devices, flip(): return lax.ppermute(block, axes, route)  5.35 us
    ppermute x1, waiting for transfers between devices, body(): lax.ppermute(far_grad, 'frame', [(0, 2), (3, 1)])  5.12 us
    ppermute x3, starting transfers between devices, fetch(): arrived = [lax.ppermute(block, axis, route) for route in routes]  4.96 us
    pallas_call x3, Pallas kernels, kernel_call(): pl.pallas_call(kernel, out_shape=outs, in_specs=[SMEM] + [VMEM] * (len(op...  4.85 us
    ppermute x3, starting transfers between devices, give_back(): back = lax.ppermute(outgoing, axis, [(p, s) for s, p in route])  4.84 us
  transfers between devices with their start and end apart: 25, of which 11 were waited for; matrix products, arithmetic and copies ran while one was open for 3% of the time, Pallas kernels for 10%

profile of v5, /device:TPU:9, one launch (start us, length us, event | category | flops | bytes accessed | tf_op | source)
XLA Modules:
  0.0 71.0 jit_solution(13425533010235431026)
XLA Ops:
  0.7 0.9 %fusion = (bf16[1,2,192,128]{3,2,1,0:T(8,128)(2,1)S(1)}, bf16[2,192,128]{2,1,0:T(8,128)(2,1)S(1)}) fusion(bf16[1,192,128]{2,1,0:T(8,128)(2,1)} %bitcast.24, bf16[1,192,128]{2,1,0:T(8,128)(2,1)} %bitcast.25), kind=kLoop, calls=%fused_computation.10 | loop fusion | flops 49152 | bytes 294912 | tf_op jit(solution)/shard_map/stack | solution.py:389
  1.6 3.2 %collective-permute-start.2 = (bf16[2,192,128]{2,1,0:T(8,128)(2,1)S(1)}, bf16[2,192,128]{2,1,0:T(8,128)(2,1)S(1)}, u32[]{:S(2)}, u32[]{:S(2)}) collective-permute-start(bf16[2,192,128]{2,1,0:T(8,128)(2,1)S(1)} %get-tuple-element.92), channel_id=1, source_target_pairs={{2,4},{4,2},{3,5},{5,3},{10,12},{12,10},{11,13},{13,11},{18,20},{2... | collective-permute-start | bytes 294920 | tf_op jit(solution)/shard_map/ppermute | solution.py:64
  4.8 1.7 %collective-permute-start.1 = (bf16[2,192,128]{2,1,0:T(8,128)(2,1)S(1)}, bf16[2,192,128]{2,1,0:T(8,128)(2,1)S(1)}, u32[]{:S(2)}, u32[]{:S(2)}) collective-permute-start(bf16[2,192,128]{2,1,0:T(8,128)(2,1)S(1)} %get-tuple-element.92), channel_id=1, source_target_pairs={{2,6},{4,0},{3,7},{5,1},{10,14},{12,8},{11,15},{13,9},{18,22},{20,... | collective-permute-start | bytes 294920 | tf_op jit(solution)/shard_map/ppermute | solution.py:64
  6.5 0.1 collective-permute-start
  6.5 1.3 %collective-permute-start.3 = (bf16[1,2,192,128]{3,2,1,0:T(8,128)(2,1)S(1)}, bf16[1,2,192,128]{3,2,1,0:T(8,128)(2,1)S(1)}, u32[]{:S(2)}, u32[]{:S(2)}) collective-permute-start(bf16[1,2,192,128]{3,2,1,0:T(8,128)(2,1)S(1)} %get-tuple-element.91), channel_id=1, source_target_pairs={{0,1},{1,0},{2,3},{3,2},{4,5},{5,4},{6,7},{7,6},{8,9},{9,8},{10,11... | collective-permute-start | bytes 294920 | tf_op jit(solution)/shard_map/ppermute | solution.py:387
  7.9 0.0 collective-permute-done.2
  7.9 1.1 %collective-permute-done.1 = bf16[2,192,128]{2,1,0:T(8,128)(2,1)S(1)} collective-permute-done((bf16[2,192,128]{2,1,0:T(8,128)(2,1)S(1)}, bf16[2,192,128]{2,1,0:T(8,128)(2,1)S(1)}, u32[]{:S(2)}, u32[]{:S(2)}) %collective-permute-start.1) | collective-permute-done | bytes 98336 | tf_op jit(solution)/shard_map/ppermute | solution.py:64
  8.9 1.5 %collective-permute-done = bf16[2,192,128]{2,1,0:T(8,128)(2,1)S(1)} collective-permute-done((bf16[2,192,128]{2,1,0:T(8,128)(2,1)S(1)}, bf16[2,192,128]{2,1,0:T(8,128)(2,1)S(1)}, u32[]{:S(2)}, u32[]{:S(2)}) %collective-permute-start) | collective-permute-done | bytes 98336 | tf_op jit(solution)/shard_map/ppermute | solution.py:64
  10.4 0.0 collective-permute-done.3.refs_0_.refs_1_
  10.5 5.7 %collective-permute-start.6 = (bf16[3,2,192,128]{3,2,1,0:T(8,128)(2,1)S(1)}, bf16[3,2,192,128]{3,2,1,0:T(8,128)(2,1)S(1)}, u32[]{:S(2)}, u32[]{:S(2)}) collective-permute-start(bf16[3,2,192,128]{3,2,1,0:T(8,128)(2,1)S(1)} %pad_maximum_fusion.refs_0_), channel_id=1, source_target_pairs={{16,9},{17,8},{8,17},{9,16},{18,11},{19,10},{10,19},{11,18},{20,13... | collective-permute-start | bytes 884744 | tf_op jit(solution)/shard_map/ppermute | solution.py:396
  16.2 1.3 %collective-permute-start.5 = (bf16[3,2,192,128]{3,2,1,0:T(8,128)(2,1)S(1)}, bf16[3,2,192,128]{3,2,1,0:T(8,128)(2,1)S(1)}, u32[]{:S(2)}, u32[]{:S(2)}) collective-permute-start(bf16[3,2,192,128]{3,2,1,0:T(8,128)(2,1)S(1)} %pad_maximum_fusion.refs_0_), channel_id=1, source_target_pairs={{16,0},{8,24},{17,1},{9,25},{18,2},{10,26},{19,3},{11,27},{20,4},{... | collective-permute-start | bytes 884744 | tf_op jit(solution)/shard_map/ppermute | solution.py:395
  17.5 0.3 collective-permute-start.7
  17.8 0.0 collective-permute-start.4
  17.8 0.1 pad_add_fusion.place
  17.8 1.2 %collective-permute-done.4.queries_other = bf16[192,128]{1,0:T(8,128)(2,1)S(1)} collective-permute-done((bf16[192,128]{1,0:T(8,128)(2,1)S(1)}, bf16[192,128]{1,0:T(8,128)(2,1)S(1)}, u32[]{:S(2)}, u32[]{:S(2)}) %collective-permute-start.4) | collective-permute-done | bytes 49184 | tf_op jit(solution)/shard_map/ppermute | solution.py:100
  19.0 1.3 %copy-done.1 = bf16[4,6,8,3072]{3,2,1,0:T(8,128)(2,1)S(1)} copy-done((bf16[4,6,8,3072]{3,2,1,0:T(8,128)(2,1)S(1)}, bf16[4,6,8,3072]{3,2,1,0:T(8,128)(2,1)}, u32[]{:S(2)}) %copy-start.1) | copy-done | bytes 1179672
  20.3 1.0 %shard_map.92 = (bf16[192,1664]{1,0:T(8,128)(2,1)S(1)}, bf16[192,1536]{1,0:T(8,128)(2,1)S(1)}, bf16[192,128]{1,0:T(8,128)(2,1)S(1)}, bf16[384,128]{1,0:T(8,128)(2,1)S(1)}) custom-call(s32[3]{0:T(128)S(1)} %pad_add_fusion.place, bf16[192,128]{1,0:T(8,128)(2,1)S(1)} %bitcast.20, bf16[192,128]{1,0:T(8,128)(2,1)S(1)} %collective-permute-done.4.queries_other, ...), custom_call_target="tpu_custom_call" | custom-call | flops 150994944 | bytes 2359296 | tf_op jit(solution)/shard_map/pallas_call | solution.py:324
  21.3 0.0 collective-permute-done.6.refs_2_.refs_4_
  21.3 1.7 %collective-permute-done.5.refs_1_.refs_3_ = bf16[3,2,192,128]{3,2,1,0:T(8,128)(2,1)S(1)} collective-permute-done((bf16[3,2,192,128]{3,2,1,0:T(8,128)(2,1)S(1)}, bf16[3,2,192,128]{3,2,1,0:T(8,128)(2,1)S(1)}, u32[]{:S(2)}, u32[]{:S(2)}) %collective-permute-start.5) | collective-permute-done | bytes 294944 | tf_op jit(solution)/shard_map/ppermute | solution.py:395
  23.0 1.2 %shard_map.93.refs_2_ = f32[136,384]{1,0:T(8,128)S(1)} custom-call(bf16[384,128]{1,0:T(8,128)(2,1)S(1)} %get-tuple-element.48.both_queries, bf16[3,2,192,128]{3,2,1,0:T(8,128)(2,1)S(1)} %pad_maximum_fusion.refs_0_, bf16[3,2,192,128]{3,2,1,0:T(8,128)(2,1)S(1)} %collective-permute-done.5.refs_1_.refs_3_, ...), custom_call_target="tpu_custom_call" | custom-call | flops 226492416 | bytes 786432 | tf_op jit(solution)/shard_map/pallas_call | solution.py:438
  24.2 0.3 collective-permute-done.7.refs_1_.refs_2_
  24.5 0.3 collective-permute-start.9
  24.7 0.8 %shard_map.94.mine = f32[136,384]{1,0:T(8,128)S(1)} custom-call(bf16[384,128]{1,0:T(8,128)(2,1)S(1)} %get-tuple-element.48.both_queries, bf16[1,2,192,128]{3,2,1,0:T(8,128)(2,1)S(1)} %collective-permute-done.3.refs_0_.refs_1_, bf16[2,2,192,128]{3,2,1,0:T(8,128)(2,1)S(1)} %collective-permute-done.7.refs_1_.refs_2_, f32[136,384]{1,0:T(8,128)S(1)} %shard_map.93.refs_2_), custom_call_target="tpu_custom_call" | custom-call | flops 113246208 | bytes 393216 | tf_op jit(solution)/shard_map/pallas_call | solution.py:438
  25.5 0.3 collective-permute-start.8
  25.8 1.2 %collective-permute-done.8.theirs = f32[136,384]{1,0:T(8,128)S(1)} collective-permute-done((f32[136,384]{1,0:T(8,128)S(1)}, f32[136,384]{1,0:T(8,128)S(1)}, u32[]{:S(2)}, u32[]{:S(2)}) %collective-permute-start.8) | collective-permute-done | bytes 208928 | tf_op jit(solution)/shard_map/ppermute | solution.py:100
  27.0 0.0 collective-permute-done.9.payload
  27.0 1.1 %shard_map.95 = (f32[8,384]{1,0:T(8,128)S(1)}, bf16[192,128]{1,0:T(8,128)(2,1)S(1)}, bf16[32,1536]{1,0:T(8,128)(2,1)S(1)}, bf16[32,1536]{1,0:T(8,128)(2,1)S(1)},...) custom-call(s32[3]{0:T(128)S(1)} %pad_add_fusion.place, f32[136,384]{1,0:T(8,128)S(1)} %shard_map.94.mine, ...), custom_call_target="tpu_custom_call" | custom-call | flops 150994944 | bytes 2359296 | tf_op jit(solution)/shard_map/pallas_call | solution.py:324
  28.2 1.3 %collective-permute-start.10 = (bf16[32,1536]{1,0:T(8,128)(2,1)S(1)}, bf16[32,1536]{1,0:T(8,128)(2,1)S(1)}, u32[]{:S(2)}, u32[]{:S(2)}) collective-permute-start(bf16[32,1536]{1,0:T(8,128)(2,1)S(1)} %get-tuple-element.67), channel_id=1, source_target_pairs={{0,1},{1,0},{8,9},{9,8},{16,17},{17,16},{24,25},{25,24},{2,3},{3,2... | collective-permute-start | bytes 294920 | tf_op jit(solution)/shard_map/ppermute | solution.py:100
  29.4 0.7 %collective-permute-start.11 = (bf16[32,1536]{1,0:T(8,128)(2,1)S(1)}, bf16[32,1536]{1,0:T(8,128)(2,1)S(1)}, u32[]{:S(2)}, u32[]{:S(2)}) collective-permute-start(bf16[32,1536]{1,0:T(8,128)(2,1)S(1)} %get-tuple-element.68), channel_id=1, source_target_pairs={{0,16},{1,17},{8,24},{9,25},{16,0},{17,1},{24,8},{25,9},{2,18},{3,... | collective-permute-start | bytes 294920 | tf_op jit(solution)/shard_map/ppermute | solution.py:100
  30.2 0.8 %collective-permute-start.12 = (bf16[32,1536]{1,0:T(8,128)(2,1)S(1)}, bf16[32,1536]{1,0:T(8,128)(2,1)S(1)}, u32[]{:S(2)}, u32[]{:S(2)}) collective-permute-start(bf16[32,1536]{1,0:T(8,128)(2,1)S(1)} %get-tuple-element.69), channel_id=1, source_target_pairs={{0,17},{1,16},{8,25},{9,24},{16,1},{17,0},{24,9},{25,8},{2,19},{3,... | collective-permute-start | bytes 294920 | tf_op jit(solution)/shard_map/ppermute | solution.py:100
  30.9 2.7 %shard_map.96 = (f32[3,2,192,128]{3,2,1,0:T(8,128)S(1)}, bf16[3,2,192,128]{3,2,1,0:T(8,128)(2,1)S(1)}, bf16[3,2,192,128]{3,2,1,0:T(8,128)(2,1)S(1)}, f32[192,128]{1,0:T(8,128)S(1)}, bf16[16,1536]{1,0:T(8,128)(2,1)S(1)}) custom-call(s32[3]{0:T(128)S(1)} %pad_add_fusion.place, f32[8,384]{1,0:T(8,128)S(1)} %get-tuple-element.60.stats, ...), custom_call_target="tpu_custom_call" | custom-call | flops 849346560 | bytes 2359296 | tf_op jit(solution)/shard_map/pallas_call | solution.py:324
  33.7 0.0 collective-permute-done.10
  33.7 0.0 collective-permute-done.11
  33.7 1.8 %collective-permute-done.12 = bf16[32,1536]{1,0:T(8,128)(2,1)S(1)} collective-permute-done((bf16[32,1536]{1,0:T(8,128)(2,1)S(1)}, bf16[32,1536]{1,0:T(8,128)(2,1)S(1)}, u32[]{:S(2)}, u32[]{:S(2)}) %collective-permute-start.12) | collective-permute-done | bytes 98336 | tf_op jit(solution)/shard_map/ppermute | solution.py:100
  35.5 0.1 add_convert_fusion.3
  35.6 2.2 %collective-permute-start.13 = (bf16[32,1536]{1,0:T(8,128)(2,1)S(1)}, bf16[32,1536]{1,0:T(8,128)(2,1)S(1)}, u32[]{:S(2)}, u32[]{:S(2)}) collective-permute-start(bf16[32,1536]{1,0:T(8,128)(2,1)S(1)} %add_convert_fusion.3), channel_id=1, source_target_pairs={{0,2},{2,0},{4,6},{6,4},{1,3},{3,1},{5,7},{7,5},{8,10},{10,8},{12,... | collective-permute-start | bytes 294920 | tf_op jit(solution)/shard_map/ppermute | solution.py:100
  37.7 0.8 %collective-permute-start.19 = (bf16[3,2,192,128]{3,2,1,0:T(8,128)(2,1)S(1)}, bf16[3,2,192,128]{3,2,1,0:T(8,128)(2,1)S(1)}, u32[]{:S(2)}, u32[]{:S(2)}) collective-permute-start(bf16[3,2,192,128]{3,2,1,0:T(8,128)(2,1)S(1)} %get-tuple-element.83), channel_id=1, source_target_pairs={{0,1},{1,0},{2,3},{3,2},{4,5},{5,4},{6,7},{7,6},{8,9},{9,8},{10,11... | collective-permute-start | bytes 884744 | tf_op jit(solution)/shard_map/ppermute | solution.py:507
  38.5 1.2 %collective-permute-done.13 = bf16[32,1536]{1,0:T(8,128)(2,1)S(1)} collective-permute-done((bf16[32,1536]{1,0:T(8,128)(2,1)S(1)}, bf16[32,1536]{1,0:T(8,128)(2,1)S(1)}, u32[]{:S(2)}, u32[]{:S(2)}) %collective-permute-start.13) | collective-permute-done | bytes 98336 | tf_op jit(solution)/shard_map/ppermute | solution.py:100
  39.8 0.9 %collective-permute-start.14 = (bf16[32,1536]{1,0:T(8,128)(2,1)S(1)}, bf16[32,1536]{1,0:T(8,128)(2,1)S(1)}, u32[]{:S(2)}, u32[]{:S(2)}) collective-permute-start(bf16[32,1536]{1,0:T(8,128)(2,1)S(1)} %add_convert_fusion.2), channel_id=1, source_target_pairs={{0,4},{2,6},{4,0},{6,2},{1,5},{3,7},{5,1},{7,3},{8,12},{10,14},{12... | collective-permute-start | bytes 294920 | tf_op jit(solution)/shard_map/ppermute | solution.py:100
  40.6 1.5 %convolution_convert_fusion = bf16[192,3072]{1,0:T(8,128)(2,1)} fusion(bf16[192,128]{1,0:T(8,128)(2,1)S(1)} %get-tuple-element.73, bf16[128,3072]{1,0:T(8,128)(2,1)S(1)} %copy-done), kind=kOutput, calls=%fused_computation | convolution fusion | flops 151584768 | bytes 2015232 | tf_op jit(solution)/shard_map/dot_general | solution.py:499
  42.1 6.0 %collective-permute-start.21 = (bf16[3,2,192,128]{3,2,1,0:T(8,128)(2,1)S(1)}, bf16[3,2,192,128]{3,2,1,0:T(8,128)(2,1)S(1)}, u32[]{:S(2)}, u32[]{:S(2)}) collective-permute-start(bf16[3,2,192,128]{3,2,1,0:T(8,128)(2,1)S(1)} %get-tuple-element.84), channel_id=1, source_target_pairs={{9,16},{8,17},{17,8},{16,9},{11,18},{10,19},{19,10},{18,11},{13,20... | collective-permute-start | bytes 884744 | tf_op jit(solution)/shard_map/ppermute | solution.py:509
  48.2 1.3 %collective-permute-start.20 = (bf16[3,2,192,128]{3,2,1,0:T(8,128)(2,1)S(1)}, bf16[3,2,192,128]{3,2,1,0:T(8,128)(2,1)S(1)}, u32[]{:S(2)}, u32[]{:S(2)}) collective-permute-start(bf16[3,2,192,128]{3,2,1,0:T(8,128)(2,1)S(1)} %get-tuple-element.84), channel_id=1, source_target_pairs={{0,16},{24,8},{1,17},{25,9},{2,18},{26,10},{3,19},{27,11},{4,20},{... | collective-permute-start | bytes 884744 | tf_op jit(solution)/shard_map/ppermute | solution.py:508
  49.5 0.0 collective-permute-done.14
  49.5 2.9 %collective-permute-start.17 = (bf16[32,1536]{1,0:T(8,128)(2,1)S(1)}, bf16[32,1536]{1,0:T(8,128)(2,1)S(1)}, u32[]{:S(2)}, u32[]{:S(2)}) collective-permute-start(bf16[32,1536]{1,0:T(8,128)(2,1)S(1)} %add_convert_fusion.1.refs_0_), channel_id=1, source_target_pairs={{0,17},{1,16},{8,25},{9,24},{16,1},{17,0},{24,9},{25,8},{2,19},{3,... | collective-permute-start | bytes 294920 | tf_op jit(solution)/shard_map/ppermute | solution.py:100
  52.4 0.0 collective-permute-start.16
  52.4 0.0 collective-permute-done.19.refs_0_
  52.4 0.5 collective-permute-start.15
  52.9 0.0 collective-permute-done.21.refs_2_
  52.9 5.1 %collective-permute-done.20.refs_1_ = bf16[3,2,192,128]{3,2,1,0:T(8,128)(2,1)S(1)} collective-permute-done((bf16[3,2,192,128]{3,2,1,0:T(8,128)(2,1)S(1)}, bf16[3,2,192,128]{3,2,1,0:T(8,128)(2,1)S(1)}, u32[]{:S(2)}, u32[]{:S(2)}) %collective-permute-start.20) | collective-permute-done | bytes 294944 | tf_op jit(solution)/shard_map/ppermute | solution.py:508
  58.0 0.1 shard_map.100
  58.1 0.2 collective-permute-start.24
  58.3 1.3 %collective-permute-start.23 = (bf16[2,192,128]{2,1,0:T(8,128)(2,1)S(1)}, bf16[2,192,128]{2,1,0:T(8,128)(2,1)S(1)}, u32[]{:S(2)}, u32[]{:S(2)}) collective-permute-start(bf16[2,192,128]{2,1,0:T(8,128)(2,1)S(1)} %get-tuple-element.86), channel_id=1, source_target_pairs={{6,2},{0,4},{7,3},{1,5},{14,10},{8,12},{15,11},{9,13},{22,18},{16,... | collective-permute-start | bytes 294920 | tf_op jit(solution)/shard_map/ppermute | solution.py:85
  59.6 0.0 collective-permute-done.17.refs_3_
  59.6 3.4 %collective-permute-start.22 = (bf16[2,192,128]{2,1,0:T(8,128)(2,1)S(1)}, bf16[2,192,128]{2,1,0:T(8,128)(2,1)S(1)}, u32[]{:S(2)}, u32[]{:S(2)}) collective-permute-start(bf16[2,192,128]{2,1,0:T(8,128)(2,1)S(1)} %get-tuple-element.86), channel_id=1, source_target_pairs={{4,2},{2,4},{5,3},{3,5},{12,10},{10,12},{13,11},{11,13},{20,18},{1... | collective-permute-start | bytes 294920 | tf_op jit(solution)/shard_map/ppermute | solution.py:85
  63.0 0.0 collective-permute-done.16.refs_2_
  63.0 0.0 collective-permute-done.15.refs_1_
  63.0 0.1 collective-permute-start.18
  63.1 1.5 %shard_map.98.refs_1_ = f32[128,3072]{1,0:T(8,128)} custom-call(s32[3]{0:T(128)S(1)} %pad_add_fusion.place, bf16[144,1536]{1,0:T(8,128)(2,1)S(1)} %shard_map.97.part), custom_call_target="tpu_custom_call" | custom-call | tf_op jit(solution)/shard_map/pallas_call | solution.py:288
  64.6 0.0 collective-permute-done.24
  64.6 1.6 %collective-permute-done.23 = bf16[2,192,128]{2,1,0:T(8,128)(2,1)S(1)} collective-permute-done((bf16[2,192,128]{2,1,0:T(8,128)(2,1)S(1)}, bf16[2,192,128]{2,1,0:T(8,128)(2,1)S(1)}, u32[]{:S(2)}, u32[]{:S(2)}) %collective-permute-start.23) | collective-permute-done | bytes 98336 | tf_op jit(solution)/shard_map/ppermute | solution.py:85
  66.2 2.0 %collective-permute-done.22 = bf16[2,192,128]{2,1,0:T(8,128)(2,1)S(1)} collective-permute-done((bf16[2,192,128]{2,1,0:T(8,128)(2,1)S(1)}, bf16[2,192,128]{2,1,0:T(8,128)(2,1)S(1)}, u32[]{:S(2)}, u32[]{:S(2)}) %collective-permute-start.22) | collective-permute-done | bytes 98336 | tf_op jit(solution)/shard_map/ppermute | solution.py:85
  68.2 0.1 add_convert_fusion
  68.3 0.6 fusion.1
  68.9 2.1 %shard_map.99 = (f32[128,3072]{1,0:T(8,128)}, bf16[192,128]{1,0:T(8,128)(2,1)}) custom-call(s32[3]{0:T(128)S(1)} %pad_add_fusion.place, bf16[144,1536]{1,0:T(8,128)(2,1)S(1)} %collective-permute-done.18.part, f32[192,128]{1,0:T(8,128)S(1)} %get-tuple-element.80.refs_0_, f32[128,3072]{1,0:T(8,128)} %shard_map.98.refs_1_), custom_call_target="tpu_custom_call", output_to_operand_aliasing={{0}: (3, {})} | custom-call | tf_op jit(solution)/shard_map/pallas_call | solution.py:288
  (12 shorter events, 0.2 us)
Async XLA Ops:
  0.6 17.1 %copy-start.2 = (bf16[4,6,8,128]{3,2,1,0:T(8,128)(2,1)S(1)}, bf16[4,6,8,128]{3,2,1,0:T(8,128)(2,1)}, u32[]{:S(2)}) copy-start(bf16[4,6,8,128]{3,2,1,0:T(8,128)(2,1)} %param.5) | copy-start | bytes 147460
  0.6 18.4 %copy-start = (bf16[128,3072]{1,0:T(8,128)(2,1)S(1)}, bf16[128,3072]{1,0:T(8,128)(2,1)}, u32[]{:S(2)}) copy-start(bf16[128,3072]{1,0:T(8,128)(2,1)} %weight.1) | copy-start | bytes 2359300
  1.6 6.3 %collective-permute-start.2 = (bf16[2,192,128]{2,1,0:T(8,128)(2,1)S(1)}, bf16[2,192,128]{2,1,0:T(8,128)(2,1)S(1)}, u32[]{:S(2)}, u32[]{:S(2)}) collective-permute-start(bf16[2,192,128]{2,1,0:T(8,128)(2,1)S(1)} %get-tuple-element.92), channel_id=1, source_target_pairs={{2,4},{4,2},{3,5},{5,3},{10,12},{12,10},{11,13},{13,11},{18,20},{2... | collective-permute-start | bytes 294920 | tf_op jit(solution)/shard_map/ppermute | solution.py:64
  4.8 4.1 %collective-permute-start.1 = (bf16[2,192,128]{2,1,0:T(8,128)(2,1)S(1)}, bf16[2,192,128]{2,1,0:T(8,128)(2,1)S(1)}, u32[]{:S(2)}, u32[]{:S(2)}) collective-permute-start(bf16[2,192,128]{2,1,0:T(8,128)(2,1)S(1)} %get-tuple-element.92), channel_id=1, source_target_pairs={{2,6},{4,0},{3,7},{5,1},{10,14},{12,8},{11,15},{13,9},{18,22},{20,... | collective-permute-start | bytes 294920 | tf_op jit(solution)/shard_map/ppermute | solution.py:64
  6.5 3.9 %collective-permute-start = (bf16[2,192,128]{2,1,0:T(8,128)(2,1)S(1)}, bf16[2,192,128]{2,1,0:T(8,128)(2,1)S(1)}, u32[]{:S(2)}, u32[]{:S(2)}) collective-permute-start(bf16[2,192,128]{2,1,0:T(8,128)(2,1)S(1)} %get-tuple-element.92), channel_id=1, source_target_pairs={{2,0},{0,2},{6,4},{4,6},{3,1},{1,3},{7,5},{5,7},{10,8},{8,10},{14,... | collective-permute-start | bytes 294920 | tf_op jit(solution)/shard_map/ppermute | solution.py:64
  6.5 3.9 %collective-permute-start.3 = (bf16[1,2,192,128]{3,2,1,0:T(8,128)(2,1)S(1)}, bf16[1,2,192,128]{3,2,1,0:T(8,128)(2,1)S(1)}, u32[]{:S(2)}, u32[]{:S(2)}) collective-permute-start(bf16[1,2,192,128]{3,2,1,0:T(8,128)(2,1)S(1)} %get-tuple-element.91), channel_id=1, source_target_pairs={{0,1},{1,0},{2,3},{3,2},{4,5},{5,4},{6,7},{7,6},{8,9},{9,8},{10,11... | collective-permute-start | bytes 294920 | tf_op jit(solution)/shard_map/ppermute | solution.py:387
  10.5 10.8 %collective-permute-start.6 = (bf16[3,2,192,128]{3,2,1,0:T(8,128)(2,1)S(1)}, bf16[3,2,192,128]{3,2,1,0:T(8,128)(2,1)S(1)}, u32[]{:S(2)}, u32[]{:S(2)}) collective-permute-start(bf16[3,2,192,128]{3,2,1,0:T(8,128)(2,1)S(1)} %pad_maximum_fusion.refs_0_), channel_id=1, source_target_pairs={{16,9},{17,8},{8,17},{9,16},{18,11},{19,10},{10,19},{11,18},{20,13... | collective-permute-start | bytes 884744 | tf_op jit(solution)/shard_map/ppermute | solution.py:396
  16.2 6.8 %collective-permute-start.5 = (bf16[3,2,192,128]{3,2,1,0:T(8,128)(2,1)S(1)}, bf16[3,2,192,128]{3,2,1,0:T(8,128)(2,1)S(1)}, u32[]{:S(2)}, u32[]{:S(2)}) collective-permute-start(bf16[3,2,192,128]{3,2,1,0:T(8,128)(2,1)S(1)} %pad_maximum_fusion.refs_0_), channel_id=1, source_target_pairs={{16,0},{8,24},{17,1},{9,25},{18,2},{10,26},{19,3},{11,27},{20,4},{... | collective-permute-start | bytes 884744 | tf_op jit(solution)/shard_map/ppermute | solution.py:395
  17.5 7.0 %collective-permute-start.7 = (bf16[2,2,192,128]{3,2,1,0:T(8,128)(2,1)S(1)}, bf16[2,2,192,128]{3,2,1,0:T(8,128)(2,1)S(1)}, u32[]{:S(2)}, u32[]{:S(2)}) collective-permute-start(bf16[2,2,192,128]{3,2,1,0:T(8,128)(2,1)S(1)} %pad_maximum_fusion.1), channel_id=1, source_target_pairs={{0,1},{1,0},{2,3},{3,2},{4,5},{5,4},{6,7},{7,6},{8,9},{9,8},{10,11... | collective-permute-start | bytes 589832 | tf_op jit(solution)/shard_map/ppermute | solution.py:393
  17.8 1.2 %collective-permute-start.4 = (bf16[192,128]{1,0:T(8,128)(2,1)S(1)}, bf16[192,128]{1,0:T(8,128)(2,1)S(1)}, u32[]{:S(2)}, u32[]{:S(2)}) collective-permute-start(bf16[192,128]{1,0:T(8,128)(2,1)S(1)} %bitcast.19), channel_id=1, source_target_pairs={{0,8},{8,0},{16,24},{24,16},{1,9},{9,1},{17,25},{25,17},{2,10},{10... | collective-permute-start | bytes 147464 | tf_op jit(solution)/shard_map/ppermute | solution.py:100
  19.0 1.3 %copy-start.1 = (bf16[4,6,8,3072]{3,2,1,0:T(8,128)(2,1)S(1)}, bf16[4,6,8,3072]{3,2,1,0:T(8,128)(2,1)}, u32[]{:S(2)}) copy-start(bf16[4,6,8,3072]{3,2,1,0:T(8,128)(2,1)} %param.9) | copy-start | bytes 3538948
  24.5 2.6 %collective-permute-start.9 = (bf16[192,1664]{1,0:T(8,128)(2,1)S(1)}, bf16[192,1664]{1,0:T(8,128)(2,1)S(1)}, u32[]{:S(2)}, u32[]{:S(2)}) collective-permute-start(bf16[192,1664]{1,0:T(8,128)(2,1)S(1)} %get-tuple-element.56), channel_id=1, source_target_pairs={{0,8},{8,0},{16,24},{24,16},{1,9},{9,1},{17,25},{25,17},{2,10},{10... | collective-permute-start | bytes 1916936 | tf_op jit(solution)/shard_map/ppermute | solution.py:100
  25.5 1.5 %collective-permute-start.8 = (f32[136,384]{1,0:T(8,128)S(1)}, f32[136,384]{1,0:T(8,128)S(1)}, u32[]{:S(2)}, u32[]{:S(2)}) collective-permute-start(f32[136,384]{1,0:T(8,128)S(1)} %shard_map.94.mine), channel_id=1, source_target_pairs={{0,8},{8,0},{16,24},{24,16},{1,9},{9,1},{17,25},{25,17},{2,10},{10... | collective-permute-start | bytes 626696 | tf_op jit(solution)/shard_map/ppermute | solution.py:100
  28.2 5.5 %collective-permute-start.10 = (bf16[32,1536]{1,0:T(8,128)(2,1)S(1)}, bf16[32,1536]{1,0:T(8,128)(2,1)S(1)}, u32[]{:S(2)}, u32[]{:S(2)}) collective-permute-start(bf16[32,1536]{1,0:T(8,128)(2,1)S(1)} %get-tuple-element.67), channel_id=1, source_target_pairs={{0,1},{1,0},{8,9},{9,8},{16,17},{17,16},{24,25},{25,24},{2,3},{3,2... | collective-permute-start | bytes 294920 | tf_op jit(solution)/shard_map/ppermute | solution.py:100
  29.4 4.3 %collective-permute-start.11 = (bf16[32,1536]{1,0:T(8,128)(2,1)S(1)}, bf16[32,1536]{1,0:T(8,128)(2,1)S(1)}, u32[]{:S(2)}, u32[]{:S(2)}) collective-permute-start(bf16[32,1536]{1,0:T(8,128)(2,1)S(1)} %get-tuple-element.68), channel_id=1, source_target_pairs={{0,16},{1,17},{8,24},{9,25},{16,0},{17,1},{24,8},{25,9},{2,18},{3,... | collective-permute-start | bytes 294920 | tf_op jit(solution)/shard_map/ppermute | solution.py:100
  30.2 5.3 %collective-permute-start.12 = (bf16[32,1536]{1,0:T(8,128)(2,1)S(1)}, bf16[32,1536]{1,0:T(8,128)(2,1)S(1)}, u32[]{:S(2)}, u32[]{:S(2)}) collective-permute-start(bf16[32,1536]{1,0:T(8,128)(2,1)S(1)} %get-tuple-element.69), channel_id=1, source_target_pairs={{0,17},{1,16},{8,25},{9,24},{16,1},{17,0},{24,9},{25,8},{2,19},{3,... | collective-permute-start | bytes 294920 | tf_op jit(solution)/shard_map/ppermute | solution.py:100
  35.6 4.2 %collective-permute-start.13 = (bf16[32,1536]{1,0:T(8,128)(2,1)S(1)}, bf16[32,1536]{1,0:T(8,128)(2,1)S(1)}, u32[]{:S(2)}, u32[]{:S(2)}) collective-permute-start(bf16[32,1536]{1,0:T(8,128)(2,1)S(1)} %add_convert_fusion.3), channel_id=1, source_target_pairs={{0,2},{2,0},{4,6},{6,4},{1,3},{3,1},{5,7},{7,5},{8,10},{10,8},{12,... | collective-permute-start | bytes 294920 | tf_op jit(solution)/shard_map/ppermute | solution.py:100
  37.7 14.7 %collective-permute-start.19 = (bf16[3,2,192,128]{3,2,1,0:T(8,128)(2,1)S(1)}, bf16[3,2,192,128]{3,2,1,0:T(8,128)(2,1)S(1)}, u32[]{:S(2)}, u32[]{:S(2)}) collective-permute-start(bf16[3,2,192,128]{3,2,1,0:T(8,128)(2,1)S(1)} %get-tuple-element.83), channel_id=1, source_target_pairs={{0,1},{1,0},{2,3},{3,2},{4,5},{5,4},{6,7},{7,6},{8,9},{9,8},{10,11... | collective-permute-start | bytes 884744 | tf_op jit(solution)/shard_map/ppermute | solution.py:507
  39.8 9.7 %collective-permute-start.14 = (bf16[32,1536]{1,0:T(8,128)(2,1)S(1)}, bf16[32,1536]{1,0:T(8,128)(2,1)S(1)}, u32[]{:S(2)}, u32[]{:S(2)}) collective-permute-start(bf16[32,1536]{1,0:T(8,128)(2,1)S(1)} %add_convert_fusion.2), channel_id=1, source_target_pairs={{0,4},{2,6},{4,0},{6,2},{1,5},{3,7},{5,1},{7,3},{8,12},{10,14},{12... | collective-permute-start | bytes 294920 | tf_op jit(solution)/shard_map/ppermute | solution.py:100
  42.1 10.8 %collective-permute-start.21 = (bf16[3,2,192,128]{3,2,1,0:T(8,128)(2,1)S(1)}, bf16[3,2,192,128]{3,2,1,0:T(8,128)(2,1)S(1)}, u32[]{:S(2)}, u32[]{:S(2)}) collective-permute-start(bf16[3,2,192,128]{3,2,1,0:T(8,128)(2,1)S(1)} %get-tuple-element.84), channel_id=1, source_target_pairs={{9,16},{8,17},{17,8},{16,9},{11,18},{10,19},{19,10},{18,11},{13,20... | collective-permute-start | bytes 884744 | tf_op jit(solution)/shard_map/ppermute | solution.py:509
  48.2 9.8 %collective-permute-start.20 = (bf16[3,2,192,128]{3,2,1,0:T(8,128)(2,1)S(1)}, bf16[3,2,192,128]{3,2,1,0:T(8,128)(2,1)S(1)}, u32[]{:S(2)}, u32[]{:S(2)}) collective-permute-start(bf16[3,2,192,128]{3,2,1,0:T(8,128)(2,1)S(1)} %get-tuple-element.84), channel_id=1, source_target_pairs={{0,16},{24,8},{1,17},{25,9},{2,18},{26,10},{3,19},{27,11},{4,20},{... | collective-permute-start | bytes 884744 | tf_op jit(solution)/shard_map/ppermute | solution.py:508
  49.5 10.1 %collective-permute-start.17 = (bf16[32,1536]{1,0:T(8,128)(2,1)S(1)}, bf16[32,1536]{1,0:T(8,128)(2,1)S(1)}, u32[]{:S(2)}, u32[]{:S(2)}) collective-permute-start(bf16[32,1536]{1,0:T(8,128)(2,1)S(1)} %add_convert_fusion.1.refs_0_), channel_id=1, source_target_pairs={{0,17},{1,16},{8,25},{9,24},{16,1},{17,0},{24,9},{25,8},{2,19},{3,... | collective-permute-start | bytes 294920 | tf_op jit(solution)/shard_map/ppermute | solution.py:100
  52.4 10.6 %collective-permute-start.16 = (bf16[32,1536]{1,0:T(8,128)(2,1)S(1)}, bf16[32,1536]{1,0:T(8,128)(2,1)S(1)}, u32[]{:S(2)}, u32[]{:S(2)}) collective-permute-start(bf16[32,1536]{1,0:T(8,128)(2,1)S(1)} %add_convert_fusion.1.refs_0_), channel_id=1, source_target_pairs={{0,16},{1,17},{8,24},{9,25},{16,0},{17,1},{24,8},{25,9},{2,18},{3,... | collective-permute-start | bytes 294920 | tf_op jit(solution)/shard_map/ppermute | solution.py:100
  52.4 10.6 %collective-permute-start.15 = (bf16[32,1536]{1,0:T(8,128)(2,1)S(1)}, bf16[32,1536]{1,0:T(8,128)(2,1)S(1)}, u32[]{:S(2)}, u32[]{:S(2)}) collective-permute-start(bf16[32,1536]{1,0:T(8,128)(2,1)S(1)} %add_convert_fusion.1.refs_0_), channel_id=1, source_target_pairs={{0,1},{1,0},{8,9},{9,8},{16,17},{17,16},{24,25},{25,24},{2,3},{3,2... | collective-permute-start | bytes 294920 | tf_op jit(solution)/shard_map/ppermute | solution.py:100
  58.1 6.5 %collective-permute-start.24 = (bf16[2,192,128]{2,1,0:T(8,128)(2,1)S(1)}, bf16[2,192,128]{2,1,0:T(8,128)(2,1)S(1)}, u32[]{:S(2)}, u32[]{:S(2)}) collective-permute-start(bf16[2,192,128]{2,1,0:T(8,128)(2,1)S(1)} %get-tuple-element.87), channel_id=1, source_target_pairs={{0,2},{2,0},{4,6},{6,4},{1,3},{3,1},{5,7},{7,5},{8,10},{10,8},{12,... | collective-permute-start | bytes 294920 | tf_op jit(solution)/shard_map/ppermute | solution.py:85
  58.3 7.9 %collective-permute-start.23 = (bf16[2,192,128]{2,1,0:T(8,128)(2,1)S(1)}, bf16[2,192,128]{2,1,0:T(8,128)(2,1)S(1)}, u32[]{:S(2)}, u32[]{:S(2)}) collective-permute-start(bf16[2,192,128]{2,1,0:T(8,128)(2,1)S(1)} %get-tuple-element.86), channel_id=1, source_target_pairs={{6,2},{0,4},{7,3},{1,5},{14,10},{8,12},{15,11},{9,13},{22,18},{16,... | collective-permute-start | bytes 294920 | tf_op jit(solution)/shard_map/ppermute | solution.py:85
  59.6 8.6 %collective-permute-start.22 = (bf16[2,192,128]{2,1,0:T(8,128)(2,1)S(1)}, bf16[2,192,128]{2,1,0:T(8,128)(2,1)S(1)}, u32[]{:S(2)}, u32[]{:S(2)}) collective-permute-start(bf16[2,192,128]{2,1,0:T(8,128)(2,1)S(1)} %get-tuple-element.86), channel_id=1, source_target_pairs={{4,2},{2,4},{5,3},{3,5},{12,10},{10,12},{13,11},{11,13},{20,18},{1... | collective-permute-start | bytes 294920 | tf_op jit(solution)/shard_map/ppermute | solution.py:85
  63.0 5.9 %collective-permute-start.18 = (bf16[144,1536]{1,0:T(8,128)(2,1)S(1)}, bf16[144,1536]{1,0:T(8,128)(2,1)S(1)}, u32[]{:S(2)}, u32[]{:S(2)}) collective-permute-start(bf16[144,1536]{1,0:T(8,128)(2,1)S(1)} %shard_map.97.part), channel_id=1, source_target_pairs={{0,8},{8,0},{16,24},{24,16},{1,9},{9,1},{17,25},{25,17},{2,10},{10... | collective-permute-start | bytes 1327112 | tf_op jit(solution)/shard_map/ppermute | solution.py:100

commit v6 on v3

--- a/solution.py
+++ b/solution.py
@@ -73,18 +73,22 @@
     return tiles
 
 
-def give_back(pieces, axis):
+def returned(pieces, axis):
     extent = lax.axis_size(axis)
     slots = slots_of(extent)
-    summed = pieces[0]
+    arrived = []
     for c, route in reversed(list(enumerate(routes_of(extent)))):
         holders = [next((k for k in range(len(slots)) if slots[k][p] == c), None) for p in range(extent)]
         used = sorted({k for k in holders if k is not None})
         choice = [k if k is not None else used[0] for k in holders]
-        outgoing = chosen({k: pieces[k + 1] for k in used}, choice, axis).astype(jnp.bfloat16)
-        back = lax.ppermute(outgoing, axis, [(p, s) for s, p in route])
-        summed = summed + back.astype(jnp.float32)
-    return summed
+        outgoing = chosen({k: pieces[k] for k in used}, choice, axis).astype(jnp.bfloat16)
+        arrived.append(lax.ppermute(outgoing, axis, [(p, s) for s, p in route]))
+    return arrived
+
+
+def give_back(pieces, axis):
+    arrived = returned(pieces[1:], axis)
+    return functools.reduce(jnp.add, [pieces[0]] + [a.astype(jnp.float32) for a in arrived])
 
 
 def flip(block, axes, bits):
@@ -256,11 +260,22 @@
 
 
 def assemble_kernel(flipped, rows, place, part, *refs):
-    whole, rows_ref, done = refs[-3 - flipped], refs[-2], refs[-1]
+    rows_ref, done = refs[-2:]
     count, width = rows_ref.shape
+    copies = []
+    if flipped:
+        query_own, _, whole, grad_query, sums = refs[:-2]
+        dim, step = query_own.shape[1], part.shape[0] - count
+        for block in range(width // dim):
+            piece = part[count:, block * dim : (block + 1) * dim].astype(jnp.float32)
+            span = slice(block * step, (block + 1) * step)
+            sums[span, :] = (query_own[span, :] + piece).astype(jnp.bfloat16)
+        copies.append(pltpu.make_async_copy(sums, grad_query, done.at[count // rows]))
+        copies[-1].start()
+    else:
+        whole = refs[0]
     core = 1 - place[0] if flipped else place[0]
     columns = pl.ds(pl.multiple_of(core * width, width), width)
-    copies = []
     for order in range(count // rows):
         span = pl.ds(pl.multiple_of((place[1] ^ order) * rows, rows), rows)
         rows_ref[span, :] = part[order * rows : (order + 1) * rows, :].astype(jnp.float32)
@@ -268,13 +283,6 @@
             pltpu.make_async_copy(rows_ref.at[span, :], whole.at[span, columns], done.at[order])
         )
         copies[-1].start()
-    if flipped:
-        query_own, grad_query = refs[0], refs[-3]
-        dim, step = grad_query.shape[1], part.shape[0] - count
-        for block in range(width // dim):
-            piece = part[count:, block * dim : (block + 1) * dim].astype(jnp.float32)
-            span = slice(block * step, (block + 1) * step)
-            grad_query[span, :] = (query_own[span, :] + piece).astype(jnp.bfloat16)
     for copy in copies:
         copy.wait()
 
@@ -282,21 +290,31 @@
 def assemble(flipped, place, part, rows, shape, whole=None, query_own=None):
     anywhere = pl.BlockSpec(memory_space=pl.ANY)
     outs, out_specs, operands, in_specs = shape, anywhere, (place, part), [SMEM, VMEM]
+    scratch = [
+        pltpu.VMEM((shape.shape[0], part.shape[1]), jnp.float32),
+        pltpu.SemaphoreType.DMA((shape.shape[0] // rows + flipped,)),
+    ]
     if flipped:
-        outs, out_specs = (shape, shaped(*query_own.shape)), (anywhere, VMEM)
+        outs, out_specs = (shape, shaped(*query_own.shape)), (anywhere, anywhere)
         operands, in_specs = operands + (query_own, whole), in_specs + [VMEM, anywhere]
+        scratch = [pltpu.VMEM(query_own.shape, jnp.bfloat16)] + scratch
     return pl.pallas_call(
         functools.partial(assemble_kernel, flipped, rows),
         out_shape=outs,
         in_specs=in_specs,
         out_specs=out_specs,
-        scratch_shapes=[
-            pltpu.VMEM((shape.shape[0], part.shape[1]), jnp.float32),
-            pltpu.SemaphoreType.DMA((shape.shape[0] // rows,)),
-        ],
+        scratch_shapes=scratch,
         input_output_aliases={3: 0} if flipped else {},
         compiler_params=PARAMS,
     )(*operands)
+
+
+def owner_kernel(own_grad, *refs):
+    for k, out in enumerate(refs[-2:]):
+        total = own_grad[k]
+        for block in refs[:-2]:
+            total = total + block[k].astype(jnp.float32)
+        out[...] = total.astype(jnp.bfloat16)
 
 
 def pack_kernel(*refs):
@@ -360,7 +378,7 @@
     rows = (part.shape[0] - query_other.shape[0]) // plane
     shape = shaped(plane * rows, 2 * part.shape[1], kind=jnp.float32)
     whole = assemble(False, place, part, rows, shape)
-    return assemble(True, place, other, rows, shape, whole, query_own)
+    return whole, lambda whole: assemble(True, place, other, rows, shape, whole, query_own)
 
 
 def body(queries, key_vectors, value_vectors, out_weight, projected_grad):
@@ -445,12 +463,10 @@
             cost_estimate=cost_of(8 * keys * tile * head_dim, moved * keys // key_count),
         )(both_queries, *operands, *carried)
 
-    partial = forward([blocks[0]] + far, (1, 2), ())
-    beside = blocks[1 : -len(far)]
-    payload, partial, *beside = lax.optimization_barrier((payload, partial, *beside))
+    partial = forward(blocks[:1], (1,), ())
+    payload, partial, *blocks[1:] = lax.optimization_barrier((payload, partial, *blocks[1:]))
     payload = flip(payload, ("frame",), (1,))
-    partial = forward(beside, (1,) * len(beside), (partial,))
-    blocks = [blocks[0]] + beside + far
+    partial = forward(blocks[1:], layout[1:], (partial,))
     partial_other = flip(partial, ("frame",), (1,))
     plane = 4
     chunks = plane if small else 0
@@ -519,6 +535,7 @@
             out_specs=[VMEM] * column_tiles,
             compiler_params=PARAMS,
         )(column_grad, *arrived)
+        pieces = list(pieces)
     else:
         arrived = jnp.concatenate(
             (
@@ -533,14 +550,24 @@
         column_grad = give_back(pieces, "width")
         pieces = [column_grad[k] for k in range(column_tiles)]
     if small:
-        grad_out_weight, grad_query = join_sum(part, query_own, query_other, place)
+        whole, finish = join_sum(part, query_own, query_other, place)
+        whole, pieces[0] = lax.optimization_barrier((whole, pieces[0]))
+        grad_out_weight, grad_query = finish(whole)
     else:
         query_other = flip(query_other, ("frame",), (1,)).reshape(-1, half // head_dim, head_dim)
         query_other = query_other.transpose(1, 0, 2).reshape(tile, head_dim)
         grad_query = (query_own + query_other.astype(jnp.float32)).astype(jnp.bfloat16)
-    own_grad = give_back(pieces, "height")
-    grad_key = own_grad[0].astype(jnp.bfloat16).reshape(key_vectors.shape)
-    grad_value = own_grad[1].astype(jnp.bfloat16).reshape(value_vectors.shape)
+    operands = (pieces[0], *returned(pieces[1:], "height"))
+    grad_key, grad_value = pl.pallas_call(
+        owner_kernel,
+        out_shape=[shaped(tile, head_dim)] * 2,
+        in_specs=[VMEM] * len(operands),
+        out_specs=[VMEM] * 2,
+        compiler_params=PARAMS,
+        cost_estimate=cost_of(10**10, 10**8),
+    )(*operands)
+    grad_key = grad_key.reshape(key_vectors.shape)
+    grad_value = grad_value.reshape(value_vectors.shape)
     grad_query = grad_query.reshape(queries.shape)
     return (projected, grad_query, grad_key, grad_value, grad_out_weight)
 

time: 68.7 us -> 67.8 us (0.987)
  the two profiles are of different devices: /device:TPU:11 before, /device:TPU:15 now
where the time goes in v6:
time: 67.8 us; the launch traced here: 67.5 us
  starting transfers between devices  31.9 us (47%)
  waiting for transfers between devices  20.2 us (30%)
  Pallas kernels  10.5 us (15%)
  matrix products  1.48 us (2%)
  local copies, waits for them, and re-layouts  1.28 us (2%)
  other arithmetic  1.17 us (2%)
  between operations  0.92 us (1%)
    ppermute x12, starting transfers between devices, flip(): return lax.ppermute(block, axes, route)  13.2 us
    ppermute x12, waiting for transfers between devices, flip(): return lax.ppermute(block, axes, route)  7.02 us
    ppermute x1, starting transfers between devices, body(): lax.ppermute(far_grad, 'frame', [(0, 2), (3, 1)])  6.34 us
    ppermute x3, starting transfers between devices, fetch(): arrived = [lax.ppermute(block, axis, route) for route in routes]  4.96 us
    ppermute x3, waiting for transfers between devices, returned(): arrived.append(lax.ppermute(outgoing, axis, [(p, s) for s, p in route]))  4.85 us
    pallas_call x3, Pallas kernels, kernel_call(): pl.pallas_call(kernel, out_shape=outs, in_specs=[SMEM] + [VMEM] * (len(op...  4.85 us
    ppermute x3, waiting for transfers between devices, fetch(): arrived = [lax.ppermute(block, axis, route) for route in routes]  3.52 us
    ppermute x3, starting transfers between devices, returned(): arrived.append(lax.ppermute(outgoing, axis, [(p, s) for s, p in route]))  3.28 us
  transfers between devices with their start and end apart: 25, of which 11 were waited for; matrix products, arithmetic and copies ran while one was open for 2% of the time, Pallas kernels for 12%

profile of v6, /device:TPU:15, one launch (start us, length us, event | category | flops | bytes accessed | tf_op | source)
XLA Modules:
  0.0 67.5 jit_solution(17430377238280819092)
XLA Ops:
  0.7 0.9 %fusion = (bf16[1,2,192,128]{3,2,1,0:T(8,128)(2,1)S(1)}, bf16[2,192,128]{2,1,0:T(8,128)(2,1)S(1)}) fusion(bf16[1,192,128]{2,1,0:T(8,128)(2,1)} %bitcast.24, bf16[1,192,128]{2,1,0:T(8,128)(2,1)} %bitcast.25), kind=kLoop, calls=%fused_computation.9 | loop fusion | flops 49152 | bytes 294912 | tf_op jit(solution)/shard_map/stack | solution.py:407
  1.6 3.2 %collective-permute-start.2 = (bf16[2,192,128]{2,1,0:T(8,128)(2,1)S(1)}, bf16[2,192,128]{2,1,0:T(8,128)(2,1)S(1)}, u32[]{:S(2)}, u32[]{:S(2)}) collective-permute-start(bf16[2,192,128]{2,1,0:T(8,128)(2,1)S(1)} %get-tuple-element.98), channel_id=1, source_target_pairs={{2,4},{4,2},{3,5},{5,3},{10,12},{12,10},{11,13},{13,11},{18,20},{2... | collective-permute-start | bytes 294920 | tf_op jit(solution)/shard_map/ppermute | solution.py:64
  4.8 1.7 %collective-permute-start.1 = (bf16[2,192,128]{2,1,0:T(8,128)(2,1)S(1)}, bf16[2,192,128]{2,1,0:T(8,128)(2,1)S(1)}, u32[]{:S(2)}, u32[]{:S(2)}) collective-permute-start(bf16[2,192,128]{2,1,0:T(8,128)(2,1)S(1)} %get-tuple-element.98), channel_id=1, source_target_pairs={{2,6},{4,0},{3,7},{5,1},{10,14},{12,8},{11,15},{13,9},{18,22},{20,... | collective-permute-start | bytes 294920 | tf_op jit(solution)/shard_map/ppermute | solution.py:64
  6.5 0.1 collective-permute-start
  6.5 0.3 collective-permute-start.3
  6.8 0.1 collective-permute-done.2
  6.9 2.0 %collective-permute-done.1 = bf16[2,192,128]{2,1,0:T(8,128)(2,1)S(1)} collective-permute-done((bf16[2,192,128]{2,1,0:T(8,128)(2,1)S(1)}, bf16[2,192,128]{2,1,0:T(8,128)(2,1)S(1)}, u32[]{:S(2)}, u32[]{:S(2)}) %collective-permute-start.1) | collective-permute-done | bytes 98336 | tf_op jit(solution)/shard_map/ppermute | solution.py:64
  8.9 1.5 %collective-permute-done = bf16[2,192,128]{2,1,0:T(8,128)(2,1)S(1)} collective-permute-done((bf16[2,192,128]{2,1,0:T(8,128)(2,1)S(1)}, bf16[2,192,128]{2,1,0:T(8,128)(2,1)S(1)}, u32[]{:S(2)}, u32[]{:S(2)}) %collective-permute-start) | collective-permute-done | bytes 98336 | tf_op jit(solution)/shard_map/ppermute | solution.py:64
  10.4 0.0 collective-permute-done.3.refs_0_.refs_1_
  10.5 0.7 %collective-permute-start.7 = (bf16[3,2,192,128]{3,2,1,0:T(8,128)(2,1)S(1)}, bf16[3,2,192,128]{3,2,1,0:T(8,128)(2,1)S(1)}, u32[]{:S(2)}, u32[]{:S(2)}) collective-permute-start(bf16[3,2,192,128]{3,2,1,0:T(8,128)(2,1)S(1)} %pad_maximum_fusion.refs_0_), channel_id=1, source_target_pairs={{16,9},{17,8},{8,17},{9,16},{18,11},{19,10},{10,19},{11,18},{20,13... | collective-permute-start | bytes 884744 | tf_op jit(solution)/shard_map/ppermute | solution.py:414
  11.1 1.3 %collective-permute-start.6 = (bf16[3,2,192,128]{3,2,1,0:T(8,128)(2,1)S(1)}, bf16[3,2,192,128]{3,2,1,0:T(8,128)(2,1)S(1)}, u32[]{:S(2)}, u32[]{:S(2)}) collective-permute-start(bf16[3,2,192,128]{3,2,1,0:T(8,128)(2,1)S(1)} %pad_maximum_fusion.refs_0_), channel_id=1, source_target_pairs={{16,0},{8,24},{17,1},{9,25},{18,2},{10,26},{19,3},{11,27},{20,4},{... | collective-permute-start | bytes 884744 | tf_op jit(solution)/shard_map/ppermute | solution.py:413
  12.4 0.3 collective-permute-start.5
  12.7 3.3 %collective-permute-start.4 = (bf16[192,128]{1,0:T(8,128)(2,1)S(1)}, bf16[192,128]{1,0:T(8,128)(2,1)S(1)}, u32[]{:S(2)}, u32[]{:S(2)}) collective-permute-start(bf16[192,128]{1,0:T(8,128)(2,1)S(1)} %bitcast.19), channel_id=1, source_target_pairs={{0,8},{8,0},{16,24},{24,16},{1,9},{9,1},{17,25},{25,17},{2,10},{10... | collective-permute-start | bytes 147464 | tf_op jit(solution)/shard_map/ppermute | solution.py:104
  16.0 0.1 pad_add_fusion.place
  16.1 0.8 %collective-permute-done.4.queries_other = bf16[192,128]{1,0:T(8,128)(2,1)S(1)} collective-permute-done((bf16[192,128]{1,0:T(8,128)(2,1)S(1)}, bf16[192,128]{1,0:T(8,128)(2,1)S(1)}, u32[]{:S(2)}, u32[]{:S(2)}) %collective-permute-start.4) | collective-permute-done | bytes 49184 | tf_op jit(solution)/shard_map/ppermute | solution.py:104
  16.9 1.3 %copy-done.1 = bf16[4,6,8,3072]{3,2,1,0:T(8,128)(2,1)S(1)} copy-done((bf16[4,6,8,3072]{3,2,1,0:T(8,128)(2,1)S(1)}, bf16[4,6,8,3072]{3,2,1,0:T(8,128)(2,1)}, u32[]{:S(2)}) %copy-start.1) | copy-done | bytes 1179672
  18.2 1.0 %shard_map.92 = (bf16[192,1664]{1,0:T(8,128)(2,1)S(1)}, bf16[192,1536]{1,0:T(8,128)(2,1)S(1)}, bf16[192,128]{1,0:T(8,128)(2,1)S(1)}, bf16[384,128]{1,0:T(8,128)(2,1)S(1)}) custom-call(s32[3]{0:T(128)S(1)} %pad_add_fusion.place, bf16[192,128]{1,0:T(8,128)(2,1)S(1)} %bitcast.20, bf16[192,128]{1,0:T(8,128)(2,1)S(1)} %collective-permute-done.4.queries_other, ...), custom_call_target="tpu_custom_call" | custom-call | flops 150994944 | bytes 2359296 | tf_op jit(solution)/shard_map/pallas_call | solution.py:342
  19.2 0.7 %shard_map.93.refs_4_ = f32[136,384]{1,0:T(8,128)S(1)} custom-call(bf16[384,128]{1,0:T(8,128)(2,1)S(1)} %get-tuple-element.52.both_queries, bf16[3,2,192,128]{3,2,1,0:T(8,128)(2,1)S(1)} %pad_maximum_fusion.refs_0_), custom_call_target="tpu_custom_call" | custom-call | flops 113246208 | bytes 393216 | tf_op jit(solution)/shard_map/pallas_call | solution.py:456
  19.9 0.0 collective-permute-done.5.refs_1_.refs_2_
  19.9 0.0 collective-permute-done.7.refs_3_.refs_4_
  19.9 2.9 %collective-permute-done.6.refs_2_.refs_3_ = bf16[3,2,192,128]{3,2,1,0:T(8,128)(2,1)S(1)} collective-permute-done((bf16[3,2,192,128]{3,2,1,0:T(8,128)(2,1)S(1)}, bf16[3,2,192,128]{3,2,1,0:T(8,128)(2,1)S(1)}, u32[]{:S(2)}, u32[]{:S(2)}) %collective-permute-start.6) | collective-permute-done | bytes 294944 | tf_op jit(solution)/shard_map/ppermute | solution.py:413
  22.8 0.4 collective-permute-start.9
  23.2 1.2 %shard_map.94.mine = f32[136,384]{1,0:T(8,128)S(1)} custom-call(bf16[384,128]{1,0:T(8,128)(2,1)S(1)} %get-tuple-element.52.both_queries, bf16[1,2,192,128]{3,2,1,0:T(8,128)(2,1)S(1)} %collective-permute-done.3.refs_0_.refs_1_, bf16[2,2,192,128]{3,2,1,0:T(8,128)(2,1)S(1)} %collective-permute-done.5.refs_1_.refs_2_, ...), custom_call_target="tpu_custom_call" | custom-call | flops 226492416 | bytes 786432 | tf_op jit(solution)/shard_map/pallas_call | solution.py:456
  24.4 0.2 collective-permute-start.8
  24.6 1.4 %collective-permute-done.8.theirs = f32[136,384]{1,0:T(8,128)S(1)} collective-permute-done((f32[136,384]{1,0:T(8,128)S(1)}, f32[136,384]{1,0:T(8,128)S(1)}, u32[]{:S(2)}, u32[]{:S(2)}) %collective-permute-start.8) | collective-permute-done | bytes 208928 | tf_op jit(solution)/shard_map/ppermute | solution.py:104
  25.9 0.0 collective-permute-done.9.payload
  26.0 1.1 %shard_map.95 = (f32[8,384]{1,0:T(8,128)S(1)}, bf16[192,128]{1,0:T(8,128)(2,1)S(1)}, bf16[32,1536]{1,0:T(8,128)(2,1)S(1)}, bf16[32,1536]{1,0:T(8,128)(2,1)S(1)},...) custom-call(s32[3]{0:T(128)S(1)} %pad_add_fusion.place, f32[136,384]{1,0:T(8,128)S(1)} %shard_map.94.mine, ...), custom_call_target="tpu_custom_call" | custom-call | flops 150994944 | bytes 2359296 | tf_op jit(solution)/shard_map/pallas_call | solution.py:342
  27.1 0.9 %collective-permute-start.10 = (bf16[32,1536]{1,0:T(8,128)(2,1)S(1)}, bf16[32,1536]{1,0:T(8,128)(2,1)S(1)}, u32[]{:S(2)}, u32[]{:S(2)}) collective-permute-start(bf16[32,1536]{1,0:T(8,128)(2,1)S(1)} %get-tuple-element.73), channel_id=1, source_target_pairs={{0,1},{1,0},{8,9},{9,8},{16,17},{17,16},{24,25},{25,24},{2,3},{3,2... | collective-permute-start | bytes 294920 | tf_op jit(solution)/shard_map/ppermute | solution.py:104
  28.0 1.2 %collective-permute-start.11 = (bf16[32,1536]{1,0:T(8,128)(2,1)S(1)}, bf16[32,1536]{1,0:T(8,128)(2,1)S(1)}, u32[]{:S(2)}, u32[]{:S(2)}) collective-permute-start(bf16[32,1536]{1,0:T(8,128)(2,1)S(1)} %get-tuple-element.74), channel_id=1, source_target_pairs={{0,16},{1,17},{8,24},{9,25},{16,0},{17,1},{24,8},{25,9},{2,18},{3,... | collective-permute-start | bytes 294920 | tf_op jit(solution)/shard_map/ppermute | solution.py:104
  29.1 0.7 collective-permute-start.12
  29.8 2.7 %shard_map.96 = (f32[3,2,192,128]{3,2,1,0:T(8,128)S(1)}, bf16[3,2,192,128]{3,2,1,0:T(8,128)(2,1)S(1)}, bf16[3,2,192,128]{3,2,1,0:T(8,128)(2,1)S(1)}, f32[192,128]{1,0:T(8,128)S(1)}, bf16[16,1536]{1,0:T(8,128)(2,1)S(1)}) custom-call(s32[3]{0:T(128)S(1)} %pad_add_fusion.place, f32[8,384]{1,0:T(8,128)S(1)} %get-tuple-element.66.stats, ...), custom_call_target="tpu_custom_call" | custom-call | flops 849346560 | bytes 2359296 | tf_op jit(solution)/shard_map/pallas_call | solution.py:342
  32.5 0.0 collective-permute-done.10
  32.5 0.0 collective-permute-done.11
  32.5 1.8 %collective-permute-done.12 = bf16[32,1536]{1,0:T(8,128)(2,1)S(1)} collective-permute-done((bf16[32,1536]{1,0:T(8,128)(2,1)S(1)}, bf16[32,1536]{1,0:T(8,128)(2,1)S(1)}, u32[]{:S(2)}, u32[]{:S(2)}) %collective-permute-start.12) | collective-permute-done | bytes 98336 | tf_op jit(solution)/shard_map/ppermute | solution.py:104
  34.3 0.1 add_convert_fusion.2
  34.4 2.2 %collective-permute-start.13 = (bf16[32,1536]{1,0:T(8,128)(2,1)S(1)}, bf16[32,1536]{1,0:T(8,128)(2,1)S(1)}, u32[]{:S(2)}, u32[]{:S(2)}) collective-permute-start(bf16[32,1536]{1,0:T(8,128)(2,1)S(1)} %add_convert_fusion.2), channel_id=1, source_target_pairs={{0,2},{2,0},{4,6},{6,4},{1,3},{3,1},{5,7},{7,5},{8,10},{10,8},{12,... | collective-permute-start | bytes 294920 | tf_op jit(solution)/shard_map/ppermute | solution.py:104
  36.6 0.7 collective-permute-start.21
  37.2 6.3 %collective-permute-start.20 = (bf16[3,2,192,128]{3,2,1,0:T(8,128)(2,1)S(1)}, bf16[3,2,192,128]{3,2,1,0:T(8,128)(2,1)S(1)}, u32[]{:S(2)}, u32[]{:S(2)}) collective-permute-start(bf16[3,2,192,128]{3,2,1,0:T(8,128)(2,1)S(1)} %get-tuple-element.87), channel_id=1, source_target_pairs={{0,16},{24,8},{1,17},{25,9},{2,18},{26,10},{3,19},{27,11},{4,20},{... | collective-permute-start | bytes 884744 | tf_op jit(solution)/shard_map/ppermute | solution.py:523
  43.6 0.9 %collective-permute-start.19 = (bf16[3,2,192,128]{3,2,1,0:T(8,128)(2,1)S(1)}, bf16[3,2,192,128]{3,2,1,0:T(8,128)(2,1)S(1)}, u32[]{:S(2)}, u32[]{:S(2)}) collective-permute-start(bf16[3,2,192,128]{3,2,1,0:T(8,128)(2,1)S(1)} %get-tuple-element.86), channel_id=1, source_target_pairs={{0,1},{1,0},{2,3},{3,2},{4,5},{5,4},{6,7},{7,6},{8,9},{9,8},{10,11... | collective-permute-start | bytes 884744 | tf_op jit(solution)/shard_map/ppermute | solution.py:522
  44.4 0.0 collective-permute-done.13
  44.5 0.1 collective-permute-start.14
  44.6 1.5 %convolution_convert_fusion = bf16[192,3072]{1,0:T(8,128)(2,1)} fusion(bf16[192,128]{1,0:T(8,128)(2,1)S(1)} %get-tuple-element.78, bf16[128,3072]{1,0:T(8,128)(2,1)S(1)} %copy-done), kind=kOutput, calls=%fused_computation | convolution fusion | flops 151584768 | bytes 2015232 | tf_op jit(solution)/shard_map/dot_general | solution.py:515
  46.0 3.1 %collective-permute-done.14 = bf16[32,1536]{1,0:T(8,128)(2,1)S(1)} collective-permute-done((bf16[32,1536]{1,0:T(8,128)(2,1)S(1)}, bf16[32,1536]{1,0:T(8,128)(2,1)S(1)}, u32[]{:S(2)}, u32[]{:S(2)}) %collective-permute-start.14) | collective-permute-done | bytes 98336 | tf_op jit(solution)/shard_map/ppermute | solution.py:104
  49.1 0.1 collective-permute-start.17
  49.2 1.6 %collective-permute-start.16 = (bf16[32,1536]{1,0:T(8,128)(2,1)S(1)}, bf16[32,1536]{1,0:T(8,128)(2,1)S(1)}, u32[]{:S(2)}, u32[]{:S(2)}) collective-permute-start(bf16[32,1536]{1,0:T(8,128)(2,1)S(1)} %add_convert_fusion.refs_0_), channel_id=1, source_target_pairs={{0,16},{1,17},{8,24},{9,25},{16,0},{17,1},{24,8},{25,9},{2,18},{3,... | collective-permute-start | bytes 294920 | tf_op jit(solution)/shard_map/ppermute | solution.py:104
  50.9 1.9 %collective-permute-done.19.refs_0_ = bf16[3,2,192,128]{3,2,1,0:T(8,128)(2,1)S(1)} collective-permute-done((bf16[3,2,192,128]{3,2,1,0:T(8,128)(2,1)S(1)}, bf16[3,2,192,128]{3,2,1,0:T(8,128)(2,1)S(1)}, u32[]{:S(2)}, u32[]{:S(2)}) %collective-permute-start.19) | collective-permute-done | bytes 294944 | tf_op jit(solution)/shard_map/ppermute | solution.py:522
  52.8 2.7 %collective-permute-start.15 = (bf16[32,1536]{1,0:T(8,128)(2,1)S(1)}, bf16[32,1536]{1,0:T(8,128)(2,1)S(1)}, u32[]{:S(2)}, u32[]{:S(2)}) collective-permute-start(bf16[32,1536]{1,0:T(8,128)(2,1)S(1)} %add_convert_fusion.refs_0_), channel_id=1, source_target_pairs={{0,1},{1,0},{8,9},{9,8},{16,17},{17,16},{24,25},{25,24},{2,3},{3,2... | collective-permute-start | bytes 294920 | tf_op jit(solution)/shard_map/ppermute | solution.py:104
  55.4 0.0 collective-permute-done.21.refs_2_
  55.4 0.0 collective-permute-done.20.refs_1_
  55.4 0.1 shard_map.99
  55.5 0.1 collective-permute-start.24
  55.6 1.3 %collective-permute-start.23 = (bf16[2,192,128]{2,1,0:T(8,128)(2,1)S(1)}, bf16[2,192,128]{2,1,0:T(8,128)(2,1)S(1)}, u32[]{:S(2)}, u32[]{:S(2)}) collective-permute-start(bf16[2,192,128]{2,1,0:T(8,128)(2,1)S(1)} %get-tuple-element.92), channel_id=1, source_target_pairs={{6,2},{0,4},{7,3},{1,5},{14,10},{8,12},{15,11},{9,13},{22,18},{16,... | collective-permute-start | bytes 294920 | tf_op jit(solution)/shard_map/ppermute | solution.py:85
  56.9 0.0 collective-permute-done.17.refs_3_
  56.9 1.9 %collective-permute-start.22 = (bf16[2,192,128]{2,1,0:T(8,128)(2,1)S(1)}, bf16[2,192,128]{2,1,0:T(8,128)(2,1)S(1)}, u32[]{:S(2)}, u32[]{:S(2)}) collective-permute-start(bf16[2,192,128]{2,1,0:T(8,128)(2,1)S(1)} %get-tuple-element.92), channel_id=1, source_target_pairs={{4,2},{2,4},{5,3},{3,5},{12,10},{10,12},{13,11},{11,13},{20,18},{1... | collective-permute-start | bytes 294920 | tf_op jit(solution)/shard_map/ppermute | solution.py:85
  58.9 0.0 collective-permute-done.16.refs_2_
  58.9 0.0 collective-permute-done.15.refs_1_
  58.9 0.1 collective-permute-start.18
  59.0 1.5 %shard_map.98.refs_1_ = f32[128,3072]{1,0:T(8,128)} custom-call(s32[3]{0:T(128)S(1)} %pad_add_fusion.place, bf16[144,1536]{1,0:T(8,128)(2,1)S(1)} %shard_map.97.part), custom_call_target="tpu_custom_call" | custom-call | tf_op jit(solution)/shard_map/pallas_call | solution.py:301
  60.5 0.0 collective-permute-done.24.refs_2_
  60.5 2.7 %collective-permute-done.23.refs_1_ = bf16[2,192,128]{2,1,0:T(8,128)(2,1)S(1)} collective-permute-done((bf16[2,192,128]{2,1,0:T(8,128)(2,1)S(1)}, bf16[2,192,128]{2,1,0:T(8,128)(2,1)S(1)}, u32[]{:S(2)}, u32[]{:S(2)}) %collective-permute-start.23) | collective-permute-done | bytes 98336 | tf_op jit(solution)/shard_map/ppermute | solution.py:85
  63.1 2.2 %collective-permute-done.22.refs_0_ = bf16[2,192,128]{2,1,0:T(8,128)(2,1)S(1)} collective-permute-done((bf16[2,192,128]{2,1,0:T(8,128)(2,1)S(1)}, bf16[2,192,128]{2,1,0:T(8,128)(2,1)S(1)}, u32[]{:S(2)}, u32[]{:S(2)}) %collective-permute-start.22) | collective-permute-done | bytes 98336 | tf_op jit(solution)/shard_map/ppermute | solution.py:85
  65.3 0.7 shard_map.101
  66.0 0.0 collective-permute-done.18.part
  66.0 1.5 %shard_map.100 = (f32[128,3072]{1,0:T(8,128)}, bf16[192,128]{1,0:T(8,128)(2,1)}) custom-call(s32[3]{0:T(128)S(1)} %pad_add_fusion.place, bf16[144,1536]{1,0:T(8,128)(2,1)S(1)} %collective-permute-done.18.part, f32[192,128]{1,0:T(8,128)S(1)} %get-tuple-element.84.refs_0_, f32[128,3072]{1,0:T(8,128)} %shard_map.98.refs_1_), custom_call_target="tpu_custom_call", output_to_operand_aliasing={{0}: (3, {})} | custom-call | tf_op jit(solution)/shard_map/pallas_call | solution.py:301
  (11 shorter events, 0.2 us)
Async XLA Ops:
  0.6 12.1 %copy-start.2 = (bf16[4,6,8,128]{3,2,1,0:T(8,128)(2,1)S(1)}, bf16[4,6,8,128]{3,2,1,0:T(8,128)(2,1)}, u32[]{:S(2)}) copy-start(bf16[4,6,8,128]{3,2,1,0:T(8,128)(2,1)} %param.5) | copy-start | bytes 147460
  0.6 16.2 %copy-start = (bf16[128,3072]{1,0:T(8,128)(2,1)S(1)}, bf16[128,3072]{1,0:T(8,128)(2,1)}, u32[]{:S(2)}) copy-start(bf16[128,3072]{1,0:T(8,128)(2,1)} %weight.1) | copy-start | bytes 2359300
  1.6 5.4 %collective-permute-start.2 = (bf16[2,192,128]{2,1,0:T(8,128)(2,1)S(1)}, bf16[2,192,128]{2,1,0:T(8,128)(2,1)S(1)}, u32[]{:S(2)}, u32[]{:S(2)}) collective-permute-start(bf16[2,192,128]{2,1,0:T(8,128)(2,1)S(1)} %get-tuple-element.98), channel_id=1, source_target_pairs={{2,4},{4,2},{3,5},{5,3},{10,12},{12,10},{11,13},{13,11},{18,20},{2... | collective-permute-start | bytes 294920 | tf_op jit(solution)/shard_map/ppermute | solution.py:64
  4.8 4.1 %collective-permute-start.1 = (bf16[2,192,128]{2,1,0:T(8,128)(2,1)S(1)}, bf16[2,192,128]{2,1,0:T(8,128)(2,1)S(1)}, u32[]{:S(2)}, u32[]{:S(2)}) collective-permute-start(bf16[2,192,128]{2,1,0:T(8,128)(2,1)S(1)} %get-tuple-element.98), channel_id=1, source_target_pairs={{2,6},{4,0},{3,7},{5,1},{10,14},{12,8},{11,15},{13,9},{18,22},{20,... | collective-permute-start | bytes 294920 | tf_op jit(solution)/shard_map/ppermute | solution.py:64
  6.5 3.9 %collective-permute-start = (bf16[2,192,128]{2,1,0:T(8,128)(2,1)S(1)}, bf16[2,192,128]{2,1,0:T(8,128)(2,1)S(1)}, u32[]{:S(2)}, u32[]{:S(2)}) collective-permute-start(bf16[2,192,128]{2,1,0:T(8,128)(2,1)S(1)} %get-tuple-element.98), channel_id=1, source_target_pairs={{2,0},{0,2},{6,4},{4,6},{3,1},{1,3},{7,5},{5,7},{10,8},{8,10},{14,... | collective-permute-start | bytes 294920 | tf_op jit(solution)/shard_map/ppermute | solution.py:64
  6.5 3.9 %collective-permute-start.3 = (bf16[1,2,192,128]{3,2,1,0:T(8,128)(2,1)S(1)}, bf16[1,2,192,128]{3,2,1,0:T(8,128)(2,1)S(1)}, u32[]{:S(2)}, u32[]{:S(2)}) collective-permute-start(bf16[1,2,192,128]{3,2,1,0:T(8,128)(2,1)S(1)} %get-tuple-element.97), channel_id=1, source_target_pairs={{0,1},{1,0},{2,3},{3,2},{4,5},{5,4},{6,7},{7,6},{8,9},{9,8},{10,11... | collective-permute-start | bytes 294920 | tf_op jit(solution)/shard_map/ppermute | solution.py:405
  10.5 9.5 %collective-permute-start.7 = (bf16[3,2,192,128]{3,2,1,0:T(8,128)(2,1)S(1)}, bf16[3,2,192,128]{3,2,1,0:T(8,128)(2,1)S(1)}, u32[]{:S(2)}, u32[]{:S(2)}) collective-permute-start(bf16[3,2,192,128]{3,2,1,0:T(8,128)(2,1)S(1)} %pad_maximum_fusion.refs_0_), channel_id=1, source_target_pairs={{16,9},{17,8},{8,17},{9,16},{18,11},{19,10},{10,19},{11,18},{20,13... | collective-permute-start | bytes 884744 | tf_op jit(solution)/shard_map/ppermute | solution.py:414
  11.1 11.7 %collective-permute-start.6 = (bf16[3,2,192,128]{3,2,1,0:T(8,128)(2,1)S(1)}, bf16[3,2,192,128]{3,2,1,0:T(8,128)(2,1)S(1)}, u32[]{:S(2)}, u32[]{:S(2)}) collective-permute-start(bf16[3,2,192,128]{3,2,1,0:T(8,128)(2,1)S(1)} %pad_maximum_fusion.refs_0_), channel_id=1, source_target_pairs={{16,0},{8,24},{17,1},{9,25},{18,2},{10,26},{19,3},{11,27},{20,4},{... | collective-permute-start | bytes 884744 | tf_op jit(solution)/shard_map/ppermute | solution.py:413
  12.4 7.5 %collective-permute-start.5 = (bf16[2,2,192,128]{3,2,1,0:T(8,128)(2,1)S(1)}, bf16[2,2,192,128]{3,2,1,0:T(8,128)(2,1)S(1)}, u32[]{:S(2)}, u32[]{:S(2)}) collective-permute-start(bf16[2,2,192,128]{3,2,1,0:T(8,128)(2,1)S(1)} %pad_maximum_fusion.1), channel_id=1, source_target_pairs={{0,1},{1,0},{2,3},{3,2},{4,5},{5,4},{6,7},{7,6},{8,9},{9,8},{10,11... | collective-permute-start | bytes 589832 | tf_op jit(solution)/shard_map/ppermute | solution.py:411
  12.7 4.1 %collective-permute-start.4 = (bf16[192,128]{1,0:T(8,128)(2,1)S(1)}, bf16[192,128]{1,0:T(8,128)(2,1)S(1)}, u32[]{:S(2)}, u32[]{:S(2)}) collective-permute-start(bf16[192,128]{1,0:T(8,128)(2,1)S(1)} %bitcast.19), channel_id=1, source_target_pairs={{0,8},{8,0},{16,24},{24,16},{1,9},{9,1},{17,25},{25,17},{2,10},{10... | collective-permute-start | bytes 147464 | tf_op jit(solution)/shard_map/ppermute | solution.py:104
  16.9 1.3 %copy-start.1 = (bf16[4,6,8,3072]{3,2,1,0:T(8,128)(2,1)S(1)}, bf16[4,6,8,3072]{3,2,1,0:T(8,128)(2,1)}, u32[]{:S(2)}) copy-start(bf16[4,6,8,3072]{3,2,1,0:T(8,128)(2,1)} %param.9) | copy-start | bytes 3538948
  22.8 3.1 %collective-permute-start.9 = (bf16[192,1664]{1,0:T(8,128)(2,1)S(1)}, bf16[192,1664]{1,0:T(8,128)(2,1)S(1)}, u32[]{:S(2)}, u32[]{:S(2)}) collective-permute-start(bf16[192,1664]{1,0:T(8,128)(2,1)S(1)} %get-tuple-element.62), channel_id=1, source_target_pairs={{0,8},{8,0},{16,24},{24,16},{1,9},{9,1},{17,25},{25,17},{2,10},{10... | collective-permute-start | bytes 1916936 | tf_op jit(solution)/shard_map/ppermute | solution.py:104
  24.4 1.5 %collective-permute-start.8 = (f32[136,384]{1,0:T(8,128)S(1)}, f32[136,384]{1,0:T(8,128)S(1)}, u32[]{:S(2)}, u32[]{:S(2)}) collective-permute-start(f32[136,384]{1,0:T(8,128)S(1)} %shard_map.94.mine), channel_id=1, source_target_pairs={{0,8},{8,0},{16,24},{24,16},{1,9},{9,1},{17,25},{25,17},{2,10},{10... | collective-permute-start | bytes 626696 | tf_op jit(solution)/shard_map/ppermute | solution.py:104
  27.1 5.5 %collective-permute-start.10 = (bf16[32,1536]{1,0:T(8,128)(2,1)S(1)}, bf16[32,1536]{1,0:T(8,128)(2,1)S(1)}, u32[]{:S(2)}, u32[]{:S(2)}) collective-permute-start(bf16[32,1536]{1,0:T(8,128)(2,1)S(1)} %get-tuple-element.73), channel_id=1, source_target_pairs={{0,1},{1,0},{8,9},{9,8},{16,17},{17,16},{24,25},{25,24},{2,3},{3,2... | collective-permute-start | bytes 294920 | tf_op jit(solution)/shard_map/ppermute | solution.py:104
  28.0 4.6 %collective-permute-start.11 = (bf16[32,1536]{1,0:T(8,128)(2,1)S(1)}, bf16[32,1536]{1,0:T(8,128)(2,1)S(1)}, u32[]{:S(2)}, u32[]{:S(2)}) collective-permute-start(bf16[32,1536]{1,0:T(8,128)(2,1)S(1)} %get-tuple-element.74), channel_id=1, source_target_pairs={{0,16},{1,17},{8,24},{9,25},{16,0},{17,1},{24,8},{25,9},{2,18},{3,... | collective-permute-start | bytes 294920 | tf_op jit(solution)/shard_map/ppermute | solution.py:104
  29.1 5.2 %collective-permute-start.12 = (bf16[32,1536]{1,0:T(8,128)(2,1)S(1)}, bf16[32,1536]{1,0:T(8,128)(2,1)S(1)}, u32[]{:S(2)}, u32[]{:S(2)}) collective-permute-start(bf16[32,1536]{1,0:T(8,128)(2,1)S(1)} %get-tuple-element.75), channel_id=1, source_target_pairs={{0,17},{1,16},{8,25},{9,24},{16,1},{17,0},{24,9},{25,8},{2,19},{3,... | collective-permute-start | bytes 294920 | tf_op jit(solution)/shard_map/ppermute | solution.py:104
  34.4 10.1 %collective-permute-start.13 = (bf16[32,1536]{1,0:T(8,128)(2,1)S(1)}, bf16[32,1536]{1,0:T(8,128)(2,1)S(1)}, u32[]{:S(2)}, u32[]{:S(2)}) collective-permute-start(bf16[32,1536]{1,0:T(8,128)(2,1)S(1)} %add_convert_fusion.2), channel_id=1, source_target_pairs={{0,2},{2,0},{4,6},{6,4},{1,3},{3,1},{5,7},{7,5},{8,10},{10,8},{12,... | collective-permute-start | bytes 294920 | tf_op jit(solution)/shard_map/ppermute | solution.py:104
  36.6 18.9 %collective-permute-start.21 = (bf16[3,2,192,128]{3,2,1,0:T(8,128)(2,1)S(1)}, bf16[3,2,192,128]{3,2,1,0:T(8,128)(2,1)S(1)}, u32[]{:S(2)}, u32[]{:S(2)}) collective-permute-start(bf16[3,2,192,128]{3,2,1,0:T(8,128)(2,1)S(1)} %get-tuple-element.87), channel_id=1, source_target_pairs={{9,16},{8,17},{17,8},{16,9},{11,18},{10,19},{19,10},{18,11},{13,20... | collective-permute-start | bytes 884744 | tf_op jit(solution)/shard_map/ppermute | solution.py:524
  37.2 18.2 %collective-permute-start.20 = (bf16[3,2,192,128]{3,2,1,0:T(8,128)(2,1)S(1)}, bf16[3,2,192,128]{3,2,1,0:T(8,128)(2,1)S(1)}, u32[]{:S(2)}, u32[]{:S(2)}) collective-permute-start(bf16[3,2,192,128]{3,2,1,0:T(8,128)(2,1)S(1)} %get-tuple-element.87), channel_id=1, source_target_pairs={{0,16},{24,8},{1,17},{25,9},{2,18},{26,10},{3,19},{27,11},{4,20},{... | collective-permute-start | bytes 884744 | tf_op jit(solution)/shard_map/ppermute | solution.py:523
  43.6 9.2 %collective-permute-start.19 = (bf16[3,2,192,128]{3,2,1,0:T(8,128)(2,1)S(1)}, bf16[3,2,192,128]{3,2,1,0:T(8,128)(2,1)S(1)}, u32[]{:S(2)}, u32[]{:S(2)}) collective-permute-start(bf16[3,2,192,128]{3,2,1,0:T(8,128)(2,1)S(1)} %get-tuple-element.86), channel_id=1, source_target_pairs={{0,1},{1,0},{2,3},{3,2},{4,5},{5,4},{6,7},{7,6},{8,9},{9,8},{10,11... | collective-permute-start | bytes 884744 | tf_op jit(solution)/shard_map/ppermute | solution.py:522
  44.5 4.6 %collective-permute-start.14 = (bf16[32,1536]{1,0:T(8,128)(2,1)S(1)}, bf16[32,1536]{1,0:T(8,128)(2,1)S(1)}, u32[]{:S(2)}, u32[]{:S(2)}) collective-permute-start(bf16[32,1536]{1,0:T(8,128)(2,1)S(1)} %add_convert_fusion.1), channel_id=1, source_target_pairs={{0,4},{2,6},{4,0},{6,2},{1,5},{3,7},{5,1},{7,3},{8,12},{10,14},{12... | collective-permute-start | bytes 294920 | tf_op jit(solution)/shard_map/ppermute | solution.py:104
  49.1 7.8 %collective-permute-start.17 = (bf16[32,1536]{1,0:T(8,128)(2,1)S(1)}, bf16[32,1536]{1,0:T(8,128)(2,1)S(1)}, u32[]{:S(2)}, u32[]{:S(2)}) collective-permute-start(bf16[32,1536]{1,0:T(8,128)(2,1)S(1)} %add_convert_fusion.refs_0_), channel_id=1, source_target_pairs={{0,17},{1,16},{8,25},{9,24},{16,1},{17,0},{24,9},{25,8},{2,19},{3,... | collective-permute-start | bytes 294920 | tf_op jit(solution)/shard_map/ppermute | solution.py:104
  49.2 9.6 %collective-permute-start.16 = (bf16[32,1536]{1,0:T(8,128)(2,1)S(1)}, bf16[32,1536]{1,0:T(8,128)(2,1)S(1)}, u32[]{:S(2)}, u32[]{:S(2)}) collective-permute-start(bf16[32,1536]{1,0:T(8,128)(2,1)S(1)} %add_convert_fusion.refs_0_), channel_id=1, source_target_pairs={{0,16},{1,17},{8,24},{9,25},{16,0},{17,1},{24,8},{25,9},{2,18},{3,... | collective-permute-start | bytes 294920 | tf_op jit(solution)/shard_map/ppermute | solution.py:104
  52.8 6.1 %collective-permute-start.15 = (bf16[32,1536]{1,0:T(8,128)(2,1)S(1)}, bf16[32,1536]{1,0:T(8,128)(2,1)S(1)}, u32[]{:S(2)}, u32[]{:S(2)}) collective-permute-start(bf16[32,1536]{1,0:T(8,128)(2,1)S(1)} %add_convert_fusion.refs_0_), channel_id=1, source_target_pairs={{0,1},{1,0},{8,9},{9,8},{16,17},{17,16},{24,25},{25,24},{2,3},{3,2... | collective-permute-start | bytes 294920 | tf_op jit(solution)/shard_map/ppermute | solution.py:104
  55.5 4.9 %collective-permute-start.24 = (bf16[2,192,128]{2,1,0:T(8,128)(2,1)S(1)}, bf16[2,192,128]{2,1,0:T(8,128)(2,1)S(1)}, u32[]{:S(2)}, u32[]{:S(2)}) collective-permute-start(bf16[2,192,128]{2,1,0:T(8,128)(2,1)S(1)} %get-tuple-element.93), channel_id=1, source_target_pairs={{0,2},{2,0},{4,6},{6,4},{1,3},{3,1},{5,7},{7,5},{8,10},{10,8},{12,... | collective-permute-start | bytes 294920 | tf_op jit(solution)/shard_map/ppermute | solution.py:85
  55.6 7.5 %collective-permute-start.23 = (bf16[2,192,128]{2,1,0:T(8,128)(2,1)S(1)}, bf16[2,192,128]{2,1,0:T(8,128)(2,1)S(1)}, u32[]{:S(2)}, u32[]{:S(2)}) collective-permute-start(bf16[2,192,128]{2,1,0:T(8,128)(2,1)S(1)} %get-tuple-element.92), channel_id=1, source_target_pairs={{6,2},{0,4},{7,3},{1,5},{14,10},{8,12},{15,11},{9,13},{22,18},{16,... | collective-permute-start | bytes 294920 | tf_op jit(solution)/shard_map/ppermute | solution.py:85
  56.9 8.4 %collective-permute-start.22 = (bf16[2,192,128]{2,1,0:T(8,128)(2,1)S(1)}, bf16[2,192,128]{2,1,0:T(8,128)(2,1)S(1)}, u32[]{:S(2)}, u32[]{:S(2)}) collective-permute-start(bf16[2,192,128]{2,1,0:T(8,128)(2,1)S(1)} %get-tuple-element.92), channel_id=1, source_target_pairs={{4,2},{2,4},{5,3},{3,5},{12,10},{10,12},{13,11},{11,13},{20,18},{1... | collective-permute-start | bytes 294920 | tf_op jit(solution)/shard_map/ppermute | solution.py:85
  58.9 7.1 %collective-permute-start.18 = (bf16[144,1536]{1,0:T(8,128)(2,1)S(1)}, bf16[144,1536]{1,0:T(8,128)(2,1)S(1)}, u32[]{:S(2)}, u32[]{:S(2)}) collective-permute-start(bf16[144,1536]{1,0:T(8,128)(2,1)S(1)} %shard_map.97.part), channel_id=1, source_target_pairs={{0,8},{8,0},{16,24},{24,16},{1,9},{9,1},{17,25},{25,17},{2,10},{10... | collective-permute-start | bytes 1327112 | tf_op jit(solution)/shard_map/ppermute | solution.py:104

commit v7 on v6

--- a/solution.py
+++ b/solution.py
@@ -13,6 +13,7 @@
 SMEM = pl.BlockSpec(memory_space=pltpu.SMEM)
 PARAMS = pltpu.CompilerParams(vmem_limit_bytes=24 * 1024 * 1024)
 STAT_ROWS = 8
+FREE = pl.CostEstimate(flops=0, bytes_accessed=0, transcendentals=0)
 
 
 def window_of(position, extent):
@@ -77,7 +78,8 @@
     extent = lax.axis_size(axis)
     slots = slots_of(extent)
     arrived = []
-    for c, route in reversed(list(enumerate(routes_of(extent)))):
+    order = (0, 2, 1) if extent == 4 else range(len(routes_of(extent)))
+    for c, route in ((c, routes_of(extent)[c]) for c in order):
         holders = [next((k for k in range(len(slots)) if slots[k][p] == c), None) for p in range(extent)]
         used = sorted({k for k in holders if k is not None})
         choice = [k if k is not None else used[0] for k in holders]
@@ -306,6 +308,7 @@
         scratch_shapes=scratch,
         input_output_aliases={3: 0} if flipped else {},
         compiler_params=PARAMS,
+        cost_estimate=cost_of(10**10, 10**8),
     )(*operands)
 
 
@@ -551,8 +554,8 @@
         pieces = [column_grad[k] for k in range(column_tiles)]
     if small:
         whole, finish = join_sum(part, query_own, query_other, place)
-        whole, pieces[0] = lax.optimization_barrier((whole, pieces[0]))
         grad_out_weight, grad_query = finish(whole)
+        grad_out_weight, pieces[0] = lax.optimization_barrier((grad_out_weight, pieces[0]))
     else:
         query_other = flip(query_other, ("frame",), (1,)).reshape(-1, half // head_dim, head_dim)
         query_other = query_other.transpose(1, 0, 2).reshape(tile, head_dim)

time: 67.8 us -> 66.4 us (0.979)
  the two profiles are of different devices: /device:TPU:15 before, /device:TPU:0 now
where the time goes in v7:
time: 66.4 us; the launch traced here: 66.1 us
  starting transfers between devices  36.4 us (55%)
  waiting for transfers between devices  14.4 us (22%)
  Pallas kernels  10.5 us (16%)
  matrix products  1.47 us (2%)
  local copies, waits for them, and re-layouts  1.28 us (2%)
  other arithmetic  1.17 us (2%)
  between operations  0.85 us (1%)
    ppermute x12, starting transfers between devices, flip(): return lax.ppermute(block, axes, route)  11.9 us
    ppermute x12, waiting for transfers between devices, flip(): return lax.ppermute(block, axes, route)  8.74 us
    ppermute x3, starting transfers between devices, fetch(): arrived = [lax.ppermute(block, axis, route) for route in routes]  8.25 us
    ppermute x3, starting transfers between devices, returned(): arrived.append(lax.ppermute(outgoing, axis, [(p, s) for s, p in route]))  5.19 us
    ppermute x1, starting transfers between devices, body(): lax.ppermute(far_grad, 'frame', [(0, 2), (3, 1)])  4.92 us
    pallas_call x3, Pallas kernels, kernel_call(): pl.pallas_call(kernel, out_shape=outs, in_specs=[SMEM] + [VMEM] * (len(op...  4.85 us
    pallas_call x2, Pallas kernels, assemble(): pl.pallas_call(functools.partial(assemble_kernel, flipped, rows), out_sha...  2.95 us
    ppermute x3, waiting for transfers between devices, fetch(): arrived = [lax.ppermute(block, axis, route) for route in routes]  2.79 us
  transfers between devices with their start and end apart: 25, of which 10 were waited for; matrix products, arithmetic and copies ran while one was open for 3% of the time, Pallas kernels for 13%

profile of v7, /device:TPU:0, one launch (start us, length us, event | category | flops | bytes accessed | tf_op | source)
XLA Modules:
  0.0 66.1 jit_solution(1766180754436439347)
XLA Ops:
  0.7 0.9 %fusion = (bf16[1,2,192,128]{3,2,1,0:T(8,128)(2,1)S(1)}, bf16[2,192,128]{2,1,0:T(8,128)(2,1)S(1)}) fusion(bf16[1,192,128]{2,1,0:T(8,128)(2,1)} %bitcast.24, bf16[1,192,128]{2,1,0:T(8,128)(2,1)} %bitcast.25), kind=kLoop, calls=%fused_computation.9 | loop fusion | flops 49152 | bytes 294912 | tf_op jit(solution)/shard_map/stack | solution.py:410
  1.6 0.7 %collective-permute-start.2 = (bf16[2,192,128]{2,1,0:T(8,128)(2,1)S(1)}, bf16[2,192,128]{2,1,0:T(8,128)(2,1)S(1)}, u32[]{:S(2)}, u32[]{:S(2)}) collective-permute-start(bf16[2,192,128]{2,1,0:T(8,128)(2,1)S(1)} %get-tuple-element.98), channel_id=1, source_target_pairs={{2,4},{4,2},{3,5},{5,3},{10,12},{12,10},{11,13},{13,11},{18,20},{2... | collective-permute-start | bytes 294920 | tf_op jit(solution)/shard_map/ppermute | solution.py:65
  2.2 1.3 %collective-permute-start.1 = (bf16[2,192,128]{2,1,0:T(8,128)(2,1)S(1)}, bf16[2,192,128]{2,1,0:T(8,128)(2,1)S(1)}, u32[]{:S(2)}, u32[]{:S(2)}) collective-permute-start(bf16[2,192,128]{2,1,0:T(8,128)(2,1)S(1)} %get-tuple-element.98), channel_id=1, source_target_pairs={{2,6},{4,0},{3,7},{5,1},{10,14},{12,8},{11,15},{13,9},{18,22},{20,... | collective-permute-start | bytes 294920 | tf_op jit(solution)/shard_map/ppermute | solution.py:65
  3.5 6.3 %collective-permute-start = (bf16[2,192,128]{2,1,0:T(8,128)(2,1)S(1)}, bf16[2,192,128]{2,1,0:T(8,128)(2,1)S(1)}, u32[]{:S(2)}, u32[]{:S(2)}) collective-permute-start(bf16[2,192,128]{2,1,0:T(8,128)(2,1)S(1)} %get-tuple-element.98), channel_id=1, source_target_pairs={{2,0},{0,2},{6,4},{4,6},{3,1},{1,3},{7,5},{5,7},{10,8},{8,10},{14,... | collective-permute-start | bytes 294920 | tf_op jit(solution)/shard_map/ppermute | solution.py:65
  9.8 1.5 %collective-permute-start.3 = (bf16[1,2,192,128]{3,2,1,0:T(8,128)(2,1)S(1)}, bf16[1,2,192,128]{3,2,1,0:T(8,128)(2,1)S(1)}, u32[]{:S(2)}, u32[]{:S(2)}) collective-permute-start(bf16[1,2,192,128]{3,2,1,0:T(8,128)(2,1)S(1)} %get-tuple-element.97), channel_id=1, source_target_pairs={{0,1},{1,0},{2,3},{3,2},{4,5},{5,4},{6,7},{7,6},{8,9},{9,8},{10,11... | collective-permute-start | bytes 294920 | tf_op jit(solution)/shard_map/ppermute | solution.py:408
  11.4 0.0 collective-permute-done.2
  11.4 1.4 %collective-permute-done.1 = bf16[2,192,128]{2,1,0:T(8,128)(2,1)S(1)} collective-permute-done((bf16[2,192,128]{2,1,0:T(8,128)(2,1)S(1)}, bf16[2,192,128]{2,1,0:T(8,128)(2,1)S(1)}, u32[]{:S(2)}, u32[]{:S(2)}) %collective-permute-start.1) | collective-permute-done | bytes 98336 | tf_op jit(solution)/shard_map/ppermute | solution.py:65
  12.8 1.4 %collective-permute-done = bf16[2,192,128]{2,1,0:T(8,128)(2,1)S(1)} collective-permute-done((bf16[2,192,128]{2,1,0:T(8,128)(2,1)S(1)}, bf16[2,192,128]{2,1,0:T(8,128)(2,1)S(1)}, u32[]{:S(2)}, u32[]{:S(2)}) %collective-permute-start) | collective-permute-done | bytes 98336 | tf_op jit(solution)/shard_map/ppermute | solution.py:65
  14.2 0.2 collective-permute-done.3.refs_0_.refs_1_
  14.5 0.7 %collective-permute-start.7 = (bf16[3,2,192,128]{3,2,1,0:T(8,128)(2,1)S(1)}, bf16[3,2,192,128]{3,2,1,0:T(8,128)(2,1)S(1)}, u32[]{:S(2)}, u32[]{:S(2)}) collective-permute-start(bf16[3,2,192,128]{3,2,1,0:T(8,128)(2,1)S(1)} %pad_maximum_fusion.refs_0_), channel_id=1, source_target_pairs={{16,9},{17,8},{8,17},{9,16},{18,11},{19,10},{10,19},{11,18},{20,13... | collective-permute-start | bytes 884744 | tf_op jit(solution)/shard_map/ppermute | solution.py:417
  15.1 1.3 %collective-permute-start.6 = (bf16[3,2,192,128]{3,2,1,0:T(8,128)(2,1)S(1)}, bf16[3,2,192,128]{3,2,1,0:T(8,128)(2,1)S(1)}, u32[]{:S(2)}, u32[]{:S(2)}) collective-permute-start(bf16[3,2,192,128]{3,2,1,0:T(8,128)(2,1)S(1)} %pad_maximum_fusion.refs_0_), channel_id=1, source_target_pairs={{16,0},{8,24},{17,1},{9,25},{18,2},{10,26},{19,3},{11,27},{20,4},{... | collective-permute-start | bytes 884744 | tf_op jit(solution)/shard_map/ppermute | solution.py:416
  16.4 1.6 %collective-permute-start.5 = (bf16[2,2,192,128]{3,2,1,0:T(8,128)(2,1)S(1)}, bf16[2,2,192,128]{3,2,1,0:T(8,128)(2,1)S(1)}, u32[]{:S(2)}, u32[]{:S(2)}) collective-permute-start(bf16[2,2,192,128]{3,2,1,0:T(8,128)(2,1)S(1)} %pad_maximum_fusion.1), channel_id=1, source_target_pairs={{0,1},{1,0},{2,3},{3,2},{4,5},{5,4},{6,7},{7,6},{8,9},{9,8},{10,11... | collective-permute-start | bytes 589832 | tf_op jit(solution)/shard_map/ppermute | solution.py:414
  18.0 2.5 %collective-permute-start.4 = (bf16[192,128]{1,0:T(8,128)(2,1)S(1)}, bf16[192,128]{1,0:T(8,128)(2,1)S(1)}, u32[]{:S(2)}, u32[]{:S(2)}) collective-permute-start(bf16[192,128]{1,0:T(8,128)(2,1)S(1)} %bitcast.19), channel_id=1, source_target_pairs={{0,8},{8,0},{16,24},{24,16},{1,9},{9,1},{17,25},{25,17},{2,10},{10... | collective-permute-start | bytes 147464 | tf_op jit(solution)/shard_map/ppermute | solution.py:106
  20.5 0.1 pad_add_fusion.place
  20.6 0.8 %collective-permute-done.4.queries_other = bf16[192,128]{1,0:T(8,128)(2,1)S(1)} collective-permute-done((bf16[192,128]{1,0:T(8,128)(2,1)S(1)}, bf16[192,128]{1,0:T(8,128)(2,1)S(1)}, u32[]{:S(2)}, u32[]{:S(2)}) %collective-permute-start.4) | collective-permute-done | bytes 49184 | tf_op jit(solution)/shard_map/ppermute | solution.py:106
  21.4 1.3 %copy-done.1 = bf16[4,6,8,3072]{3,2,1,0:T(8,128)(2,1)S(1)} copy-done((bf16[4,6,8,3072]{3,2,1,0:T(8,128)(2,1)S(1)}, bf16[4,6,8,3072]{3,2,1,0:T(8,128)(2,1)}, u32[]{:S(2)}) %copy-start.1) | copy-done | bytes 1179672
  22.7 1.0 %shard_map.92 = (bf16[192,1664]{1,0:T(8,128)(2,1)S(1)}, bf16[192,1536]{1,0:T(8,128)(2,1)S(1)}, bf16[192,128]{1,0:T(8,128)(2,1)S(1)}, bf16[384,128]{1,0:T(8,128)(2,1)S(1)}) custom-call(s32[3]{0:T(128)S(1)} %pad_add_fusion.place, bf16[192,128]{1,0:T(8,128)(2,1)S(1)} %bitcast.20, bf16[192,128]{1,0:T(8,128)(2,1)S(1)} %collective-permute-done.4.queries_other, ...), custom_call_target="tpu_custom_call" | custom-call | flops 150994944 | bytes 2359296 | tf_op jit(solution)/shard_map/pallas_call | solution.py:345
  23.7 0.7 %shard_map.93.refs_4_ = f32[136,384]{1,0:T(8,128)S(1)} custom-call(bf16[384,128]{1,0:T(8,128)(2,1)S(1)} %get-tuple-element.52.both_queries, bf16[3,2,192,128]{3,2,1,0:T(8,128)(2,1)S(1)} %pad_maximum_fusion.refs_0_), custom_call_target="tpu_custom_call" | custom-call | flops 113246208 | bytes 393216 | tf_op jit(solution)/shard_map/pallas_call | solution.py:459
  24.4 2.6 %collective-permute-done.5.refs_1_.refs_2_ = bf16[2,2,192,128]{3,2,1,0:T(8,128)(2,1)S(1)} collective-permute-done((bf16[2,2,192,128]{3,2,1,0:T(8,128)(2,1)S(1)}, bf16[2,2,192,128]{3,2,1,0:T(8,128)(2,1)S(1)}, u32[]{:S(2)}, u32[]{:S(2)}) %collective-permute-start.5) | collective-permute-done | bytes 196640 | tf_op jit(solution)/shard_map/ppermute | solution.py:414
  27.0 0.0 collective-permute-done.7.refs_3_.refs_4_
  27.0 0.0 collective-permute-done.6.refs_2_.refs_3_
  27.0 0.3 collective-permute-start.9
  27.3 1.2 %shard_map.94.mine = f32[136,384]{1,0:T(8,128)S(1)} custom-call(bf16[384,128]{1,0:T(8,128)(2,1)S(1)} %get-tuple-element.52.both_queries, bf16[1,2,192,128]{3,2,1,0:T(8,128)(2,1)S(1)} %collective-permute-done.3.refs_0_.refs_1_, bf16[2,2,192,128]{3,2,1,0:T(8,128)(2,1)S(1)} %collective-permute-done.5.refs_1_.refs_2_, ...), custom_call_target="tpu_custom_call" | custom-call | flops 226492416 | bytes 786432 | tf_op jit(solution)/shard_map/pallas_call | solution.py:459
  28.5 0.3 collective-permute-start.8
  28.8 1.2 %collective-permute-done.8.theirs = f32[136,384]{1,0:T(8,128)S(1)} collective-permute-done((f32[136,384]{1,0:T(8,128)S(1)}, f32[136,384]{1,0:T(8,128)S(1)}, u32[]{:S(2)}, u32[]{:S(2)}) %collective-permute-start.8) | collective-permute-done | bytes 208928 | tf_op jit(solution)/shard_map/ppermute | solution.py:106
  30.0 0.0 collective-permute-done.9.payload
  30.0 1.1 %shard_map.95 = (f32[8,384]{1,0:T(8,128)S(1)}, bf16[192,128]{1,0:T(8,128)(2,1)S(1)}, bf16[32,1536]{1,0:T(8,128)(2,1)S(1)}, bf16[32,1536]{1,0:T(8,128)(2,1)S(1)},...) custom-call(s32[3]{0:T(128)S(1)} %pad_add_fusion.place, f32[136,384]{1,0:T(8,128)S(1)} %shard_map.94.mine, ...), custom_call_target="tpu_custom_call" | custom-call | flops 150994944 | bytes 2359296 | tf_op jit(solution)/shard_map/pallas_call | solution.py:345
  31.1 1.5 %collective-permute-start.10 = (bf16[32,1536]{1,0:T(8,128)(2,1)S(1)}, bf16[32,1536]{1,0:T(8,128)(2,1)S(1)}, u32[]{:S(2)}, u32[]{:S(2)}) collective-permute-start(bf16[32,1536]{1,0:T(8,128)(2,1)S(1)} %get-tuple-element.73), channel_id=1, source_target_pairs={{0,1},{1,0},{8,9},{9,8},{16,17},{17,16},{24,25},{25,24},{2,3},{3,2... | collective-permute-start | bytes 294920 | tf_op jit(solution)/shard_map/ppermute | solution.py:106
  32.6 0.3 collective-permute-start.11
  32.9 1.8 %collective-permute-start.12 = (bf16[32,1536]{1,0:T(8,128)(2,1)S(1)}, bf16[32,1536]{1,0:T(8,128)(2,1)S(1)}, u32[]{:S(2)}, u32[]{:S(2)}) collective-permute-start(bf16[32,1536]{1,0:T(8,128)(2,1)S(1)} %get-tuple-element.75), channel_id=1, source_target_pairs={{0,17},{1,16},{8,25},{9,24},{16,1},{17,0},{24,9},{25,8},{2,19},{3,... | collective-permute-start | bytes 294920 | tf_op jit(solution)/shard_map/ppermute | solution.py:106
  34.7 2.7 %shard_map.96 = (f32[3,2,192,128]{3,2,1,0:T(8,128)S(1)}, bf16[3,2,192,128]{3,2,1,0:T(8,128)(2,1)S(1)}, bf16[3,2,192,128]{3,2,1,0:T(8,128)(2,1)S(1)}, f32[192,128]{1,0:T(8,128)S(1)}, bf16[16,1536]{1,0:T(8,128)(2,1)S(1)}) custom-call(s32[3]{0:T(128)S(1)} %pad_add_fusion.place, f32[8,384]{1,0:T(8,128)S(1)} %get-tuple-element.66.stats, ...), custom_call_target="tpu_custom_call" | custom-call | flops 849346560 | bytes 2359296 | tf_op jit(solution)/shard_map/pallas_call | solution.py:345
  37.4 0.0 collective-permute-done.10
  37.4 0.8 %collective-permute-done.11 = bf16[32,1536]{1,0:T(8,128)(2,1)S(1)} collective-permute-done((bf16[32,1536]{1,0:T(8,128)(2,1)S(1)}, bf16[32,1536]{1,0:T(8,128)(2,1)S(1)}, u32[]{:S(2)}, u32[]{:S(2)}) %collective-permute-start.11) | collective-permute-done | bytes 98336 | tf_op jit(solution)/shard_map/ppermute | solution.py:106
  38.2 1.2 %collective-permute-done.12 = bf16[32,1536]{1,0:T(8,128)(2,1)S(1)} collective-permute-done((bf16[32,1536]{1,0:T(8,128)(2,1)S(1)}, bf16[32,1536]{1,0:T(8,128)(2,1)S(1)}, u32[]{:S(2)}, u32[]{:S(2)}) %collective-permute-start.12) | collective-permute-done | bytes 98336 | tf_op jit(solution)/shard_map/ppermute | solution.py:106
  39.4 0.1 add_convert_fusion.2
  39.5 0.1 collective-permute-start.13
  39.6 0.7 %collective-permute-start.21 = (bf16[3,2,192,128]{3,2,1,0:T(8,128)(2,1)S(1)}, bf16[3,2,192,128]{3,2,1,0:T(8,128)(2,1)S(1)}, u32[]{:S(2)}, u32[]{:S(2)}) collective-permute-start(bf16[3,2,192,128]{3,2,1,0:T(8,128)(2,1)S(1)} %get-tuple-element.89), channel_id=1, source_target_pairs={{9,16},{8,17},{17,8},{16,9},{11,18},{10,19},{19,10},{18,11},{13,20... | collective-permute-start | bytes 884744 | tf_op jit(solution)/shard_map/ppermute | solution.py:527
  40.3 4.9 %collective-permute-start.20 = (bf16[3,2,192,128]{3,2,1,0:T(8,128)(2,1)S(1)}, bf16[3,2,192,128]{3,2,1,0:T(8,128)(2,1)S(1)}, u32[]{:S(2)}, u32[]{:S(2)}) collective-permute-start(bf16[3,2,192,128]{3,2,1,0:T(8,128)(2,1)S(1)} %get-tuple-element.89), channel_id=1, source_target_pairs={{0,16},{24,8},{1,17},{25,9},{2,18},{26,10},{3,19},{27,11},{4,20},{... | collective-permute-start | bytes 884744 | tf_op jit(solution)/shard_map/ppermute | solution.py:526
  45.2 0.5 collective-permute-start.19
  45.7 0.0 collective-permute-done.13
  45.7 1.5 %collective-permute-start.14 = (bf16[32,1536]{1,0:T(8,128)(2,1)S(1)}, bf16[32,1536]{1,0:T(8,128)(2,1)S(1)}, u32[]{:S(2)}, u32[]{:S(2)}) collective-permute-start(bf16[32,1536]{1,0:T(8,128)(2,1)S(1)} %add_convert_fusion.1), channel_id=1, source_target_pairs={{0,4},{2,6},{4,0},{6,2},{1,5},{3,7},{5,1},{7,3},{8,12},{10,14},{12... | collective-permute-start | bytes 294920 | tf_op jit(solution)/shard_map/ppermute | solution.py:106
  47.2 1.5 %convolution_convert_fusion = bf16[192,3072]{1,0:T(8,128)(2,1)} fusion(bf16[192,128]{1,0:T(8,128)(2,1)S(1)} %get-tuple-element.78, bf16[128,3072]{1,0:T(8,128)(2,1)S(1)} %copy-done), kind=kOutput, calls=%fused_computation | convolution fusion | flops 151584768 | bytes 2015232 | tf_op jit(solution)/shard_map/dot_general | solution.py:518
  48.7 4.4 %collective-permute-done.14 = bf16[32,1536]{1,0:T(8,128)(2,1)S(1)} collective-permute-done((bf16[32,1536]{1,0:T(8,128)(2,1)S(1)}, bf16[32,1536]{1,0:T(8,128)(2,1)S(1)}, u32[]{:S(2)}, u32[]{:S(2)}) %collective-permute-start.14) | collective-permute-done | bytes 98336 | tf_op jit(solution)/shard_map/ppermute | solution.py:106
  53.1 1.3 %collective-permute-start.17 = (bf16[32,1536]{1,0:T(8,128)(2,1)S(1)}, bf16[32,1536]{1,0:T(8,128)(2,1)S(1)}, u32[]{:S(2)}, u32[]{:S(2)}) collective-permute-start(bf16[32,1536]{1,0:T(8,128)(2,1)S(1)} %add_convert_fusion.refs_0_), channel_id=1, source_target_pairs={{0,17},{1,16},{8,25},{9,24},{16,1},{17,0},{24,9},{25,8},{2,19},{3,... | collective-permute-start | bytes 294920 | tf_op jit(solution)/shard_map/ppermute | solution.py:106
  54.4 0.3 collective-permute-start.16
  54.6 0.0 collective-permute-done.19.refs_0_
  54.6 2.0 %collective-permute-start.15 = (bf16[32,1536]{1,0:T(8,128)(2,1)S(1)}, bf16[32,1536]{1,0:T(8,128)(2,1)S(1)}, u32[]{:S(2)}, u32[]{:S(2)}) collective-permute-start(bf16[32,1536]{1,0:T(8,128)(2,1)S(1)} %add_convert_fusion.refs_0_), channel_id=1, source_target_pairs={{0,1},{1,0},{8,9},{9,8},{16,17},{17,16},{24,25},{25,24},{2,3},{3,2... | collective-permute-start | bytes 294920 | tf_op jit(solution)/shard_map/ppermute | solution.py:106
  56.6 0.0 collective-permute-done.21.refs_2_
  56.6 0.0 collective-permute-done.20.refs_1_
  56.6 0.1 shard_map.100
  56.8 3.3 %collective-permute-start.24 = (bf16[2,192,128]{2,1,0:T(8,128)(2,1)S(1)}, bf16[2,192,128]{2,1,0:T(8,128)(2,1)S(1)}, u32[]{:S(2)}, u32[]{:S(2)}) collective-permute-start(bf16[2,192,128]{2,1,0:T(8,128)(2,1)S(1)} %get-tuple-element.93), channel_id=1, source_target_pairs={{6,2},{0,4},{7,3},{1,5},{14,10},{8,12},{15,11},{9,13},{22,18},{16,... | collective-permute-start | bytes 294920 | tf_op jit(solution)/shard_map/ppermute | solution.py:87
  60.1 0.7 %collective-permute-start.23 = (bf16[2,192,128]{2,1,0:T(8,128)(2,1)S(1)}, bf16[2,192,128]{2,1,0:T(8,128)(2,1)S(1)}, u32[]{:S(2)}, u32[]{:S(2)}) collective-permute-start(bf16[2,192,128]{2,1,0:T(8,128)(2,1)S(1)} %get-tuple-element.93), channel_id=1, source_target_pairs={{4,2},{2,4},{5,3},{3,5},{12,10},{10,12},{13,11},{11,13},{20,18},{1... | collective-permute-start | bytes 294920 | tf_op jit(solution)/shard_map/ppermute | solution.py:87
  60.7 0.0 collective-permute-done.17.refs_3_
  60.7 1.3 %collective-permute-start.22 = (bf16[2,192,128]{2,1,0:T(8,128)(2,1)S(1)}, bf16[2,192,128]{2,1,0:T(8,128)(2,1)S(1)}, u32[]{:S(2)}, u32[]{:S(2)}) collective-permute-start(bf16[2,192,128]{2,1,0:T(8,128)(2,1)S(1)} %get-tuple-element.92), channel_id=1, source_target_pairs={{0,2},{2,0},{4,6},{6,4},{1,3},{3,1},{5,7},{7,5},{8,10},{10,8},{12,... | collective-permute-start | bytes 294920 | tf_op jit(solution)/shard_map/ppermute | solution.py:87
  62.0 0.0 collective-permute-done.16.refs_2_
  62.0 0.0 collective-permute-done.15.refs_1_
  62.0 0.1 collective-permute-start.18
  62.1 1.5 %shard_map.98.refs_1_ = f32[128,3072]{1,0:T(8,128)} custom-call(s32[3]{0:T(128)S(1)} %pad_add_fusion.place, bf16[144,1536]{1,0:T(8,128)(2,1)S(1)} %shard_map.97.part), custom_call_target="tpu_custom_call" | custom-call | flops 10000000000 | bytes 100000000 | tf_op jit(solution)/shard_map/pallas_call | solution.py:303
  63.6 0.3 collective-permute-done.18.part
  63.9 1.5 %shard_map.99 = (f32[128,3072]{1,0:T(8,128)}, bf16[192,128]{1,0:T(8,128)(2,1)}) custom-call(s32[3]{0:T(128)S(1)} %pad_add_fusion.place, bf16[144,1536]{1,0:T(8,128)(2,1)S(1)} %collective-permute-done.18.part, f32[192,128]{1,0:T(8,128)S(1)} %get-tuple-element.84.refs_0_, f32[128,3072]{1,0:T(8,128)} %shard_map.98.refs_1_), custom_call_target="tpu_custom_call", output_to_operand_aliasing={{0}: (3, {})} | custom-call | flops 10000000000 | bytes 100000000 | tf_op jit(solution)/shard_map/pallas_call | solution.py:303
  65.4 0.0 collective-permute-done.22.refs_0_
  65.4 0.0 collective-permute-done.24.refs_2_
  65.4 0.0 collective-permute-done.23.refs_1_
  65.4 0.7 %shard_map.101 = (bf16[192,128]{1,0:T(8,128)(2,1)}, bf16[192,128]{1,0:T(8,128)(2,1)}) custom-call(f32[2,192,128]{2,1,0:T(8,128)S(1)} %get-tuple-element.91.own_grad, bf16[2,192,128]{2,1,0:T(8,128)(2,1)S(1)} %collective-permute-done.22.refs_0_, bf16[2,192,128]{2,1,0:T(8,128)(2,1)S(1)} %collective-permute-done.23.refs_1_, ...), custom_call_target="tpu_custom_call" | custom-call | flops 10000000000 | bytes 100000000 | tf_op jit(solution)/shard_map/pallas_call | solution.py:564
  (11 shorter events, 0.2 us)
Async XLA Ops:
  0.6 17.4 %copy-start.2 = (bf16[4,6,8,128]{3,2,1,0:T(8,128)(2,1)S(1)}, bf16[4,6,8,128]{3,2,1,0:T(8,128)(2,1)}, u32[]{:S(2)}) copy-start(bf16[4,6,8,128]{3,2,1,0:T(8,128)(2,1)} %param.5) | copy-start | bytes 147460
  0.6 20.8 %copy-start = (bf16[128,3072]{1,0:T(8,128)(2,1)S(1)}, bf16[128,3072]{1,0:T(8,128)(2,1)}, u32[]{:S(2)}) copy-start(bf16[128,3072]{1,0:T(8,128)(2,1)} %weight.1) | copy-start | bytes 2359300
  1.6 9.8 %collective-permute-start.2 = (bf16[2,192,128]{2,1,0:T(8,128)(2,1)S(1)}, bf16[2,192,128]{2,1,0:T(8,128)(2,1)S(1)}, u32[]{:S(2)}, u32[]{:S(2)}) collective-permute-start(bf16[2,192,128]{2,1,0:T(8,128)(2,1)S(1)} %get-tuple-element.98), channel_id=1, source_target_pairs={{2,4},{4,2},{3,5},{5,3},{10,12},{12,10},{11,13},{13,11},{18,20},{2... | collective-permute-start | bytes 294920 | tf_op jit(solution)/shard_map/ppermute | solution.py:65
  2.2 10.5 %collective-permute-start.1 = (bf16[2,192,128]{2,1,0:T(8,128)(2,1)S(1)}, bf16[2,192,128]{2,1,0:T(8,128)(2,1)S(1)}, u32[]{:S(2)}, u32[]{:S(2)}) collective-permute-start(bf16[2,192,128]{2,1,0:T(8,128)(2,1)S(1)} %get-tuple-element.98), channel_id=1, source_target_pairs={{2,6},{4,0},{3,7},{5,1},{10,14},{12,8},{11,15},{13,9},{18,22},{20,... | collective-permute-start | bytes 294920 | tf_op jit(solution)/shard_map/ppermute | solution.py:65
  3.5 10.6 %collective-permute-start = (bf16[2,192,128]{2,1,0:T(8,128)(2,1)S(1)}, bf16[2,192,128]{2,1,0:T(8,128)(2,1)S(1)}, u32[]{:S(2)}, u32[]{:S(2)}) collective-permute-start(bf16[2,192,128]{2,1,0:T(8,128)(2,1)S(1)} %get-tuple-element.98), channel_id=1, source_target_pairs={{2,0},{0,2},{6,4},{4,6},{3,1},{1,3},{7,5},{5,7},{10,8},{8,10},{14,... | collective-permute-start | bytes 294920 | tf_op jit(solution)/shard_map/ppermute | solution.py:65
  9.8 4.6 %collective-permute-start.3 = (bf16[1,2,192,128]{3,2,1,0:T(8,128)(2,1)S(1)}, bf16[1,2,192,128]{3,2,1,0:T(8,128)(2,1)S(1)}, u32[]{:S(2)}, u32[]{:S(2)}) collective-permute-start(bf16[1,2,192,128]{3,2,1,0:T(8,128)(2,1)S(1)} %get-tuple-element.97), channel_id=1, source_target_pairs={{0,1},{1,0},{2,3},{3,2},{4,5},{5,4},{6,7},{7,6},{8,9},{9,8},{10,11... | collective-permute-start | bytes 294920 | tf_op jit(solution)/shard_map/ppermute | solution.py:408
  14.5 12.5 %collective-permute-start.7 = (bf16[3,2,192,128]{3,2,1,0:T(8,128)(2,1)S(1)}, bf16[3,2,192,128]{3,2,1,0:T(8,128)(2,1)S(1)}, u32[]{:S(2)}, u32[]{:S(2)}) collective-permute-start(bf16[3,2,192,128]{3,2,1,0:T(8,128)(2,1)S(1)} %pad_maximum_fusion.refs_0_), channel_id=1, source_target_pairs={{16,9},{17,8},{8,17},{9,16},{18,11},{19,10},{10,19},{11,18},{20,13... | collective-permute-start | bytes 884744 | tf_op jit(solution)/shard_map/ppermute | solution.py:417
  15.1 11.9 %collective-permute-start.6 = (bf16[3,2,192,128]{3,2,1,0:T(8,128)(2,1)S(1)}, bf16[3,2,192,128]{3,2,1,0:T(8,128)(2,1)S(1)}, u32[]{:S(2)}, u32[]{:S(2)}) collective-permute-start(bf16[3,2,192,128]{3,2,1,0:T(8,128)(2,1)S(1)} %pad_maximum_fusion.refs_0_), channel_id=1, source_target_pairs={{16,0},{8,24},{17,1},{9,25},{18,2},{10,26},{19,3},{11,27},{20,4},{... | collective-permute-start | bytes 884744 | tf_op jit(solution)/shard_map/ppermute | solution.py:416
  16.4 10.6 %collective-permute-start.5 = (bf16[2,2,192,128]{3,2,1,0:T(8,128)(2,1)S(1)}, bf16[2,2,192,128]{3,2,1,0:T(8,128)(2,1)S(1)}, u32[]{:S(2)}, u32[]{:S(2)}) collective-permute-start(bf16[2,2,192,128]{3,2,1,0:T(8,128)(2,1)S(1)} %pad_maximum_fusion.1), channel_id=1, source_target_pairs={{0,1},{1,0},{2,3},{3,2},{4,5},{5,4},{6,7},{7,6},{8,9},{9,8},{10,11... | collective-permute-start | bytes 589832 | tf_op jit(solution)/shard_map/ppermute | solution.py:414
  18.0 3.4 %collective-permute-start.4 = (bf16[192,128]{1,0:T(8,128)(2,1)S(1)}, bf16[192,128]{1,0:T(8,128)(2,1)S(1)}, u32[]{:S(2)}, u32[]{:S(2)}) collective-permute-start(bf16[192,128]{1,0:T(8,128)(2,1)S(1)} %bitcast.19), channel_id=1, source_target_pairs={{0,8},{8,0},{16,24},{24,16},{1,9},{9,1},{17,25},{25,17},{2,10},{10... | collective-permute-start | bytes 147464 | tf_op jit(solution)/shard_map/ppermute | solution.py:106
  21.4 1.3 %copy-start.1 = (bf16[4,6,8,3072]{3,2,1,0:T(8,128)(2,1)S(1)}, bf16[4,6,8,3072]{3,2,1,0:T(8,128)(2,1)}, u32[]{:S(2)}) copy-start(bf16[4,6,8,3072]{3,2,1,0:T(8,128)(2,1)} %param.9) | copy-start | bytes 3538948
  27.0 3.0 %collective-permute-start.9 = (bf16[192,1664]{1,0:T(8,128)(2,1)S(1)}, bf16[192,1664]{1,0:T(8,128)(2,1)S(1)}, u32[]{:S(2)}, u32[]{:S(2)}) collective-permute-start(bf16[192,1664]{1,0:T(8,128)(2,1)S(1)} %get-tuple-element.62), channel_id=1, source_target_pairs={{0,8},{8,0},{16,24},{24,16},{1,9},{9,1},{17,25},{25,17},{2,10},{10... | collective-permute-start | bytes 1916936 | tf_op jit(solution)/shard_map/ppermute | solution.py:106
  28.5 1.5 %collective-permute-start.8 = (f32[136,384]{1,0:T(8,128)S(1)}, f32[136,384]{1,0:T(8,128)S(1)}, u32[]{:S(2)}, u32[]{:S(2)}) collective-permute-start(f32[136,384]{1,0:T(8,128)S(1)} %shard_map.94.mine), channel_id=1, source_target_pairs={{0,8},{8,0},{16,24},{24,16},{1,9},{9,1},{17,25},{25,17},{2,10},{10... | collective-permute-start | bytes 626696 | tf_op jit(solution)/shard_map/ppermute | solution.py:106
  31.1 6.3 %collective-permute-start.10 = (bf16[32,1536]{1,0:T(8,128)(2,1)S(1)}, bf16[32,1536]{1,0:T(8,128)(2,1)S(1)}, u32[]{:S(2)}, u32[]{:S(2)}) collective-permute-start(bf16[32,1536]{1,0:T(8,128)(2,1)S(1)} %get-tuple-element.73), channel_id=1, source_target_pairs={{0,1},{1,0},{8,9},{9,8},{16,17},{17,16},{24,25},{25,24},{2,3},{3,2... | collective-permute-start | bytes 294920 | tf_op jit(solution)/shard_map/ppermute | solution.py:106
  32.6 5.6 %collective-permute-start.11 = (bf16[32,1536]{1,0:T(8,128)(2,1)S(1)}, bf16[32,1536]{1,0:T(8,128)(2,1)S(1)}, u32[]{:S(2)}, u32[]{:S(2)}) collective-permute-start(bf16[32,1536]{1,0:T(8,128)(2,1)S(1)} %get-tuple-element.74), channel_id=1, source_target_pairs={{0,16},{1,17},{8,24},{9,25},{16,0},{17,1},{24,8},{25,9},{2,18},{3,... | collective-permute-start | bytes 294920 | tf_op jit(solution)/shard_map/ppermute | solution.py:106
  32.9 6.6 %collective-permute-start.12 = (bf16[32,1536]{1,0:T(8,128)(2,1)S(1)}, bf16[32,1536]{1,0:T(8,128)(2,1)S(1)}, u32[]{:S(2)}, u32[]{:S(2)}) collective-permute-start(bf16[32,1536]{1,0:T(8,128)(2,1)S(1)} %get-tuple-element.75), channel_id=1, source_target_pairs={{0,17},{1,16},{8,25},{9,24},{16,1},{17,0},{24,9},{25,8},{2,19},{3,... | collective-permute-start | bytes 294920 | tf_op jit(solution)/shard_map/ppermute | solution.py:106
  39.5 6.2 %collective-permute-start.13 = (bf16[32,1536]{1,0:T(8,128)(2,1)S(1)}, bf16[32,1536]{1,0:T(8,128)(2,1)S(1)}, u32[]{:S(2)}, u32[]{:S(2)}) collective-permute-start(bf16[32,1536]{1,0:T(8,128)(2,1)S(1)} %add_convert_fusion.2), channel_id=1, source_target_pairs={{0,2},{2,0},{4,6},{6,4},{1,3},{3,1},{5,7},{7,5},{8,10},{10,8},{12,... | collective-permute-start | bytes 294920 | tf_op jit(solution)/shard_map/ppermute | solution.py:106
  39.6 17.0 %collective-permute-start.21 = (bf16[3,2,192,128]{3,2,1,0:T(8,128)(2,1)S(1)}, bf16[3,2,192,128]{3,2,1,0:T(8,128)(2,1)S(1)}, u32[]{:S(2)}, u32[]{:S(2)}) collective-permute-start(bf16[3,2,192,128]{3,2,1,0:T(8,128)(2,1)S(1)} %get-tuple-element.89), channel_id=1, source_target_pairs={{9,16},{8,17},{17,8},{16,9},{11,18},{10,19},{19,10},{18,11},{13,20... | collective-permute-start | bytes 884744 | tf_op jit(solution)/shard_map/ppermute | solution.py:527
  40.3 16.4 %collective-permute-start.20 = (bf16[3,2,192,128]{3,2,1,0:T(8,128)(2,1)S(1)}, bf16[3,2,192,128]{3,2,1,0:T(8,128)(2,1)S(1)}, u32[]{:S(2)}, u32[]{:S(2)}) collective-permute-start(bf16[3,2,192,128]{3,2,1,0:T(8,128)(2,1)S(1)} %get-tuple-element.89), channel_id=1, source_target_pairs={{0,16},{24,8},{1,17},{25,9},{2,18},{26,10},{3,19},{27,11},{4,20},{... | collective-permute-start | bytes 884744 | tf_op jit(solution)/shard_map/ppermute | solution.py:526
  45.2 9.4 %collective-permute-start.19 = (bf16[3,2,192,128]{3,2,1,0:T(8,128)(2,1)S(1)}, bf16[3,2,192,128]{3,2,1,0:T(8,128)(2,1)S(1)}, u32[]{:S(2)}, u32[]{:S(2)}) collective-permute-start(bf16[3,2,192,128]{3,2,1,0:T(8,128)(2,1)S(1)} %get-tuple-element.88), channel_id=1, source_target_pairs={{0,1},{1,0},{2,3},{3,2},{4,5},{5,4},{6,7},{7,6},{8,9},{9,8},{10,11... | collective-permute-start | bytes 884744 | tf_op jit(solution)/shard_map/ppermute | solution.py:525
  45.7 7.3 %collective-permute-start.14 = (bf16[32,1536]{1,0:T(8,128)(2,1)S(1)}, bf16[32,1536]{1,0:T(8,128)(2,1)S(1)}, u32[]{:S(2)}, u32[]{:S(2)}) collective-permute-start(bf16[32,1536]{1,0:T(8,128)(2,1)S(1)} %add_convert_fusion.1), channel_id=1, source_target_pairs={{0,4},{2,6},{4,0},{6,2},{1,5},{3,7},{5,1},{7,3},{8,12},{10,14},{12... | collective-permute-start | bytes 294920 | tf_op jit(solution)/shard_map/ppermute | solution.py:106
  53.1 7.7 %collective-permute-start.17 = (bf16[32,1536]{1,0:T(8,128)(2,1)S(1)}, bf16[32,1536]{1,0:T(8,128)(2,1)S(1)}, u32[]{:S(2)}, u32[]{:S(2)}) collective-permute-start(bf16[32,1536]{1,0:T(8,128)(2,1)S(1)} %add_convert_fusion.refs_0_), channel_id=1, source_target_pairs={{0,17},{1,16},{8,25},{9,24},{16,1},{17,0},{24,9},{25,8},{2,19},{3,... | collective-permute-start | bytes 294920 | tf_op jit(solution)/shard_map/ppermute | solution.py:106
  54.4 7.6 %collective-permute-start.16 = (bf16[32,1536]{1,0:T(8,128)(2,1)S(1)}, bf16[32,1536]{1,0:T(8,128)(2,1)S(1)}, u32[]{:S(2)}, u32[]{:S(2)}) collective-permute-start(bf16[32,1536]{1,0:T(8,128)(2,1)S(1)} %add_convert_fusion.refs_0_), channel_id=1, source_target_pairs={{0,16},{1,17},{8,24},{9,25},{16,0},{17,1},{24,8},{25,9},{2,18},{3,... | collective-permute-start | bytes 294920 | tf_op jit(solution)/shard_map/ppermute | solution.py:106
  54.6 7.4 %collective-permute-start.15 = (bf16[32,1536]{1,0:T(8,128)(2,1)S(1)}, bf16[32,1536]{1,0:T(8,128)(2,1)S(1)}, u32[]{:S(2)}, u32[]{:S(2)}) collective-permute-start(bf16[32,1536]{1,0:T(8,128)(2,1)S(1)} %add_convert_fusion.refs_0_), channel_id=1, source_target_pairs={{0,1},{1,0},{8,9},{9,8},{16,17},{17,16},{24,25},{25,24},{2,3},{3,2... | collective-permute-start | bytes 294920 | tf_op jit(solution)/shard_map/ppermute | solution.py:106
  56.8 8.7 %collective-permute-start.24 = (bf16[2,192,128]{2,1,0:T(8,128)(2,1)S(1)}, bf16[2,192,128]{2,1,0:T(8,128)(2,1)S(1)}, u32[]{:S(2)}, u32[]{:S(2)}) collective-permute-start(bf16[2,192,128]{2,1,0:T(8,128)(2,1)S(1)} %get-tuple-element.93), channel_id=1, source_target_pairs={{6,2},{0,4},{7,3},{1,5},{14,10},{8,12},{15,11},{9,13},{22,18},{16,... | collective-permute-start | bytes 294920 | tf_op jit(solution)/shard_map/ppermute | solution.py:87
  60.1 5.4 %collective-permute-start.23 = (bf16[2,192,128]{2,1,0:T(8,128)(2,1)S(1)}, bf16[2,192,128]{2,1,0:T(8,128)(2,1)S(1)}, u32[]{:S(2)}, u32[]{:S(2)}) collective-permute-start(bf16[2,192,128]{2,1,0:T(8,128)(2,1)S(1)} %get-tuple-element.93), channel_id=1, source_target_pairs={{4,2},{2,4},{5,3},{3,5},{12,10},{10,12},{13,11},{11,13},{20,18},{1... | collective-permute-start | bytes 294920 | tf_op jit(solution)/shard_map/ppermute | solution.py:87
  60.7 4.7 %collective-permute-start.22 = (bf16[2,192,128]{2,1,0:T(8,128)(2,1)S(1)}, bf16[2,192,128]{2,1,0:T(8,128)(2,1)S(1)}, u32[]{:S(2)}, u32[]{:S(2)}) collective-permute-start(bf16[2,192,128]{2,1,0:T(8,128)(2,1)S(1)} %get-tuple-element.92), channel_id=1, source_target_pairs={{0,2},{2,0},{4,6},{6,4},{1,3},{3,1},{5,7},{7,5},{8,10},{10,8},{12,... | collective-permute-start | bytes 294920 | tf_op jit(solution)/shard_map/ppermute | solution.py:87
  62.0 1.9 %collective-permute-start.18 = (bf16[144,1536]{1,0:T(8,128)(2,1)S(1)}, bf16[144,1536]{1,0:T(8,128)(2,1)S(1)}, u32[]{:S(2)}, u32[]{:S(2)}) collective-permute-start(bf16[144,1536]{1,0:T(8,128)(2,1)S(1)} %shard_map.97.part), channel_id=1, source_target_pairs={{0,8},{8,0},{16,24},{24,16},{1,9},{9,1},{17,25},{25,17},{2,10},{10... | collective-permute-start | bytes 1327112 | tf_op jit(solution)/shard_map/ppermute | solution.py:106

commit v8 on v7

--- a/solution.py
+++ b/solution.py
@@ -400,7 +400,7 @@
     tile = query_rows.shape[0]
 
     own = jnp.stack((key_vectors.reshape(tile, head_dim), value_vectors.reshape(tile, head_dim)))
-    cross = [(2 * s + y, 2 * p + 1 - y) for s, p in ((2, 1), (1, 2)) for y in (0, 1)]
+    cross = [(2 * s + y, 2 * p + 1 - y) for s, p in ((2, 0), (1, 3)) for y in (0, 1)]
 
     if small:
         swap = [(0, 1), (1, 0)]
@@ -413,7 +413,7 @@
         )
         others_beside = lax.ppermute(others, "width", swap)
         far = [
-            lax.ppermute(column, "frame", [(2, 0), (1, 3)]),
+            lax.ppermute(column, "frame", [(2, 1), (1, 2)]),
             lax.ppermute(column, ("frame", "width"), cross),
         ]
         blocks = [column, own_beside, others_beside, *far]
@@ -523,7 +523,7 @@
     if small:
         arrived = [
             lax.ppermute(beside_grads[0], "width", [(0, 1), (1, 0)]),
-            lax.ppermute(far_grad, "frame", [(0, 2), (3, 1)]),
+            lax.ppermute(far_grad, "frame", [(1, 2), (2, 1)]),
             lax.ppermute(far_grad, ("frame", "width"), [(p, s) for s, p in cross]),
         ]
         other, projected = lax.optimization_barrier((other, projected))

time: 66.4 us -> 65.7 us (0.989)
  waiting for transfers between devices: 14.4 us -> 13 us
    ppermute x2, starting transfers between devices: 6.21 us -> 1.36 us  [the longest x1 0.68 us: body(): lax.ppermute(far_grad, 'frame', [(1, 2), (2, 1)])]
    ppermute x1, starting transfers between devices: 0.67 us -> 3.2 us  [body(): lax.ppermute(far_grad, ('frame', 'width'), [(p, s) for s, p in cross])]
    ppermute x1, waiting for transfers between devices: 2.57 us -> 0.95 us  [body(): others_beside = lax.ppermute(others, 'width', swap)]
    ppermute x12, starting transfers between devices: 11.9 us -> 13.4 us  [flip(): return lax.ppermute(block, axes, route)]
    ppermute x1, starting transfers between devices: 0.47 us -> 1.19 us  [body(): lax.ppermute(beside_grads[0], 'width', [(0, 1), (1, 0)])]
where the time goes in v8:
time: 65.7 us; the launch traced here: 65.4 us
  starting transfers between devices  37 us (56%)
  waiting for transfers between devices  13 us (20%)
  Pallas kernels  10.5 us (16%)
  matrix products  1.47 us (2%)
  local copies, waits for them, and re-layouts  1.28 us (2%)
  other arithmetic  1.17 us (2%)
  between operations  0.85 us (1%)
    ppermute x12, starting transfers between devices, flip(): return lax.ppermute(block, axes, route)  13.4 us
    ppermute x12, waiting for transfers between devices, flip(): return lax.ppermute(block, axes, route)  9.02 us
    ppermute x3, starting transfers between devices, fetch(): arrived = [lax.ppermute(block, axis, route) for route in routes]  8.25 us
    ppermute x3, starting transfers between devices, returned(): arrived.append(lax.ppermute(outgoing, axis, [(p, s) for s, p in route]))  5.21 us
    pallas_call x3, Pallas kernels, kernel_call(): pl.pallas_call(kernel, out_shape=outs, in_specs=[SMEM] + [VMEM] * (len(op...  4.85 us
    ppermute x1, starting transfers between devices, body(): lax.ppermute(far_grad, ('frame', 'width'), [(p, s) for s, p in cross])  3.2 us
    pallas_call x2, Pallas kernels, assemble(): pl.pallas_call(functools.partial(assemble_kernel, flipped, rows), out_sha...  2.95 us
    ppermute x3, waiting for transfers between devices, fetch(): arrived = [lax.ppermute(block, axis, route) for route in routes]  2.79 us
  transfers between devices with their start and end apart: 25, of which 10 were waited for; matrix products, arithmetic and copies ran while one was open for 3% of the time, Pallas kernels for 13%

profile of v8, /device:TPU:0, one launch (start us, length us, event | category | flops | bytes accessed | tf_op | source)
XLA Modules:
  0.0 65.4 jit_solution(16673565132682622077)
XLA Ops:
  0.7 0.9 %fusion = (bf16[1,2,192,128]{3,2,1,0:T(8,128)(2,1)S(1)}, bf16[2,192,128]{2,1,0:T(8,128)(2,1)S(1)}) fusion(bf16[1,192,128]{2,1,0:T(8,128)(2,1)} %bitcast.24, bf16[1,192,128]{2,1,0:T(8,128)(2,1)} %bitcast.25), kind=kLoop, calls=%fused_computation.9 | loop fusion | flops 49152 | bytes 294912 | tf_op jit(solution)/shard_map/stack | solution.py:410
  1.6 0.7 %collective-permute-start.2 = (bf16[2,192,128]{2,1,0:T(8,128)(2,1)S(1)}, bf16[2,192,128]{2,1,0:T(8,128)(2,1)S(1)}, u32[]{:S(2)}, u32[]{:S(2)}) collective-permute-start(bf16[2,192,128]{2,1,0:T(8,128)(2,1)S(1)} %get-tuple-element.98), channel_id=1, source_target_pairs={{2,4},{4,2},{3,5},{5,3},{10,12},{12,10},{11,13},{13,11},{18,20},{2... | collective-permute-start | bytes 294920 | tf_op jit(solution)/shard_map/ppermute | solution.py:65
  2.2 1.3 %collective-permute-start.1 = (bf16[2,192,128]{2,1,0:T(8,128)(2,1)S(1)}, bf16[2,192,128]{2,1,0:T(8,128)(2,1)S(1)}, u32[]{:S(2)}, u32[]{:S(2)}) collective-permute-start(bf16[2,192,128]{2,1,0:T(8,128)(2,1)S(1)} %get-tuple-element.98), channel_id=1, source_target_pairs={{2,6},{4,0},{3,7},{5,1},{10,14},{12,8},{11,15},{13,9},{18,22},{20,... | collective-permute-start | bytes 294920 | tf_op jit(solution)/shard_map/ppermute | solution.py:65
  3.5 6.3 %collective-permute-start = (bf16[2,192,128]{2,1,0:T(8,128)(2,1)S(1)}, bf16[2,192,128]{2,1,0:T(8,128)(2,1)S(1)}, u32[]{:S(2)}, u32[]{:S(2)}) collective-permute-start(bf16[2,192,128]{2,1,0:T(8,128)(2,1)S(1)} %get-tuple-element.98), channel_id=1, source_target_pairs={{2,0},{0,2},{6,4},{4,6},{3,1},{1,3},{7,5},{5,7},{10,8},{8,10},{14,... | collective-permute-start | bytes 294920 | tf_op jit(solution)/shard_map/ppermute | solution.py:65
  9.8 1.5 %collective-permute-start.3 = (bf16[1,2,192,128]{3,2,1,0:T(8,128)(2,1)S(1)}, bf16[1,2,192,128]{3,2,1,0:T(8,128)(2,1)S(1)}, u32[]{:S(2)}, u32[]{:S(2)}) collective-permute-start(bf16[1,2,192,128]{3,2,1,0:T(8,128)(2,1)S(1)} %get-tuple-element.97), channel_id=1, source_target_pairs={{0,1},{1,0},{2,3},{3,2},{4,5},{5,4},{6,7},{7,6},{8,9},{9,8},{10,11... | collective-permute-start | bytes 294920 | tf_op jit(solution)/shard_map/ppermute | solution.py:408
  11.4 0.0 collective-permute-done.2
  11.4 1.4 %collective-permute-done.1 = bf16[2,192,128]{2,1,0:T(8,128)(2,1)S(1)} collective-permute-done((bf16[2,192,128]{2,1,0:T(8,128)(2,1)S(1)}, bf16[2,192,128]{2,1,0:T(8,128)(2,1)S(1)}, u32[]{:S(2)}, u32[]{:S(2)}) %collective-permute-start.1) | collective-permute-done | bytes 98336 | tf_op jit(solution)/shard_map/ppermute | solution.py:65
  12.8 1.4 %collective-permute-done = bf16[2,192,128]{2,1,0:T(8,128)(2,1)S(1)} collective-permute-done((bf16[2,192,128]{2,1,0:T(8,128)(2,1)S(1)}, bf16[2,192,128]{2,1,0:T(8,128)(2,1)S(1)}, u32[]{:S(2)}, u32[]{:S(2)}) %collective-permute-start) | collective-permute-done | bytes 98336 | tf_op jit(solution)/shard_map/ppermute | solution.py:65
  14.2 0.2 collective-permute-done.3.refs_0_.refs_1_
  14.5 1.3 %collective-permute-start.7 = (bf16[3,2,192,128]{3,2,1,0:T(8,128)(2,1)S(1)}, bf16[3,2,192,128]{3,2,1,0:T(8,128)(2,1)S(1)}, u32[]{:S(2)}, u32[]{:S(2)}) collective-permute-start(bf16[3,2,192,128]{3,2,1,0:T(8,128)(2,1)S(1)} %pad_maximum_fusion.refs_0_), channel_id=1, source_target_pairs={{16,1},{17,0},{8,25},{9,24},{18,3},{19,2},{10,27},{11,26},{20,5},{... | collective-permute-start | bytes 884744 | tf_op jit(solution)/shard_map/ppermute | solution.py:417
  15.7 0.7 %collective-permute-start.6 = (bf16[3,2,192,128]{3,2,1,0:T(8,128)(2,1)S(1)}, bf16[3,2,192,128]{3,2,1,0:T(8,128)(2,1)S(1)}, u32[]{:S(2)}, u32[]{:S(2)}) collective-permute-start(bf16[3,2,192,128]{3,2,1,0:T(8,128)(2,1)S(1)} %pad_maximum_fusion.refs_0_), channel_id=1, source_target_pairs={{16,8},{8,16},{17,9},{9,17},{18,10},{10,18},{19,11},{11,19},{20,12... | collective-permute-start | bytes 884744 | tf_op jit(solution)/shard_map/ppermute | solution.py:416
  16.4 1.6 %collective-permute-start.5 = (bf16[2,2,192,128]{3,2,1,0:T(8,128)(2,1)S(1)}, bf16[2,2,192,128]{3,2,1,0:T(8,128)(2,1)S(1)}, u32[]{:S(2)}, u32[]{:S(2)}) collective-permute-start(bf16[2,2,192,128]{3,2,1,0:T(8,128)(2,1)S(1)} %pad_maximum_fusion.1), channel_id=1, source_target_pairs={{0,1},{1,0},{2,3},{3,2},{4,5},{5,4},{6,7},{7,6},{8,9},{9,8},{10,11... | collective-permute-start | bytes 589832 | tf_op jit(solution)/shard_map/ppermute | solution.py:414
  18.0 3.7 %collective-permute-start.4 = (bf16[192,128]{1,0:T(8,128)(2,1)S(1)}, bf16[192,128]{1,0:T(8,128)(2,1)S(1)}, u32[]{:S(2)}, u32[]{:S(2)}) collective-permute-start(bf16[192,128]{1,0:T(8,128)(2,1)S(1)} %bitcast.19), channel_id=1, source_target_pairs={{0,8},{8,0},{16,24},{24,16},{1,9},{9,1},{17,25},{25,17},{2,10},{10... | collective-permute-start | bytes 147464 | tf_op jit(solution)/shard_map/ppermute | solution.py:106
  21.7 0.1 pad_add_fusion.place
  21.8 0.8 %collective-permute-done.4.queries_other = bf16[192,128]{1,0:T(8,128)(2,1)S(1)} collective-permute-done((bf16[192,128]{1,0:T(8,128)(2,1)S(1)}, bf16[192,128]{1,0:T(8,128)(2,1)S(1)}, u32[]{:S(2)}, u32[]{:S(2)}) %collective-permute-start.4) | collective-permute-done | bytes 49184 | tf_op jit(solution)/shard_map/ppermute | solution.py:106
  22.6 1.3 %copy-done.1 = bf16[4,6,8,3072]{3,2,1,0:T(8,128)(2,1)S(1)} copy-done((bf16[4,6,8,3072]{3,2,1,0:T(8,128)(2,1)S(1)}, bf16[4,6,8,3072]{3,2,1,0:T(8,128)(2,1)}, u32[]{:S(2)}) %copy-start.1) | copy-done | bytes 1179672
  23.8 1.0 %shard_map.92 = (bf16[192,1664]{1,0:T(8,128)(2,1)S(1)}, bf16[192,1536]{1,0:T(8,128)(2,1)S(1)}, bf16[192,128]{1,0:T(8,128)(2,1)S(1)}, bf16[384,128]{1,0:T(8,128)(2,1)S(1)}) custom-call(s32[3]{0:T(128)S(1)} %pad_add_fusion.place, bf16[192,128]{1,0:T(8,128)(2,1)S(1)} %bitcast.20, bf16[192,128]{1,0:T(8,128)(2,1)S(1)} %collective-permute-done.4.queries_other, ...), custom_call_target="tpu_custom_call" | custom-call | flops 150994944 | bytes 2359296 | tf_op jit(solution)/shard_map/pallas_call | solution.py:345
  24.9 0.7 %shard_map.93.refs_4_ = f32[136,384]{1,0:T(8,128)S(1)} custom-call(bf16[384,128]{1,0:T(8,128)(2,1)S(1)} %get-tuple-element.52.both_queries, bf16[3,2,192,128]{3,2,1,0:T(8,128)(2,1)S(1)} %pad_maximum_fusion.refs_0_), custom_call_target="tpu_custom_call" | custom-call | flops 113246208 | bytes 393216 | tf_op jit(solution)/shard_map/pallas_call | solution.py:459
  25.6 0.9 %collective-permute-done.5.refs_1_.refs_2_ = bf16[2,2,192,128]{3,2,1,0:T(8,128)(2,1)S(1)} collective-permute-done((bf16[2,2,192,128]{3,2,1,0:T(8,128)(2,1)S(1)}, bf16[2,2,192,128]{3,2,1,0:T(8,128)(2,1)S(1)}, u32[]{:S(2)}, u32[]{:S(2)}) %collective-permute-start.5) | collective-permute-done | bytes 196640 | tf_op jit(solution)/shard_map/ppermute | solution.py:414
  26.5 0.0 collective-permute-done.7.refs_3_.refs_4_
  26.5 0.0 collective-permute-done.6.refs_2_.refs_3_
  26.5 0.7 %collective-permute-start.9 = (bf16[192,1664]{1,0:T(8,128)(2,1)S(1)}, bf16[192,1664]{1,0:T(8,128)(2,1)S(1)}, u32[]{:S(2)}, u32[]{:S(2)}) collective-permute-start(bf16[192,1664]{1,0:T(8,128)(2,1)S(1)} %get-tuple-element.62), channel_id=1, source_target_pairs={{0,8},{8,0},{16,24},{24,16},{1,9},{9,1},{17,25},{25,17},{2,10},{10... | collective-permute-start | bytes 1916936 | tf_op jit(solution)/shard_map/ppermute | solution.py:106
  27.3 1.2 %shard_map.94.mine = f32[136,384]{1,0:T(8,128)S(1)} custom-call(bf16[384,128]{1,0:T(8,128)(2,1)S(1)} %get-tuple-element.52.both_queries, bf16[1,2,192,128]{3,2,1,0:T(8,128)(2,1)S(1)} %collective-permute-done.3.refs_0_.refs_1_, bf16[2,2,192,128]{3,2,1,0:T(8,128)(2,1)S(1)} %collective-permute-done.5.refs_1_.refs_2_, ...), custom_call_target="tpu_custom_call" | custom-call | flops 226492416 | bytes 786432 | tf_op jit(solution)/shard_map/pallas_call | solution.py:459
  28.5 0.1 collective-permute-start.8
  28.5 1.4 %collective-permute-done.8.theirs = f32[136,384]{1,0:T(8,128)S(1)} collective-permute-done((f32[136,384]{1,0:T(8,128)S(1)}, f32[136,384]{1,0:T(8,128)S(1)}, u32[]{:S(2)}, u32[]{:S(2)}) %collective-permute-start.8) | collective-permute-done | bytes 208928 | tf_op jit(solution)/shard_map/ppermute | solution.py:106
  30.0 0.0 collective-permute-done.9.payload
  30.0 1.1 %shard_map.95 = (f32[8,384]{1,0:T(8,128)S(1)}, bf16[192,128]{1,0:T(8,128)(2,1)S(1)}, bf16[32,1536]{1,0:T(8,128)(2,1)S(1)}, bf16[32,1536]{1,0:T(8,128)(2,1)S(1)},...) custom-call(s32[3]{0:T(128)S(1)} %pad_add_fusion.place, f32[136,384]{1,0:T(8,128)S(1)} %shard_map.94.mine, ...), custom_call_target="tpu_custom_call" | custom-call | flops 150994944 | bytes 2359296 | tf_op jit(solution)/shard_map/pallas_call | solution.py:345
  31.1 1.6 %collective-permute-start.10 = (bf16[32,1536]{1,0:T(8,128)(2,1)S(1)}, bf16[32,1536]{1,0:T(8,128)(2,1)S(1)}, u32[]{:S(2)}, u32[]{:S(2)}) collective-permute-start(bf16[32,1536]{1,0:T(8,128)(2,1)S(1)} %get-tuple-element.73), channel_id=1, source_target_pairs={{0,1},{1,0},{8,9},{9,8},{16,17},{17,16},{24,25},{25,24},{2,3},{3,2... | collective-permute-start | bytes 294920 | tf_op jit(solution)/shard_map/ppermute | solution.py:106
  32.7 0.2 collective-permute-start.11
  32.9 1.8 %collective-permute-start.12 = (bf16[32,1536]{1,0:T(8,128)(2,1)S(1)}, bf16[32,1536]{1,0:T(8,128)(2,1)S(1)}, u32[]{:S(2)}, u32[]{:S(2)}) collective-permute-start(bf16[32,1536]{1,0:T(8,128)(2,1)S(1)} %get-tuple-element.75), channel_id=1, source_target_pairs={{0,17},{1,16},{8,25},{9,24},{16,1},{17,0},{24,9},{25,8},{2,19},{3,... | collective-permute-start | bytes 294920 | tf_op jit(solution)/shard_map/ppermute | solution.py:106
  34.7 2.7 %shard_map.96 = (f32[3,2,192,128]{3,2,1,0:T(8,128)S(1)}, bf16[3,2,192,128]{3,2,1,0:T(8,128)(2,1)S(1)}, bf16[3,2,192,128]{3,2,1,0:T(8,128)(2,1)S(1)}, f32[192,128]{1,0:T(8,128)S(1)}, bf16[16,1536]{1,0:T(8,128)(2,1)S(1)}) custom-call(s32[3]{0:T(128)S(1)} %pad_add_fusion.place, f32[8,384]{1,0:T(8,128)S(1)} %get-tuple-element.66.stats, ...), custom_call_target="tpu_custom_call" | custom-call | flops 849346560 | bytes 2359296 | tf_op jit(solution)/shard_map/pallas_call | solution.py:345
  37.4 0.0 collective-permute-done.10
  37.4 0.9 %collective-permute-done.11 = bf16[32,1536]{1,0:T(8,128)(2,1)S(1)} collective-permute-done((bf16[32,1536]{1,0:T(8,128)(2,1)S(1)}, bf16[32,1536]{1,0:T(8,128)(2,1)S(1)}, u32[]{:S(2)}, u32[]{:S(2)}) %collective-permute-start.11) | collective-permute-done | bytes 98336 | tf_op jit(solution)/shard_map/ppermute | solution.py:106
  38.3 1.0 %collective-permute-done.12 = bf16[32,1536]{1,0:T(8,128)(2,1)S(1)} collective-permute-done((bf16[32,1536]{1,0:T(8,128)(2,1)S(1)}, bf16[32,1536]{1,0:T(8,128)(2,1)S(1)}, u32[]{:S(2)}, u32[]{:S(2)}) %collective-permute-start.12) | collective-permute-done | bytes 98336 | tf_op jit(solution)/shard_map/ppermute | solution.py:106
  39.3 0.1 add_convert_fusion.2
  39.4 0.1 collective-permute-start.13
  39.5 3.2 %collective-permute-start.21 = (bf16[3,2,192,128]{3,2,1,0:T(8,128)(2,1)S(1)}, bf16[3,2,192,128]{3,2,1,0:T(8,128)(2,1)S(1)}, u32[]{:S(2)}, u32[]{:S(2)}) collective-permute-start(bf16[3,2,192,128]{3,2,1,0:T(8,128)(2,1)S(1)} %get-tuple-element.89), channel_id=1, source_target_pairs={{1,16},{0,17},{25,8},{24,9},{3,18},{2,19},{27,10},{26,11},{5,20},{... | collective-permute-start | bytes 884744 | tf_op jit(solution)/shard_map/ppermute | solution.py:527
  42.7 0.7 %collective-permute-start.20 = (bf16[3,2,192,128]{3,2,1,0:T(8,128)(2,1)S(1)}, bf16[3,2,192,128]{3,2,1,0:T(8,128)(2,1)S(1)}, u32[]{:S(2)}, u32[]{:S(2)}) collective-permute-start(bf16[3,2,192,128]{3,2,1,0:T(8,128)(2,1)S(1)} %get-tuple-element.89), channel_id=1, source_target_pairs={{8,16},{16,8},{9,17},{17,9},{10,18},{18,10},{11,19},{19,11},{12,20... | collective-permute-start | bytes 884744 | tf_op jit(solution)/shard_map/ppermute | solution.py:526
  43.4 1.2 %collective-permute-start.19 = (bf16[3,2,192,128]{3,2,1,0:T(8,128)(2,1)S(1)}, bf16[3,2,192,128]{3,2,1,0:T(8,128)(2,1)S(1)}, u32[]{:S(2)}, u32[]{:S(2)}) collective-permute-start(bf16[3,2,192,128]{3,2,1,0:T(8,128)(2,1)S(1)} %get-tuple-element.88), channel_id=1, source_target_pairs={{0,1},{1,0},{2,3},{3,2},{4,5},{5,4},{6,7},{7,6},{8,9},{9,8},{10,11... | collective-permute-start | bytes 884744 | tf_op jit(solution)/shard_map/ppermute | solution.py:525
  44.6 0.0 collective-permute-done.13
  44.6 1.7 %collective-permute-start.14 = (bf16[32,1536]{1,0:T(8,128)(2,1)S(1)}, bf16[32,1536]{1,0:T(8,128)(2,1)S(1)}, u32[]{:S(2)}, u32[]{:S(2)}) collective-permute-start(bf16[32,1536]{1,0:T(8,128)(2,1)S(1)} %add_convert_fusion.1), channel_id=1, source_target_pairs={{0,4},{2,6},{4,0},{6,2},{1,5},{3,7},{5,1},{7,3},{8,12},{10,14},{12... | collective-permute-start | bytes 294920 | tf_op jit(solution)/shard_map/ppermute | solution.py:106
  46.3 1.5 %convolution_convert_fusion = bf16[192,3072]{1,0:T(8,128)(2,1)} fusion(bf16[192,128]{1,0:T(8,128)(2,1)S(1)} %get-tuple-element.78, bf16[128,3072]{1,0:T(8,128)(2,1)S(1)} %copy-done), kind=kOutput, calls=%fused_computation | convolution fusion | flops 151584768 | bytes 2015232 | tf_op jit(solution)/shard_map/dot_general | solution.py:518
  47.8 4.6 %collective-permute-done.14 = bf16[32,1536]{1,0:T(8,128)(2,1)S(1)} collective-permute-done((bf16[32,1536]{1,0:T(8,128)(2,1)S(1)}, bf16[32,1536]{1,0:T(8,128)(2,1)S(1)}, u32[]{:S(2)}, u32[]{:S(2)}) %collective-permute-start.14) | collective-permute-done | bytes 98336 | tf_op jit(solution)/shard_map/ppermute | solution.py:106
  52.3 0.3 collective-permute-start.17
  52.7 2.3 %collective-permute-start.16 = (bf16[32,1536]{1,0:T(8,128)(2,1)S(1)}, bf16[32,1536]{1,0:T(8,128)(2,1)S(1)}, u32[]{:S(2)}, u32[]{:S(2)}) collective-permute-start(bf16[32,1536]{1,0:T(8,128)(2,1)S(1)} %add_convert_fusion.refs_0_), channel_id=1, source_target_pairs={{0,16},{1,17},{8,24},{9,25},{16,0},{17,1},{24,8},{25,9},{2,18},{3,... | collective-permute-start | bytes 294920 | tf_op jit(solution)/shard_map/ppermute | solution.py:106
  54.9 0.0 collective-permute-done.19.refs_0_
  55.0 0.9 %collective-permute-start.15 = (bf16[32,1536]{1,0:T(8,128)(2,1)S(1)}, bf16[32,1536]{1,0:T(8,128)(2,1)S(1)}, u32[]{:S(2)}, u32[]{:S(2)}) collective-permute-start(bf16[32,1536]{1,0:T(8,128)(2,1)S(1)} %add_convert_fusion.refs_0_), channel_id=1, source_target_pairs={{0,1},{1,0},{8,9},{9,8},{16,17},{17,16},{24,25},{25,24},{2,3},{3,2... | collective-permute-start | bytes 294920 | tf_op jit(solution)/shard_map/ppermute | solution.py:106
  55.9 0.0 collective-permute-done.21.refs_2_
  55.9 0.0 collective-permute-done.20.refs_1_
  55.9 0.1 shard_map.100
  56.0 3.3 %collective-permute-start.24 = (bf16[2,192,128]{2,1,0:T(8,128)(2,1)S(1)}, bf16[2,192,128]{2,1,0:T(8,128)(2,1)S(1)}, u32[]{:S(2)}, u32[]{:S(2)}) collective-permute-start(bf16[2,192,128]{2,1,0:T(8,128)(2,1)S(1)} %get-tuple-element.93), channel_id=1, source_target_pairs={{6,2},{0,4},{7,3},{1,5},{14,10},{8,12},{15,11},{9,13},{22,18},{16,... | collective-permute-start | bytes 294920 | tf_op jit(solution)/shard_map/ppermute | solution.py:87
  59.3 0.7 %collective-permute-start.23 = (bf16[2,192,128]{2,1,0:T(8,128)(2,1)S(1)}, bf16[2,192,128]{2,1,0:T(8,128)(2,1)S(1)}, u32[]{:S(2)}, u32[]{:S(2)}) collective-permute-start(bf16[2,192,128]{2,1,0:T(8,128)(2,1)S(1)} %get-tuple-element.93), channel_id=1, source_target_pairs={{4,2},{2,4},{5,3},{3,5},{12,10},{10,12},{13,11},{11,13},{20,18},{1... | collective-permute-start | bytes 294920 | tf_op jit(solution)/shard_map/ppermute | solution.py:87
  60.0 0.0 collective-permute-done.17.refs_3_
  60.0 1.3 %collective-permute-start.22 = (bf16[2,192,128]{2,1,0:T(8,128)(2,1)S(1)}, bf16[2,192,128]{2,1,0:T(8,128)(2,1)S(1)}, u32[]{:S(2)}, u32[]{:S(2)}) collective-permute-start(bf16[2,192,128]{2,1,0:T(8,128)(2,1)S(1)} %get-tuple-element.92), channel_id=1, source_target_pairs={{0,2},{2,0},{4,6},{6,4},{1,3},{3,1},{5,7},{7,5},{8,10},{10,8},{12,... | collective-permute-start | bytes 294920 | tf_op jit(solution)/shard_map/ppermute | solution.py:87
  61.3 0.0 collective-permute-done.16.refs_2_
  61.3 0.0 collective-permute-done.15.refs_1_
  61.3 0.1 collective-permute-start.18
  61.4 1.5 %shard_map.98.refs_1_ = f32[128,3072]{1,0:T(8,128)} custom-call(s32[3]{0:T(128)S(1)} %pad_add_fusion.place, bf16[144,1536]{1,0:T(8,128)(2,1)S(1)} %shard_map.97.part), custom_call_target="tpu_custom_call" | custom-call | flops 10000000000 | bytes 100000000 | tf_op jit(solution)/shard_map/pallas_call | solution.py:303
  62.9 0.3 collective-permute-done.18.part
  63.2 1.5 %shard_map.99 = (f32[128,3072]{1,0:T(8,128)}, bf16[192,128]{1,0:T(8,128)(2,1)}) custom-call(s32[3]{0:T(128)S(1)} %pad_add_fusion.place, bf16[144,1536]{1,0:T(8,128)(2,1)S(1)} %collective-permute-done.18.part, f32[192,128]{1,0:T(8,128)S(1)} %get-tuple-element.84.refs_0_, f32[128,3072]{1,0:T(8,128)} %shard_map.98.refs_1_), custom_call_target="tpu_custom_call", output_to_operand_aliasing={{0}: (3, {})} | custom-call | flops 10000000000 | bytes 100000000 | tf_op jit(solution)/shard_map/pallas_call | solution.py:303
  64.7 0.0 collective-permute-done.22.refs_0_
  64.7 0.0 collective-permute-done.24.refs_2_
  64.7 0.0 collective-permute-done.23.refs_1_
  64.7 0.7 %shard_map.101 = (bf16[192,128]{1,0:T(8,128)(2,1)}, bf16[192,128]{1,0:T(8,128)(2,1)}) custom-call(f32[2,192,128]{2,1,0:T(8,128)S(1)} %get-tuple-element.91.own_grad, bf16[2,192,128]{2,1,0:T(8,128)(2,1)S(1)} %collective-permute-done.22.refs_0_, bf16[2,192,128]{2,1,0:T(8,128)(2,1)S(1)} %collective-permute-done.23.refs_1_, ...), custom_call_target="tpu_custom_call" | custom-call | flops 10000000000 | bytes 100000000 | tf_op jit(solution)/shard_map/pallas_call | solution.py:564
  (11 shorter events, 0.2 us)
Async XLA Ops:
  0.6 17.4 %copy-start.2 = (bf16[4,6,8,128]{3,2,1,0:T(8,128)(2,1)S(1)}, bf16[4,6,8,128]{3,2,1,0:T(8,128)(2,1)}, u32[]{:S(2)}) copy-start(bf16[4,6,8,128]{3,2,1,0:T(8,128)(2,1)} %param.5) | copy-start | bytes 147460
  0.6 21.9 %copy-start = (bf16[128,3072]{1,0:T(8,128)(2,1)S(1)}, bf16[128,3072]{1,0:T(8,128)(2,1)}, u32[]{:S(2)}) copy-start(bf16[128,3072]{1,0:T(8,128)(2,1)} %weight.1) | copy-start | bytes 2359300
  1.6 9.8 %collective-permute-start.2 = (bf16[2,192,128]{2,1,0:T(8,128)(2,1)S(1)}, bf16[2,192,128]{2,1,0:T(8,128)(2,1)S(1)}, u32[]{:S(2)}, u32[]{:S(2)}) collective-permute-start(bf16[2,192,128]{2,1,0:T(8,128)(2,1)S(1)} %get-tuple-element.98), channel_id=1, source_target_pairs={{2,4},{4,2},{3,5},{5,3},{10,12},{12,10},{11,13},{13,11},{18,20},{2... | collective-permute-start | bytes 294920 | tf_op jit(solution)/shard_map/ppermute | solution.py:65
  2.2 10.5 %collective-permute-start.1 = (bf16[2,192,128]{2,1,0:T(8,128)(2,1)S(1)}, bf16[2,192,128]{2,1,0:T(8,128)(2,1)S(1)}, u32[]{:S(2)}, u32[]{:S(2)}) collective-permute-start(bf16[2,192,128]{2,1,0:T(8,128)(2,1)S(1)} %get-tuple-element.98), channel_id=1, source_target_pairs={{2,6},{4,0},{3,7},{5,1},{10,14},{12,8},{11,15},{13,9},{18,22},{20,... | collective-permute-start | bytes 294920 | tf_op jit(solution)/shard_map/ppermute | solution.py:65
  3.5 10.6 %collective-permute-start = (bf16[2,192,128]{2,1,0:T(8,128)(2,1)S(1)}, bf16[2,192,128]{2,1,0:T(8,128)(2,1)S(1)}, u32[]{:S(2)}, u32[]{:S(2)}) collective-permute-start(bf16[2,192,128]{2,1,0:T(8,128)(2,1)S(1)} %get-tuple-element.98), channel_id=1, source_target_pairs={{2,0},{0,2},{6,4},{4,6},{3,1},{1,3},{7,5},{5,7},{10,8},{8,10},{14,... | collective-permute-start | bytes 294920 | tf_op jit(solution)/shard_map/ppermute | solution.py:65
  9.8 4.6 %collective-permute-start.3 = (bf16[1,2,192,128]{3,2,1,0:T(8,128)(2,1)S(1)}, bf16[1,2,192,128]{3,2,1,0:T(8,128)(2,1)S(1)}, u32[]{:S(2)}, u32[]{:S(2)}) collective-permute-start(bf16[1,2,192,128]{3,2,1,0:T(8,128)(2,1)S(1)} %get-tuple-element.97), channel_id=1, source_target_pairs={{0,1},{1,0},{2,3},{3,2},{4,5},{5,4},{6,7},{7,6},{8,9},{9,8},{10,11... | collective-permute-start | bytes 294920 | tf_op jit(solution)/shard_map/ppermute | solution.py:408
  14.5 12.1 %collective-permute-start.7 = (bf16[3,2,192,128]{3,2,1,0:T(8,128)(2,1)S(1)}, bf16[3,2,192,128]{3,2,1,0:T(8,128)(2,1)S(1)}, u32[]{:S(2)}, u32[]{:S(2)}) collective-permute-start(bf16[3,2,192,128]{3,2,1,0:T(8,128)(2,1)S(1)} %pad_maximum_fusion.refs_0_), channel_id=1, source_target_pairs={{16,1},{17,0},{8,25},{9,24},{18,3},{19,2},{10,27},{11,26},{20,5},{... | collective-permute-start | bytes 884744 | tf_op jit(solution)/shard_map/ppermute | solution.py:417
  15.7 10.8 %collective-permute-start.6 = (bf16[3,2,192,128]{3,2,1,0:T(8,128)(2,1)S(1)}, bf16[3,2,192,128]{3,2,1,0:T(8,128)(2,1)S(1)}, u32[]{:S(2)}, u32[]{:S(2)}) collective-permute-start(bf16[3,2,192,128]{3,2,1,0:T(8,128)(2,1)S(1)} %pad_maximum_fusion.refs_0_), channel_id=1, source_target_pairs={{16,8},{8,16},{17,9},{9,17},{18,10},{10,18},{19,11},{11,19},{20,12... | collective-permute-start | bytes 884744 | tf_op jit(solution)/shard_map/ppermute | solution.py:416
  16.4 10.1 %collective-permute-start.5 = (bf16[2,2,192,128]{3,2,1,0:T(8,128)(2,1)S(1)}, bf16[2,2,192,128]{3,2,1,0:T(8,128)(2,1)S(1)}, u32[]{:S(2)}, u32[]{:S(2)}) collective-permute-start(bf16[2,2,192,128]{3,2,1,0:T(8,128)(2,1)S(1)} %pad_maximum_fusion.1), channel_id=1, source_target_pairs={{0,1},{1,0},{2,3},{3,2},{4,5},{5,4},{6,7},{7,6},{8,9},{9,8},{10,11... | collective-permute-start | bytes 589832 | tf_op jit(solution)/shard_map/ppermute | solution.py:414
  18.0 4.5 %collective-permute-start.4 = (bf16[192,128]{1,0:T(8,128)(2,1)S(1)}, bf16[192,128]{1,0:T(8,128)(2,1)S(1)}, u32[]{:S(2)}, u32[]{:S(2)}) collective-permute-start(bf16[192,128]{1,0:T(8,128)(2,1)S(1)} %bitcast.19), channel_id=1, source_target_pairs={{0,8},{8,0},{16,24},{24,16},{1,9},{9,1},{17,25},{25,17},{2,10},{10... | collective-permute-start | bytes 147464 | tf_op jit(solution)/shard_map/ppermute | solution.py:106
  22.6 1.3 %copy-start.1 = (bf16[4,6,8,3072]{3,2,1,0:T(8,128)(2,1)S(1)}, bf16[4,6,8,3072]{3,2,1,0:T(8,128)(2,1)}, u32[]{:S(2)}) copy-start(bf16[4,6,8,3072]{3,2,1,0:T(8,128)(2,1)} %param.9) | copy-start | bytes 3538948
  26.5 3.4 %collective-permute-start.9 = (bf16[192,1664]{1,0:T(8,128)(2,1)S(1)}, bf16[192,1664]{1,0:T(8,128)(2,1)S(1)}, u32[]{:S(2)}, u32[]{:S(2)}) collective-permute-start(bf16[192,1664]{1,0:T(8,128)(2,1)S(1)} %get-tuple-element.62), channel_id=1, source_target_pairs={{0,8},{8,0},{16,24},{24,16},{1,9},{9,1},{17,25},{25,17},{2,10},{10... | collective-permute-start | bytes 1916936 | tf_op jit(solution)/shard_map/ppermute | solution.py:106
  28.5 1.5 %collective-permute-start.8 = (f32[136,384]{1,0:T(8,128)S(1)}, f32[136,384]{1,0:T(8,128)S(1)}, u32[]{:S(2)}, u32[]{:S(2)}) collective-permute-start(f32[136,384]{1,0:T(8,128)S(1)} %shard_map.94.mine), channel_id=1, source_target_pairs={{0,8},{8,0},{16,24},{24,16},{1,9},{9,1},{17,25},{25,17},{2,10},{10... | collective-permute-start | bytes 626696 | tf_op jit(solution)/shard_map/ppermute | solution.py:106
  31.1 6.3 %collective-permute-start.10 = (bf16[32,1536]{1,0:T(8,128)(2,1)S(1)}, bf16[32,1536]{1,0:T(8,128)(2,1)S(1)}, u32[]{:S(2)}, u32[]{:S(2)}) collective-permute-start(bf16[32,1536]{1,0:T(8,128)(2,1)S(1)} %get-tuple-element.73), channel_id=1, source_target_pairs={{0,1},{1,0},{8,9},{9,8},{16,17},{17,16},{24,25},{25,24},{2,3},{3,2... | collective-permute-start | bytes 294920 | tf_op jit(solution)/shard_map/ppermute | solution.py:106
  32.7 5.6 %collective-permute-start.11 = (bf16[32,1536]{1,0:T(8,128)(2,1)S(1)}, bf16[32,1536]{1,0:T(8,128)(2,1)S(1)}, u32[]{:S(2)}, u32[]{:S(2)}) collective-permute-start(bf16[32,1536]{1,0:T(8,128)(2,1)S(1)} %get-tuple-element.74), channel_id=1, source_target_pairs={{0,16},{1,17},{8,24},{9,25},{16,0},{17,1},{24,8},{25,9},{2,18},{3,... | collective-permute-start | bytes 294920 | tf_op jit(solution)/shard_map/ppermute | solution.py:106
  32.9 6.4 %collective-permute-start.12 = (bf16[32,1536]{1,0:T(8,128)(2,1)S(1)}, bf16[32,1536]{1,0:T(8,128)(2,1)S(1)}, u32[]{:S(2)}, u32[]{:S(2)}) collective-permute-start(bf16[32,1536]{1,0:T(8,128)(2,1)S(1)} %get-tuple-element.75), channel_id=1, source_target_pairs={{0,17},{1,16},{8,25},{9,24},{16,1},{17,0},{24,9},{25,8},{2,19},{3,... | collective-permute-start | bytes 294920 | tf_op jit(solution)/shard_map/ppermute | solution.py:106
  39.4 5.2 %collective-permute-start.13 = (bf16[32,1536]{1,0:T(8,128)(2,1)S(1)}, bf16[32,1536]{1,0:T(8,128)(2,1)S(1)}, u32[]{:S(2)}, u32[]{:S(2)}) collective-permute-start(bf16[32,1536]{1,0:T(8,128)(2,1)S(1)} %add_convert_fusion.2), channel_id=1, source_target_pairs={{0,2},{2,0},{4,6},{6,4},{1,3},{3,1},{5,7},{7,5},{8,10},{10,8},{12,... | collective-permute-start | bytes 294920 | tf_op jit(solution)/shard_map/ppermute | solution.py:106
  39.5 16.4 %collective-permute-start.21 = (bf16[3,2,192,128]{3,2,1,0:T(8,128)(2,1)S(1)}, bf16[3,2,192,128]{3,2,1,0:T(8,128)(2,1)S(1)}, u32[]{:S(2)}, u32[]{:S(2)}) collective-permute-start(bf16[3,2,192,128]{3,2,1,0:T(8,128)(2,1)S(1)} %get-tuple-element.89), channel_id=1, source_target_pairs={{1,16},{0,17},{25,8},{24,9},{3,18},{2,19},{27,10},{26,11},{5,20},{... | collective-permute-start | bytes 884744 | tf_op jit(solution)/shard_map/ppermute | solution.py:527
  42.7 13.2 %collective-permute-start.20 = (bf16[3,2,192,128]{3,2,1,0:T(8,128)(2,1)S(1)}, bf16[3,2,192,128]{3,2,1,0:T(8,128)(2,1)S(1)}, u32[]{:S(2)}, u32[]{:S(2)}) collective-permute-start(bf16[3,2,192,128]{3,2,1,0:T(8,128)(2,1)S(1)} %get-tuple-element.89), channel_id=1, source_target_pairs={{8,16},{16,8},{9,17},{17,9},{10,18},{18,10},{11,19},{19,11},{12,20... | collective-permute-start | bytes 884744 | tf_op jit(solution)/shard_map/ppermute | solution.py:526
  43.4 11.6 %collective-permute-start.19 = (bf16[3,2,192,128]{3,2,1,0:T(8,128)(2,1)S(1)}, bf16[3,2,192,128]{3,2,1,0:T(8,128)(2,1)S(1)}, u32[]{:S(2)}, u32[]{:S(2)}) collective-permute-start(bf16[3,2,192,128]{3,2,1,0:T(8,128)(2,1)S(1)} %get-tuple-element.88), channel_id=1, source_target_pairs={{0,1},{1,0},{2,3},{3,2},{4,5},{5,4},{6,7},{7,6},{8,9},{9,8},{10,11... | collective-permute-start | bytes 884744 | tf_op jit(solution)/shard_map/ppermute | solution.py:525
  44.6 7.7 %collective-permute-start.14 = (bf16[32,1536]{1,0:T(8,128)(2,1)S(1)}, bf16[32,1536]{1,0:T(8,128)(2,1)S(1)}, u32[]{:S(2)}, u32[]{:S(2)}) collective-permute-start(bf16[32,1536]{1,0:T(8,128)(2,1)S(1)} %add_convert_fusion.1), channel_id=1, source_target_pairs={{0,4},{2,6},{4,0},{6,2},{1,5},{3,7},{5,1},{7,3},{8,12},{10,14},{12... | collective-permute-start | bytes 294920 | tf_op jit(solution)/shard_map/ppermute | solution.py:106
  52.3 7.7 %collective-permute-start.17 = (bf16[32,1536]{1,0:T(8,128)(2,1)S(1)}, bf16[32,1536]{1,0:T(8,128)(2,1)S(1)}, u32[]{:S(2)}, u32[]{:S(2)}) collective-permute-start(bf16[32,1536]{1,0:T(8,128)(2,1)S(1)} %add_convert_fusion.refs_0_), channel_id=1, source_target_pairs={{0,17},{1,16},{8,25},{9,24},{16,1},{17,0},{24,9},{25,8},{2,19},{3,... | collective-permute-start | bytes 294920 | tf_op jit(solution)/shard_map/ppermute | solution.py:106
  52.7 8.6 %collective-permute-start.16 = (bf16[32,1536]{1,0:T(8,128)(2,1)S(1)}, bf16[32,1536]{1,0:T(8,128)(2,1)S(1)}, u32[]{:S(2)}, u32[]{:S(2)}) collective-permute-start(bf16[32,1536]{1,0:T(8,128)(2,1)S(1)} %add_convert_fusion.refs_0_), channel_id=1, source_target_pairs={{0,16},{1,17},{8,24},{9,25},{16,0},{17,1},{24,8},{25,9},{2,18},{3,... | collective-permute-start | bytes 294920 | tf_op jit(solution)/shard_map/ppermute | solution.py:106
  55.0 6.3 %collective-permute-start.15 = (bf16[32,1536]{1,0:T(8,128)(2,1)S(1)}, bf16[32,1536]{1,0:T(8,128)(2,1)S(1)}, u32[]{:S(2)}, u32[]{:S(2)}) collective-permute-start(bf16[32,1536]{1,0:T(8,128)(2,1)S(1)} %add_convert_fusion.refs_0_), channel_id=1, source_target_pairs={{0,1},{1,0},{8,9},{9,8},{16,17},{17,16},{24,25},{25,24},{2,3},{3,2... | collective-permute-start | bytes 294920 | tf_op jit(solution)/shard_map/ppermute | solution.py:106
  56.0 8.7 %collective-permute-start.24 = (bf16[2,192,128]{2,1,0:T(8,128)(2,1)S(1)}, bf16[2,192,128]{2,1,0:T(8,128)(2,1)S(1)}, u32[]{:S(2)}, u32[]{:S(2)}) collective-permute-start(bf16[2,192,128]{2,1,0:T(8,128)(2,1)S(1)} %get-tuple-element.93), channel_id=1, source_target_pairs={{6,2},{0,4},{7,3},{1,5},{14,10},{8,12},{15,11},{9,13},{22,18},{16,... | collective-permute-start | bytes 294920 | tf_op jit(solution)/shard_map/ppermute | solution.py:87
  59.3 5.4 %collective-permute-start.23 = (bf16[2,192,128]{2,1,0:T(8,128)(2,1)S(1)}, bf16[2,192,128]{2,1,0:T(8,128)(2,1)S(1)}, u32[]{:S(2)}, u32[]{:S(2)}) collective-permute-start(bf16[2,192,128]{2,1,0:T(8,128)(2,1)S(1)} %get-tuple-element.93), channel_id=1, source_target_pairs={{4,2},{2,4},{5,3},{3,5},{12,10},{10,12},{13,11},{11,13},{20,18},{1... | collective-permute-start | bytes 294920 | tf_op jit(solution)/shard_map/ppermute | solution.py:87
  60.0 4.7 %collective-permute-start.22 = (bf16[2,192,128]{2,1,0:T(8,128)(2,1)S(1)}, bf16[2,192,128]{2,1,0:T(8,128)(2,1)S(1)}, u32[]{:S(2)}, u32[]{:S(2)}) collective-permute-start(bf16[2,192,128]{2,1,0:T(8,128)(2,1)S(1)} %get-tuple-element.92), channel_id=1, source_target_pairs={{0,2},{2,0},{4,6},{6,4},{1,3},{3,1},{5,7},{7,5},{8,10},{10,8},{12,... | collective-permute-start | bytes 294920 | tf_op jit(solution)/shard_map/ppermute | solution.py:87
  61.3 1.9 %collective-permute-start.18 = (bf16[144,1536]{1,0:T(8,128)(2,1)S(1)}, bf16[144,1536]{1,0:T(8,128)(2,1)S(1)}, u32[]{:S(2)}, u32[]{:S(2)}) collective-permute-start(bf16[144,1536]{1,0:T(8,128)(2,1)S(1)} %shard_map.97.part), channel_id=1, source_target_pairs={{0,8},{8,0},{16,24},{24,16},{1,9},{9,1},{17,25},{25,17},{2,10},{10... | collective-permute-start | bytes 1327112 | tf_op jit(solution)/shard_map/ppermute | solution.py:106

commit v9 on v8

--- a/solution.py
+++ b/solution.py
@@ -223,18 +223,20 @@
 
 
 def backward_kernel(
-    inv_root, layout, targets, place, stats, both_queries, payload, grad_rows, *refs
+    inv_root, layout, targets, carried, last, place, stats, both_queries, payload, grad_rows, *refs
 ):
     groups, rest = split_groups(layout, refs)
+    given, rest = (rest[0], rest[1:]) if carried else (None, rest)
     count = 1 + max(out for out, _ in targets)
-    outs, (query_own, query_other, both_grads, both_out) = rest[:count], rest[count:]
+    outs, rest = rest[:count], rest[count:]
+    both_grads = rest[-2] if last else rest[-1]
     tile, dim = grad_rows.shape
     columns = payload.shape[1]
     both_tiles(place, grad_rows[...], payload[:, columns - dim :], both_grads)
     query_rows, out_grads = both_queries[...], both_grads[...]
     level, row_dot = stats[0:1, :], stats[1:2, :]
     along = (((1,), (1,)), ((), ()))
-    query_grad = jnp.zeros((dim, 2 * tile), jnp.float32)
+    query_grad = given[...] if carried else jnp.zeros((dim, 2 * tile), jnp.float32)
     for group, (target, first) in zip(groups, targets):
         out, tiles = outs[target], group[0].shape[0]
         keys, values = rows_of(group, 0), rows_of(group, 1)
@@ -252,6 +254,10 @@
         query_grad = query_grad + lax.dot_general(
             keys, score_grad, (((0,), (0,)), ((), ())), preferred_element_type=jnp.float32
         )
+    if not last:
+        rest[0][...] = query_grad
+        return
+    query_own, query_other, both_out = rest[0], rest[1], rest[-1]
     both_out[...] = query_grad.T * inv_root
     query_own[...] = both_out[pl.ds(pl.multiple_of(place[0] * tile, tile), tile), :]
     other = both_out[pl.ds(pl.multiple_of((1 - place[0]) * tile, tile), tile), :]
@@ -413,8 +419,8 @@
         )
         others_beside = lax.ppermute(others, "width", swap)
         far = [
+            lax.ppermute(column, ("frame", "width"), cross),
             lax.ppermute(column, "frame", [(2, 1), (1, 2)]),
-            lax.ppermute(column, ("frame", "width"), cross),
         ]
         blocks = [column, own_beside, others_beside, *far]
         layout = (1, 1, 1, 2)
@@ -489,24 +495,40 @@
         cost=cost_of(4 * tile * head_dim * half, 4 * tile * model_dim),
     )
     stats, attended, *terms = merged
-    back = kernel_call(
-        functools.partial(backward_kernel, inv_root, layout, targets),
-        (place, stats, both_queries, payload, grad_rows, *blocks),
-        (
-            shaped(*grad_shapes[0], kind=jnp.float32),
-            *[shaped(*shape) for shape in grad_shapes[1:]],
-            shaped(tile, head_dim, kind=jnp.float32),
-            shaped(tile * head_dim // half, half),
-        ),
-        scratch=(
-            pltpu.VMEM((2 * tile, head_dim), jnp.bfloat16),
-            pltpu.VMEM((2 * tile, head_dim), jnp.float32),
-        ),
-        cost=cost_of(5 * product, 2 * moved),
+    def backward(operands, groups, places, outs, carried=(), last=False):
+        scratch = [pltpu.VMEM((2 * tile, head_dim), jnp.bfloat16)]
+        if last:
+            scratch.append(pltpu.VMEM((2 * tile, head_dim), jnp.float32))
+            sums = (
+                shaped(tile, head_dim, kind=jnp.float32),
+                shaped(tile * head_dim // half, half),
+            )
+        else:
+            sums = (shaped(head_dim, 2 * tile, kind=jnp.float32),)
+        return kernel_call(
+            functools.partial(backward_kernel, inv_root, groups, places, bool(carried), last),
+            (place, stats, both_queries, payload, grad_rows, *operands, *carried),
+            (*outs, *sums),
+            scratch=scratch,
+            cost=cost_of(10**9 if not last else 10**10, 10**8),
+        )
+
+    near = len(blocks) - len(far)
+    *near_grads, query_grad = backward(
+        blocks[:near],
+        layout[:-1],
+        targets[:-1],
+        (shaped(*grad_shapes[0], kind=jnp.float32), *[shaped(*g) for g in grad_shapes[1:-1]]),
     )
     if small:
-        terms[0], *back = lax.optimization_barrier((terms[0], *back))
+        terms[0], query_grad = lax.optimization_barrier((terms[0], query_grad))
         part = sum_over_plane(terms)
+        part, query_grad = lax.optimization_barrier((part, query_grad))
+    far_grad, query_own, query_other = backward(
+        blocks[near:], layout[-1:], ((0, 0),), (shaped(*grad_shapes[-1]),), (query_grad,), True
+    )
+    back = (*near_grads, far_grad, query_own, query_other)
+    if small:
         other = flip(part, ("height",), (1,))
         part = (part.astype(jnp.float32) + other.astype(jnp.float32)).astype(jnp.bfloat16)
         part, attended = lax.optimization_barrier((part, attended))

time: 65.7 us -> 66.4 us (1.011)
  starting transfers between devices: 37 us -> 34.3 us
  waiting for transfers between devices: 13 us -> 15.7 us
  Pallas kernels: 10.5 us -> 11.3 us
    ppermute x3, starting transfers between devices: 5.21 us -> 2.79 us  [returned(): arrived.append(lax.ppermute(outgoing, axis, [(p, s) for s, p in route]))]
    ppermute x1, waiting for transfers between devices: 0.01 us -> 2.25 us  [body(): lax.ppermute(column, ('frame', 'width'), cross)]
    ppermute x12, starting transfers between devices: 13.4 us -> 12.2 us  [flip(): return lax.ppermute(block, axes, route)]
    ppermute x12, waiting for transfers between devices: 9.02 us -> 10.2 us  [flip(): return lax.ppermute(block, axes, route)]
    ppermute x1, waiting for transfers between devices: 0.95 us -> 0.01 us  [body(): others_beside = lax.ppermute(others, 'width', swap)]
    pallas_call x3 -> x4, Pallas kernels: 4.85 us -> 5.57 us  [kernel_call(): pl.pallas_call(kernel, out_shape=outs, in_specs=[SMEM] + [VMEM] * (len(op...]
  transfers between devices with their start and end apart: 25 -> 25, of which waited for: 10 -> 12; matrix products, arithmetic and copies ran while one was open for 3% -> 3% of each run, Pallas kernels for 13% -> 14%
where the time goes in v9:
time: 66.4 us; the launch traced here: 66 us
  starting transfers between devices  34.3 us (52%)
  waiting for transfers between devices  15.7 us (24%)
  Pallas kernels  11.3 us (17%)
  matrix products  1.47 us (2%)
  local copies, waits for them, and re-layouts  1.28 us (2%)
  other arithmetic  1.17 us (2%)
  between operations  0.88 us (1%)
    ppermute x12, starting transfers between devices, flip(): return lax.ppermute(block, axes, route)  12.2 us
    ppermute x12, waiting for transfers between devices, flip(): return lax.ppermute(block, axes, route)  10.2 us
    ppermute x3, starting transfers between devices, fetch(): arrived = [lax.ppermute(block, axis, route) for route in routes]  8.25 us
    pallas_call x4, Pallas kernels, kernel_call(): pl.pallas_call(kernel, out_shape=outs, in_specs=[SMEM] + [VMEM] * (len(op...  5.57 us
    ppermute x1, starting transfers between devices, body(): lax.ppermute(far_grad, ('frame', 'width'), [(p, s) for s, p in cross])  3.75 us
    pallas_call x2, Pallas kernels, assemble(): pl.pallas_call(functools.partial(assemble_kernel, flipped, rows), out_sha...  2.95 us
    ppermute x3, starting transfers between devices, returned(): arrived.append(lax.ppermute(outgoing, axis, [(p, s) for s, p in route]))  2.79 us
    ppermute x3, waiting for transfers between devices, fetch(): arrived = [lax.ppermute(block, axis, route) for route in routes]  2.79 us
  transfers between devices with their start and end apart: 25, of which 12 were waited for; matrix products, arithmetic and copies ran while one was open for 3% of the time, Pallas kernels for 14%

profile of v9, /device:TPU:0, one launch (start us, length us, event | category | flops | bytes accessed | tf_op | source)
XLA Modules:
  0.0 66.0 jit_solution(572691827047305645)
XLA Ops:
  0.7 0.9 %fusion = (bf16[1,2,192,128]{3,2,1,0:T(8,128)(2,1)S(1)}, bf16[2,192,128]{2,1,0:T(8,128)(2,1)S(1)}) fusion(bf16[1,192,128]{2,1,0:T(8,128)(2,1)} %bitcast.24, bf16[1,192,128]{2,1,0:T(8,128)(2,1)} %bitcast.25), kind=kLoop, calls=%fused_computation.9 | loop fusion | flops 49152 | bytes 294912 | tf_op jit(solution)/shard_map/stack | solution.py:416
  1.6 0.7 %collective-permute-start.2 = (bf16[2,192,128]{2,1,0:T(8,128)(2,1)S(1)}, bf16[2,192,128]{2,1,0:T(8,128)(2,1)S(1)}, u32[]{:S(2)}, u32[]{:S(2)}) collective-permute-start(bf16[2,192,128]{2,1,0:T(8,128)(2,1)S(1)} %get-tuple-element.96), channel_id=1, source_target_pairs={{2,4},{4,2},{3,5},{5,3},{10,12},{12,10},{11,13},{13,11},{18,20},{2... | collective-permute-start | bytes 294920 | tf_op jit(solution)/shard_map/ppermute | solution.py:65
  2.2 1.3 %collective-permute-start.1 = (bf16[2,192,128]{2,1,0:T(8,128)(2,1)S(1)}, bf16[2,192,128]{2,1,0:T(8,128)(2,1)S(1)}, u32[]{:S(2)}, u32[]{:S(2)}) collective-permute-start(bf16[2,192,128]{2,1,0:T(8,128)(2,1)S(1)} %get-tuple-element.96), channel_id=1, source_target_pairs={{2,6},{4,0},{3,7},{5,1},{10,14},{12,8},{11,15},{13,9},{18,22},{20,... | collective-permute-start | bytes 294920 | tf_op jit(solution)/shard_map/ppermute | solution.py:65
  3.5 6.3 %collective-permute-start = (bf16[2,192,128]{2,1,0:T(8,128)(2,1)S(1)}, bf16[2,192,128]{2,1,0:T(8,128)(2,1)S(1)}, u32[]{:S(2)}, u32[]{:S(2)}) collective-permute-start(bf16[2,192,128]{2,1,0:T(8,128)(2,1)S(1)} %get-tuple-element.96), channel_id=1, source_target_pairs={{2,0},{0,2},{6,4},{4,6},{3,1},{1,3},{7,5},{5,7},{10,8},{8,10},{14,... | collective-permute-start | bytes 294920 | tf_op jit(solution)/shard_map/ppermute | solution.py:65
  9.8 1.5 %collective-permute-start.3 = (bf16[1,2,192,128]{3,2,1,0:T(8,128)(2,1)S(1)}, bf16[1,2,192,128]{3,2,1,0:T(8,128)(2,1)S(1)}, u32[]{:S(2)}, u32[]{:S(2)}) collective-permute-start(bf16[1,2,192,128]{3,2,1,0:T(8,128)(2,1)S(1)} %get-tuple-element.95), channel_id=1, source_target_pairs={{0,1},{1,0},{2,3},{3,2},{4,5},{5,4},{6,7},{7,6},{8,9},{9,8},{10,11... | collective-permute-start | bytes 294920 | tf_op jit(solution)/shard_map/ppermute | solution.py:414
  11.4 0.0 collective-permute-done.2
  11.4 1.4 %collective-permute-done.1 = bf16[2,192,128]{2,1,0:T(8,128)(2,1)S(1)} collective-permute-done((bf16[2,192,128]{2,1,0:T(8,128)(2,1)S(1)}, bf16[2,192,128]{2,1,0:T(8,128)(2,1)S(1)}, u32[]{:S(2)}, u32[]{:S(2)}) %collective-permute-start.1) | collective-permute-done | bytes 98336 | tf_op jit(solution)/shard_map/ppermute | solution.py:65
  12.8 1.4 %collective-permute-done = bf16[2,192,128]{2,1,0:T(8,128)(2,1)S(1)} collective-permute-done((bf16[2,192,128]{2,1,0:T(8,128)(2,1)S(1)}, bf16[2,192,128]{2,1,0:T(8,128)(2,1)S(1)}, u32[]{:S(2)}, u32[]{:S(2)}) %collective-permute-start) | collective-permute-done | bytes 98336 | tf_op jit(solution)/shard_map/ppermute | solution.py:65
  14.2 0.2 collective-permute-done.3.refs_0_.refs_1_
  14.5 0.7 %collective-permute-start.7 = (bf16[3,2,192,128]{3,2,1,0:T(8,128)(2,1)S(1)}, bf16[3,2,192,128]{3,2,1,0:T(8,128)(2,1)S(1)}, u32[]{:S(2)}, u32[]{:S(2)}) collective-permute-start(bf16[3,2,192,128]{3,2,1,0:T(8,128)(2,1)S(1)} %pad_maximum_fusion.refs_0_), channel_id=1, source_target_pairs={{16,8},{8,16},{17,9},{9,17},{18,10},{10,18},{19,11},{11,19},{20,12... | collective-permute-start | bytes 884744 | tf_op jit(solution)/shard_map/ppermute | solution.py:423
  15.1 1.3 %collective-permute-start.6 = (bf16[3,2,192,128]{3,2,1,0:T(8,128)(2,1)S(1)}, bf16[3,2,192,128]{3,2,1,0:T(8,128)(2,1)S(1)}, u32[]{:S(2)}, u32[]{:S(2)}) collective-permute-start(bf16[3,2,192,128]{3,2,1,0:T(8,128)(2,1)S(1)} %pad_maximum_fusion.refs_0_), channel_id=1, source_target_pairs={{16,1},{17,0},{8,25},{9,24},{18,3},{19,2},{10,27},{11,26},{20,5},{... | collective-permute-start | bytes 884744 | tf_op jit(solution)/shard_map/ppermute | solution.py:422
  16.4 1.6 %collective-permute-start.5 = (bf16[2,2,192,128]{3,2,1,0:T(8,128)(2,1)S(1)}, bf16[2,2,192,128]{3,2,1,0:T(8,128)(2,1)S(1)}, u32[]{:S(2)}, u32[]{:S(2)}) collective-permute-start(bf16[2,2,192,128]{3,2,1,0:T(8,128)(2,1)S(1)} %pad_maximum_fusion.1), channel_id=1, source_target_pairs={{0,1},{1,0},{2,3},{3,2},{4,5},{5,4},{6,7},{7,6},{8,9},{9,8},{10,11... | collective-permute-start | bytes 589832 | tf_op jit(solution)/shard_map/ppermute | solution.py:420
  18.0 2.6 %collective-permute-start.4 = (bf16[192,128]{1,0:T(8,128)(2,1)S(1)}, bf16[192,128]{1,0:T(8,128)(2,1)S(1)}, u32[]{:S(2)}, u32[]{:S(2)}) collective-permute-start(bf16[192,128]{1,0:T(8,128)(2,1)S(1)} %bitcast.19), channel_id=1, source_target_pairs={{0,8},{8,0},{16,24},{24,16},{1,9},{9,1},{17,25},{25,17},{2,10},{10... | collective-permute-start | bytes 147464 | tf_op jit(solution)/shard_map/ppermute | solution.py:106
  20.6 0.1 pad_add_fusion.place
  20.7 0.8 %collective-permute-done.4.queries_other = bf16[192,128]{1,0:T(8,128)(2,1)S(1)} collective-permute-done((bf16[192,128]{1,0:T(8,128)(2,1)S(1)}, bf16[192,128]{1,0:T(8,128)(2,1)S(1)}, u32[]{:S(2)}, u32[]{:S(2)}) %collective-permute-start.4) | collective-permute-done | bytes 49184 | tf_op jit(solution)/shard_map/ppermute | solution.py:106
  21.5 1.3 %copy-done.1 = bf16[4,6,8,3072]{3,2,1,0:T(8,128)(2,1)S(1)} copy-done((bf16[4,6,8,3072]{3,2,1,0:T(8,128)(2,1)S(1)}, bf16[4,6,8,3072]{3,2,1,0:T(8,128)(2,1)}, u32[]{:S(2)}) %copy-start.1) | copy-done | bytes 1179672
  22.7 1.0 %shard_map.92 = (bf16[192,1664]{1,0:T(8,128)(2,1)S(1)}, bf16[192,1536]{1,0:T(8,128)(2,1)S(1)}, bf16[192,128]{1,0:T(8,128)(2,1)S(1)}, bf16[384,128]{1,0:T(8,128)(2,1)S(1)}) custom-call(s32[3]{0:T(128)S(1)} %pad_add_fusion.place, bf16[192,128]{1,0:T(8,128)(2,1)S(1)} %bitcast.20, bf16[192,128]{1,0:T(8,128)(2,1)S(1)} %collective-permute-done.4.queries_other, ...), custom_call_target="tpu_custom_call" | custom-call | flops 150994944 | bytes 2359296 | tf_op jit(solution)/shard_map/pallas_call | solution.py:351
  23.8 0.7 %shard_map.93.refs_4_ = f32[136,384]{1,0:T(8,128)S(1)} custom-call(bf16[384,128]{1,0:T(8,128)(2,1)S(1)} %get-tuple-element.51.both_queries, bf16[3,2,192,128]{3,2,1,0:T(8,128)(2,1)S(1)} %pad_maximum_fusion.refs_0_), custom_call_target="tpu_custom_call" | custom-call | flops 113246208 | bytes 393216 | tf_op jit(solution)/shard_map/pallas_call | solution.py:465
  24.5 0.0 collective-permute-done.5.refs_1_.refs_2_
  24.5 0.0 collective-permute-done.7.refs_3_.refs_1_
  24.5 2.2 %collective-permute-done.6.refs_2_.refs_0_ = bf16[3,2,192,128]{3,2,1,0:T(8,128)(2,1)S(1)} collective-permute-done((bf16[3,2,192,128]{3,2,1,0:T(8,128)(2,1)S(1)}, bf16[3,2,192,128]{3,2,1,0:T(8,128)(2,1)S(1)}, u32[]{:S(2)}, u32[]{:S(2)}) %collective-permute-start.6) | collective-permute-done | bytes 294944 | tf_op jit(solution)/shard_map/ppermute | solution.py:422
  26.8 0.5 collective-permute-start.9
  27.3 1.2 %shard_map.94.mine = f32[136,384]{1,0:T(8,128)S(1)} custom-call(bf16[384,128]{1,0:T(8,128)(2,1)S(1)} %get-tuple-element.51.both_queries, bf16[1,2,192,128]{3,2,1,0:T(8,128)(2,1)S(1)} %collective-permute-done.3.refs_0_.refs_1_, bf16[2,2,192,128]{3,2,1,0:T(8,128)(2,1)S(1)} %collective-permute-done.5.refs_1_.refs_2_, ...), custom_call_target="tpu_custom_call" | custom-call | flops 226492416 | bytes 786432 | tf_op jit(solution)/shard_map/pallas_call | solution.py:465
  28.5 0.1 collective-permute-start.8
  28.5 1.4 %collective-permute-done.8.theirs = f32[136,384]{1,0:T(8,128)S(1)} collective-permute-done((f32[136,384]{1,0:T(8,128)S(1)}, f32[136,384]{1,0:T(8,128)S(1)}, u32[]{:S(2)}, u32[]{:S(2)}) %collective-permute-start.8) | collective-permute-done | bytes 208928 | tf_op jit(solution)/shard_map/ppermute | solution.py:106
  30.0 0.0 collective-permute-done.9.payload
  30.0 1.1 %shard_map.95 = (f32[8,384]{1,0:T(8,128)S(1)}, bf16[192,128]{1,0:T(8,128)(2,1)S(1)}, bf16[32,1536]{1,0:T(8,128)(2,1)S(1)}, bf16[32,1536]{1,0:T(8,128)(2,1)S(1)},...) custom-call(s32[3]{0:T(128)S(1)} %pad_add_fusion.place, f32[136,384]{1,0:T(8,128)S(1)} %shard_map.94.mine, ...), custom_call_target="tpu_custom_call" | custom-call | flops 150994944 | bytes 2359296 | tf_op jit(solution)/shard_map/pallas_call | solution.py:351
  31.1 1.6 %collective-permute-start.10 = (bf16[32,1536]{1,0:T(8,128)(2,1)S(1)}, bf16[32,1536]{1,0:T(8,128)(2,1)S(1)}, u32[]{:S(2)}, u32[]{:S(2)}) collective-permute-start(bf16[32,1536]{1,0:T(8,128)(2,1)S(1)} %get-tuple-element.68), channel_id=1, source_target_pairs={{0,1},{1,0},{8,9},{9,8},{16,17},{17,16},{24,25},{25,24},{2,3},{3,2... | collective-permute-start | bytes 294920 | tf_op jit(solution)/shard_map/ppermute | solution.py:106
  32.7 1.0 %collective-permute-start.11 = (bf16[32,1536]{1,0:T(8,128)(2,1)S(1)}, bf16[32,1536]{1,0:T(8,128)(2,1)S(1)}, u32[]{:S(2)}, u32[]{:S(2)}) collective-permute-start(bf16[32,1536]{1,0:T(8,128)(2,1)S(1)} %get-tuple-element.69), channel_id=1, source_target_pairs={{0,16},{1,17},{8,24},{9,25},{16,0},{17,1},{24,8},{25,9},{2,18},{3,... | collective-permute-start | bytes 294920 | tf_op jit(solution)/shard_map/ppermute | solution.py:106
  33.7 1.0 %collective-permute-start.12 = (bf16[32,1536]{1,0:T(8,128)(2,1)S(1)}, bf16[32,1536]{1,0:T(8,128)(2,1)S(1)}, u32[]{:S(2)}, u32[]{:S(2)}) collective-permute-start(bf16[32,1536]{1,0:T(8,128)(2,1)S(1)} %get-tuple-element.70), channel_id=1, source_target_pairs={{0,17},{1,16},{8,25},{9,24},{16,1},{17,0},{24,9},{25,8},{2,19},{3,... | collective-permute-start | bytes 294920 | tf_op jit(solution)/shard_map/ppermute | solution.py:106
  34.7 2.0 %shard_map.96 = (f32[3,2,192,128]{3,2,1,0:T(8,128)S(1)}, bf16[3,2,192,128]{3,2,1,0:T(8,128)(2,1)S(1)}, f32[128,384]{1,0:T(8,128)S(1)}) custom-call(s32[3]{0:T(128)S(1)} %pad_add_fusion.place, f32[8,384]{1,0:T(8,128)S(1)} %get-tuple-element.65.stats, bf16[384,128]{1,0:T(8,128)(2,1)S(1)} %get-tuple-element.51.both_queries, ...), custom_call_target="tpu_custom_call" | custom-call | flops 1000000000 | bytes 100000000 | tf_op jit(solution)/shard_map/pallas_call | solution.py:351
  36.7 1.6 %collective-permute-start.19 = (bf16[3,2,192,128]{3,2,1,0:T(8,128)(2,1)S(1)}, bf16[3,2,192,128]{3,2,1,0:T(8,128)(2,1)S(1)}, u32[]{:S(2)}, u32[]{:S(2)}) collective-permute-start(bf16[3,2,192,128]{3,2,1,0:T(8,128)(2,1)S(1)} %get-tuple-element.86), channel_id=1, source_target_pairs={{0,1},{1,0},{2,3},{3,2},{4,5},{5,4},{6,7},{7,6},{8,9},{9,8},{10,11... | collective-permute-start | bytes 884744 | tf_op jit(solution)/shard_map/ppermute | solution.py:547
  38.3 0.0 collective-permute-done.10
  38.3 0.0 collective-permute-done.11
  38.3 1.4 %collective-permute-done.12 = bf16[32,1536]{1,0:T(8,128)(2,1)S(1)} collective-permute-done((bf16[32,1536]{1,0:T(8,128)(2,1)S(1)}, bf16[32,1536]{1,0:T(8,128)(2,1)S(1)}, u32[]{:S(2)}, u32[]{:S(2)}) %collective-permute-start.12) | collective-permute-done | bytes 98336 | tf_op jit(solution)/shard_map/ppermute | solution.py:106
  39.7 0.1 add_convert_fusion.2
  39.7 0.2 collective-permute-start.13
  39.9 1.4 %shard_map.97 = (bf16[3,2,192,128]{3,2,1,0:T(8,128)(2,1)S(1)}, f32[192,128]{1,0:T(8,128)S(1)}, bf16[16,1536]{1,0:T(8,128)(2,1)S(1)}) custom-call(s32[3]{0:T(128)S(1)} %pad_add_fusion.place, f32[8,384]{1,0:T(8,128)S(1)} %get-tuple-element.65.stats, bf16[384,128]{1,0:T(8,128)(2,1)S(1)} %get-tuple-element.51.both_queries, ...), custom_call_target="tpu_custom_call" | custom-call | flops 10000000000 | bytes 100000000 | tf_op jit(solution)/shard_map/pallas_call | solution.py:351
  41.3 3.8 %collective-permute-start.21 = (bf16[3,2,192,128]{3,2,1,0:T(8,128)(2,1)S(1)}, bf16[3,2,192,128]{3,2,1,0:T(8,128)(2,1)S(1)}, u32[]{:S(2)}, u32[]{:S(2)}) collective-permute-start(bf16[3,2,192,128]{3,2,1,0:T(8,128)(2,1)S(1)} %get-tuple-element.87), channel_id=1, source_target_pairs={{1,16},{0,17},{25,8},{24,9},{3,18},{2,19},{27,10},{26,11},{5,20},{... | collective-permute-start | bytes 884744 | tf_op jit(solution)/shard_map/ppermute | solution.py:549
  45.1 0.7 %collective-permute-start.20 = (bf16[3,2,192,128]{3,2,1,0:T(8,128)(2,1)S(1)}, bf16[3,2,192,128]{3,2,1,0:T(8,128)(2,1)S(1)}, u32[]{:S(2)}, u32[]{:S(2)}) collective-permute-start(bf16[3,2,192,128]{3,2,1,0:T(8,128)(2,1)S(1)} %get-tuple-element.87), channel_id=1, source_target_pairs={{8,16},{16,8},{9,17},{17,9},{10,18},{18,10},{11,19},{19,11},{12,20... | collective-permute-start | bytes 884744 | tf_op jit(solution)/shard_map/ppermute | solution.py:548
  45.8 0.0 collective-permute-done.13
  45.8 1.7 %collective-permute-start.14 = (bf16[32,1536]{1,0:T(8,128)(2,1)S(1)}, bf16[32,1536]{1,0:T(8,128)(2,1)S(1)}, u32[]{:S(2)}, u32[]{:S(2)}) collective-permute-start(bf16[32,1536]{1,0:T(8,128)(2,1)S(1)} %add_convert_fusion.1), channel_id=1, source_target_pairs={{0,4},{2,6},{4,0},{6,2},{1,5},{3,7},{5,1},{7,3},{8,12},{10,14},{12... | collective-permute-start | bytes 294920 | tf_op jit(solution)/shard_map/ppermute | solution.py:106
  47.5 1.5 %convolution_convert_fusion = bf16[192,3072]{1,0:T(8,128)(2,1)} fusion(bf16[192,128]{1,0:T(8,128)(2,1)S(1)} %get-tuple-element.75, bf16[128,3072]{1,0:T(8,128)(2,1)S(1)} %copy-done), kind=kOutput, calls=%fused_computation | convolution fusion | flops 151584768 | bytes 2015232 | tf_op jit(solution)/shard_map/dot_general | solution.py:540
  49.0 5.3 %collective-permute-done.14 = bf16[32,1536]{1,0:T(8,128)(2,1)S(1)} collective-permute-done((bf16[32,1536]{1,0:T(8,128)(2,1)S(1)}, bf16[32,1536]{1,0:T(8,128)(2,1)S(1)}, u32[]{:S(2)}, u32[]{:S(2)}) %collective-permute-start.14) | collective-permute-done | bytes 98336 | tf_op jit(solution)/shard_map/ppermute | solution.py:106
  54.2 0.1 collective-permute-start.17
  54.3 2.1 %collective-permute-start.16 = (bf16[32,1536]{1,0:T(8,128)(2,1)S(1)}, bf16[32,1536]{1,0:T(8,128)(2,1)S(1)}, u32[]{:S(2)}, u32[]{:S(2)}) collective-permute-start(bf16[32,1536]{1,0:T(8,128)(2,1)S(1)} %add_convert_fusion.refs_0_), channel_id=1, source_target_pairs={{0,16},{1,17},{8,24},{9,25},{16,0},{17,1},{24,8},{25,9},{2,18},{3,... | collective-permute-start | bytes 294920 | tf_op jit(solution)/shard_map/ppermute | solution.py:106
  56.4 0.0 collective-permute-done.19.refs_0_
  56.4 1.4 %collective-permute-start.15 = (bf16[32,1536]{1,0:T(8,128)(2,1)S(1)}, bf16[32,1536]{1,0:T(8,128)(2,1)S(1)}, u32[]{:S(2)}, u32[]{:S(2)}) collective-permute-start(bf16[32,1536]{1,0:T(8,128)(2,1)S(1)} %add_convert_fusion.refs_0_), channel_id=1, source_target_pairs={{0,1},{1,0},{8,9},{9,8},{16,17},{17,16},{24,25},{25,24},{2,3},{3,2... | collective-permute-start | bytes 294920 | tf_op jit(solution)/shard_map/ppermute | solution.py:106
  57.8 0.0 collective-permute-done.21.refs_2_
  57.8 0.0 collective-permute-done.20.refs_1_
  57.8 0.1 shard_map.101
  57.9 1.5 %collective-permute-start.24 = (bf16[2,192,128]{2,1,0:T(8,128)(2,1)S(1)}, bf16[2,192,128]{2,1,0:T(8,128)(2,1)S(1)}, u32[]{:S(2)}, u32[]{:S(2)}) collective-permute-start(bf16[2,192,128]{2,1,0:T(8,128)(2,1)S(1)} %get-tuple-element.91), channel_id=1, source_target_pairs={{6,2},{0,4},{7,3},{1,5},{14,10},{8,12},{15,11},{9,13},{22,18},{16,... | collective-permute-start | bytes 294920 | tf_op jit(solution)/shard_map/ppermute | solution.py:87
  59.4 0.7 %collective-permute-start.23 = (bf16[2,192,128]{2,1,0:T(8,128)(2,1)S(1)}, bf16[2,192,128]{2,1,0:T(8,128)(2,1)S(1)}, u32[]{:S(2)}, u32[]{:S(2)}) collective-permute-start(bf16[2,192,128]{2,1,0:T(8,128)(2,1)S(1)} %get-tuple-element.91), channel_id=1, source_target_pairs={{4,2},{2,4},{5,3},{3,5},{12,10},{10,12},{13,11},{11,13},{20,18},{1... | collective-permute-start | bytes 294920 | tf_op jit(solution)/shard_map/ppermute | solution.py:87
  60.1 0.6 collective-permute-done.17.refs_3_
  60.7 0.6 collective-permute-start.22
  61.4 0.0 collective-permute-done.16.refs_2_
  61.4 0.4 collective-permute-done.15.refs_1_
  61.8 0.1 collective-permute-start.18
  61.9 1.5 %shard_map.99.refs_1_ = f32[128,3072]{1,0:T(8,128)} custom-call(s32[3]{0:T(128)S(1)} %pad_add_fusion.place, bf16[144,1536]{1,0:T(8,128)(2,1)S(1)} %shard_map.98.part), custom_call_target="tpu_custom_call" | custom-call | flops 10000000000 | bytes 100000000 | tf_op jit(solution)/shard_map/pallas_call | solution.py:309
  63.4 0.3 collective-permute-done.18.part
  63.7 1.5 %shard_map.100 = (f32[128,3072]{1,0:T(8,128)}, bf16[192,128]{1,0:T(8,128)(2,1)}) custom-call(s32[3]{0:T(128)S(1)} %pad_add_fusion.place, bf16[144,1536]{1,0:T(8,128)(2,1)S(1)} %collective-permute-done.18.part, f32[192,128]{1,0:T(8,128)S(1)} %get-tuple-element.82.refs_0_, f32[128,3072]{1,0:T(8,128)} %shard_map.99.refs_1_), custom_call_target="tpu_custom_call", output_to_operand_aliasing={{0}: (3, {})} | custom-call | flops 10000000000 | bytes 100000000 | tf_op jit(solution)/shard_map/pallas_call | solution.py:309
  65.2 0.2 collective-permute-done.22.refs_0_
  65.4 0.0 collective-permute-done.24.refs_2_
  65.4 0.7 %shard_map.102 = (bf16[192,128]{1,0:T(8,128)(2,1)}, bf16[192,128]{1,0:T(8,128)(2,1)}) custom-call(f32[2,192,128]{2,1,0:T(8,128)S(1)} %get-tuple-element.89.own_grad, bf16[2,192,128]{2,1,0:T(8,128)(2,1)S(1)} %collective-permute-done.22.refs_0_, bf16[2,192,128]{2,1,0:T(8,128)(2,1)S(1)} %collective-permute-done.23.refs_1_, ...), custom_call_target="tpu_custom_call" | custom-call | flops 10000000000 | bytes 100000000 | tf_op jit(solution)/shard_map/pallas_call | solution.py:586
  (12 shorter events, 0.2 us)
Async XLA Ops:
  0.6 17.4 %copy-start.2 = (bf16[4,6,8,128]{3,2,1,0:T(8,128)(2,1)S(1)}, bf16[4,6,8,128]{3,2,1,0:T(8,128)(2,1)}, u32[]{:S(2)}) copy-start(bf16[4,6,8,128]{3,2,1,0:T(8,128)(2,1)} %param.5) | copy-start | bytes 147460
  0.6 20.8 %copy-start = (bf16[128,3072]{1,0:T(8,128)(2,1)S(1)}, bf16[128,3072]{1,0:T(8,128)(2,1)}, u32[]{:S(2)}) copy-start(bf16[128,3072]{1,0:T(8,128)(2,1)} %weight.1) | copy-start | bytes 2359300
  1.6 9.8 %collective-permute-start.2 = (bf16[2,192,128]{2,1,0:T(8,128)(2,1)S(1)}, bf16[2,192,128]{2,1,0:T(8,128)(2,1)S(1)}, u32[]{:S(2)}, u32[]{:S(2)}) collective-permute-start(bf16[2,192,128]{2,1,0:T(8,128)(2,1)S(1)} %get-tuple-element.96), channel_id=1, source_target_pairs={{2,4},{4,2},{3,5},{5,3},{10,12},{12,10},{11,13},{13,11},{18,20},{2... | collective-permute-start | bytes 294920 | tf_op jit(solution)/shard_map/ppermute | solution.py:65
  2.2 10.5 %collective-permute-start.1 = (bf16[2,192,128]{2,1,0:T(8,128)(2,1)S(1)}, bf16[2,192,128]{2,1,0:T(8,128)(2,1)S(1)}, u32[]{:S(2)}, u32[]{:S(2)}) collective-permute-start(bf16[2,192,128]{2,1,0:T(8,128)(2,1)S(1)} %get-tuple-element.96), channel_id=1, source_target_pairs={{2,6},{4,0},{3,7},{5,1},{10,14},{12,8},{11,15},{13,9},{18,22},{20,... | collective-permute-start | bytes 294920 | tf_op jit(solution)/shard_map/ppermute | solution.py:65
  3.5 10.6 %collective-permute-start = (bf16[2,192,128]{2,1,0:T(8,128)(2,1)S(1)}, bf16[2,192,128]{2,1,0:T(8,128)(2,1)S(1)}, u32[]{:S(2)}, u32[]{:S(2)}) collective-permute-start(bf16[2,192,128]{2,1,0:T(8,128)(2,1)S(1)} %get-tuple-element.96), channel_id=1, source_target_pairs={{2,0},{0,2},{6,4},{4,6},{3,1},{1,3},{7,5},{5,7},{10,8},{8,10},{14,... | collective-permute-start | bytes 294920 | tf_op jit(solution)/shard_map/ppermute | solution.py:65
  9.8 4.6 %collective-permute-start.3 = (bf16[1,2,192,128]{3,2,1,0:T(8,128)(2,1)S(1)}, bf16[1,2,192,128]{3,2,1,0:T(8,128)(2,1)S(1)}, u32[]{:S(2)}, u32[]{:S(2)}) collective-permute-start(bf16[1,2,192,128]{3,2,1,0:T(8,128)(2,1)S(1)} %get-tuple-element.95), channel_id=1, source_target_pairs={{0,1},{1,0},{2,3},{3,2},{4,5},{5,4},{6,7},{7,6},{8,9},{9,8},{10,11... | collective-permute-start | bytes 294920 | tf_op jit(solution)/shard_map/ppermute | solution.py:414
  14.5 10.0 %collective-permute-start.7 = (bf16[3,2,192,128]{3,2,1,0:T(8,128)(2,1)S(1)}, bf16[3,2,192,128]{3,2,1,0:T(8,128)(2,1)S(1)}, u32[]{:S(2)}, u32[]{:S(2)}) collective-permute-start(bf16[3,2,192,128]{3,2,1,0:T(8,128)(2,1)S(1)} %pad_maximum_fusion.refs_0_), channel_id=1, source_target_pairs={{16,8},{8,16},{17,9},{9,17},{18,10},{10,18},{19,11},{11,19},{20,12... | collective-permute-start | bytes 884744 | tf_op jit(solution)/shard_map/ppermute | solution.py:423
  15.1 11.6 %collective-permute-start.6 = (bf16[3,2,192,128]{3,2,1,0:T(8,128)(2,1)S(1)}, bf16[3,2,192,128]{3,2,1,0:T(8,128)(2,1)S(1)}, u32[]{:S(2)}, u32[]{:S(2)}) collective-permute-start(bf16[3,2,192,128]{3,2,1,0:T(8,128)(2,1)S(1)} %pad_maximum_fusion.refs_0_), channel_id=1, source_target_pairs={{16,1},{17,0},{8,25},{9,24},{18,3},{19,2},{10,27},{11,26},{20,5},{... | collective-permute-start | bytes 884744 | tf_op jit(solution)/shard_map/ppermute | solution.py:422
  16.4 8.1 %collective-permute-start.5 = (bf16[2,2,192,128]{3,2,1,0:T(8,128)(2,1)S(1)}, bf16[2,2,192,128]{3,2,1,0:T(8,128)(2,1)S(1)}, u32[]{:S(2)}, u32[]{:S(2)}) collective-permute-start(bf16[2,2,192,128]{3,2,1,0:T(8,128)(2,1)S(1)} %pad_maximum_fusion.1), channel_id=1, source_target_pairs={{0,1},{1,0},{2,3},{3,2},{4,5},{5,4},{6,7},{7,6},{8,9},{9,8},{10,11... | collective-permute-start | bytes 589832 | tf_op jit(solution)/shard_map/ppermute | solution.py:420
  18.0 3.5 %collective-permute-start.4 = (bf16[192,128]{1,0:T(8,128)(2,1)S(1)}, bf16[192,128]{1,0:T(8,128)(2,1)S(1)}, u32[]{:S(2)}, u32[]{:S(2)}) collective-permute-start(bf16[192,128]{1,0:T(8,128)(2,1)S(1)} %bitcast.19), channel_id=1, source_target_pairs={{0,8},{8,0},{16,24},{24,16},{1,9},{9,1},{17,25},{25,17},{2,10},{10... | collective-permute-start | bytes 147464 | tf_op jit(solution)/shard_map/ppermute | solution.py:106
  21.5 1.3 %copy-start.1 = (bf16[4,6,8,3072]{3,2,1,0:T(8,128)(2,1)S(1)}, bf16[4,6,8,3072]{3,2,1,0:T(8,128)(2,1)}, u32[]{:S(2)}) copy-start(bf16[4,6,8,3072]{3,2,1,0:T(8,128)(2,1)} %param.9) | copy-start | bytes 3538948
  26.8 3.2 %collective-permute-start.9 = (bf16[192,1664]{1,0:T(8,128)(2,1)S(1)}, bf16[192,1664]{1,0:T(8,128)(2,1)S(1)}, u32[]{:S(2)}, u32[]{:S(2)}) collective-permute-start(bf16[192,1664]{1,0:T(8,128)(2,1)S(1)} %get-tuple-element.61), channel_id=1, source_target_pairs={{0,8},{8,0},{16,24},{24,16},{1,9},{9,1},{17,25},{25,17},{2,10},{10... | collective-permute-start | bytes 1916936 | tf_op jit(solution)/shard_map/ppermute | solution.py:106
  28.5 1.5 %collective-permute-start.8 = (f32[136,384]{1,0:T(8,128)S(1)}, f32[136,384]{1,0:T(8,128)S(1)}, u32[]{:S(2)}, u32[]{:S(2)}) collective-permute-start(f32[136,384]{1,0:T(8,128)S(1)} %shard_map.94.mine), channel_id=1, source_target_pairs={{0,8},{8,0},{16,24},{24,16},{1,9},{9,1},{17,25},{25,17},{2,10},{10... | collective-permute-start | bytes 626696 | tf_op jit(solution)/shard_map/ppermute | solution.py:106
  31.1 7.2 %collective-permute-start.10 = (bf16[32,1536]{1,0:T(8,128)(2,1)S(1)}, bf16[32,1536]{1,0:T(8,128)(2,1)S(1)}, u32[]{:S(2)}, u32[]{:S(2)}) collective-permute-start(bf16[32,1536]{1,0:T(8,128)(2,1)S(1)} %get-tuple-element.68), channel_id=1, source_target_pairs={{0,1},{1,0},{8,9},{9,8},{16,17},{17,16},{24,25},{25,24},{2,3},{3,2... | collective-permute-start | bytes 294920 | tf_op jit(solution)/shard_map/ppermute | solution.py:106
  32.7 5.6 %collective-permute-start.11 = (bf16[32,1536]{1,0:T(8,128)(2,1)S(1)}, bf16[32,1536]{1,0:T(8,128)(2,1)S(1)}, u32[]{:S(2)}, u32[]{:S(2)}) collective-permute-start(bf16[32,1536]{1,0:T(8,128)(2,1)S(1)} %get-tuple-element.69), channel_id=1, source_target_pairs={{0,16},{1,17},{8,24},{9,25},{16,0},{17,1},{24,8},{25,9},{2,18},{3,... | collective-permute-start | bytes 294920 | tf_op jit(solution)/shard_map/ppermute | solution.py:106
  33.7 6.0 %collective-permute-start.12 = (bf16[32,1536]{1,0:T(8,128)(2,1)S(1)}, bf16[32,1536]{1,0:T(8,128)(2,1)S(1)}, u32[]{:S(2)}, u32[]{:S(2)}) collective-permute-start(bf16[32,1536]{1,0:T(8,128)(2,1)S(1)} %get-tuple-element.70), channel_id=1, source_target_pairs={{0,17},{1,16},{8,25},{9,24},{16,1},{17,0},{24,9},{25,8},{2,19},{3,... | collective-permute-start | bytes 294920 | tf_op jit(solution)/shard_map/ppermute | solution.py:106
  36.7 19.7 %collective-permute-start.19 = (bf16[3,2,192,128]{3,2,1,0:T(8,128)(2,1)S(1)}, bf16[3,2,192,128]{3,2,1,0:T(8,128)(2,1)S(1)}, u32[]{:S(2)}, u32[]{:S(2)}) collective-permute-start(bf16[3,2,192,128]{3,2,1,0:T(8,128)(2,1)S(1)} %get-tuple-element.86), channel_id=1, source_target_pairs={{0,1},{1,0},{2,3},{3,2},{4,5},{5,4},{6,7},{7,6},{8,9},{9,8},{10,11... | collective-permute-start | bytes 884744 | tf_op jit(solution)/shard_map/ppermute | solution.py:547
  39.7 6.1 %collective-permute-start.13 = (bf16[32,1536]{1,0:T(8,128)(2,1)S(1)}, bf16[32,1536]{1,0:T(8,128)(2,1)S(1)}, u32[]{:S(2)}, u32[]{:S(2)}) collective-permute-start(bf16[32,1536]{1,0:T(8,128)(2,1)S(1)} %add_convert_fusion.2), channel_id=1, source_target_pairs={{0,2},{2,0},{4,6},{6,4},{1,3},{3,1},{5,7},{7,5},{8,10},{10,8},{12,... | collective-permute-start | bytes 294920 | tf_op jit(solution)/shard_map/ppermute | solution.py:106
  41.3 16.5 %collective-permute-start.21 = (bf16[3,2,192,128]{3,2,1,0:T(8,128)(2,1)S(1)}, bf16[3,2,192,128]{3,2,1,0:T(8,128)(2,1)S(1)}, u32[]{:S(2)}, u32[]{:S(2)}) collective-permute-start(bf16[3,2,192,128]{3,2,1,0:T(8,128)(2,1)S(1)} %get-tuple-element.87), channel_id=1, source_target_pairs={{1,16},{0,17},{25,8},{24,9},{3,18},{2,19},{27,10},{26,11},{5,20},{... | collective-permute-start | bytes 884744 | tf_op jit(solution)/shard_map/ppermute | solution.py:549
  45.1 12.7 %collective-permute-start.20 = (bf16[3,2,192,128]{3,2,1,0:T(8,128)(2,1)S(1)}, bf16[3,2,192,128]{3,2,1,0:T(8,128)(2,1)S(1)}, u32[]{:S(2)}, u32[]{:S(2)}) collective-permute-start(bf16[3,2,192,128]{3,2,1,0:T(8,128)(2,1)S(1)} %get-tuple-element.87), channel_id=1, source_target_pairs={{8,16},{16,8},{9,17},{17,9},{10,18},{18,10},{11,19},{19,11},{12,20... | collective-permute-start | bytes 884744 | tf_op jit(solution)/shard_map/ppermute | solution.py:548
  45.8 8.4 %collective-permute-start.14 = (bf16[32,1536]{1,0:T(8,128)(2,1)S(1)}, bf16[32,1536]{1,0:T(8,128)(2,1)S(1)}, u32[]{:S(2)}, u32[]{:S(2)}) collective-permute-start(bf16[32,1536]{1,0:T(8,128)(2,1)S(1)} %add_convert_fusion.1), channel_id=1, source_target_pairs={{0,4},{2,6},{4,0},{6,2},{1,5},{3,7},{5,1},{7,3},{8,12},{10,14},{12... | collective-permute-start | bytes 294920 | tf_op jit(solution)/shard_map/ppermute | solution.py:106
  54.2 6.5 %collective-permute-start.17 = (bf16[32,1536]{1,0:T(8,128)(2,1)S(1)}, bf16[32,1536]{1,0:T(8,128)(2,1)S(1)}, u32[]{:S(2)}, u32[]{:S(2)}) collective-permute-start(bf16[32,1536]{1,0:T(8,128)(2,1)S(1)} %add_convert_fusion.refs_0_), channel_id=1, source_target_pairs={{0,17},{1,16},{8,25},{9,24},{16,1},{17,0},{24,9},{25,8},{2,19},{3,... | collective-permute-start | bytes 294920 | tf_op jit(solution)/shard_map/ppermute | solution.py:106
  54.3 7.1 %collective-permute-start.16 = (bf16[32,1536]{1,0:T(8,128)(2,1)S(1)}, bf16[32,1536]{1,0:T(8,128)(2,1)S(1)}, u32[]{:S(2)}, u32[]{:S(2)}) collective-permute-start(bf16[32,1536]{1,0:T(8,128)(2,1)S(1)} %add_convert_fusion.refs_0_), channel_id=1, source_target_pairs={{0,16},{1,17},{8,24},{9,25},{16,0},{17,1},{24,8},{25,9},{2,18},{3,... | collective-permute-start | bytes 294920 | tf_op jit(solution)/shard_map/ppermute | solution.py:106
  56.4 5.3 %collective-permute-start.15 = (bf16[32,1536]{1,0:T(8,128)(2,1)S(1)}, bf16[32,1536]{1,0:T(8,128)(2,1)S(1)}, u32[]{:S(2)}, u32[]{:S(2)}) collective-permute-start(bf16[32,1536]{1,0:T(8,128)(2,1)S(1)} %add_convert_fusion.refs_0_), channel_id=1, source_target_pairs={{0,1},{1,0},{8,9},{9,8},{16,17},{17,16},{24,25},{25,24},{2,3},{3,2... | collective-permute-start | bytes 294920 | tf_op jit(solution)/shard_map/ppermute | solution.py:106
  57.9 7.4 %collective-permute-start.24 = (bf16[2,192,128]{2,1,0:T(8,128)(2,1)S(1)}, bf16[2,192,128]{2,1,0:T(8,128)(2,1)S(1)}, u32[]{:S(2)}, u32[]{:S(2)}) collective-permute-start(bf16[2,192,128]{2,1,0:T(8,128)(2,1)S(1)} %get-tuple-element.91), channel_id=1, source_target_pairs={{6,2},{0,4},{7,3},{1,5},{14,10},{8,12},{15,11},{9,13},{22,18},{16,... | collective-permute-start | bytes 294920 | tf_op jit(solution)/shard_map/ppermute | solution.py:87
  59.4 5.9 %collective-permute-start.23 = (bf16[2,192,128]{2,1,0:T(8,128)(2,1)S(1)}, bf16[2,192,128]{2,1,0:T(8,128)(2,1)S(1)}, u32[]{:S(2)}, u32[]{:S(2)}) collective-permute-start(bf16[2,192,128]{2,1,0:T(8,128)(2,1)S(1)} %get-tuple-element.91), channel_id=1, source_target_pairs={{4,2},{2,4},{5,3},{3,5},{12,10},{10,12},{13,11},{11,13},{20,18},{1... | collective-permute-start | bytes 294920 | tf_op jit(solution)/shard_map/ppermute | solution.py:87
  60.7 4.6 %collective-permute-start.22 = (bf16[2,192,128]{2,1,0:T(8,128)(2,1)S(1)}, bf16[2,192,128]{2,1,0:T(8,128)(2,1)S(1)}, u32[]{:S(2)}, u32[]{:S(2)}) collective-permute-start(bf16[2,192,128]{2,1,0:T(8,128)(2,1)S(1)} %get-tuple-element.90), channel_id=1, source_target_pairs={{0,2},{2,0},{4,6},{6,4},{1,3},{3,1},{5,7},{7,5},{8,10},{10,8},{12,... | collective-permute-start | bytes 294920 | tf_op jit(solution)/shard_map/ppermute | solution.py:87
  61.8 1.9 %collective-permute-start.18 = (bf16[144,1536]{1,0:T(8,128)(2,1)S(1)}, bf16[144,1536]{1,0:T(8,128)(2,1)S(1)}, u32[]{:S(2)}, u32[]{:S(2)}) collective-permute-start(bf16[144,1536]{1,0:T(8,128)(2,1)S(1)} %shard_map.98.part), channel_id=1, source_target_pairs={{0,8},{8,0},{16,24},{24,16},{1,9},{9,1},{17,25},{25,17},{2,10},{10... | collective-permute-start | bytes 1327112 | tf_op jit(solution)/shard_map/ppermute | solution.py:106

commit v10 on v9

--- a/solution.py
+++ b/solution.py
@@ -419,8 +419,8 @@
         )
         others_beside = lax.ppermute(others, "width", swap)
         far = [
+            lax.ppermute(column, "frame", [(2, 1), (1, 2)]),
             lax.ppermute(column, ("frame", "width"), cross),
-            lax.ppermute(column, "frame", [(2, 1), (1, 2)]),
         ]
         blocks = [column, own_beside, others_beside, *far]
         layout = (1, 1, 1, 2)

time: 66.4 us -> 65.2 us (0.982)
  waiting for transfers between devices: 15.7 us -> 13.8 us
  starting transfers between devices: 34.3 us -> 35.1 us
    ppermute x1, waiting for transfers between devices: 2.25 us -> 0.01 us  [body(): lax.ppermute(column, ('frame', 'width'), cross)]
    ppermute x12, starting transfers between devices: 12.2 us -> 13.4 us  [flip(): return lax.ppermute(block, axes, route)]
    ppermute x1, waiting for transfers between devices: 0.01 us -> 0.95 us  [body(): others_beside = lax.ppermute(others, 'width', swap)]
    ppermute x12, waiting for transfers between devices: 10.2 us -> 9.57 us  [flip(): return lax.ppermute(block, axes, route)]
  transfers between devices with their start and end apart: 25 -> 25, of which waited for: 12 -> 12; matrix products, arithmetic and copies ran while one was open for 3% -> 3% of each run, Pallas kernels for 14% -> 15%
where the time goes in v10:
time: 65.2 us; the launch traced here: 64.9 us
  starting transfers between devices  35.1 us (54%)
  waiting for transfers between devices  13.8 us (21%)
  Pallas kernels  11.3 us (17%)
  matrix products  1.48 us (2%)
  local copies, waits for them, and re-layouts  1.28 us (2%)
  other arithmetic  1.17 us (2%)
  between operations  0.86 us (1%)
    ppermute x12, starting transfers between devices, flip(): return lax.ppermute(block, axes, route)  13.4 us
    ppermute x12, waiting for transfers between devices, flip(): return lax.ppermute(block, axes, route)  9.57 us
    ppermute x3, starting transfers between devices, fetch(): arrived = [lax.ppermute(block, axis, route) for route in routes]  8.25 us
    pallas_call x4, Pallas kernels, kernel_call(): pl.pallas_call(kernel, out_shape=outs, in_specs=[SMEM] + [VMEM] * (len(op...  5.57 us
    ppermute x1, starting transfers between devices, body(): lax.ppermute(far_grad, ('frame', 'width'), [(p, s) for s, p in cross])  3.2 us
    pallas_call x2, Pallas kernels, assemble(): pl.pallas_call(functools.partial(assemble_kernel, flipped, rows), out_sha...  2.95 us
    ppermute x3, starting transfers between devices, returned(): arrived.append(lax.ppermute(outgoing, axis, [(p, s) for s, p in route]))  2.88 us
    ppermute x3, waiting for transfers between devices, fetch(): arrived = [lax.ppermute(block, axis, route) for route in routes]  2.79 us
  transfers between devices with their start and end apart: 25, of which 12 were waited for; matrix products, arithmetic and copies ran while one was open for 3% of the time, Pallas kernels for 15%

profile of v10, /device:TPU:0, one launch (start us, length us, event | category | flops | bytes accessed | tf_op | source)
XLA Modules:
  0.0 64.9 jit_solution(11511229660995981712)
XLA Ops:
  0.7 0.9 %fusion = (bf16[1,2,192,128]{3,2,1,0:T(8,128)(2,1)S(1)}, bf16[2,192,128]{2,1,0:T(8,128)(2,1)S(1)}) fusion(bf16[1,192,128]{2,1,0:T(8,128)(2,1)} %bitcast.24, bf16[1,192,128]{2,1,0:T(8,128)(2,1)} %bitcast.25), kind=kLoop, calls=%fused_computation.9 | loop fusion | flops 49152 | bytes 294912 | tf_op jit(solution)/shard_map/stack | solution.py:416
  1.6 0.7 %collective-permute-start.2 = (bf16[2,192,128]{2,1,0:T(8,128)(2,1)S(1)}, bf16[2,192,128]{2,1,0:T(8,128)(2,1)S(1)}, u32[]{:S(2)}, u32[]{:S(2)}) collective-permute-start(bf16[2,192,128]{2,1,0:T(8,128)(2,1)S(1)} %get-tuple-element.96), channel_id=1, source_target_pairs={{2,4},{4,2},{3,5},{5,3},{10,12},{12,10},{11,13},{13,11},{18,20},{2... | collective-permute-start | bytes 294920 | tf_op jit(solution)/shard_map/ppermute | solution.py:65
  2.2 1.3 %collective-permute-start.1 = (bf16[2,192,128]{2,1,0:T(8,128)(2,1)S(1)}, bf16[2,192,128]{2,1,0:T(8,128)(2,1)S(1)}, u32[]{:S(2)}, u32[]{:S(2)}) collective-permute-start(bf16[2,192,128]{2,1,0:T(8,128)(2,1)S(1)} %get-tuple-element.96), channel_id=1, source_target_pairs={{2,6},{4,0},{3,7},{5,1},{10,14},{12,8},{11,15},{13,9},{18,22},{20,... | collective-permute-start | bytes 294920 | tf_op jit(solution)/shard_map/ppermute | solution.py:65
  3.5 6.3 %collective-permute-start = (bf16[2,192,128]{2,1,0:T(8,128)(2,1)S(1)}, bf16[2,192,128]{2,1,0:T(8,128)(2,1)S(1)}, u32[]{:S(2)}, u32[]{:S(2)}) collective-permute-start(bf16[2,192,128]{2,1,0:T(8,128)(2,1)S(1)} %get-tuple-element.96), channel_id=1, source_target_pairs={{2,0},{0,2},{6,4},{4,6},{3,1},{1,3},{7,5},{5,7},{10,8},{8,10},{14,... | collective-permute-start | bytes 294920 | tf_op jit(solution)/shard_map/ppermute | solution.py:65
  9.8 1.5 %collective-permute-start.3 = (bf16[1,2,192,128]{3,2,1,0:T(8,128)(2,1)S(1)}, bf16[1,2,192,128]{3,2,1,0:T(8,128)(2,1)S(1)}, u32[]{:S(2)}, u32[]{:S(2)}) collective-permute-start(bf16[1,2,192,128]{3,2,1,0:T(8,128)(2,1)S(1)} %get-tuple-element.95), channel_id=1, source_target_pairs={{0,1},{1,0},{2,3},{3,2},{4,5},{5,4},{6,7},{7,6},{8,9},{9,8},{10,11... | collective-permute-start | bytes 294920 | tf_op jit(solution)/shard_map/ppermute | solution.py:414
  11.4 0.0 collective-permute-done.2
  11.4 1.4 %collective-permute-done.1 = bf16[2,192,128]{2,1,0:T(8,128)(2,1)S(1)} collective-permute-done((bf16[2,192,128]{2,1,0:T(8,128)(2,1)S(1)}, bf16[2,192,128]{2,1,0:T(8,128)(2,1)S(1)}, u32[]{:S(2)}, u32[]{:S(2)}) %collective-permute-start.1) | collective-permute-done | bytes 98336 | tf_op jit(solution)/shard_map/ppermute | solution.py:65
  12.8 1.4 %collective-permute-done = bf16[2,192,128]{2,1,0:T(8,128)(2,1)S(1)} collective-permute-done((bf16[2,192,128]{2,1,0:T(8,128)(2,1)S(1)}, bf16[2,192,128]{2,1,0:T(8,128)(2,1)S(1)}, u32[]{:S(2)}, u32[]{:S(2)}) %collective-permute-start) | collective-permute-done | bytes 98336 | tf_op jit(solution)/shard_map/ppermute | solution.py:65
  14.2 0.2 collective-permute-done.3.refs_0_.refs_1_
  14.5 1.3 %collective-permute-start.7 = (bf16[3,2,192,128]{3,2,1,0:T(8,128)(2,1)S(1)}, bf16[3,2,192,128]{3,2,1,0:T(8,128)(2,1)S(1)}, u32[]{:S(2)}, u32[]{:S(2)}) collective-permute-start(bf16[3,2,192,128]{3,2,1,0:T(8,128)(2,1)S(1)} %pad_maximum_fusion.refs_0_), channel_id=1, source_target_pairs={{16,1},{17,0},{8,25},{9,24},{18,3},{19,2},{10,27},{11,26},{20,5},{... | collective-permute-start | bytes 884744 | tf_op jit(solution)/shard_map/ppermute | solution.py:423
  15.7 0.7 %collective-permute-start.6 = (bf16[3,2,192,128]{3,2,1,0:T(8,128)(2,1)S(1)}, bf16[3,2,192,128]{3,2,1,0:T(8,128)(2,1)S(1)}, u32[]{:S(2)}, u32[]{:S(2)}) collective-permute-start(bf16[3,2,192,128]{3,2,1,0:T(8,128)(2,1)S(1)} %pad_maximum_fusion.refs_0_), channel_id=1, source_target_pairs={{16,8},{8,16},{17,9},{9,17},{18,10},{10,18},{19,11},{11,19},{20,12... | collective-permute-start | bytes 884744 | tf_op jit(solution)/shard_map/ppermute | solution.py:422
  16.4 1.6 %collective-permute-start.5 = (bf16[2,2,192,128]{3,2,1,0:T(8,128)(2,1)S(1)}, bf16[2,2,192,128]{3,2,1,0:T(8,128)(2,1)S(1)}, u32[]{:S(2)}, u32[]{:S(2)}) collective-permute-start(bf16[2,2,192,128]{3,2,1,0:T(8,128)(2,1)S(1)} %pad_maximum_fusion.1), channel_id=1, source_target_pairs={{0,1},{1,0},{2,3},{3,2},{4,5},{5,4},{6,7},{7,6},{8,9},{9,8},{10,11... | collective-permute-start | bytes 589832 | tf_op jit(solution)/shard_map/ppermute | solution.py:420
  18.0 3.7 %collective-permute-start.4 = (bf16[192,128]{1,0:T(8,128)(2,1)S(1)}, bf16[192,128]{1,0:T(8,128)(2,1)S(1)}, u32[]{:S(2)}, u32[]{:S(2)}) collective-permute-start(bf16[192,128]{1,0:T(8,128)(2,1)S(1)} %bitcast.19), channel_id=1, source_target_pairs={{0,8},{8,0},{16,24},{24,16},{1,9},{9,1},{17,25},{25,17},{2,10},{10... | collective-permute-start | bytes 147464 | tf_op jit(solution)/shard_map/ppermute | solution.py:106
  21.7 0.1 pad_add_fusion.place
  21.8 0.8 %collective-permute-done.4.queries_other = bf16[192,128]{1,0:T(8,128)(2,1)S(1)} collective-permute-done((bf16[192,128]{1,0:T(8,128)(2,1)S(1)}, bf16[192,128]{1,0:T(8,128)(2,1)S(1)}, u32[]{:S(2)}, u32[]{:S(2)}) %collective-permute-start.4) | collective-permute-done | bytes 49184 | tf_op jit(solution)/shard_map/ppermute | solution.py:106
  22.6 1.3 %copy-done.1 = bf16[4,6,8,3072]{3,2,1,0:T(8,128)(2,1)S(1)} copy-done((bf16[4,6,8,3072]{3,2,1,0:T(8,128)(2,1)S(1)}, bf16[4,6,8,3072]{3,2,1,0:T(8,128)(2,1)}, u32[]{:S(2)}) %copy-start.1) | copy-done | bytes 1179672
  23.8 1.0 %shard_map.92 = (bf16[192,1664]{1,0:T(8,128)(2,1)S(1)}, bf16[192,1536]{1,0:T(8,128)(2,1)S(1)}, bf16[192,128]{1,0:T(8,128)(2,1)S(1)}, bf16[384,128]{1,0:T(8,128)(2,1)S(1)}) custom-call(s32[3]{0:T(128)S(1)} %pad_add_fusion.place, bf16[192,128]{1,0:T(8,128)(2,1)S(1)} %bitcast.20, bf16[192,128]{1,0:T(8,128)(2,1)S(1)} %collective-permute-done.4.queries_other, ...), custom_call_target="tpu_custom_call" | custom-call | flops 150994944 | bytes 2359296 | tf_op jit(solution)/shard_map/pallas_call | solution.py:351
  24.9 0.7 %shard_map.93.refs_4_ = f32[136,384]{1,0:T(8,128)S(1)} custom-call(bf16[384,128]{1,0:T(8,128)(2,1)S(1)} %get-tuple-element.51.both_queries, bf16[3,2,192,128]{3,2,1,0:T(8,128)(2,1)S(1)} %pad_maximum_fusion.refs_0_), custom_call_target="tpu_custom_call" | custom-call | flops 113246208 | bytes 393216 | tf_op jit(solution)/shard_map/pallas_call | solution.py:465
  25.6 0.9 %collective-permute-done.5.refs_1_.refs_2_ = bf16[2,2,192,128]{3,2,1,0:T(8,128)(2,1)S(1)} collective-permute-done((bf16[2,2,192,128]{3,2,1,0:T(8,128)(2,1)S(1)}, bf16[2,2,192,128]{3,2,1,0:T(8,128)(2,1)S(1)}, u32[]{:S(2)}, u32[]{:S(2)}) %collective-permute-start.5) | collective-permute-done | bytes 196640 | tf_op jit(solution)/shard_map/ppermute | solution.py:420
  26.5 0.0 collective-permute-done.7.refs_3_.refs_1_
  26.5 0.0 collective-permute-done.6.refs_2_.refs_0_
  26.5 0.7 %collective-permute-start.9 = (bf16[192,1664]{1,0:T(8,128)(2,1)S(1)}, bf16[192,1664]{1,0:T(8,128)(2,1)S(1)}, u32[]{:S(2)}, u32[]{:S(2)}) collective-permute-start(bf16[192,1664]{1,0:T(8,128)(2,1)S(1)} %get-tuple-element.61), channel_id=1, source_target_pairs={{0,8},{8,0},{16,24},{24,16},{1,9},{9,1},{17,25},{25,17},{2,10},{10... | collective-permute-start | bytes 1916936 | tf_op jit(solution)/shard_map/ppermute | solution.py:106
  27.3 1.2 %shard_map.94.mine = f32[136,384]{1,0:T(8,128)S(1)} custom-call(bf16[384,128]{1,0:T(8,128)(2,1)S(1)} %get-tuple-element.51.both_queries, bf16[1,2,192,128]{3,2,1,0:T(8,128)(2,1)S(1)} %collective-permute-done.3.refs_0_.refs_1_, bf16[2,2,192,128]{3,2,1,0:T(8,128)(2,1)S(1)} %collective-permute-done.5.refs_1_.refs_2_, ...), custom_call_target="tpu_custom_call" | custom-call | flops 226492416 | bytes 786432 | tf_op jit(solution)/shard_map/pallas_call | solution.py:465
  28.5 0.1 collective-permute-start.8
  28.5 1.4 %collective-permute-done.8.theirs = f32[136,384]{1,0:T(8,128)S(1)} collective-permute-done((f32[136,384]{1,0:T(8,128)S(1)}, f32[136,384]{1,0:T(8,128)S(1)}, u32[]{:S(2)}, u32[]{:S(2)}) %collective-permute-start.8) | collective-permute-done | bytes 208928 | tf_op jit(solution)/shard_map/ppermute | solution.py:106
  30.0 0.0 collective-permute-done.9.payload
  30.0 1.1 %shard_map.95 = (f32[8,384]{1,0:T(8,128)S(1)}, bf16[192,128]{1,0:T(8,128)(2,1)S(1)}, bf16[32,1536]{1,0:T(8,128)(2,1)S(1)}, bf16[32,1536]{1,0:T(8,128)(2,1)S(1)},...) custom-call(s32[3]{0:T(128)S(1)} %pad_add_fusion.place, f32[136,384]{1,0:T(8,128)S(1)} %shard_map.94.mine, ...), custom_call_target="tpu_custom_call" | custom-call | flops 150994944 | bytes 2359296 | tf_op jit(solution)/shard_map/pallas_call | solution.py:351
  31.1 1.6 %collective-permute-start.10 = (bf16[32,1536]{1,0:T(8,128)(2,1)S(1)}, bf16[32,1536]{1,0:T(8,128)(2,1)S(1)}, u32[]{:S(2)}, u32[]{:S(2)}) collective-permute-start(bf16[32,1536]{1,0:T(8,128)(2,1)S(1)} %get-tuple-element.68), channel_id=1, source_target_pairs={{0,1},{1,0},{8,9},{9,8},{16,17},{17,16},{24,25},{25,24},{2,3},{3,2... | collective-permute-start | bytes 294920 | tf_op jit(solution)/shard_map/ppermute | solution.py:106
  32.7 0.2 collective-permute-start.11
  32.9 1.8 %collective-permute-start.12 = (bf16[32,1536]{1,0:T(8,128)(2,1)S(1)}, bf16[32,1536]{1,0:T(8,128)(2,1)S(1)}, u32[]{:S(2)}, u32[]{:S(2)}) collective-permute-start(bf16[32,1536]{1,0:T(8,128)(2,1)S(1)} %get-tuple-element.70), channel_id=1, source_target_pairs={{0,17},{1,16},{8,25},{9,24},{16,1},{17,0},{24,9},{25,8},{2,19},{3,... | collective-permute-start | bytes 294920 | tf_op jit(solution)/shard_map/ppermute | solution.py:106
  34.7 2.0 %shard_map.96 = (f32[3,2,192,128]{3,2,1,0:T(8,128)S(1)}, bf16[3,2,192,128]{3,2,1,0:T(8,128)(2,1)S(1)}, f32[128,384]{1,0:T(8,128)S(1)}) custom-call(s32[3]{0:T(128)S(1)} %pad_add_fusion.place, f32[8,384]{1,0:T(8,128)S(1)} %get-tuple-element.65.stats, bf16[384,128]{1,0:T(8,128)(2,1)S(1)} %get-tuple-element.51.both_queries, ...), custom_call_target="tpu_custom_call" | custom-call | flops 1000000000 | bytes 100000000 | tf_op jit(solution)/shard_map/pallas_call | solution.py:351
  36.7 1.6 %collective-permute-start.19 = (bf16[3,2,192,128]{3,2,1,0:T(8,128)(2,1)S(1)}, bf16[3,2,192,128]{3,2,1,0:T(8,128)(2,1)S(1)}, u32[]{:S(2)}, u32[]{:S(2)}) collective-permute-start(bf16[3,2,192,128]{3,2,1,0:T(8,128)(2,1)S(1)} %get-tuple-element.86), channel_id=1, source_target_pairs={{0,1},{1,0},{2,3},{3,2},{4,5},{5,4},{6,7},{7,6},{8,9},{9,8},{10,11... | collective-permute-start | bytes 884744 | tf_op jit(solution)/shard_map/ppermute | solution.py:547
  38.3 0.0 collective-permute-done.10
  38.3 0.0 collective-permute-done.11
  38.3 1.1 %collective-permute-done.12 = bf16[32,1536]{1,0:T(8,128)(2,1)S(1)} collective-permute-done((bf16[32,1536]{1,0:T(8,128)(2,1)S(1)}, bf16[32,1536]{1,0:T(8,128)(2,1)S(1)}, u32[]{:S(2)}, u32[]{:S(2)}) %collective-permute-start.12) | collective-permute-done | bytes 98336 | tf_op jit(solution)/shard_map/ppermute | solution.py:106
  39.4 0.1 add_convert_fusion.2
  39.4 0.1 collective-permute-start.13
  39.6 1.4 %shard_map.97 = (bf16[3,2,192,128]{3,2,1,0:T(8,128)(2,1)S(1)}, f32[192,128]{1,0:T(8,128)S(1)}, bf16[16,1536]{1,0:T(8,128)(2,1)S(1)}) custom-call(s32[3]{0:T(128)S(1)} %pad_add_fusion.place, f32[8,384]{1,0:T(8,128)S(1)} %get-tuple-element.65.stats, bf16[384,128]{1,0:T(8,128)(2,1)S(1)} %get-tuple-element.51.both_queries, ...), custom_call_target="tpu_custom_call" | custom-call | flops 10000000000 | bytes 100000000 | tf_op jit(solution)/shard_map/pallas_call | solution.py:351
  41.0 3.2 %collective-permute-start.21 = (bf16[3,2,192,128]{3,2,1,0:T(8,128)(2,1)S(1)}, bf16[3,2,192,128]{3,2,1,0:T(8,128)(2,1)S(1)}, u32[]{:S(2)}, u32[]{:S(2)}) collective-permute-start(bf16[3,2,192,128]{3,2,1,0:T(8,128)(2,1)S(1)} %get-tuple-element.87), channel_id=1, source_target_pairs={{1,16},{0,17},{25,8},{24,9},{3,18},{2,19},{27,10},{26,11},{5,20},{... | collective-permute-start | bytes 884744 | tf_op jit(solution)/shard_map/ppermute | solution.py:549
  44.2 0.7 %collective-permute-start.20 = (bf16[3,2,192,128]{3,2,1,0:T(8,128)(2,1)S(1)}, bf16[3,2,192,128]{3,2,1,0:T(8,128)(2,1)S(1)}, u32[]{:S(2)}, u32[]{:S(2)}) collective-permute-start(bf16[3,2,192,128]{3,2,1,0:T(8,128)(2,1)S(1)} %get-tuple-element.87), channel_id=1, source_target_pairs={{8,16},{16,8},{9,17},{17,9},{10,18},{18,10},{11,19},{19,11},{12,20... | collective-permute-start | bytes 884744 | tf_op jit(solution)/shard_map/ppermute | solution.py:548
  44.9 0.0 collective-permute-done.13
  44.9 1.6 %collective-permute-start.14 = (bf16[32,1536]{1,0:T(8,128)(2,1)S(1)}, bf16[32,1536]{1,0:T(8,128)(2,1)S(1)}, u32[]{:S(2)}, u32[]{:S(2)}) collective-permute-start(bf16[32,1536]{1,0:T(8,128)(2,1)S(1)} %add_convert_fusion.1), channel_id=1, source_target_pairs={{0,4},{2,6},{4,0},{6,2},{1,5},{3,7},{5,1},{7,3},{8,12},{10,14},{12... | collective-permute-start | bytes 294920 | tf_op jit(solution)/shard_map/ppermute | solution.py:106
  46.6 1.5 %convolution_convert_fusion = bf16[192,3072]{1,0:T(8,128)(2,1)} fusion(bf16[192,128]{1,0:T(8,128)(2,1)S(1)} %get-tuple-element.75, bf16[128,3072]{1,0:T(8,128)(2,1)S(1)} %copy-done), kind=kOutput, calls=%fused_computation | convolution fusion | flops 151584768 | bytes 2015232 | tf_op jit(solution)/shard_map/dot_general | solution.py:540
  48.1 5.1 %collective-permute-done.14 = bf16[32,1536]{1,0:T(8,128)(2,1)S(1)} collective-permute-done((bf16[32,1536]{1,0:T(8,128)(2,1)S(1)}, bf16[32,1536]{1,0:T(8,128)(2,1)S(1)}, u32[]{:S(2)}, u32[]{:S(2)}) %collective-permute-start.14) | collective-permute-done | bytes 98336 | tf_op jit(solution)/shard_map/ppermute | solution.py:106
  53.2 0.1 collective-permute-start.17
  53.3 2.3 %collective-permute-start.16 = (bf16[32,1536]{1,0:T(8,128)(2,1)S(1)}, bf16[32,1536]{1,0:T(8,128)(2,1)S(1)}, u32[]{:S(2)}, u32[]{:S(2)}) collective-permute-start(bf16[32,1536]{1,0:T(8,128)(2,1)S(1)} %add_convert_fusion.refs_0_), channel_id=1, source_target_pairs={{0,16},{1,17},{8,24},{9,25},{16,0},{17,1},{24,8},{25,9},{2,18},{3,... | collective-permute-start | bytes 294920 | tf_op jit(solution)/shard_map/ppermute | solution.py:106
  55.5 0.0 collective-permute-done.19.refs_0_
  55.5 1.2 %collective-permute-start.15 = (bf16[32,1536]{1,0:T(8,128)(2,1)S(1)}, bf16[32,1536]{1,0:T(8,128)(2,1)S(1)}, u32[]{:S(2)}, u32[]{:S(2)}) collective-permute-start(bf16[32,1536]{1,0:T(8,128)(2,1)S(1)} %add_convert_fusion.refs_0_), channel_id=1, source_target_pairs={{0,1},{1,0},{8,9},{9,8},{16,17},{17,16},{24,25},{25,24},{2,3},{3,2... | collective-permute-start | bytes 294920 | tf_op jit(solution)/shard_map/ppermute | solution.py:106
  56.7 0.0 collective-permute-done.21.refs_2_
  56.7 0.0 collective-permute-done.20.refs_1_
  56.7 0.1 shard_map.101
  56.9 1.5 %collective-permute-start.24 = (bf16[2,192,128]{2,1,0:T(8,128)(2,1)S(1)}, bf16[2,192,128]{2,1,0:T(8,128)(2,1)S(1)}, u32[]{:S(2)}, u32[]{:S(2)}) collective-permute-start(bf16[2,192,128]{2,1,0:T(8,128)(2,1)S(1)} %get-tuple-element.91), channel_id=1, source_target_pairs={{6,2},{0,4},{7,3},{1,5},{14,10},{8,12},{15,11},{9,13},{22,18},{16,... | collective-permute-start | bytes 294920 | tf_op jit(solution)/shard_map/ppermute | solution.py:87
  58.4 0.7 %collective-permute-start.23 = (bf16[2,192,128]{2,1,0:T(8,128)(2,1)S(1)}, bf16[2,192,128]{2,1,0:T(8,128)(2,1)S(1)}, u32[]{:S(2)}, u32[]{:S(2)}) collective-permute-start(bf16[2,192,128]{2,1,0:T(8,128)(2,1)S(1)} %get-tuple-element.91), channel_id=1, source_target_pairs={{4,2},{2,4},{5,3},{3,5},{12,10},{10,12},{13,11},{11,13},{20,18},{1... | collective-permute-start | bytes 294920 | tf_op jit(solution)/shard_map/ppermute | solution.py:87
  59.0 0.5 collective-permute-done.17.refs_3_
  59.6 0.7 %collective-permute-start.22 = (bf16[2,192,128]{2,1,0:T(8,128)(2,1)S(1)}, bf16[2,192,128]{2,1,0:T(8,128)(2,1)S(1)}, u32[]{:S(2)}, u32[]{:S(2)}) collective-permute-start(bf16[2,192,128]{2,1,0:T(8,128)(2,1)S(1)} %get-tuple-element.90), channel_id=1, source_target_pairs={{0,2},{2,0},{4,6},{6,4},{1,3},{3,1},{5,7},{7,5},{8,10},{10,8},{12,... | collective-permute-start | bytes 294920 | tf_op jit(solution)/shard_map/ppermute | solution.py:87
  60.3 0.3 collective-permute-done.15.refs_1_
  60.6 0.1 collective-permute-start.18
  60.7 1.5 %shard_map.99.refs_1_ = f32[128,3072]{1,0:T(8,128)} custom-call(s32[3]{0:T(128)S(1)} %pad_add_fusion.place, bf16[144,1536]{1,0:T(8,128)(2,1)S(1)} %shard_map.98.part), custom_call_target="tpu_custom_call" | custom-call | flops 10000000000 | bytes 100000000 | tf_op jit(solution)/shard_map/pallas_call | solution.py:309
  62.2 0.3 collective-permute-done.18.part
  62.5 1.5 %shard_map.100 = (f32[128,3072]{1,0:T(8,128)}, bf16[192,128]{1,0:T(8,128)(2,1)}) custom-call(s32[3]{0:T(128)S(1)} %pad_add_fusion.place, bf16[144,1536]{1,0:T(8,128)(2,1)S(1)} %collective-permute-done.18.part, f32[192,128]{1,0:T(8,128)S(1)} %get-tuple-element.82.refs_0_, f32[128,3072]{1,0:T(8,128)} %shard_map.99.refs_1_), custom_call_target="tpu_custom_call", output_to_operand_aliasing={{0}: (3, {})} | custom-call | flops 10000000000 | bytes 100000000 | tf_op jit(solution)/shard_map/pallas_call | solution.py:309
  64.0 0.2 collective-permute-done.22.refs_0_
  64.2 0.0 collective-permute-done.24.refs_2_
  64.2 0.0 collective-permute-done.23.refs_1_
  64.2 0.7 %shard_map.102 = (bf16[192,128]{1,0:T(8,128)(2,1)}, bf16[192,128]{1,0:T(8,128)(2,1)}) custom-call(f32[2,192,128]{2,1,0:T(8,128)S(1)} %get-tuple-element.89.own_grad, bf16[2,192,128]{2,1,0:T(8,128)(2,1)S(1)} %collective-permute-done.22.refs_0_, bf16[2,192,128]{2,1,0:T(8,128)(2,1)S(1)} %collective-permute-done.23.refs_1_, ...), custom_call_target="tpu_custom_call" | custom-call | flops 10000000000 | bytes 100000000 | tf_op jit(solution)/shard_map/pallas_call | solution.py:586
  (12 shorter events, 0.2 us)
Async XLA Ops:
  0.6 17.4 %copy-start.2 = (bf16[4,6,8,128]{3,2,1,0:T(8,128)(2,1)S(1)}, bf16[4,6,8,128]{3,2,1,0:T(8,128)(2,1)}, u32[]{:S(2)}) copy-start(bf16[4,6,8,128]{3,2,1,0:T(8,128)(2,1)} %param.5) | copy-start | bytes 147460
  0.6 21.9 %copy-start = (bf16[128,3072]{1,0:T(8,128)(2,1)S(1)}, bf16[128,3072]{1,0:T(8,128)(2,1)}, u32[]{:S(2)}) copy-start(bf16[128,3072]{1,0:T(8,128)(2,1)} %weight.1) | copy-start | bytes 2359300
  1.6 9.8 %collective-permute-start.2 = (bf16[2,192,128]{2,1,0:T(8,128)(2,1)S(1)}, bf16[2,192,128]{2,1,0:T(8,128)(2,1)S(1)}, u32[]{:S(2)}, u32[]{:S(2)}) collective-permute-start(bf16[2,192,128]{2,1,0:T(8,128)(2,1)S(1)} %get-tuple-element.96), channel_id=1, source_target_pairs={{2,4},{4,2},{3,5},{5,3},{10,12},{12,10},{11,13},{13,11},{18,20},{2... | collective-permute-start | bytes 294920 | tf_op jit(solution)/shard_map/ppermute | solution.py:65
  2.2 10.5 %collective-permute-start.1 = (bf16[2,192,128]{2,1,0:T(8,128)(2,1)S(1)}, bf16[2,192,128]{2,1,0:T(8,128)(2,1)S(1)}, u32[]{:S(2)}, u32[]{:S(2)}) collective-permute-start(bf16[2,192,128]{2,1,0:T(8,128)(2,1)S(1)} %get-tuple-element.96), channel_id=1, source_target_pairs={{2,6},{4,0},{3,7},{5,1},{10,14},{12,8},{11,15},{13,9},{18,22},{20,... | collective-permute-start | bytes 294920 | tf_op jit(solution)/shard_map/ppermute | solution.py:65
  3.5 10.6 %collective-permute-start = (bf16[2,192,128]{2,1,0:T(8,128)(2,1)S(1)}, bf16[2,192,128]{2,1,0:T(8,128)(2,1)S(1)}, u32[]{:S(2)}, u32[]{:S(2)}) collective-permute-start(bf16[2,192,128]{2,1,0:T(8,128)(2,1)S(1)} %get-tuple-element.96), channel_id=1, source_target_pairs={{2,0},{0,2},{6,4},{4,6},{3,1},{1,3},{7,5},{5,7},{10,8},{8,10},{14,... | collective-permute-start | bytes 294920 | tf_op jit(solution)/shard_map/ppermute | solution.py:65
  9.8 4.6 %collective-permute-start.3 = (bf16[1,2,192,128]{3,2,1,0:T(8,128)(2,1)S(1)}, bf16[1,2,192,128]{3,2,1,0:T(8,128)(2,1)S(1)}, u32[]{:S(2)}, u32[]{:S(2)}) collective-permute-start(bf16[1,2,192,128]{3,2,1,0:T(8,128)(2,1)S(1)} %get-tuple-element.95), channel_id=1, source_target_pairs={{0,1},{1,0},{2,3},{3,2},{4,5},{5,4},{6,7},{7,6},{8,9},{9,8},{10,11... | collective-permute-start | bytes 294920 | tf_op jit(solution)/shard_map/ppermute | solution.py:414
  14.5 12.1 %collective-permute-start.7 = (bf16[3,2,192,128]{3,2,1,0:T(8,128)(2,1)S(1)}, bf16[3,2,192,128]{3,2,1,0:T(8,128)(2,1)S(1)}, u32[]{:S(2)}, u32[]{:S(2)}) collective-permute-start(bf16[3,2,192,128]{3,2,1,0:T(8,128)(2,1)S(1)} %pad_maximum_fusion.refs_0_), channel_id=1, source_target_pairs={{16,1},{17,0},{8,25},{9,24},{18,3},{19,2},{10,27},{11,26},{20,5},{... | collective-permute-start | bytes 884744 | tf_op jit(solution)/shard_map/ppermute | solution.py:423
  15.7 10.8 %collective-permute-start.6 = (bf16[3,2,192,128]{3,2,1,0:T(8,128)(2,1)S(1)}, bf16[3,2,192,128]{3,2,1,0:T(8,128)(2,1)S(1)}, u32[]{:S(2)}, u32[]{:S(2)}) collective-permute-start(bf16[3,2,192,128]{3,2,1,0:T(8,128)(2,1)S(1)} %pad_maximum_fusion.refs_0_), channel_id=1, source_target_pairs={{16,8},{8,16},{17,9},{9,17},{18,10},{10,18},{19,11},{11,19},{20,12... | collective-permute-start | bytes 884744 | tf_op jit(solution)/shard_map/ppermute | solution.py:422
  16.4 10.1 %collective-permute-start.5 = (bf16[2,2,192,128]{3,2,1,0:T(8,128)(2,1)S(1)}, bf16[2,2,192,128]{3,2,1,0:T(8,128)(2,1)S(1)}, u32[]{:S(2)}, u32[]{:S(2)}) collective-permute-start(bf16[2,2,192,128]{3,2,1,0:T(8,128)(2,1)S(1)} %pad_maximum_fusion.1), channel_id=1, source_target_pairs={{0,1},{1,0},{2,3},{3,2},{4,5},{5,4},{6,7},{7,6},{8,9},{9,8},{10,11... | collective-permute-start | bytes 589832 | tf_op jit(solution)/shard_map/ppermute | solution.py:420
  18.0 4.5 %collective-permute-start.4 = (bf16[192,128]{1,0:T(8,128)(2,1)S(1)}, bf16[192,128]{1,0:T(8,128)(2,1)S(1)}, u32[]{:S(2)}, u32[]{:S(2)}) collective-permute-start(bf16[192,128]{1,0:T(8,128)(2,1)S(1)} %bitcast.19), channel_id=1, source_target_pairs={{0,8},{8,0},{16,24},{24,16},{1,9},{9,1},{17,25},{25,17},{2,10},{10... | collective-permute-start | bytes 147464 | tf_op jit(solution)/shard_map/ppermute | solution.py:106
  22.6 1.3 %copy-start.1 = (bf16[4,6,8,3072]{3,2,1,0:T(8,128)(2,1)S(1)}, bf16[4,6,8,3072]{3,2,1,0:T(8,128)(2,1)}, u32[]{:S(2)}) copy-start(bf16[4,6,8,3072]{3,2,1,0:T(8,128)(2,1)} %param.9) | copy-start | bytes 3538948
  26.5 3.4 %collective-permute-start.9 = (bf16[192,1664]{1,0:T(8,128)(2,1)S(1)}, bf16[192,1664]{1,0:T(8,128)(2,1)S(1)}, u32[]{:S(2)}, u32[]{:S(2)}) collective-permute-start(bf16[192,1664]{1,0:T(8,128)(2,1)S(1)} %get-tuple-element.61), channel_id=1, source_target_pairs={{0,8},{8,0},{16,24},{24,16},{1,9},{9,1},{17,25},{25,17},{2,10},{10... | collective-permute-start | bytes 1916936 | tf_op jit(solution)/shard_map/ppermute | solution.py:106
  28.5 1.5 %collective-permute-start.8 = (f32[136,384]{1,0:T(8,128)S(1)}, f32[136,384]{1,0:T(8,128)S(1)}, u32[]{:S(2)}, u32[]{:S(2)}) collective-permute-start(f32[136,384]{1,0:T(8,128)S(1)} %shard_map.94.mine), channel_id=1, source_target_pairs={{0,8},{8,0},{16,24},{24,16},{1,9},{9,1},{17,25},{25,17},{2,10},{10... | collective-permute-start | bytes 626696 | tf_op jit(solution)/shard_map/ppermute | solution.py:106
  31.1 7.2 %collective-permute-start.10 = (bf16[32,1536]{1,0:T(8,128)(2,1)S(1)}, bf16[32,1536]{1,0:T(8,128)(2,1)S(1)}, u32[]{:S(2)}, u32[]{:S(2)}) collective-permute-start(bf16[32,1536]{1,0:T(8,128)(2,1)S(1)} %get-tuple-element.68), channel_id=1, source_target_pairs={{0,1},{1,0},{8,9},{9,8},{16,17},{17,16},{24,25},{25,24},{2,3},{3,2... | collective-permute-start | bytes 294920 | tf_op jit(solution)/shard_map/ppermute | solution.py:106
  32.7 5.6 %collective-permute-start.11 = (bf16[32,1536]{1,0:T(8,128)(2,1)S(1)}, bf16[32,1536]{1,0:T(8,128)(2,1)S(1)}, u32[]{:S(2)}, u32[]{:S(2)}) collective-permute-start(bf16[32,1536]{1,0:T(8,128)(2,1)S(1)} %get-tuple-element.69), channel_id=1, source_target_pairs={{0,16},{1,17},{8,24},{9,25},{16,0},{17,1},{24,8},{25,9},{2,18},{3,... | collective-permute-start | bytes 294920 | tf_op jit(solution)/shard_map/ppermute | solution.py:106
  32.9 6.5 %collective-permute-start.12 = (bf16[32,1536]{1,0:T(8,128)(2,1)S(1)}, bf16[32,1536]{1,0:T(8,128)(2,1)S(1)}, u32[]{:S(2)}, u32[]{:S(2)}) collective-permute-start(bf16[32,1536]{1,0:T(8,128)(2,1)S(1)} %get-tuple-element.70), channel_id=1, source_target_pairs={{0,17},{1,16},{8,25},{9,24},{16,1},{17,0},{24,9},{25,8},{2,19},{3,... | collective-permute-start | bytes 294920 | tf_op jit(solution)/shard_map/ppermute | solution.py:106
  36.7 18.8 %collective-permute-start.19 = (bf16[3,2,192,128]{3,2,1,0:T(8,128)(2,1)S(1)}, bf16[3,2,192,128]{3,2,1,0:T(8,128)(2,1)S(1)}, u32[]{:S(2)}, u32[]{:S(2)}) collective-permute-start(bf16[3,2,192,128]{3,2,1,0:T(8,128)(2,1)S(1)} %get-tuple-element.86), channel_id=1, source_target_pairs={{0,1},{1,0},{2,3},{3,2},{4,5},{5,4},{6,7},{7,6},{8,9},{9,8},{10,11... | collective-permute-start | bytes 884744 | tf_op jit(solution)/shard_map/ppermute | solution.py:547
  39.4 5.5 %collective-permute-start.13 = (bf16[32,1536]{1,0:T(8,128)(2,1)S(1)}, bf16[32,1536]{1,0:T(8,128)(2,1)S(1)}, u32[]{:S(2)}, u32[]{:S(2)}) collective-permute-start(bf16[32,1536]{1,0:T(8,128)(2,1)S(1)} %add_convert_fusion.2), channel_id=1, source_target_pairs={{0,2},{2,0},{4,6},{6,4},{1,3},{3,1},{5,7},{7,5},{8,10},{10,8},{12,... | collective-permute-start | bytes 294920 | tf_op jit(solution)/shard_map/ppermute | solution.py:106
  41.0 15.7 %collective-permute-start.21 = (bf16[3,2,192,128]{3,2,1,0:T(8,128)(2,1)S(1)}, bf16[3,2,192,128]{3,2,1,0:T(8,128)(2,1)S(1)}, u32[]{:S(2)}, u32[]{:S(2)}) collective-permute-start(bf16[3,2,192,128]{3,2,1,0:T(8,128)(2,1)S(1)} %get-tuple-element.87), channel_id=1, source_target_pairs={{1,16},{0,17},{25,8},{24,9},{3,18},{2,19},{27,10},{26,11},{5,20},{... | collective-permute-start | bytes 884744 | tf_op jit(solution)/shard_map/ppermute | solution.py:549
  44.2 12.5 %collective-permute-start.20 = (bf16[3,2,192,128]{3,2,1,0:T(8,128)(2,1)S(1)}, bf16[3,2,192,128]{3,2,1,0:T(8,128)(2,1)S(1)}, u32[]{:S(2)}, u32[]{:S(2)}) collective-permute-start(bf16[3,2,192,128]{3,2,1,0:T(8,128)(2,1)S(1)} %get-tuple-element.87), channel_id=1, source_target_pairs={{8,16},{16,8},{9,17},{17,9},{10,18},{18,10},{11,19},{19,11},{12,20... | collective-permute-start | bytes 884744 | tf_op jit(solution)/shard_map/ppermute | solution.py:548
  44.9 8.2 %collective-permute-start.14 = (bf16[32,1536]{1,0:T(8,128)(2,1)S(1)}, bf16[32,1536]{1,0:T(8,128)(2,1)S(1)}, u32[]{:S(2)}, u32[]{:S(2)}) collective-permute-start(bf16[32,1536]{1,0:T(8,128)(2,1)S(1)} %add_convert_fusion.1), channel_id=1, source_target_pairs={{0,4},{2,6},{4,0},{6,2},{1,5},{3,7},{5,1},{7,3},{8,12},{10,14},{12... | collective-permute-start | bytes 294920 | tf_op jit(solution)/shard_map/ppermute | solution.py:106
  53.2 6.4 %collective-permute-start.17 = (bf16[32,1536]{1,0:T(8,128)(2,1)S(1)}, bf16[32,1536]{1,0:T(8,128)(2,1)S(1)}, u32[]{:S(2)}, u32[]{:S(2)}) collective-permute-start(bf16[32,1536]{1,0:T(8,128)(2,1)S(1)} %add_convert_fusion.refs_0_), channel_id=1, source_target_pairs={{0,17},{1,16},{8,25},{9,24},{16,1},{17,0},{24,9},{25,8},{2,19},{3,... | collective-permute-start | bytes 294920 | tf_op jit(solution)/shard_map/ppermute | solution.py:106
  53.3 7.1 %collective-permute-start.16 = (bf16[32,1536]{1,0:T(8,128)(2,1)S(1)}, bf16[32,1536]{1,0:T(8,128)(2,1)S(1)}, u32[]{:S(2)}, u32[]{:S(2)}) collective-permute-start(bf16[32,1536]{1,0:T(8,128)(2,1)S(1)} %add_convert_fusion.refs_0_), channel_id=1, source_target_pairs={{0,16},{1,17},{8,24},{9,25},{16,0},{17,1},{24,8},{25,9},{2,18},{3,... | collective-permute-start | bytes 294920 | tf_op jit(solution)/shard_map/ppermute | solution.py:106
  55.5 5.1 %collective-permute-start.15 = (bf16[32,1536]{1,0:T(8,128)(2,1)S(1)}, bf16[32,1536]{1,0:T(8,128)(2,1)S(1)}, u32[]{:S(2)}, u32[]{:S(2)}) collective-permute-start(bf16[32,1536]{1,0:T(8,128)(2,1)S(1)} %add_convert_fusion.refs_0_), channel_id=1, source_target_pairs={{0,1},{1,0},{8,9},{9,8},{16,17},{17,16},{24,25},{25,24},{2,3},{3,2... | collective-permute-start | bytes 294920 | tf_op jit(solution)/shard_map/ppermute | solution.py:106
  56.9 7.3 %collective-permute-start.24 = (bf16[2,192,128]{2,1,0:T(8,128)(2,1)S(1)}, bf16[2,192,128]{2,1,0:T(8,128)(2,1)S(1)}, u32[]{:S(2)}, u32[]{:S(2)}) collective-permute-start(bf16[2,192,128]{2,1,0:T(8,128)(2,1)S(1)} %get-tuple-element.91), channel_id=1, source_target_pairs={{6,2},{0,4},{7,3},{1,5},{14,10},{8,12},{15,11},{9,13},{22,18},{16,... | collective-permute-start | bytes 294920 | tf_op jit(solution)/shard_map/ppermute | solution.py:87
  58.4 5.8 %collective-permute-start.23 = (bf16[2,192,128]{2,1,0:T(8,128)(2,1)S(1)}, bf16[2,192,128]{2,1,0:T(8,128)(2,1)S(1)}, u32[]{:S(2)}, u32[]{:S(2)}) collective-permute-start(bf16[2,192,128]{2,1,0:T(8,128)(2,1)S(1)} %get-tuple-element.91), channel_id=1, source_target_pairs={{4,2},{2,4},{5,3},{3,5},{12,10},{10,12},{13,11},{11,13},{20,18},{1... | collective-permute-start | bytes 294920 | tf_op jit(solution)/shard_map/ppermute | solution.py:87
  59.6 4.6 %collective-permute-start.22 = (bf16[2,192,128]{2,1,0:T(8,128)(2,1)S(1)}, bf16[2,192,128]{2,1,0:T(8,128)(2,1)S(1)}, u32[]{:S(2)}, u32[]{:S(2)}) collective-permute-start(bf16[2,192,128]{2,1,0:T(8,128)(2,1)S(1)} %get-tuple-element.90), channel_id=1, source_target_pairs={{0,2},{2,0},{4,6},{6,4},{1,3},{3,1},{5,7},{7,5},{8,10},{10,8},{12,... | collective-permute-start | bytes 294920 | tf_op jit(solution)/shard_map/ppermute | solution.py:87
  60.6 1.9 %collective-permute-start.18 = (bf16[144,1536]{1,0:T(8,128)(2,1)S(1)}, bf16[144,1536]{1,0:T(8,128)(2,1)S(1)}, u32[]{:S(2)}, u32[]{:S(2)}) collective-permute-start(bf16[144,1536]{1,0:T(8,128)(2,1)S(1)} %shard_map.98.part), channel_id=1, source_target_pairs={{0,8},{8,0},{16,24},{24,16},{1,9},{9,1},{17,25},{25,17},{2,10},{10... | collective-permute-start | bytes 1327112 | tf_op jit(solution)/shard_map/ppermute | solution.py:106

commit v11 on v8

--- a/solution.py
+++ b/solution.py
@@ -227,7 +227,8 @@
 ):
     groups, rest = split_groups(layout, refs)
     count = 1 + max(out for out, _ in targets)
-    outs, (query_own, query_other, both_grads, both_out) = rest[:count], rest[count:]
+    outs, rest = rest[:count], rest[count:]
+    both_grads = rest[-1]
     tile, dim = grad_rows.shape
     columns = payload.shape[1]
     both_tiles(place, grad_rows[...], payload[:, columns - dim :], both_grads)
@@ -252,7 +253,12 @@
         query_grad = query_grad + lax.dot_general(
             keys, score_grad, (((0,), (0,)), ((), ())), preferred_element_type=jnp.float32
         )
-    both_out[...] = query_grad.T * inv_root
+    rest[0][...] = query_grad
+
+
+def query_kernel(inv_root, place, query_grad, query_own, query_other, both_out):
+    tile, dim = query_own.shape
+    both_out[...] = query_grad[...].T * inv_root
     query_own[...] = both_out[pl.ds(pl.multiple_of(place[0] * tile, tile), tile), :]
     other = both_out[pl.ds(pl.multiple_of((1 - place[0]) * tile, tile), tile), :]
     other = other.astype(jnp.bfloat16)
@@ -489,24 +495,35 @@
         cost=cost_of(4 * tile * head_dim * half, 4 * tile * model_dim),
     )
     stats, attended, *terms = merged
-    back = kernel_call(
+    *near_grads, far_grad, query_grad = kernel_call(
         functools.partial(backward_kernel, inv_root, layout, targets),
         (place, stats, both_queries, payload, grad_rows, *blocks),
         (
             shaped(*grad_shapes[0], kind=jnp.float32),
             *[shaped(*shape) for shape in grad_shapes[1:]],
+            shaped(head_dim, 2 * tile, kind=jnp.float32),
+        ),
+        scratch=(pltpu.VMEM((2 * tile, head_dim), jnp.bfloat16),),
+        cost=cost_of(5 * product, 2 * moved),
+    )
+    if small:
+        terms[0], query_grad = lax.optimization_barrier((terms[0], query_grad))
+        part = sum_over_plane(terms)
+        part, query_grad = lax.optimization_barrier((part, query_grad))
+    query_own, query_other = kernel_call(
+        functools.partial(query_kernel, inv_root),
+        (place, query_grad),
+        (
             shaped(tile, head_dim, kind=jnp.float32),
             shaped(tile * head_dim // half, half),
         ),
-        scratch=(
-            pltpu.VMEM((2 * tile, head_dim), jnp.bfloat16),
-            pltpu.VMEM((2 * tile, head_dim), jnp.float32),
-        ),
-        cost=cost_of(5 * product, 2 * moved),
+        scratch=(pltpu.VMEM((2 * tile, head_dim), jnp.float32),),
+        cost=cost_of(10**10, 10**8),
     )
     if small:
-        terms[0], *back = lax.optimization_barrier((terms[0], *back))
-        part = sum_over_plane(terms)
+        far_grad, query_own = lax.optimization_barrier((far_grad, query_own))
+    back = (*near_grads, far_grad, query_own, query_other)
+    if small:
         other = flip(part, ("height",), (1,))
         part = (part.astype(jnp.float32) + other.astype(jnp.float32)).astype(jnp.bfloat16)
         part, attended = lax.optimization_barrier((part, attended))

time: 65.7 us -> 64.4 us (0.980)
  starting transfers between devices: 37 us -> 35.1 us
    ppermute x3, starting transfers between devices: 5.21 us -> 2.9 us  [returned(): arrived.append(lax.ppermute(outgoing, axis, [(p, s) for s, p in route]))]
    pallas_call x3 -> x4, Pallas kernels: 4.85 us -> 5.43 us  [kernel_call(): pl.pallas_call(kernel, out_shape=outs, in_specs=[SMEM] + [VMEM] * (len(op...]
  transfers between devices with their start and end apart: 25 -> 25, of which waited for: 10 -> 12; matrix products, arithmetic and copies ran while one was open for 3% -> 3% of each run, Pallas kernels for 13% -> 15%
where the time goes in v11:
time: 64.4 us; the launch traced here: 64.1 us
  starting transfers between devices  35.1 us (55%)
  waiting for transfers between devices  13.1 us (20%)
  Pallas kernels  11.1 us (17%)
  matrix products  1.47 us (2%)
  local copies, waits for them, and re-layouts  1.28 us (2%)
  other arithmetic  1.17 us (2%)
  between operations  0.86 us (1%)
    ppermute x12, starting transfers between devices, flip(): return lax.ppermute(block, axes, route)  13.4 us
    ppermute x12, waiting for transfers between devices, flip(): return lax.ppermute(block, axes, route)  8.88 us
    ppermute x3, starting transfers between devices, fetch(): arrived = [lax.ppermute(block, axis, route) for route in routes]  8.25 us
    pallas_call x4, Pallas kernels, kernel_call(): pl.pallas_call(kernel, out_shape=outs, in_specs=[SMEM] + [VMEM] * (len(op...  5.43 us
    ppermute x1, starting transfers between devices, body(): lax.ppermute(far_grad, ('frame', 'width'), [(p, s) for s, p in cross])  3.2 us
    pallas_call x2, Pallas kernels, assemble(): pl.pallas_call(functools.partial(assemble_kernel, flipped, rows), out_sha...  2.95 us
    ppermute x3, starting transfers between devices, returned(): arrived.append(lax.ppermute(outgoing, axis, [(p, s) for s, p in route]))  2.9 us
    ppermute x3, waiting for transfers between devices, fetch(): arrived = [lax.ppermute(block, axis, route) for route in routes]  2.79 us
  transfers between devices with their start and end apart: 25, of which 12 were waited for; matrix products, arithmetic and copies ran while one was open for 3% of the time, Pallas kernels for 15%

profile of v11, /device:TPU:0, one launch (start us, length us, event | category | flops | bytes accessed | tf_op | source)
XLA Modules:
  0.0 64.1 jit_solution(17269938521112595235)
XLA Ops:
  0.7 0.9 %fusion = (bf16[1,2,192,128]{3,2,1,0:T(8,128)(2,1)S(1)}, bf16[2,192,128]{2,1,0:T(8,128)(2,1)S(1)}) fusion(bf16[1,192,128]{2,1,0:T(8,128)(2,1)} %bitcast.24, bf16[1,192,128]{2,1,0:T(8,128)(2,1)} %bitcast.25), kind=kLoop, calls=%fused_computation.9 | loop fusion | flops 49152 | bytes 294912 | tf_op jit(solution)/shard_map/stack | solution.py:416
  1.6 0.7 %collective-permute-start.2 = (bf16[2,192,128]{2,1,0:T(8,128)(2,1)S(1)}, bf16[2,192,128]{2,1,0:T(8,128)(2,1)S(1)}, u32[]{:S(2)}, u32[]{:S(2)}) collective-permute-start(bf16[2,192,128]{2,1,0:T(8,128)(2,1)S(1)} %get-tuple-element.100), channel_id=1, source_target_pairs={{2,4},{4,2},{3,5},{5,3},{10,12},{12,10},{11,13},{13,11},{18,20},{2... | collective-permute-start | bytes 294920 | tf_op jit(solution)/shard_map/ppermute | solution.py:65
  2.2 1.3 %collective-permute-start.1 = (bf16[2,192,128]{2,1,0:T(8,128)(2,1)S(1)}, bf16[2,192,128]{2,1,0:T(8,128)(2,1)S(1)}, u32[]{:S(2)}, u32[]{:S(2)}) collective-permute-start(bf16[2,192,128]{2,1,0:T(8,128)(2,1)S(1)} %get-tuple-element.100), channel_id=1, source_target_pairs={{2,6},{4,0},{3,7},{5,1},{10,14},{12,8},{11,15},{13,9},{18,22},{20,... | collective-permute-start | bytes 294920 | tf_op jit(solution)/shard_map/ppermute | solution.py:65
  3.5 6.3 %collective-permute-start = (bf16[2,192,128]{2,1,0:T(8,128)(2,1)S(1)}, bf16[2,192,128]{2,1,0:T(8,128)(2,1)S(1)}, u32[]{:S(2)}, u32[]{:S(2)}) collective-permute-start(bf16[2,192,128]{2,1,0:T(8,128)(2,1)S(1)} %get-tuple-element.100), channel_id=1, source_target_pairs={{2,0},{0,2},{6,4},{4,6},{3,1},{1,3},{7,5},{5,7},{10,8},{8,10},{14,... | collective-permute-start | bytes 294920 | tf_op jit(solution)/shard_map/ppermute | solution.py:65
  9.8 1.5 %collective-permute-start.3 = (bf16[1,2,192,128]{3,2,1,0:T(8,128)(2,1)S(1)}, bf16[1,2,192,128]{3,2,1,0:T(8,128)(2,1)S(1)}, u32[]{:S(2)}, u32[]{:S(2)}) collective-permute-start(bf16[1,2,192,128]{3,2,1,0:T(8,128)(2,1)S(1)} %get-tuple-element.99), channel_id=1, source_target_pairs={{0,1},{1,0},{2,3},{3,2},{4,5},{5,4},{6,7},{7,6},{8,9},{9,8},{10,11... | collective-permute-start | bytes 294920 | tf_op jit(solution)/shard_map/ppermute | solution.py:414
  11.4 0.0 collective-permute-done.2
  11.4 1.4 %collective-permute-done.1 = bf16[2,192,128]{2,1,0:T(8,128)(2,1)S(1)} collective-permute-done((bf16[2,192,128]{2,1,0:T(8,128)(2,1)S(1)}, bf16[2,192,128]{2,1,0:T(8,128)(2,1)S(1)}, u32[]{:S(2)}, u32[]{:S(2)}) %collective-permute-start.1) | collective-permute-done | bytes 98336 | tf_op jit(solution)/shard_map/ppermute | solution.py:65
  12.8 1.4 %collective-permute-done = bf16[2,192,128]{2,1,0:T(8,128)(2,1)S(1)} collective-permute-done((bf16[2,192,128]{2,1,0:T(8,128)(2,1)S(1)}, bf16[2,192,128]{2,1,0:T(8,128)(2,1)S(1)}, u32[]{:S(2)}, u32[]{:S(2)}) %collective-permute-start) | collective-permute-done | bytes 98336 | tf_op jit(solution)/shard_map/ppermute | solution.py:65
  14.2 0.2 collective-permute-done.3.refs_0_.refs_1_
  14.5 1.3 %collective-permute-start.7 = (bf16[3,2,192,128]{3,2,1,0:T(8,128)(2,1)S(1)}, bf16[3,2,192,128]{3,2,1,0:T(8,128)(2,1)S(1)}, u32[]{:S(2)}, u32[]{:S(2)}) collective-permute-start(bf16[3,2,192,128]{3,2,1,0:T(8,128)(2,1)S(1)} %pad_maximum_fusion.refs_0_), channel_id=1, source_target_pairs={{16,1},{17,0},{8,25},{9,24},{18,3},{19,2},{10,27},{11,26},{20,5},{... | collective-permute-start | bytes 884744 | tf_op jit(solution)/shard_map/ppermute | solution.py:423
  15.7 0.7 %collective-permute-start.6 = (bf16[3,2,192,128]{3,2,1,0:T(8,128)(2,1)S(1)}, bf16[3,2,192,128]{3,2,1,0:T(8,128)(2,1)S(1)}, u32[]{:S(2)}, u32[]{:S(2)}) collective-permute-start(bf16[3,2,192,128]{3,2,1,0:T(8,128)(2,1)S(1)} %pad_maximum_fusion.refs_0_), channel_id=1, source_target_pairs={{16,8},{8,16},{17,9},{9,17},{18,10},{10,18},{19,11},{11,19},{20,12... | collective-permute-start | bytes 884744 | tf_op jit(solution)/shard_map/ppermute | solution.py:422
  16.4 1.6 %collective-permute-start.5 = (bf16[2,2,192,128]{3,2,1,0:T(8,128)(2,1)S(1)}, bf16[2,2,192,128]{3,2,1,0:T(8,128)(2,1)S(1)}, u32[]{:S(2)}, u32[]{:S(2)}) collective-permute-start(bf16[2,2,192,128]{3,2,1,0:T(8,128)(2,1)S(1)} %pad_maximum_fusion.1), channel_id=1, source_target_pairs={{0,1},{1,0},{2,3},{3,2},{4,5},{5,4},{6,7},{7,6},{8,9},{9,8},{10,11... | collective-permute-start | bytes 589832 | tf_op jit(solution)/shard_map/ppermute | solution.py:420
  18.0 3.7 %collective-permute-start.4 = (bf16[192,128]{1,0:T(8,128)(2,1)S(1)}, bf16[192,128]{1,0:T(8,128)(2,1)S(1)}, u32[]{:S(2)}, u32[]{:S(2)}) collective-permute-start(bf16[192,128]{1,0:T(8,128)(2,1)S(1)} %bitcast.19), channel_id=1, source_target_pairs={{0,8},{8,0},{16,24},{24,16},{1,9},{9,1},{17,25},{25,17},{2,10},{10... | collective-permute-start | bytes 147464 | tf_op jit(solution)/shard_map/ppermute | solution.py:106
  21.7 0.1 pad_add_fusion.place
  21.8 0.8 %collective-permute-done.4.queries_other = bf16[192,128]{1,0:T(8,128)(2,1)S(1)} collective-permute-done((bf16[192,128]{1,0:T(8,128)(2,1)S(1)}, bf16[192,128]{1,0:T(8,128)(2,1)S(1)}, u32[]{:S(2)}, u32[]{:S(2)}) %collective-permute-start.4) | collective-permute-done | bytes 49184 | tf_op jit(solution)/shard_map/ppermute | solution.py:106
  22.6 1.3 %copy-done.1 = bf16[4,6,8,3072]{3,2,1,0:T(8,128)(2,1)S(1)} copy-done((bf16[4,6,8,3072]{3,2,1,0:T(8,128)(2,1)S(1)}, bf16[4,6,8,3072]{3,2,1,0:T(8,128)(2,1)}, u32[]{:S(2)}) %copy-start.1) | copy-done | bytes 1179672
  23.8 1.0 %shard_map.92 = (bf16[192,1664]{1,0:T(8,128)(2,1)S(1)}, bf16[192,1536]{1,0:T(8,128)(2,1)S(1)}, bf16[192,128]{1,0:T(8,128)(2,1)S(1)}, bf16[384,128]{1,0:T(8,128)(2,1)S(1)}) custom-call(s32[3]{0:T(128)S(1)} %pad_add_fusion.place, bf16[192,128]{1,0:T(8,128)(2,1)S(1)} %bitcast.20, bf16[192,128]{1,0:T(8,128)(2,1)S(1)} %collective-permute-done.4.queries_other, ...), custom_call_target="tpu_custom_call" | custom-call | flops 150994944 | bytes 2359296 | tf_op jit(solution)/shard_map/pallas_call | solution.py:351
  24.9 0.7 %shard_map.93.refs_4_ = f32[136,384]{1,0:T(8,128)S(1)} custom-call(bf16[384,128]{1,0:T(8,128)(2,1)S(1)} %get-tuple-element.53.both_queries, bf16[3,2,192,128]{3,2,1,0:T(8,128)(2,1)S(1)} %pad_maximum_fusion.refs_0_), custom_call_target="tpu_custom_call" | custom-call | flops 113246208 | bytes 393216 | tf_op jit(solution)/shard_map/pallas_call | solution.py:465
  25.6 0.9 %collective-permute-done.5.refs_1_.refs_2_ = bf16[2,2,192,128]{3,2,1,0:T(8,128)(2,1)S(1)} collective-permute-done((bf16[2,2,192,128]{3,2,1,0:T(8,128)(2,1)S(1)}, bf16[2,2,192,128]{3,2,1,0:T(8,128)(2,1)S(1)}, u32[]{:S(2)}, u32[]{:S(2)}) %collective-permute-start.5) | collective-permute-done | bytes 196640 | tf_op jit(solution)/shard_map/ppermute | solution.py:420
  26.5 0.0 collective-permute-done.7.refs_3_.refs_4_
  26.5 0.0 collective-permute-done.6.refs_2_.refs_3_
  26.5 0.7 %collective-permute-start.9 = (bf16[192,1664]{1,0:T(8,128)(2,1)S(1)}, bf16[192,1664]{1,0:T(8,128)(2,1)S(1)}, u32[]{:S(2)}, u32[]{:S(2)}) collective-permute-start(bf16[192,1664]{1,0:T(8,128)(2,1)S(1)} %get-tuple-element.63), channel_id=1, source_target_pairs={{0,8},{8,0},{16,24},{24,16},{1,9},{9,1},{17,25},{25,17},{2,10},{10... | collective-permute-start | bytes 1916936 | tf_op jit(solution)/shard_map/ppermute | solution.py:106
  27.3 1.2 %shard_map.94.mine = f32[136,384]{1,0:T(8,128)S(1)} custom-call(bf16[384,128]{1,0:T(8,128)(2,1)S(1)} %get-tuple-element.53.both_queries, bf16[1,2,192,128]{3,2,1,0:T(8,128)(2,1)S(1)} %collective-permute-done.3.refs_0_.refs_1_, bf16[2,2,192,128]{3,2,1,0:T(8,128)(2,1)S(1)} %collective-permute-done.5.refs_1_.refs_2_, ...), custom_call_target="tpu_custom_call" | custom-call | flops 226492416 | bytes 786432 | tf_op jit(solution)/shard_map/pallas_call | solution.py:465
  28.5 0.1 collective-permute-start.8
  28.5 1.4 %collective-permute-done.8.theirs = f32[136,384]{1,0:T(8,128)S(1)} collective-permute-done((f32[136,384]{1,0:T(8,128)S(1)}, f32[136,384]{1,0:T(8,128)S(1)}, u32[]{:S(2)}, u32[]{:S(2)}) %collective-permute-start.8) | collective-permute-done | bytes 208928 | tf_op jit(solution)/shard_map/ppermute | solution.py:106
  30.0 0.0 collective-permute-done.9.payload
  30.0 1.1 %shard_map.95 = (f32[8,384]{1,0:T(8,128)S(1)}, bf16[192,128]{1,0:T(8,128)(2,1)S(1)}, bf16[32,1536]{1,0:T(8,128)(2,1)S(1)}, bf16[32,1536]{1,0:T(8,128)(2,1)S(1)},...) custom-call(s32[3]{0:T(128)S(1)} %pad_add_fusion.place, f32[136,384]{1,0:T(8,128)S(1)} %shard_map.94.mine, ...), custom_call_target="tpu_custom_call" | custom-call | flops 150994944 | bytes 2359296 | tf_op jit(solution)/shard_map/pallas_call | solution.py:351
  31.1 1.6 %collective-permute-start.10 = (bf16[32,1536]{1,0:T(8,128)(2,1)S(1)}, bf16[32,1536]{1,0:T(8,128)(2,1)S(1)}, u32[]{:S(2)}, u32[]{:S(2)}) collective-permute-start(bf16[32,1536]{1,0:T(8,128)(2,1)S(1)} %get-tuple-element.70), channel_id=1, source_target_pairs={{0,1},{1,0},{8,9},{9,8},{16,17},{17,16},{24,25},{25,24},{2,3},{3,2... | collective-permute-start | bytes 294920 | tf_op jit(solution)/shard_map/ppermute | solution.py:106
  32.7 0.2 collective-permute-start.11
  32.9 1.8 %collective-permute-start.12 = (bf16[32,1536]{1,0:T(8,128)(2,1)S(1)}, bf16[32,1536]{1,0:T(8,128)(2,1)S(1)}, u32[]{:S(2)}, u32[]{:S(2)}) collective-permute-start(bf16[32,1536]{1,0:T(8,128)(2,1)S(1)} %get-tuple-element.72), channel_id=1, source_target_pairs={{0,17},{1,16},{8,25},{9,24},{16,1},{17,0},{24,9},{25,8},{2,19},{3,... | collective-permute-start | bytes 294920 | tf_op jit(solution)/shard_map/ppermute | solution.py:106
  34.7 2.6 %shard_map.96 = (f32[3,2,192,128]{3,2,1,0:T(8,128)S(1)}, bf16[3,2,192,128]{3,2,1,0:T(8,128)(2,1)S(1)}, bf16[3,2,192,128]{3,2,1,0:T(8,128)(2,1)S(1)}, f32[128,384]{1,0:T(8,128)S(1)}) custom-call(s32[3]{0:T(128)S(1)} %pad_add_fusion.place, f32[8,384]{1,0:T(8,128)S(1)} %get-tuple-element.67.stats, bf16[384,128]{1,0:T(8,128)(2,1)S(1)} %get-tuple-element.53.both_queries, ...), custom_call_target="tpu_custom_call" | custom-call | flops 849346560 | bytes 2359296 | tf_op jit(solution)/shard_map/pallas_call | solution.py:351
  37.3 1.6 %collective-permute-start.19 = (bf16[3,2,192,128]{3,2,1,0:T(8,128)(2,1)S(1)}, bf16[3,2,192,128]{3,2,1,0:T(8,128)(2,1)S(1)}, u32[]{:S(2)}, u32[]{:S(2)}) collective-permute-start(bf16[3,2,192,128]{3,2,1,0:T(8,128)(2,1)S(1)} %get-tuple-element.90), channel_id=1, source_target_pairs={{0,1},{1,0},{2,3},{3,2},{4,5},{5,4},{6,7},{7,6},{8,9},{9,8},{10,11... | collective-permute-start | bytes 884744 | tf_op jit(solution)/shard_map/ppermute | solution.py:542
  38.9 0.0 collective-permute-done.10
  38.9 0.0 collective-permute-done.11
  38.9 0.4 collective-permute-done.12
  39.3 0.1 add_convert_fusion.2
  39.4 0.1 collective-permute-start.13
  39.5 0.7 %shard_map.97 = (f32[192,128]{1,0:T(8,128)S(1)}, bf16[16,1536]{1,0:T(8,128)(2,1)S(1)}) custom-call(s32[3]{0:T(128)S(1)} %pad_add_fusion.place, f32[128,384]{1,0:T(8,128)S(1)} %get-tuple-element.82.query_grad), custom_call_target="tpu_custom_call" | custom-call | flops 10000000000 | bytes 100000000 | tf_op jit(solution)/shard_map/pallas_call | solution.py:351
  40.2 3.2 %collective-permute-start.21 = (bf16[3,2,192,128]{3,2,1,0:T(8,128)(2,1)S(1)}, bf16[3,2,192,128]{3,2,1,0:T(8,128)(2,1)S(1)}, u32[]{:S(2)}, u32[]{:S(2)}) collective-permute-start(bf16[3,2,192,128]{3,2,1,0:T(8,128)(2,1)S(1)} %get-tuple-element.91), channel_id=1, source_target_pairs={{1,16},{0,17},{25,8},{24,9},{3,18},{2,19},{27,10},{26,11},{5,20},{... | collective-permute-start | bytes 884744 | tf_op jit(solution)/shard_map/ppermute | solution.py:544
  43.4 0.7 %collective-permute-start.20 = (bf16[3,2,192,128]{3,2,1,0:T(8,128)(2,1)S(1)}, bf16[3,2,192,128]{3,2,1,0:T(8,128)(2,1)S(1)}, u32[]{:S(2)}, u32[]{:S(2)}) collective-permute-start(bf16[3,2,192,128]{3,2,1,0:T(8,128)(2,1)S(1)} %get-tuple-element.91), channel_id=1, source_target_pairs={{8,16},{16,8},{9,17},{17,9},{10,18},{18,10},{11,19},{19,11},{12,20... | collective-permute-start | bytes 884744 | tf_op jit(solution)/shard_map/ppermute | solution.py:543
  44.1 0.0 collective-permute-done.13
  44.1 1.7 %collective-permute-start.14 = (bf16[32,1536]{1,0:T(8,128)(2,1)S(1)}, bf16[32,1536]{1,0:T(8,128)(2,1)S(1)}, u32[]{:S(2)}, u32[]{:S(2)}) collective-permute-start(bf16[32,1536]{1,0:T(8,128)(2,1)S(1)} %add_convert_fusion.1), channel_id=1, source_target_pairs={{0,4},{2,6},{4,0},{6,2},{1,5},{3,7},{5,1},{7,3},{8,12},{10,14},{12... | collective-permute-start | bytes 294920 | tf_op jit(solution)/shard_map/ppermute | solution.py:106
  45.8 1.5 %convolution_convert_fusion = bf16[192,3072]{1,0:T(8,128)(2,1)} fusion(bf16[192,128]{1,0:T(8,128)(2,1)S(1)} %get-tuple-element.77, bf16[128,3072]{1,0:T(8,128)(2,1)S(1)} %copy-done), kind=kOutput, calls=%fused_computation | convolution fusion | flops 151584768 | bytes 2015232 | tf_op jit(solution)/shard_map/dot_general | solution.py:535
  47.3 5.1 %collective-permute-done.14 = bf16[32,1536]{1,0:T(8,128)(2,1)S(1)} collective-permute-done((bf16[32,1536]{1,0:T(8,128)(2,1)S(1)}, bf16[32,1536]{1,0:T(8,128)(2,1)S(1)}, u32[]{:S(2)}, u32[]{:S(2)}) %collective-permute-start.14) | collective-permute-done | bytes 98336 | tf_op jit(solution)/shard_map/ppermute | solution.py:106
  52.4 0.1 collective-permute-start.17
  52.4 2.4 %collective-permute-start.16 = (bf16[32,1536]{1,0:T(8,128)(2,1)S(1)}, bf16[32,1536]{1,0:T(8,128)(2,1)S(1)}, u32[]{:S(2)}, u32[]{:S(2)}) collective-permute-start(bf16[32,1536]{1,0:T(8,128)(2,1)S(1)} %add_convert_fusion.refs_0_), channel_id=1, source_target_pairs={{0,16},{1,17},{8,24},{9,25},{16,0},{17,1},{24,8},{25,9},{2,18},{3,... | collective-permute-start | bytes 294920 | tf_op jit(solution)/shard_map/ppermute | solution.py:106
  54.8 0.0 collective-permute-done.19.refs_0_
  54.8 1.1 %collective-permute-start.15 = (bf16[32,1536]{1,0:T(8,128)(2,1)S(1)}, bf16[32,1536]{1,0:T(8,128)(2,1)S(1)}, u32[]{:S(2)}, u32[]{:S(2)}) collective-permute-start(bf16[32,1536]{1,0:T(8,128)(2,1)S(1)} %add_convert_fusion.refs_0_), channel_id=1, source_target_pairs={{0,1},{1,0},{8,9},{9,8},{16,17},{17,16},{24,25},{25,24},{2,3},{3,2... | collective-permute-start | bytes 294920 | tf_op jit(solution)/shard_map/ppermute | solution.py:106
  55.9 0.0 collective-permute-done.21.refs_2_
  55.9 0.0 collective-permute-done.20.refs_1_
  55.9 0.1 shard_map.101
  56.1 1.5 %collective-permute-start.24 = (bf16[2,192,128]{2,1,0:T(8,128)(2,1)S(1)}, bf16[2,192,128]{2,1,0:T(8,128)(2,1)S(1)}, u32[]{:S(2)}, u32[]{:S(2)}) collective-permute-start(bf16[2,192,128]{2,1,0:T(8,128)(2,1)S(1)} %get-tuple-element.95), channel_id=1, source_target_pairs={{6,2},{0,4},{7,3},{1,5},{14,10},{8,12},{15,11},{9,13},{22,18},{16,... | collective-permute-start | bytes 294920 | tf_op jit(solution)/shard_map/ppermute | solution.py:87
  57.6 0.7 %collective-permute-start.23 = (bf16[2,192,128]{2,1,0:T(8,128)(2,1)S(1)}, bf16[2,192,128]{2,1,0:T(8,128)(2,1)S(1)}, u32[]{:S(2)}, u32[]{:S(2)}) collective-permute-start(bf16[2,192,128]{2,1,0:T(8,128)(2,1)S(1)} %get-tuple-element.95), channel_id=1, source_target_pairs={{4,2},{2,4},{5,3},{3,5},{12,10},{10,12},{13,11},{11,13},{20,18},{1... | collective-permute-start | bytes 294920 | tf_op jit(solution)/shard_map/ppermute | solution.py:87
  58.2 0.5 collective-permute-done.17.refs_3_
  58.8 0.7 %collective-permute-start.22 = (bf16[2,192,128]{2,1,0:T(8,128)(2,1)S(1)}, bf16[2,192,128]{2,1,0:T(8,128)(2,1)S(1)}, u32[]{:S(2)}, u32[]{:S(2)}) collective-permute-start(bf16[2,192,128]{2,1,0:T(8,128)(2,1)S(1)} %get-tuple-element.94), channel_id=1, source_target_pairs={{0,2},{2,0},{4,6},{6,4},{1,3},{3,1},{5,7},{7,5},{8,10},{10,8},{12,... | collective-permute-start | bytes 294920 | tf_op jit(solution)/shard_map/ppermute | solution.py:87
  59.5 0.0 collective-permute-done.16.refs_2_
  59.5 0.3 collective-permute-done.15.refs_1_
  59.8 0.1 collective-permute-start.18
  59.9 1.5 %shard_map.99.refs_1_ = f32[128,3072]{1,0:T(8,128)} custom-call(s32[3]{0:T(128)S(1)} %pad_add_fusion.place, bf16[144,1536]{1,0:T(8,128)(2,1)S(1)} %shard_map.98.part), custom_call_target="tpu_custom_call" | custom-call | flops 10000000000 | bytes 100000000 | tf_op jit(solution)/shard_map/pallas_call | solution.py:309
  61.4 0.3 collective-permute-done.18.part
  61.7 1.5 %shard_map.100 = (f32[128,3072]{1,0:T(8,128)}, bf16[192,128]{1,0:T(8,128)(2,1)}) custom-call(s32[3]{0:T(128)S(1)} %pad_add_fusion.place, bf16[144,1536]{1,0:T(8,128)(2,1)S(1)} %collective-permute-done.18.part, f32[192,128]{1,0:T(8,128)S(1)} %get-tuple-element.86.refs_0_, f32[128,3072]{1,0:T(8,128)} %shard_map.99.refs_1_), custom_call_target="tpu_custom_call", output_to_operand_aliasing={{0}: (3, {})} | custom-call | flops 10000000000 | bytes 100000000 | tf_op jit(solution)/shard_map/pallas_call | solution.py:309
  63.2 0.2 collective-permute-done.22.refs_0_
  63.4 0.0 collective-permute-done.24.refs_2_
  63.4 0.7 %shard_map.102 = (bf16[192,128]{1,0:T(8,128)(2,1)}, bf16[192,128]{1,0:T(8,128)(2,1)}) custom-call(f32[2,192,128]{2,1,0:T(8,128)S(1)} %get-tuple-element.93.own_grad, bf16[2,192,128]{2,1,0:T(8,128)(2,1)S(1)} %collective-permute-done.22.refs_0_, bf16[2,192,128]{2,1,0:T(8,128)(2,1)S(1)} %collective-permute-done.23.refs_1_, ...), custom_call_target="tpu_custom_call" | custom-call | flops 10000000000 | bytes 100000000 | tf_op jit(solution)/shard_map/pallas_call | solution.py:581
  (12 shorter events, 0.2 us)
Async XLA Ops:
  0.6 17.4 %copy-start.2 = (bf16[4,6,8,128]{3,2,1,0:T(8,128)(2,1)S(1)}, bf16[4,6,8,128]{3,2,1,0:T(8,128)(2,1)}, u32[]{:S(2)}) copy-start(bf16[4,6,8,128]{3,2,1,0:T(8,128)(2,1)} %param.5) | copy-start | bytes 147460
  0.6 21.9 %copy-start = (bf16[128,3072]{1,0:T(8,128)(2,1)S(1)}, bf16[128,3072]{1,0:T(8,128)(2,1)}, u32[]{:S(2)}) copy-start(bf16[128,3072]{1,0:T(8,128)(2,1)} %weight.1) | copy-start | bytes 2359300
  1.6 9.8 %collective-permute-start.2 = (bf16[2,192,128]{2,1,0:T(8,128)(2,1)S(1)}, bf16[2,192,128]{2,1,0:T(8,128)(2,1)S(1)}, u32[]{:S(2)}, u32[]{:S(2)}) collective-permute-start(bf16[2,192,128]{2,1,0:T(8,128)(2,1)S(1)} %get-tuple-element.100), channel_id=1, source_target_pairs={{2,4},{4,2},{3,5},{5,3},{10,12},{12,10},{11,13},{13,11},{18,20},{2... | collective-permute-start | bytes 294920 | tf_op jit(solution)/shard_map/ppermute | solution.py:65
  2.2 10.5 %collective-permute-start.1 = (bf16[2,192,128]{2,1,0:T(8,128)(2,1)S(1)}, bf16[2,192,128]{2,1,0:T(8,128)(2,1)S(1)}, u32[]{:S(2)}, u32[]{:S(2)}) collective-permute-start(bf16[2,192,128]{2,1,0:T(8,128)(2,1)S(1)} %get-tuple-element.100), channel_id=1, source_target_pairs={{2,6},{4,0},{3,7},{5,1},{10,14},{12,8},{11,15},{13,9},{18,22},{20,... | collective-permute-start | bytes 294920 | tf_op jit(solution)/shard_map/ppermute | solution.py:65
  3.5 10.6 %collective-permute-start = (bf16[2,192,128]{2,1,0:T(8,128)(2,1)S(1)}, bf16[2,192,128]{2,1,0:T(8,128)(2,1)S(1)}, u32[]{:S(2)}, u32[]{:S(2)}) collective-permute-start(bf16[2,192,128]{2,1,0:T(8,128)(2,1)S(1)} %get-tuple-element.100), channel_id=1, source_target_pairs={{2,0},{0,2},{6,4},{4,6},{3,1},{1,3},{7,5},{5,7},{10,8},{8,10},{14,... | collective-permute-start | bytes 294920 | tf_op jit(solution)/shard_map/ppermute | solution.py:65
  9.8 4.6 %collective-permute-start.3 = (bf16[1,2,192,128]{3,2,1,0:T(8,128)(2,1)S(1)}, bf16[1,2,192,128]{3,2,1,0:T(8,128)(2,1)S(1)}, u32[]{:S(2)}, u32[]{:S(2)}) collective-permute-start(bf16[1,2,192,128]{3,2,1,0:T(8,128)(2,1)S(1)} %get-tuple-element.99), channel_id=1, source_target_pairs={{0,1},{1,0},{2,3},{3,2},{4,5},{5,4},{6,7},{7,6},{8,9},{9,8},{10,11... | collective-permute-start | bytes 294920 | tf_op jit(solution)/shard_map/ppermute | solution.py:414
  14.5 12.1 %collective-permute-start.7 = (bf16[3,2,192,128]{3,2,1,0:T(8,128)(2,1)S(1)}, bf16[3,2,192,128]{3,2,1,0:T(8,128)(2,1)S(1)}, u32[]{:S(2)}, u32[]{:S(2)}) collective-permute-start(bf16[3,2,192,128]{3,2,1,0:T(8,128)(2,1)S(1)} %pad_maximum_fusion.refs_0_), channel_id=1, source_target_pairs={{16,1},{17,0},{8,25},{9,24},{18,3},{19,2},{10,27},{11,26},{20,5},{... | collective-permute-start | bytes 884744 | tf_op jit(solution)/shard_map/ppermute | solution.py:423
  15.7 10.8 %collective-permute-start.6 = (bf16[3,2,192,128]{3,2,1,0:T(8,128)(2,1)S(1)}, bf16[3,2,192,128]{3,2,1,0:T(8,128)(2,1)S(1)}, u32[]{:S(2)}, u32[]{:S(2)}) collective-permute-start(bf16[3,2,192,128]{3,2,1,0:T(8,128)(2,1)S(1)} %pad_maximum_fusion.refs_0_), channel_id=1, source_target_pairs={{16,8},{8,16},{17,9},{9,17},{18,10},{10,18},{19,11},{11,19},{20,12... | collective-permute-start | bytes 884744 | tf_op jit(solution)/shard_map/ppermute | solution.py:422
  16.4 10.1 %collective-permute-start.5 = (bf16[2,2,192,128]{3,2,1,0:T(8,128)(2,1)S(1)}, bf16[2,2,192,128]{3,2,1,0:T(8,128)(2,1)S(1)}, u32[]{:S(2)}, u32[]{:S(2)}) collective-permute-start(bf16[2,2,192,128]{3,2,1,0:T(8,128)(2,1)S(1)} %pad_maximum_fusion.1), channel_id=1, source_target_pairs={{0,1},{1,0},{2,3},{3,2},{4,5},{5,4},{6,7},{7,6},{8,9},{9,8},{10,11... | collective-permute-start | bytes 589832 | tf_op jit(solution)/shard_map/ppermute | solution.py:420
  18.0 4.5 %collective-permute-start.4 = (bf16[192,128]{1,0:T(8,128)(2,1)S(1)}, bf16[192,128]{1,0:T(8,128)(2,1)S(1)}, u32[]{:S(2)}, u32[]{:S(2)}) collective-permute-start(bf16[192,128]{1,0:T(8,128)(2,1)S(1)} %bitcast.19), channel_id=1, source_target_pairs={{0,8},{8,0},{16,24},{24,16},{1,9},{9,1},{17,25},{25,17},{2,10},{10... | collective-permute-start | bytes 147464 | tf_op jit(solution)/shard_map/ppermute | solution.py:106
  22.6 1.3 %copy-start.1 = (bf16[4,6,8,3072]{3,2,1,0:T(8,128)(2,1)S(1)}, bf16[4,6,8,3072]{3,2,1,0:T(8,128)(2,1)}, u32[]{:S(2)}) copy-start(bf16[4,6,8,3072]{3,2,1,0:T(8,128)(2,1)} %param.9) | copy-start | bytes 3538948
  26.5 3.4 %collective-permute-start.9 = (bf16[192,1664]{1,0:T(8,128)(2,1)S(1)}, bf16[192,1664]{1,0:T(8,128)(2,1)S(1)}, u32[]{:S(2)}, u32[]{:S(2)}) collective-permute-start(bf16[192,1664]{1,0:T(8,128)(2,1)S(1)} %get-tuple-element.63), channel_id=1, source_target_pairs={{0,8},{8,0},{16,24},{24,16},{1,9},{9,1},{17,25},{25,17},{2,10},{10... | collective-permute-start | bytes 1916936 | tf_op jit(solution)/shard_map/ppermute | solution.py:106
  28.5 1.5 %collective-permute-start.8 = (f32[136,384]{1,0:T(8,128)S(1)}, f32[136,384]{1,0:T(8,128)S(1)}, u32[]{:S(2)}, u32[]{:S(2)}) collective-permute-start(f32[136,384]{1,0:T(8,128)S(1)} %shard_map.94.mine), channel_id=1, source_target_pairs={{0,8},{8,0},{16,24},{24,16},{1,9},{9,1},{17,25},{25,17},{2,10},{10... | collective-permute-start | bytes 626696 | tf_op jit(solution)/shard_map/ppermute | solution.py:106
  31.1 7.8 %collective-permute-start.10 = (bf16[32,1536]{1,0:T(8,128)(2,1)S(1)}, bf16[32,1536]{1,0:T(8,128)(2,1)S(1)}, u32[]{:S(2)}, u32[]{:S(2)}) collective-permute-start(bf16[32,1536]{1,0:T(8,128)(2,1)S(1)} %get-tuple-element.70), channel_id=1, source_target_pairs={{0,1},{1,0},{8,9},{9,8},{16,17},{17,16},{24,25},{25,24},{2,3},{3,2... | collective-permute-start | bytes 294920 | tf_op jit(solution)/shard_map/ppermute | solution.py:106
  32.7 6.2 %collective-permute-start.11 = (bf16[32,1536]{1,0:T(8,128)(2,1)S(1)}, bf16[32,1536]{1,0:T(8,128)(2,1)S(1)}, u32[]{:S(2)}, u32[]{:S(2)}) collective-permute-start(bf16[32,1536]{1,0:T(8,128)(2,1)S(1)} %get-tuple-element.71), channel_id=1, source_target_pairs={{0,16},{1,17},{8,24},{9,25},{16,0},{17,1},{24,8},{25,9},{2,18},{3,... | collective-permute-start | bytes 294920 | tf_op jit(solution)/shard_map/ppermute | solution.py:106
  32.9 6.4 %collective-permute-start.12 = (bf16[32,1536]{1,0:T(8,128)(2,1)S(1)}, bf16[32,1536]{1,0:T(8,128)(2,1)S(1)}, u32[]{:S(2)}, u32[]{:S(2)}) collective-permute-start(bf16[32,1536]{1,0:T(8,128)(2,1)S(1)} %get-tuple-element.72), channel_id=1, source_target_pairs={{0,17},{1,16},{8,25},{9,24},{16,1},{17,0},{24,9},{25,8},{2,19},{3,... | collective-permute-start | bytes 294920 | tf_op jit(solution)/shard_map/ppermute | solution.py:106
  37.3 17.5 %collective-permute-start.19 = (bf16[3,2,192,128]{3,2,1,0:T(8,128)(2,1)S(1)}, bf16[3,2,192,128]{3,2,1,0:T(8,128)(2,1)S(1)}, u32[]{:S(2)}, u32[]{:S(2)}) collective-permute-start(bf16[3,2,192,128]{3,2,1,0:T(8,128)(2,1)S(1)} %get-tuple-element.90), channel_id=1, source_target_pairs={{0,1},{1,0},{2,3},{3,2},{4,5},{5,4},{6,7},{7,6},{8,9},{9,8},{10,11... | collective-permute-start | bytes 884744 | tf_op jit(solution)/shard_map/ppermute | solution.py:542
  39.4 4.7 %collective-permute-start.13 = (bf16[32,1536]{1,0:T(8,128)(2,1)S(1)}, bf16[32,1536]{1,0:T(8,128)(2,1)S(1)}, u32[]{:S(2)}, u32[]{:S(2)}) collective-permute-start(bf16[32,1536]{1,0:T(8,128)(2,1)S(1)} %add_convert_fusion.2), channel_id=1, source_target_pairs={{0,2},{2,0},{4,6},{6,4},{1,3},{3,1},{5,7},{7,5},{8,10},{10,8},{12,... | collective-permute-start | bytes 294920 | tf_op jit(solution)/shard_map/ppermute | solution.py:106
  40.2 15.7 %collective-permute-start.21 = (bf16[3,2,192,128]{3,2,1,0:T(8,128)(2,1)S(1)}, bf16[3,2,192,128]{3,2,1,0:T(8,128)(2,1)S(1)}, u32[]{:S(2)}, u32[]{:S(2)}) collective-permute-start(bf16[3,2,192,128]{3,2,1,0:T(8,128)(2,1)S(1)} %get-tuple-element.91), channel_id=1, source_target_pairs={{1,16},{0,17},{25,8},{24,9},{3,18},{2,19},{27,10},{26,11},{5,20},{... | collective-permute-start | bytes 884744 | tf_op jit(solution)/shard_map/ppermute | solution.py:544
  43.4 12.5 %collective-permute-start.20 = (bf16[3,2,192,128]{3,2,1,0:T(8,128)(2,1)S(1)}, bf16[3,2,192,128]{3,2,1,0:T(8,128)(2,1)S(1)}, u32[]{:S(2)}, u32[]{:S(2)}) collective-permute-start(bf16[3,2,192,128]{3,2,1,0:T(8,128)(2,1)S(1)} %get-tuple-element.91), channel_id=1, source_target_pairs={{8,16},{16,8},{9,17},{17,9},{10,18},{18,10},{11,19},{19,11},{12,20... | collective-permute-start | bytes 884744 | tf_op jit(solution)/shard_map/ppermute | solution.py:543
  44.1 8.2 %collective-permute-start.14 = (bf16[32,1536]{1,0:T(8,128)(2,1)S(1)}, bf16[32,1536]{1,0:T(8,128)(2,1)S(1)}, u32[]{:S(2)}, u32[]{:S(2)}) collective-permute-start(bf16[32,1536]{1,0:T(8,128)(2,1)S(1)} %add_convert_fusion.1), channel_id=1, source_target_pairs={{0,4},{2,6},{4,0},{6,2},{1,5},{3,7},{5,1},{7,3},{8,12},{10,14},{12... | collective-permute-start | bytes 294920 | tf_op jit(solution)/shard_map/ppermute | solution.py:106
  52.4 6.4 %collective-permute-start.17 = (bf16[32,1536]{1,0:T(8,128)(2,1)S(1)}, bf16[32,1536]{1,0:T(8,128)(2,1)S(1)}, u32[]{:S(2)}, u32[]{:S(2)}) collective-permute-start(bf16[32,1536]{1,0:T(8,128)(2,1)S(1)} %add_convert_fusion.refs_0_), channel_id=1, source_target_pairs={{0,17},{1,16},{8,25},{9,24},{16,1},{17,0},{24,9},{25,8},{2,19},{3,... | collective-permute-start | bytes 294920 | tf_op jit(solution)/shard_map/ppermute | solution.py:106
  52.4 7.1 %collective-permute-start.16 = (bf16[32,1536]{1,0:T(8,128)(2,1)S(1)}, bf16[32,1536]{1,0:T(8,128)(2,1)S(1)}, u32[]{:S(2)}, u32[]{:S(2)}) collective-permute-start(bf16[32,1536]{1,0:T(8,128)(2,1)S(1)} %add_convert_fusion.refs_0_), channel_id=1, source_target_pairs={{0,16},{1,17},{8,24},{9,25},{16,0},{17,1},{24,8},{25,9},{2,18},{3,... | collective-permute-start | bytes 294920 | tf_op jit(solution)/shard_map/ppermute | solution.py:106
  54.8 5.0 %collective-permute-start.15 = (bf16[32,1536]{1,0:T(8,128)(2,1)S(1)}, bf16[32,1536]{1,0:T(8,128)(2,1)S(1)}, u32[]{:S(2)}, u32[]{:S(2)}) collective-permute-start(bf16[32,1536]{1,0:T(8,128)(2,1)S(1)} %add_convert_fusion.refs_0_), channel_id=1, source_target_pairs={{0,1},{1,0},{8,9},{9,8},{16,17},{17,16},{24,25},{25,24},{2,3},{3,2... | collective-permute-start | bytes 294920 | tf_op jit(solution)/shard_map/ppermute | solution.py:106
  56.1 7.3 %collective-permute-start.24 = (bf16[2,192,128]{2,1,0:T(8,128)(2,1)S(1)}, bf16[2,192,128]{2,1,0:T(8,128)(2,1)S(1)}, u32[]{:S(2)}, u32[]{:S(2)}) collective-permute-start(bf16[2,192,128]{2,1,0:T(8,128)(2,1)S(1)} %get-tuple-element.95), channel_id=1, source_target_pairs={{6,2},{0,4},{7,3},{1,5},{14,10},{8,12},{15,11},{9,13},{22,18},{16,... | collective-permute-start | bytes 294920 | tf_op jit(solution)/shard_map/ppermute | solution.py:87
  57.6 5.8 %collective-permute-start.23 = (bf16[2,192,128]{2,1,0:T(8,128)(2,1)S(1)}, bf16[2,192,128]{2,1,0:T(8,128)(2,1)S(1)}, u32[]{:S(2)}, u32[]{:S(2)}) collective-permute-start(bf16[2,192,128]{2,1,0:T(8,128)(2,1)S(1)} %get-tuple-element.95), channel_id=1, source_target_pairs={{4,2},{2,4},{5,3},{3,5},{12,10},{10,12},{13,11},{11,13},{20,18},{1... | collective-permute-start | bytes 294920 | tf_op jit(solution)/shard_map/ppermute | solution.py:87
  58.8 4.6 %collective-permute-start.22 = (bf16[2,192,128]{2,1,0:T(8,128)(2,1)S(1)}, bf16[2,192,128]{2,1,0:T(8,128)(2,1)S(1)}, u32[]{:S(2)}, u32[]{:S(2)}) collective-permute-start(bf16[2,192,128]{2,1,0:T(8,128)(2,1)S(1)} %get-tuple-element.94), channel_id=1, source_target_pairs={{0,2},{2,0},{4,6},{6,4},{1,3},{3,1},{5,7},{7,5},{8,10},{10,8},{12,... | collective-permute-start | bytes 294920 | tf_op jit(solution)/shard_map/ppermute | solution.py:87
  59.8 1.9 %collective-permute-start.18 = (bf16[144,1536]{1,0:T(8,128)(2,1)S(1)}, bf16[144,1536]{1,0:T(8,128)(2,1)S(1)}, u32[]{:S(2)}, u32[]{:S(2)}) collective-permute-start(bf16[144,1536]{1,0:T(8,128)(2,1)S(1)} %shard_map.98.part), channel_id=1, source_target_pairs={{0,8},{8,0},{16,24},{24,16},{1,9},{9,1},{17,25},{25,17},{2,10},{10... | collective-permute-start | bytes 1327112 | tf_op jit(solution)/shard_map/ppermute | solution.py:106

commit v12 on v11

--- a/solution.py
+++ b/solution.py
@@ -173,11 +173,10 @@
 
 
 def merge_kernel(scale, plane, place, mine, theirs, payload, grads_half, grad_rows, *refs):
-    stats, attended_own, terms, both_grads, both_attended, term_rows = (
+    stats, attended_own, terms, both_attended, term_rows = (
         refs[0],
         refs[1],
-        refs[2:-3],
-        refs[-3],
+        refs[2:-2],
         refs[-2],
         refs[-1],
     )
@@ -190,10 +189,8 @@
     total = share_a * sum_a + share_b * sum_b
     mixed = mine[:dim, :] * (share_a / total) + theirs[:dim, :] * (share_b / total)
     attended_t = mixed.astype(jnp.bfloat16).astype(jnp.float32)
-    both_tiles(place, grad_rows[...], payload[:, half:], both_grads)
-    row_dot = jnp.sum(both_grads[...].astype(jnp.float32).T * attended_t, axis=0, keepdims=True)
-    row = lax.broadcasted_iota(jnp.int32, (STAT_ROWS, mixed.shape[1]), 0)
-    stats[...] = jnp.where(row == 0, top + jnp.log(total), row_dot)
+    stats[:dim, :] = attended_t
+    stats[dim:, :] = jnp.broadcast_to(top + jnp.log(total), (STAT_ROWS, mixed.shape[1]))
     both_attended[...] = attended_t.T.astype(jnp.bfloat16)
     rows_mine = both_attended[pl.ds(pl.multiple_of(place[0] * tile, tile), tile), :]
     rows_theirs = both_attended[pl.ds(pl.multiple_of((1 - place[0]) * tile, tile), tile), :]
@@ -233,7 +230,8 @@
     columns = payload.shape[1]
     both_tiles(place, grad_rows[...], payload[:, columns - dim :], both_grads)
     query_rows, out_grads = both_queries[...], both_grads[...]
-    level, row_dot = stats[0:1, :], stats[1:2, :]
+    level = stats[dim : dim + 1, :]
+    row_dot = jnp.sum(out_grads.astype(jnp.float32).T * stats[:dim, :], axis=0, keepdims=True)
     along = (((1,), (1,)), ((), ()))
     query_grad = jnp.zeros((dim, 2 * tile), jnp.float32)
     for group, (target, first) in zip(groups, targets):
@@ -327,10 +325,10 @@
 
 
 def pack_kernel(*refs):
-    start = 0
+    end = refs[-1].shape[0]
     for piece in refs[:-1]:
-        refs[-1][start : start + piece.shape[0], :] = piece[...]
-        start += piece.shape[0]
+        refs[-1][end - piece.shape[0] : end, :] = piece[...]
+        end -= piece.shape[0]
 
 
 def combine_kernel(column, *refs):
@@ -375,7 +373,7 @@
 
 def join_sum(part, query_own, query_other, place):
     plane = len(part)
-    pieces = part + [query_other]
+    pieces = [query_other] + part[::-1]
     part = pl.pallas_call(
         pack_kernel,
         out_shape=shaped(sum(p.shape[0] for p in pieces), pieces[0].shape[1]),
@@ -483,12 +481,11 @@
         functools.partial(merge_kernel, 1.0 / float(math.prod(extents)), plane),
         (place, partial, partial_other, payload, grads_half, grad_rows),
         (
-            shaped(STAT_ROWS, 2 * tile, kind=jnp.float32),
+            shaped(head_dim + STAT_ROWS, 2 * tile, kind=jnp.float32),
             shaped(tile, head_dim),
             *[shaped(head_dim // plane, half)] * chunks,
         ),
         scratch=(
-            pltpu.VMEM((2 * tile, head_dim), jnp.bfloat16),
             pltpu.VMEM((2 * tile, head_dim), jnp.bfloat16),
             pltpu.VMEM((head_dim, half), jnp.float32),
         ),

time: 64.4 us -> 64.5 us (level)
  transfers between devices with their start and end apart: 25 -> 25, of which waited for: 12 -> 10; matrix products, arithmetic and copies ran while one was open for 3% -> 3% of each run, Pallas kernels for 15% -> 15%
where the time goes in v12:
time: 64.5 us; the launch traced here: 64.1 us
  starting transfers between devices  35.6 us (55%)
  waiting for transfers between devices  12.6 us (20%)
  Pallas kernels  11.1 us (17%)
  matrix products  1.47 us (2%)
  local copies, waits for them, and re-layouts  1.28 us (2%)
  other arithmetic  1.16 us (2%)
  between operations  0.89 us (1%)
    ppermute x12, starting transfers between devices, flip(): return lax.ppermute(block, axes, route)  13.4 us
    ppermute x12, waiting for transfers between devices, flip(): return lax.ppermute(block, axes, route)  8.66 us
    ppermute x3, starting transfers between devices, fetch(): arrived = [lax.ppermute(block, axis, route) for route in routes]  8.25 us
    pallas_call x4, Pallas kernels, kernel_call(): pl.pallas_call(kernel, out_shape=outs, in_specs=[SMEM] + [VMEM] * (len(op...  5.43 us
    ppermute x3, starting transfers between devices, returned(): arrived.append(lax.ppermute(outgoing, axis, [(p, s) for s, p in route]))  3.42 us
    ppermute x1, starting transfers between devices, body(): lax.ppermute(far_grad, ('frame', 'width'), [(p, s) for s, p in cross])  3.2 us
    pallas_call x2, Pallas kernels, assemble(): pl.pallas_call(functools.partial(assemble_kernel, flipped, rows), out_sha...  2.95 us
    ppermute x3, waiting for transfers between devices, fetch(): arrived = [lax.ppermute(block, axis, route) for route in routes]  2.79 us
  transfers between devices with their start and end apart: 25, of which 10 were waited for; matrix products, arithmetic and copies ran while one was open for 3% of the time, Pallas kernels for 15%

profile of v12, /device:TPU:0, one launch (start us, length us, event | category | flops | bytes accessed | tf_op | source)
XLA Modules:
  0.0 64.1 jit_solution(14254749993343292569)
XLA Ops:
  0.7 0.9 %fusion = (bf16[1,2,192,128]{3,2,1,0:T(8,128)(2,1)S(1)}, bf16[2,192,128]{2,1,0:T(8,128)(2,1)S(1)}) fusion(bf16[1,192,128]{2,1,0:T(8,128)(2,1)} %bitcast.24, bf16[1,192,128]{2,1,0:T(8,128)(2,1)} %bitcast.25), kind=kLoop, calls=%fused_computation.9 | loop fusion | flops 49152 | bytes 294912 | tf_op jit(solution)/shard_map/stack | solution.py:414
  1.6 0.7 %collective-permute-start.2 = (bf16[2,192,128]{2,1,0:T(8,128)(2,1)S(1)}, bf16[2,192,128]{2,1,0:T(8,128)(2,1)S(1)}, u32[]{:S(2)}, u32[]{:S(2)}) collective-permute-start(bf16[2,192,128]{2,1,0:T(8,128)(2,1)S(1)} %get-tuple-element.100), channel_id=1, source_target_pairs={{2,4},{4,2},{3,5},{5,3},{10,12},{12,10},{11,13},{13,11},{18,20},{2... | collective-permute-start | bytes 294920 | tf_op jit(solution)/shard_map/ppermute | solution.py:65
  2.2 1.3 %collective-permute-start.1 = (bf16[2,192,128]{2,1,0:T(8,128)(2,1)S(1)}, bf16[2,192,128]{2,1,0:T(8,128)(2,1)S(1)}, u32[]{:S(2)}, u32[]{:S(2)}) collective-permute-start(bf16[2,192,128]{2,1,0:T(8,128)(2,1)S(1)} %get-tuple-element.100), channel_id=1, source_target_pairs={{2,6},{4,0},{3,7},{5,1},{10,14},{12,8},{11,15},{13,9},{18,22},{20,... | collective-permute-start | bytes 294920 | tf_op jit(solution)/shard_map/ppermute | solution.py:65
  3.5 6.3 %collective-permute-start = (bf16[2,192,128]{2,1,0:T(8,128)(2,1)S(1)}, bf16[2,192,128]{2,1,0:T(8,128)(2,1)S(1)}, u32[]{:S(2)}, u32[]{:S(2)}) collective-permute-start(bf16[2,192,128]{2,1,0:T(8,128)(2,1)S(1)} %get-tuple-element.100), channel_id=1, source_target_pairs={{2,0},{0,2},{6,4},{4,6},{3,1},{1,3},{7,5},{5,7},{10,8},{8,10},{14,... | collective-permute-start | bytes 294920 | tf_op jit(solution)/shard_map/ppermute | solution.py:65
  9.8 1.5 %collective-permute-start.3 = (bf16[1,2,192,128]{3,2,1,0:T(8,128)(2,1)S(1)}, bf16[1,2,192,128]{3,2,1,0:T(8,128)(2,1)S(1)}, u32[]{:S(2)}, u32[]{:S(2)}) collective-permute-start(bf16[1,2,192,128]{3,2,1,0:T(8,128)(2,1)S(1)} %get-tuple-element.99), channel_id=1, source_target_pairs={{0,1},{1,0},{2,3},{3,2},{4,5},{5,4},{6,7},{7,6},{8,9},{9,8},{10,11... | collective-permute-start | bytes 294920 | tf_op jit(solution)/shard_map/ppermute | solution.py:412
  11.4 0.0 collective-permute-done.2
  11.4 1.4 %collective-permute-done.1 = bf16[2,192,128]{2,1,0:T(8,128)(2,1)S(1)} collective-permute-done((bf16[2,192,128]{2,1,0:T(8,128)(2,1)S(1)}, bf16[2,192,128]{2,1,0:T(8,128)(2,1)S(1)}, u32[]{:S(2)}, u32[]{:S(2)}) %collective-permute-start.1) | collective-permute-done | bytes 98336 | tf_op jit(solution)/shard_map/ppermute | solution.py:65
  12.8 1.4 %collective-permute-done = bf16[2,192,128]{2,1,0:T(8,128)(2,1)S(1)} collective-permute-done((bf16[2,192,128]{2,1,0:T(8,128)(2,1)S(1)}, bf16[2,192,128]{2,1,0:T(8,128)(2,1)S(1)}, u32[]{:S(2)}, u32[]{:S(2)}) %collective-permute-start) | collective-permute-done | bytes 98336 | tf_op jit(solution)/shard_map/ppermute | solution.py:65
  14.2 0.2 collective-permute-done.3.refs_0_.refs_1_
  14.5 1.3 %collective-permute-start.7 = (bf16[3,2,192,128]{3,2,1,0:T(8,128)(2,1)S(1)}, bf16[3,2,192,128]{3,2,1,0:T(8,128)(2,1)S(1)}, u32[]{:S(2)}, u32[]{:S(2)}) collective-permute-start(bf16[3,2,192,128]{3,2,1,0:T(8,128)(2,1)S(1)} %pad_maximum_fusion.refs_0_), channel_id=1, source_target_pairs={{16,1},{17,0},{8,25},{9,24},{18,3},{19,2},{10,27},{11,26},{20,5},{... | collective-permute-start | bytes 884744 | tf_op jit(solution)/shard_map/ppermute | solution.py:421
  15.7 0.7 %collective-permute-start.6 = (bf16[3,2,192,128]{3,2,1,0:T(8,128)(2,1)S(1)}, bf16[3,2,192,128]{3,2,1,0:T(8,128)(2,1)S(1)}, u32[]{:S(2)}, u32[]{:S(2)}) collective-permute-start(bf16[3,2,192,128]{3,2,1,0:T(8,128)(2,1)S(1)} %pad_maximum_fusion.refs_0_), channel_id=1, source_target_pairs={{16,8},{8,16},{17,9},{9,17},{18,10},{10,18},{19,11},{11,19},{20,12... | collective-permute-start | bytes 884744 | tf_op jit(solution)/shard_map/ppermute | solution.py:420
  16.4 1.6 %collective-permute-start.5 = (bf16[2,2,192,128]{3,2,1,0:T(8,128)(2,1)S(1)}, bf16[2,2,192,128]{3,2,1,0:T(8,128)(2,1)S(1)}, u32[]{:S(2)}, u32[]{:S(2)}) collective-permute-start(bf16[2,2,192,128]{3,2,1,0:T(8,128)(2,1)S(1)} %pad_maximum_fusion.1), channel_id=1, source_target_pairs={{0,1},{1,0},{2,3},{3,2},{4,5},{5,4},{6,7},{7,6},{8,9},{9,8},{10,11... | collective-permute-start | bytes 589832 | tf_op jit(solution)/shard_map/ppermute | solution.py:418
  18.0 3.7 %collective-permute-start.4 = (bf16[192,128]{1,0:T(8,128)(2,1)S(1)}, bf16[192,128]{1,0:T(8,128)(2,1)S(1)}, u32[]{:S(2)}, u32[]{:S(2)}) collective-permute-start(bf16[192,128]{1,0:T(8,128)(2,1)S(1)} %bitcast.19), channel_id=1, source_target_pairs={{0,8},{8,0},{16,24},{24,16},{1,9},{9,1},{17,25},{25,17},{2,10},{10... | collective-permute-start | bytes 147464 | tf_op jit(solution)/shard_map/ppermute | solution.py:106
  21.7 0.1 pad_add_fusion.place
  21.8 0.8 %collective-permute-done.4.queries_other = bf16[192,128]{1,0:T(8,128)(2,1)S(1)} collective-permute-done((bf16[192,128]{1,0:T(8,128)(2,1)S(1)}, bf16[192,128]{1,0:T(8,128)(2,1)S(1)}, u32[]{:S(2)}, u32[]{:S(2)}) %collective-permute-start.4) | collective-permute-done | bytes 49184 | tf_op jit(solution)/shard_map/ppermute | solution.py:106
  22.6 1.3 %copy-done.1 = bf16[4,6,8,3072]{3,2,1,0:T(8,128)(2,1)S(1)} copy-done((bf16[4,6,8,3072]{3,2,1,0:T(8,128)(2,1)S(1)}, bf16[4,6,8,3072]{3,2,1,0:T(8,128)(2,1)}, u32[]{:S(2)}) %copy-start.1) | copy-done | bytes 1179672
  23.8 1.0 %shard_map.92 = (bf16[192,1664]{1,0:T(8,128)(2,1)S(1)}, bf16[192,1536]{1,0:T(8,128)(2,1)S(1)}, bf16[192,128]{1,0:T(8,128)(2,1)S(1)}, bf16[384,128]{1,0:T(8,128)(2,1)S(1)}) custom-call(s32[3]{0:T(128)S(1)} %pad_add_fusion.place, bf16[192,128]{1,0:T(8,128)(2,1)S(1)} %bitcast.20, bf16[192,128]{1,0:T(8,128)(2,1)S(1)} %collective-permute-done.4.queries_other, ...), custom_call_target="tpu_custom_call" | custom-call | flops 150994944 | bytes 2359296 | tf_op jit(solution)/shard_map/pallas_call | solution.py:349
  24.9 0.7 %shard_map.93.refs_4_ = f32[136,384]{1,0:T(8,128)S(1)} custom-call(bf16[384,128]{1,0:T(8,128)(2,1)S(1)} %get-tuple-element.53.both_queries, bf16[3,2,192,128]{3,2,1,0:T(8,128)(2,1)S(1)} %pad_maximum_fusion.refs_0_), custom_call_target="tpu_custom_call" | custom-call | flops 113246208 | bytes 393216 | tf_op jit(solution)/shard_map/pallas_call | solution.py:463
  25.6 0.9 %collective-permute-done.5.refs_1_.refs_2_ = bf16[2,2,192,128]{3,2,1,0:T(8,128)(2,1)S(1)} collective-permute-done((bf16[2,2,192,128]{3,2,1,0:T(8,128)(2,1)S(1)}, bf16[2,2,192,128]{3,2,1,0:T(8,128)(2,1)S(1)}, u32[]{:S(2)}, u32[]{:S(2)}) %collective-permute-start.5) | collective-permute-done | bytes 196640 | tf_op jit(solution)/shard_map/ppermute | solution.py:418
  26.5 0.0 collective-permute-done.7.refs_3_.refs_4_
  26.5 0.0 collective-permute-done.6.refs_2_.refs_3_
  26.5 0.7 %collective-permute-start.9 = (bf16[192,1664]{1,0:T(8,128)(2,1)S(1)}, bf16[192,1664]{1,0:T(8,128)(2,1)S(1)}, u32[]{:S(2)}, u32[]{:S(2)}) collective-permute-start(bf16[192,1664]{1,0:T(8,128)(2,1)S(1)} %get-tuple-element.63), channel_id=1, source_target_pairs={{0,8},{8,0},{16,24},{24,16},{1,9},{9,1},{17,25},{25,17},{2,10},{10... | collective-permute-start | bytes 1916936 | tf_op jit(solution)/shard_map/ppermute | solution.py:106
  27.3 1.2 %shard_map.94.mine = f32[136,384]{1,0:T(8,128)S(1)} custom-call(bf16[384,128]{1,0:T(8,128)(2,1)S(1)} %get-tuple-element.53.both_queries, bf16[1,2,192,128]{3,2,1,0:T(8,128)(2,1)S(1)} %collective-permute-done.3.refs_0_.refs_1_, bf16[2,2,192,128]{3,2,1,0:T(8,128)(2,1)S(1)} %collective-permute-done.5.refs_1_.refs_2_, ...), custom_call_target="tpu_custom_call" | custom-call | flops 226492416 | bytes 786432 | tf_op jit(solution)/shard_map/pallas_call | solution.py:463
  28.5 0.1 collective-permute-start.8
  28.5 1.4 %collective-permute-done.8.theirs = f32[136,384]{1,0:T(8,128)S(1)} collective-permute-done((f32[136,384]{1,0:T(8,128)S(1)}, f32[136,384]{1,0:T(8,128)S(1)}, u32[]{:S(2)}, u32[]{:S(2)}) %collective-permute-start.8) | collective-permute-done | bytes 208928 | tf_op jit(solution)/shard_map/ppermute | solution.py:106
  30.0 0.0 collective-permute-done.9.payload
  30.0 1.1 %shard_map.95 = (f32[136,384]{1,0:T(8,128)S(1)}, bf16[192,128]{1,0:T(8,128)(2,1)S(1)}, bf16[32,1536]{1,0:T(8,128)(2,1)S(1)}, bf16[32,1536]{1,0:T(8,128)(2,1)S(1)...) custom-call(s32[3]{0:T(128)S(1)} %pad_add_fusion.place, f32[136,384]{1,0:T(8,128)S(1)} %shard_map.94.mine, ...), custom_call_target="tpu_custom_call" | custom-call | flops 150994944 | bytes 2359296 | tf_op jit(solution)/shard_map/pallas_call | solution.py:349
  31.1 1.6 %collective-permute-start.10 = (bf16[32,1536]{1,0:T(8,128)(2,1)S(1)}, bf16[32,1536]{1,0:T(8,128)(2,1)S(1)}, u32[]{:S(2)}, u32[]{:S(2)}) collective-permute-start(bf16[32,1536]{1,0:T(8,128)(2,1)S(1)} %get-tuple-element.70), channel_id=1, source_target_pairs={{0,1},{1,0},{8,9},{9,8},{16,17},{17,16},{24,25},{25,24},{2,3},{3,2... | collective-permute-start | bytes 294920 | tf_op jit(solution)/shard_map/ppermute | solution.py:106
  32.7 0.2 collective-permute-start.11
  32.8 1.8 %collective-permute-start.12 = (bf16[32,1536]{1,0:T(8,128)(2,1)S(1)}, bf16[32,1536]{1,0:T(8,128)(2,1)S(1)}, u32[]{:S(2)}, u32[]{:S(2)}) collective-permute-start(bf16[32,1536]{1,0:T(8,128)(2,1)S(1)} %get-tuple-element.72), channel_id=1, source_target_pairs={{0,17},{1,16},{8,25},{9,24},{16,1},{17,0},{24,9},{25,8},{2,19},{3,... | collective-permute-start | bytes 294920 | tf_op jit(solution)/shard_map/ppermute | solution.py:106
  34.7 2.6 %shard_map.96 = (f32[3,2,192,128]{3,2,1,0:T(8,128)S(1)}, bf16[3,2,192,128]{3,2,1,0:T(8,128)(2,1)S(1)}, bf16[3,2,192,128]{3,2,1,0:T(8,128)(2,1)S(1)}, f32[128,384]{1,0:T(8,128)S(1)}) custom-call(s32[3]{0:T(128)S(1)} %pad_add_fusion.place, f32[136,384]{1,0:T(8,128)S(1)} %get-tuple-element.67.stats, bf16[384,128]{1,0:T(8,128)(2,1)S(1)} %get-tuple-element.53.both_queries, ...), custom_call_target="tpu_custom_call" | custom-call | flops 849346560 | bytes 2359296 | tf_op jit(solution)/shard_map/pallas_call | solution.py:349
  37.3 1.6 %collective-permute-start.19 = (bf16[3,2,192,128]{3,2,1,0:T(8,128)(2,1)S(1)}, bf16[3,2,192,128]{3,2,1,0:T(8,128)(2,1)S(1)}, u32[]{:S(2)}, u32[]{:S(2)}) collective-permute-start(bf16[3,2,192,128]{3,2,1,0:T(8,128)(2,1)S(1)} %get-tuple-element.90), channel_id=1, source_target_pairs={{0,1},{1,0},{2,3},{3,2},{4,5},{5,4},{6,7},{7,6},{8,9},{9,8},{10,11... | collective-permute-start | bytes 884744 | tf_op jit(solution)/shard_map/ppermute | solution.py:539
  38.9 0.0 collective-permute-done.10
  38.9 0.0 collective-permute-done.11
  38.9 0.4 collective-permute-done.12
  39.3 0.1 add_convert_fusion.2
  39.4 0.1 collective-permute-start.13
  39.5 0.7 %shard_map.97 = (f32[192,128]{1,0:T(8,128)S(1)}, bf16[16,1536]{1,0:T(8,128)(2,1)S(1)}) custom-call(s32[3]{0:T(128)S(1)} %pad_add_fusion.place, f32[128,384]{1,0:T(8,128)S(1)} %get-tuple-element.79.query_grad), custom_call_target="tpu_custom_call" | custom-call | flops 10000000000 | bytes 100000000 | tf_op jit(solution)/shard_map/pallas_call | solution.py:349
  40.2 3.2 %collective-permute-start.21 = (bf16[3,2,192,128]{3,2,1,0:T(8,128)(2,1)S(1)}, bf16[3,2,192,128]{3,2,1,0:T(8,128)(2,1)S(1)}, u32[]{:S(2)}, u32[]{:S(2)}) collective-permute-start(bf16[3,2,192,128]{3,2,1,0:T(8,128)(2,1)S(1)} %get-tuple-element.91), channel_id=1, source_target_pairs={{1,16},{0,17},{25,8},{24,9},{3,18},{2,19},{27,10},{26,11},{5,20},{... | collective-permute-start | bytes 884744 | tf_op jit(solution)/shard_map/ppermute | solution.py:541
  43.4 0.7 %collective-permute-start.20 = (bf16[3,2,192,128]{3,2,1,0:T(8,128)(2,1)S(1)}, bf16[3,2,192,128]{3,2,1,0:T(8,128)(2,1)S(1)}, u32[]{:S(2)}, u32[]{:S(2)}) collective-permute-start(bf16[3,2,192,128]{3,2,1,0:T(8,128)(2,1)S(1)} %get-tuple-element.91), channel_id=1, source_target_pairs={{8,16},{16,8},{9,17},{17,9},{10,18},{18,10},{11,19},{19,11},{12,20... | collective-permute-start | bytes 884744 | tf_op jit(solution)/shard_map/ppermute | solution.py:540
  44.1 0.0 collective-permute-done.13
  44.1 1.6 %collective-permute-start.14 = (bf16[32,1536]{1,0:T(8,128)(2,1)S(1)}, bf16[32,1536]{1,0:T(8,128)(2,1)S(1)}, u32[]{:S(2)}, u32[]{:S(2)}) collective-permute-start(bf16[32,1536]{1,0:T(8,128)(2,1)S(1)} %add_convert_fusion.1), channel_id=1, source_target_pairs={{0,4},{2,6},{4,0},{6,2},{1,5},{3,7},{5,1},{7,3},{8,12},{10,14},{12... | collective-permute-start | bytes 294920 | tf_op jit(solution)/shard_map/ppermute | solution.py:106
  45.8 1.5 %convolution_convert_fusion = bf16[192,3072]{1,0:T(8,128)(2,1)} fusion(bf16[192,128]{1,0:T(8,128)(2,1)S(1)} %get-tuple-element.77, bf16[128,3072]{1,0:T(8,128)(2,1)S(1)} %copy-done), kind=kOutput, calls=%fused_computation | convolution fusion | flops 151584768 | bytes 2015232 | tf_op jit(solution)/shard_map/dot_general | solution.py:532
  47.2 5.1 %collective-permute-done.14 = bf16[32,1536]{1,0:T(8,128)(2,1)S(1)} collective-permute-done((bf16[32,1536]{1,0:T(8,128)(2,1)S(1)}, bf16[32,1536]{1,0:T(8,128)(2,1)S(1)}, u32[]{:S(2)}, u32[]{:S(2)}) %collective-permute-start.14) | collective-permute-done | bytes 98336 | tf_op jit(solution)/shard_map/ppermute | solution.py:106
  52.4 1.0 %collective-permute-start.17 = (bf16[32,1536]{1,0:T(8,128)(2,1)S(1)}, bf16[32,1536]{1,0:T(8,128)(2,1)S(1)}, u32[]{:S(2)}, u32[]{:S(2)}) collective-permute-start(bf16[32,1536]{1,0:T(8,128)(2,1)S(1)} %add_convert_fusion.refs_4_), channel_id=1, source_target_pairs={{0,1},{1,0},{8,9},{9,8},{16,17},{17,16},{24,25},{25,24},{2,3},{3,2... | collective-permute-start | bytes 294920 | tf_op jit(solution)/shard_map/ppermute | solution.py:106
  53.3 0.0 collective-permute-start.16
  53.3 0.0 collective-permute-done.19.refs_0_
  53.4 2.6 %collective-permute-start.15 = (bf16[32,1536]{1,0:T(8,128)(2,1)S(1)}, bf16[32,1536]{1,0:T(8,128)(2,1)S(1)}, u32[]{:S(2)}, u32[]{:S(2)}) collective-permute-start(bf16[32,1536]{1,0:T(8,128)(2,1)S(1)} %add_convert_fusion.refs_4_), channel_id=1, source_target_pairs={{0,17},{1,16},{8,25},{9,24},{16,1},{17,0},{24,9},{25,8},{2,19},{3,... | collective-permute-start | bytes 294920 | tf_op jit(solution)/shard_map/ppermute | solution.py:106
  55.9 0.0 collective-permute-done.21.refs_2_
  55.9 0.0 collective-permute-done.20.refs_1_
  55.9 0.1 shard_map.101
  56.1 1.5 %collective-permute-start.24 = (bf16[2,192,128]{2,1,0:T(8,128)(2,1)S(1)}, bf16[2,192,128]{2,1,0:T(8,128)(2,1)S(1)}, u32[]{:S(2)}, u32[]{:S(2)}) collective-permute-start(bf16[2,192,128]{2,1,0:T(8,128)(2,1)S(1)} %get-tuple-element.95), channel_id=1, source_target_pairs={{6,2},{0,4},{7,3},{1,5},{14,10},{8,12},{15,11},{9,13},{22,18},{16,... | collective-permute-start | bytes 294920 | tf_op jit(solution)/shard_map/ppermute | solution.py:87
  57.6 0.7 %collective-permute-start.23 = (bf16[2,192,128]{2,1,0:T(8,128)(2,1)S(1)}, bf16[2,192,128]{2,1,0:T(8,128)(2,1)S(1)}, u32[]{:S(2)}, u32[]{:S(2)}) collective-permute-start(bf16[2,192,128]{2,1,0:T(8,128)(2,1)S(1)} %get-tuple-element.95), channel_id=1, source_target_pairs={{4,2},{2,4},{5,3},{3,5},{12,10},{10,12},{13,11},{11,13},{20,18},{1... | collective-permute-start | bytes 294920 | tf_op jit(solution)/shard_map/ppermute | solution.py:87
  58.2 0.0 collective-permute-done.17.refs_3_
  58.2 1.3 %collective-permute-start.22 = (bf16[2,192,128]{2,1,0:T(8,128)(2,1)S(1)}, bf16[2,192,128]{2,1,0:T(8,128)(2,1)S(1)}, u32[]{:S(2)}, u32[]{:S(2)}) collective-permute-start(bf16[2,192,128]{2,1,0:T(8,128)(2,1)S(1)} %get-tuple-element.94), channel_id=1, source_target_pairs={{0,2},{2,0},{4,6},{6,4},{1,3},{3,1},{5,7},{7,5},{8,10},{10,8},{12,... | collective-permute-start | bytes 294920 | tf_op jit(solution)/shard_map/ppermute | solution.py:87
  59.5 0.0 collective-permute-done.16.refs_2_
  59.5 0.6 collective-permute-done.15.refs_1_
  60.1 0.1 collective-permute-start.18
  60.2 1.5 %shard_map.99.refs_1_ = f32[128,3072]{1,0:T(8,128)} custom-call(s32[3]{0:T(128)S(1)} %pad_add_fusion.place, bf16[144,1536]{1,0:T(8,128)(2,1)S(1)} %shard_map.98.part), custom_call_target="tpu_custom_call" | custom-call | flops 10000000000 | bytes 100000000 | tf_op jit(solution)/shard_map/pallas_call | solution.py:307
  61.6 0.3 collective-permute-done.18.part
  62.0 1.5 %shard_map.100 = (f32[128,3072]{1,0:T(8,128)}, bf16[192,128]{1,0:T(8,128)(2,1)}) custom-call(s32[3]{0:T(128)S(1)} %pad_add_fusion.place, bf16[144,1536]{1,0:T(8,128)(2,1)S(1)} %collective-permute-done.18.part, f32[192,128]{1,0:T(8,128)S(1)} %get-tuple-element.86.refs_0_, f32[128,3072]{1,0:T(8,128)} %shard_map.99.refs_1_), custom_call_target="tpu_custom_call", output_to_operand_aliasing={{0}: (3, {})} | custom-call | flops 10000000000 | bytes 100000000 | tf_op jit(solution)/shard_map/pallas_call | solution.py:307
  63.4 0.0 collective-permute-done.22.refs_0_
  63.5 0.0 collective-permute-done.23.refs_1_
  63.5 0.7 %shard_map.102 = (bf16[192,128]{1,0:T(8,128)(2,1)}, bf16[192,128]{1,0:T(8,128)(2,1)}) custom-call(f32[2,192,128]{2,1,0:T(8,128)S(1)} %get-tuple-element.93.own_grad, bf16[2,192,128]{2,1,0:T(8,128)(2,1)S(1)} %collective-permute-done.22.refs_0_, bf16[2,192,128]{2,1,0:T(8,128)(2,1)S(1)} %collective-permute-done.23.refs_1_, ...), custom_call_target="tpu_custom_call" | custom-call | flops 10000000000 | bytes 100000000 | tf_op jit(solution)/shard_map/pallas_call | solution.py:578
  (12 shorter events, 0.2 us)
Async XLA Ops:
  0.6 17.4 %copy-start.2 = (bf16[4,6,8,128]{3,2,1,0:T(8,128)(2,1)S(1)}, bf16[4,6,8,128]{3,2,1,0:T(8,128)(2,1)}, u32[]{:S(2)}) copy-start(bf16[4,6,8,128]{3,2,1,0:T(8,128)(2,1)} %param.5) | copy-start | bytes 147460
  0.6 21.9 %copy-start = (bf16[128,3072]{1,0:T(8,128)(2,1)S(1)}, bf16[128,3072]{1,0:T(8,128)(2,1)}, u32[]{:S(2)}) copy-start(bf16[128,3072]{1,0:T(8,128)(2,1)} %weight.1) | copy-start | bytes 2359300
  1.6 9.8 %collective-permute-start.2 = (bf16[2,192,128]{2,1,0:T(8,128)(2,1)S(1)}, bf16[2,192,128]{2,1,0:T(8,128)(2,1)S(1)}, u32[]{:S(2)}, u32[]{:S(2)}) collective-permute-start(bf16[2,192,128]{2,1,0:T(8,128)(2,1)S(1)} %get-tuple-element.100), channel_id=1, source_target_pairs={{2,4},{4,2},{3,5},{5,3},{10,12},{12,10},{11,13},{13,11},{18,20},{2... | collective-permute-start | bytes 294920 | tf_op jit(solution)/shard_map/ppermute | solution.py:65
  2.2 10.5 %collective-permute-start.1 = (bf16[2,192,128]{2,1,0:T(8,128)(2,1)S(1)}, bf16[2,192,128]{2,1,0:T(8,128)(2,1)S(1)}, u32[]{:S(2)}, u32[]{:S(2)}) collective-permute-start(bf16[2,192,128]{2,1,0:T(8,128)(2,1)S(1)} %get-tuple-element.100), channel_id=1, source_target_pairs={{2,6},{4,0},{3,7},{5,1},{10,14},{12,8},{11,15},{13,9},{18,22},{20,... | collective-permute-start | bytes 294920 | tf_op jit(solution)/shard_map/ppermute | solution.py:65
  3.5 10.6 %collective-permute-start = (bf16[2,192,128]{2,1,0:T(8,128)(2,1)S(1)}, bf16[2,192,128]{2,1,0:T(8,128)(2,1)S(1)}, u32[]{:S(2)}, u32[]{:S(2)}) collective-permute-start(bf16[2,192,128]{2,1,0:T(8,128)(2,1)S(1)} %get-tuple-element.100), channel_id=1, source_target_pairs={{2,0},{0,2},{6,4},{4,6},{3,1},{1,3},{7,5},{5,7},{10,8},{8,10},{14,... | collective-permute-start | bytes 294920 | tf_op jit(solution)/shard_map/ppermute | solution.py:65
  9.8 4.6 %collective-permute-start.3 = (bf16[1,2,192,128]{3,2,1,0:T(8,128)(2,1)S(1)}, bf16[1,2,192,128]{3,2,1,0:T(8,128)(2,1)S(1)}, u32[]{:S(2)}, u32[]{:S(2)}) collective-permute-start(bf16[1,2,192,128]{3,2,1,0:T(8,128)(2,1)S(1)} %get-tuple-element.99), channel_id=1, source_target_pairs={{0,1},{1,0},{2,3},{3,2},{4,5},{5,4},{6,7},{7,6},{8,9},{9,8},{10,11... | collective-permute-start | bytes 294920 | tf_op jit(solution)/shard_map/ppermute | solution.py:412
  14.5 12.1 %collective-permute-start.7 = (bf16[3,2,192,128]{3,2,1,0:T(8,128)(2,1)S(1)}, bf16[3,2,192,128]{3,2,1,0:T(8,128)(2,1)S(1)}, u32[]{:S(2)}, u32[]{:S(2)}) collective-permute-start(bf16[3,2,192,128]{3,2,1,0:T(8,128)(2,1)S(1)} %pad_maximum_fusion.refs_0_), channel_id=1, source_target_pairs={{16,1},{17,0},{8,25},{9,24},{18,3},{19,2},{10,27},{11,26},{20,5},{... | collective-permute-start | bytes 884744 | tf_op jit(solution)/shard_map/ppermute | solution.py:421
  15.7 10.8 %collective-permute-start.6 = (bf16[3,2,192,128]{3,2,1,0:T(8,128)(2,1)S(1)}, bf16[3,2,192,128]{3,2,1,0:T(8,128)(2,1)S(1)}, u32[]{:S(2)}, u32[]{:S(2)}) collective-permute-start(bf16[3,2,192,128]{3,2,1,0:T(8,128)(2,1)S(1)} %pad_maximum_fusion.refs_0_), channel_id=1, source_target_pairs={{16,8},{8,16},{17,9},{9,17},{18,10},{10,18},{19,11},{11,19},{20,12... | collective-permute-start | bytes 884744 | tf_op jit(solution)/shard_map/ppermute | solution.py:420
  16.4 10.1 %collective-permute-start.5 = (bf16[2,2,192,128]{3,2,1,0:T(8,128)(2,1)S(1)}, bf16[2,2,192,128]{3,2,1,0:T(8,128)(2,1)S(1)}, u32[]{:S(2)}, u32[]{:S(2)}) collective-permute-start(bf16[2,2,192,128]{3,2,1,0:T(8,128)(2,1)S(1)} %pad_maximum_fusion.1), channel_id=1, source_target_pairs={{0,1},{1,0},{2,3},{3,2},{4,5},{5,4},{6,7},{7,6},{8,9},{9,8},{10,11... | collective-permute-start | bytes 589832 | tf_op jit(solution)/shard_map/ppermute | solution.py:418
  18.0 4.5 %collective-permute-start.4 = (bf16[192,128]{1,0:T(8,128)(2,1)S(1)}, bf16[192,128]{1,0:T(8,128)(2,1)S(1)}, u32[]{:S(2)}, u32[]{:S(2)}) collective-permute-start(bf16[192,128]{1,0:T(8,128)(2,1)S(1)} %bitcast.19), channel_id=1, source_target_pairs={{0,8},{8,0},{16,24},{24,16},{1,9},{9,1},{17,25},{25,17},{2,10},{10... | collective-permute-start | bytes 147464 | tf_op jit(solution)/shard_map/ppermute | solution.py:106
  22.6 1.3 %copy-start.1 = (bf16[4,6,8,3072]{3,2,1,0:T(8,128)(2,1)S(1)}, bf16[4,6,8,3072]{3,2,1,0:T(8,128)(2,1)}, u32[]{:S(2)}) copy-start(bf16[4,6,8,3072]{3,2,1,0:T(8,128)(2,1)} %param.9) | copy-start | bytes 3538948
  26.5 3.4 %collective-permute-start.9 = (bf16[192,1664]{1,0:T(8,128)(2,1)S(1)}, bf16[192,1664]{1,0:T(8,128)(2,1)S(1)}, u32[]{:S(2)}, u32[]{:S(2)}) collective-permute-start(bf16[192,1664]{1,0:T(8,128)(2,1)S(1)} %get-tuple-element.63), channel_id=1, source_target_pairs={{0,8},{8,0},{16,24},{24,16},{1,9},{9,1},{17,25},{25,17},{2,10},{10... | collective-permute-start | bytes 1916936 | tf_op jit(solution)/shard_map/ppermute | solution.py:106
  28.5 1.5 %collective-permute-start.8 = (f32[136,384]{1,0:T(8,128)S(1)}, f32[136,384]{1,0:T(8,128)S(1)}, u32[]{:S(2)}, u32[]{:S(2)}) collective-permute-start(f32[136,384]{1,0:T(8,128)S(1)} %shard_map.94.mine), channel_id=1, source_target_pairs={{0,8},{8,0},{16,24},{24,16},{1,9},{9,1},{17,25},{25,17},{2,10},{10... | collective-permute-start | bytes 626696 | tf_op jit(solution)/shard_map/ppermute | solution.py:106
  31.1 7.8 %collective-permute-start.10 = (bf16[32,1536]{1,0:T(8,128)(2,1)S(1)}, bf16[32,1536]{1,0:T(8,128)(2,1)S(1)}, u32[]{:S(2)}, u32[]{:S(2)}) collective-permute-start(bf16[32,1536]{1,0:T(8,128)(2,1)S(1)} %get-tuple-element.70), channel_id=1, source_target_pairs={{0,1},{1,0},{8,9},{9,8},{16,17},{17,16},{24,25},{25,24},{2,3},{3,2... | collective-permute-start | bytes 294920 | tf_op jit(solution)/shard_map/ppermute | solution.py:106
  32.7 6.2 %collective-permute-start.11 = (bf16[32,1536]{1,0:T(8,128)(2,1)S(1)}, bf16[32,1536]{1,0:T(8,128)(2,1)S(1)}, u32[]{:S(2)}, u32[]{:S(2)}) collective-permute-start(bf16[32,1536]{1,0:T(8,128)(2,1)S(1)} %get-tuple-element.71), channel_id=1, source_target_pairs={{0,16},{1,17},{8,24},{9,25},{16,0},{17,1},{24,8},{25,9},{2,18},{3,... | collective-permute-start | bytes 294920 | tf_op jit(solution)/shard_map/ppermute | solution.py:106
  32.8 6.5 %collective-permute-start.12 = (bf16[32,1536]{1,0:T(8,128)(2,1)S(1)}, bf16[32,1536]{1,0:T(8,128)(2,1)S(1)}, u32[]{:S(2)}, u32[]{:S(2)}) collective-permute-start(bf16[32,1536]{1,0:T(8,128)(2,1)S(1)} %get-tuple-element.72), channel_id=1, source_target_pairs={{0,17},{1,16},{8,25},{9,24},{16,1},{17,0},{24,9},{25,8},{2,19},{3,... | collective-permute-start | bytes 294920 | tf_op jit(solution)/shard_map/ppermute | solution.py:106
  37.3 16.1 %collective-permute-start.19 = (bf16[3,2,192,128]{3,2,1,0:T(8,128)(2,1)S(1)}, bf16[3,2,192,128]{3,2,1,0:T(8,128)(2,1)S(1)}, u32[]{:S(2)}, u32[]{:S(2)}) collective-permute-start(bf16[3,2,192,128]{3,2,1,0:T(8,128)(2,1)S(1)} %get-tuple-element.90), channel_id=1, source_target_pairs={{0,1},{1,0},{2,3},{3,2},{4,5},{5,4},{6,7},{7,6},{8,9},{9,8},{10,11... | collective-permute-start | bytes 884744 | tf_op jit(solution)/shard_map/ppermute | solution.py:539
  39.4 4.7 %collective-permute-start.13 = (bf16[32,1536]{1,0:T(8,128)(2,1)S(1)}, bf16[32,1536]{1,0:T(8,128)(2,1)S(1)}, u32[]{:S(2)}, u32[]{:S(2)}) collective-permute-start(bf16[32,1536]{1,0:T(8,128)(2,1)S(1)} %add_convert_fusion.2), channel_id=1, source_target_pairs={{0,2},{2,0},{4,6},{6,4},{1,3},{3,1},{5,7},{7,5},{8,10},{10,8},{12,... | collective-permute-start | bytes 294920 | tf_op jit(solution)/shard_map/ppermute | solution.py:106
  40.2 15.7 %collective-permute-start.21 = (bf16[3,2,192,128]{3,2,1,0:T(8,128)(2,1)S(1)}, bf16[3,2,192,128]{3,2,1,0:T(8,128)(2,1)S(1)}, u32[]{:S(2)}, u32[]{:S(2)}) collective-permute-start(bf16[3,2,192,128]{3,2,1,0:T(8,128)(2,1)S(1)} %get-tuple-element.91), channel_id=1, source_target_pairs={{1,16},{0,17},{25,8},{24,9},{3,18},{2,19},{27,10},{26,11},{5,20},{... | collective-permute-start | bytes 884744 | tf_op jit(solution)/shard_map/ppermute | solution.py:541
  43.4 12.5 %collective-permute-start.20 = (bf16[3,2,192,128]{3,2,1,0:T(8,128)(2,1)S(1)}, bf16[3,2,192,128]{3,2,1,0:T(8,128)(2,1)S(1)}, u32[]{:S(2)}, u32[]{:S(2)}) collective-permute-start(bf16[3,2,192,128]{3,2,1,0:T(8,128)(2,1)S(1)} %get-tuple-element.91), channel_id=1, source_target_pairs={{8,16},{16,8},{9,17},{17,9},{10,18},{18,10},{11,19},{19,11},{12,20... | collective-permute-start | bytes 884744 | tf_op jit(solution)/shard_map/ppermute | solution.py:540
  44.1 8.2 %collective-permute-start.14 = (bf16[32,1536]{1,0:T(8,128)(2,1)S(1)}, bf16[32,1536]{1,0:T(8,128)(2,1)S(1)}, u32[]{:S(2)}, u32[]{:S(2)}) collective-permute-start(bf16[32,1536]{1,0:T(8,128)(2,1)S(1)} %add_convert_fusion.1), channel_id=1, source_target_pairs={{0,4},{2,6},{4,0},{6,2},{1,5},{3,7},{5,1},{7,3},{8,12},{10,14},{12... | collective-permute-start | bytes 294920 | tf_op jit(solution)/shard_map/ppermute | solution.py:106
  52.4 5.9 %collective-permute-start.17 = (bf16[32,1536]{1,0:T(8,128)(2,1)S(1)}, bf16[32,1536]{1,0:T(8,128)(2,1)S(1)}, u32[]{:S(2)}, u32[]{:S(2)}) collective-permute-start(bf16[32,1536]{1,0:T(8,128)(2,1)S(1)} %add_convert_fusion.refs_4_), channel_id=1, source_target_pairs={{0,1},{1,0},{8,9},{9,8},{16,17},{17,16},{24,25},{25,24},{2,3},{3,2... | collective-permute-start | bytes 294920 | tf_op jit(solution)/shard_map/ppermute | solution.py:106
  53.3 6.2 %collective-permute-start.16 = (bf16[32,1536]{1,0:T(8,128)(2,1)S(1)}, bf16[32,1536]{1,0:T(8,128)(2,1)S(1)}, u32[]{:S(2)}, u32[]{:S(2)}) collective-permute-start(bf16[32,1536]{1,0:T(8,128)(2,1)S(1)} %add_convert_fusion.refs_4_), channel_id=1, source_target_pairs={{0,16},{1,17},{8,24},{9,25},{16,0},{17,1},{24,8},{25,9},{2,18},{3,... | collective-permute-start | bytes 294920 | tf_op jit(solution)/shard_map/ppermute | solution.py:106
  53.4 6.7 %collective-permute-start.15 = (bf16[32,1536]{1,0:T(8,128)(2,1)S(1)}, bf16[32,1536]{1,0:T(8,128)(2,1)S(1)}, u32[]{:S(2)}, u32[]{:S(2)}) collective-permute-start(bf16[32,1536]{1,0:T(8,128)(2,1)S(1)} %add_convert_fusion.refs_4_), channel_id=1, source_target_pairs={{0,17},{1,16},{8,25},{9,24},{16,1},{17,0},{24,9},{25,8},{2,19},{3,... | collective-permute-start | bytes 294920 | tf_op jit(solution)/shard_map/ppermute | solution.py:106
  56.1 7.4 %collective-permute-start.24 = (bf16[2,192,128]{2,1,0:T(8,128)(2,1)S(1)}, bf16[2,192,128]{2,1,0:T(8,128)(2,1)S(1)}, u32[]{:S(2)}, u32[]{:S(2)}) collective-permute-start(bf16[2,192,128]{2,1,0:T(8,128)(2,1)S(1)} %get-tuple-element.95), channel_id=1, source_target_pairs={{6,2},{0,4},{7,3},{1,5},{14,10},{8,12},{15,11},{9,13},{22,18},{16,... | collective-permute-start | bytes 294920 | tf_op jit(solution)/shard_map/ppermute | solution.py:87
  57.6 5.9 %collective-permute-start.23 = (bf16[2,192,128]{2,1,0:T(8,128)(2,1)S(1)}, bf16[2,192,128]{2,1,0:T(8,128)(2,1)S(1)}, u32[]{:S(2)}, u32[]{:S(2)}) collective-permute-start(bf16[2,192,128]{2,1,0:T(8,128)(2,1)S(1)} %get-tuple-element.95), channel_id=1, source_target_pairs={{4,2},{2,4},{5,3},{3,5},{12,10},{10,12},{13,11},{11,13},{20,18},{1... | collective-permute-start | bytes 294920 | tf_op jit(solution)/shard_map/ppermute | solution.py:87
  58.2 5.2 %collective-permute-start.22 = (bf16[2,192,128]{2,1,0:T(8,128)(2,1)S(1)}, bf16[2,192,128]{2,1,0:T(8,128)(2,1)S(1)}, u32[]{:S(2)}, u32[]{:S(2)}) collective-permute-start(bf16[2,192,128]{2,1,0:T(8,128)(2,1)S(1)} %get-tuple-element.94), channel_id=1, source_target_pairs={{0,2},{2,0},{4,6},{6,4},{1,3},{3,1},{5,7},{7,5},{8,10},{10,8},{12,... | collective-permute-start | bytes 294920 | tf_op jit(solution)/shard_map/ppermute | solution.py:87
  60.1 1.9 %collective-permute-start.18 = (bf16[144,1536]{1,0:T(8,128)(2,1)S(1)}, bf16[144,1536]{1,0:T(8,128)(2,1)S(1)}, u32[]{:S(2)}, u32[]{:S(2)}) collective-permute-start(bf16[144,1536]{1,0:T(8,128)(2,1)S(1)} %shard_map.98.part), channel_id=1, source_target_pairs={{0,8},{8,0},{16,24},{24,16},{1,9},{9,1},{17,25},{25,17},{2,10},{10... | collective-permute-start | bytes 1327112 | tf_op jit(solution)/shard_map/ppermute | solution.py:106

commit v13 on v11

--- a/solution.py
+++ b/solution.py
@@ -469,11 +469,11 @@
             out_specs=VMEM,
             scratch_shapes=[pltpu.VMEM((keys, 2 * tile), jnp.float32)],
             compiler_params=PARAMS,
-            cost_estimate=cost_of(8 * keys * tile * head_dim, moved * keys // key_count),
+            cost_estimate=cost_of(5 * 10**9 if carried else 10**8, 10**6),
         )(both_queries, *operands, *carried)
 
     partial = forward(blocks[:1], (1,), ())
-    payload, partial, *blocks[1:] = lax.optimization_barrier((payload, partial, *blocks[1:]))
+    payload, partial = lax.optimization_barrier((payload, partial))
     payload = flip(payload, ("frame",), (1,))
     partial = forward(blocks[1:], layout[1:], (partial,))
     partial_other = flip(partial, ("frame",), (1,))

time: 64.4 us -> 63.7 us (0.989)
  waiting for transfers between devices: 13.1 us -> 11.4 us
  starting transfers between devices: 35.1 us -> 36.1 us
    ppermute x12, waiting for transfers between devices: 8.88 us -> 7.84 us  [flip(): return lax.ppermute(block, axes, route)]
  transfers between devices with their start and end apart: 25 -> 25, of which waited for: 12 -> 10; matrix products, arithmetic and copies ran while one was open for 3% -> 3% of each run, Pallas kernels for 15% -> 15%
where the time goes in v13:
time: 63.7 us; the launch traced here: 63.4 us
  starting transfers between devices  36.1 us (57%)
  waiting for transfers between devices  11.4 us (18%)
  Pallas kernels  11.1 us (17%)
  matrix products  1.47 us (2%)
  local copies, waits for them, and re-layouts  1.28 us (2%)
  other arithmetic  1.17 us (2%)
  between operations  0.88 us (1%)
    ppermute x12, starting transfers between devices, flip(): return lax.ppermute(block, axes, route)  13.9 us
    ppermute x3, starting transfers between devices, fetch(): arrived = [lax.ppermute(block, axis, route) for route in routes]  8.25 us
    ppermute x12, waiting for transfers between devices, flip(): return lax.ppermute(block, axes, route)  7.84 us
    pallas_call x4, Pallas kernels, kernel_call(): pl.pallas_call(kernel, out_shape=outs, in_specs=[SMEM] + [VMEM] * (len(op...  5.43 us
    ppermute x3, starting transfers between devices, returned(): arrived.append(lax.ppermute(outgoing, axis, [(p, s) for s, p in route]))  3.44 us
    ppermute x1, starting transfers between devices, body(): lax.ppermute(far_grad, ('frame', 'width'), [(p, s) for s, p in cross])  3.16 us
    pallas_call x2, Pallas kernels, assemble(): pl.pallas_call(functools.partial(assemble_kernel, flipped, rows), out_sha...  2.95 us
    ppermute x3, waiting for transfers between devices, fetch(): arrived = [lax.ppermute(block, axis, route) for route in routes]  2.79 us
  transfers between devices with their start and end apart: 25, of which 10 were waited for; matrix products, arithmetic and copies ran while one was open for 3% of the time, Pallas kernels for 15%

profile of v13, /device:TPU:0, one launch (start us, length us, event | category | flops | bytes accessed | tf_op | source)
XLA Modules:
  0.0 63.4 jit_solution(11421555163840799776)
XLA Ops:
  0.7 0.9 %fusion = (bf16[1,2,192,128]{3,2,1,0:T(8,128)(2,1)S(1)}, bf16[2,192,128]{2,1,0:T(8,128)(2,1)S(1)}) fusion(bf16[1,192,128]{2,1,0:T(8,128)(2,1)} %bitcast.24, bf16[1,192,128]{2,1,0:T(8,128)(2,1)} %bitcast.25), kind=kLoop, calls=%fused_computation.9 | loop fusion | flops 49152 | bytes 294912 | tf_op jit(solution)/shard_map/stack | solution.py:416
  1.6 0.7 %collective-permute-start.2 = (bf16[2,192,128]{2,1,0:T(8,128)(2,1)S(1)}, bf16[2,192,128]{2,1,0:T(8,128)(2,1)S(1)}, u32[]{:S(2)}, u32[]{:S(2)}) collective-permute-start(bf16[2,192,128]{2,1,0:T(8,128)(2,1)S(1)} %get-tuple-element.92), channel_id=1, source_target_pairs={{2,4},{4,2},{3,5},{5,3},{10,12},{12,10},{11,13},{13,11},{18,20},{2... | collective-permute-start | bytes 294920 | tf_op jit(solution)/shard_map/ppermute | solution.py:65
  2.2 1.3 %collective-permute-start.1 = (bf16[2,192,128]{2,1,0:T(8,128)(2,1)S(1)}, bf16[2,192,128]{2,1,0:T(8,128)(2,1)S(1)}, u32[]{:S(2)}, u32[]{:S(2)}) collective-permute-start(bf16[2,192,128]{2,1,0:T(8,128)(2,1)S(1)} %get-tuple-element.92), channel_id=1, source_target_pairs={{2,6},{4,0},{3,7},{5,1},{10,14},{12,8},{11,15},{13,9},{18,22},{20,... | collective-permute-start | bytes 294920 | tf_op jit(solution)/shard_map/ppermute | solution.py:65
  3.5 6.3 %collective-permute-start = (bf16[2,192,128]{2,1,0:T(8,128)(2,1)S(1)}, bf16[2,192,128]{2,1,0:T(8,128)(2,1)S(1)}, u32[]{:S(2)}, u32[]{:S(2)}) collective-permute-start(bf16[2,192,128]{2,1,0:T(8,128)(2,1)S(1)} %get-tuple-element.92), channel_id=1, source_target_pairs={{2,0},{0,2},{6,4},{4,6},{3,1},{1,3},{7,5},{5,7},{10,8},{8,10},{14,... | collective-permute-start | bytes 294920 | tf_op jit(solution)/shard_map/ppermute | solution.py:65
  9.8 1.5 %collective-permute-start.3 = (bf16[1,2,192,128]{3,2,1,0:T(8,128)(2,1)S(1)}, bf16[1,2,192,128]{3,2,1,0:T(8,128)(2,1)S(1)}, u32[]{:S(2)}, u32[]{:S(2)}) collective-permute-start(bf16[1,2,192,128]{3,2,1,0:T(8,128)(2,1)S(1)} %get-tuple-element.91), channel_id=1, source_target_pairs={{0,1},{1,0},{2,3},{3,2},{4,5},{5,4},{6,7},{7,6},{8,9},{9,8},{10,11... | collective-permute-start | bytes 294920 | tf_op jit(solution)/shard_map/ppermute | solution.py:414
  11.4 0.0 collective-permute-done.2
  11.4 1.4 %collective-permute-done.1 = bf16[2,192,128]{2,1,0:T(8,128)(2,1)S(1)} collective-permute-done((bf16[2,192,128]{2,1,0:T(8,128)(2,1)S(1)}, bf16[2,192,128]{2,1,0:T(8,128)(2,1)S(1)}, u32[]{:S(2)}, u32[]{:S(2)}) %collective-permute-start.1) | collective-permute-done | bytes 98336 | tf_op jit(solution)/shard_map/ppermute | solution.py:65
  12.8 1.4 %collective-permute-done = bf16[2,192,128]{2,1,0:T(8,128)(2,1)S(1)} collective-permute-done((bf16[2,192,128]{2,1,0:T(8,128)(2,1)S(1)}, bf16[2,192,128]{2,1,0:T(8,128)(2,1)S(1)}, u32[]{:S(2)}, u32[]{:S(2)}) %collective-permute-start) | collective-permute-done | bytes 98336 | tf_op jit(solution)/shard_map/ppermute | solution.py:65
  14.2 0.2 collective-permute-done.3.refs_0_.refs_1_
  14.5 1.3 %collective-permute-start.7 = (bf16[3,2,192,128]{3,2,1,0:T(8,128)(2,1)S(1)}, bf16[3,2,192,128]{3,2,1,0:T(8,128)(2,1)S(1)}, u32[]{:S(2)}, u32[]{:S(2)}) collective-permute-start(bf16[3,2,192,128]{3,2,1,0:T(8,128)(2,1)S(1)} %pad_maximum_fusion.refs_0_), channel_id=1, source_target_pairs={{16,1},{17,0},{8,25},{9,24},{18,3},{19,2},{10,27},{11,26},{20,5},{... | collective-permute-start | bytes 884744 | tf_op jit(solution)/shard_map/ppermute | solution.py:423
  15.7 0.7 %collective-permute-start.6 = (bf16[3,2,192,128]{3,2,1,0:T(8,128)(2,1)S(1)}, bf16[3,2,192,128]{3,2,1,0:T(8,128)(2,1)S(1)}, u32[]{:S(2)}, u32[]{:S(2)}) collective-permute-start(bf16[3,2,192,128]{3,2,1,0:T(8,128)(2,1)S(1)} %pad_maximum_fusion.refs_0_), channel_id=1, source_target_pairs={{16,8},{8,16},{17,9},{9,17},{18,10},{10,18},{19,11},{11,19},{20,12... | collective-permute-start | bytes 884744 | tf_op jit(solution)/shard_map/ppermute | solution.py:422
  16.4 1.6 %collective-permute-start.5 = (bf16[2,2,192,128]{3,2,1,0:T(8,128)(2,1)S(1)}, bf16[2,2,192,128]{3,2,1,0:T(8,128)(2,1)S(1)}, u32[]{:S(2)}, u32[]{:S(2)}) collective-permute-start(bf16[2,2,192,128]{3,2,1,0:T(8,128)(2,1)S(1)} %pad_maximum_fusion.1), channel_id=1, source_target_pairs={{0,1},{1,0},{2,3},{3,2},{4,5},{5,4},{6,7},{7,6},{8,9},{9,8},{10,11... | collective-permute-start | bytes 589832 | tf_op jit(solution)/shard_map/ppermute | solution.py:420
  18.0 3.7 %collective-permute-start.4 = (bf16[192,128]{1,0:T(8,128)(2,1)S(1)}, bf16[192,128]{1,0:T(8,128)(2,1)S(1)}, u32[]{:S(2)}, u32[]{:S(2)}) collective-permute-start(bf16[192,128]{1,0:T(8,128)(2,1)S(1)} %bitcast.19), channel_id=1, source_target_pairs={{0,8},{8,0},{16,24},{24,16},{1,9},{9,1},{17,25},{25,17},{2,10},{10... | collective-permute-start | bytes 147464 | tf_op jit(solution)/shard_map/ppermute | solution.py:106
  21.7 0.1 pad_add_fusion.place
  21.8 0.8 %collective-permute-done.4.queries_other = bf16[192,128]{1,0:T(8,128)(2,1)S(1)} collective-permute-done((bf16[192,128]{1,0:T(8,128)(2,1)S(1)}, bf16[192,128]{1,0:T(8,128)(2,1)S(1)}, u32[]{:S(2)}, u32[]{:S(2)}) %collective-permute-start.4) | collective-permute-done | bytes 49184 | tf_op jit(solution)/shard_map/ppermute | solution.py:106
  22.6 1.3 %copy-done.1 = bf16[4,6,8,3072]{3,2,1,0:T(8,128)(2,1)S(1)} copy-done((bf16[4,6,8,3072]{3,2,1,0:T(8,128)(2,1)S(1)}, bf16[4,6,8,3072]{3,2,1,0:T(8,128)(2,1)}, u32[]{:S(2)}) %copy-start.1) | copy-done | bytes 1179672
  23.8 1.0 %shard_map.92 = (bf16[192,1664]{1,0:T(8,128)(2,1)S(1)}, bf16[192,1536]{1,0:T(8,128)(2,1)S(1)}, bf16[192,128]{1,0:T(8,128)(2,1)S(1)}, bf16[384,128]{1,0:T(8,128)(2,1)S(1)}) custom-call(s32[3]{0:T(128)S(1)} %pad_add_fusion.place, bf16[192,128]{1,0:T(8,128)(2,1)S(1)} %bitcast.20, bf16[192,128]{1,0:T(8,128)(2,1)S(1)} %collective-permute-done.4.queries_other, ...), custom_call_target="tpu_custom_call" | custom-call | flops 150994944 | bytes 2359296 | tf_op jit(solution)/shard_map/pallas_call | solution.py:351
  24.9 0.7 %shard_map.93.refs_4_ = f32[136,384]{1,0:T(8,128)S(1)} custom-call(bf16[384,128]{1,0:T(8,128)(2,1)S(1)} %get-tuple-element.49.both_queries, bf16[3,2,192,128]{3,2,1,0:T(8,128)(2,1)S(1)} %pad_maximum_fusion.refs_0_), custom_call_target="tpu_custom_call" | custom-call | flops 100000000 | bytes 1000000 | tf_op jit(solution)/shard_map/pallas_call | solution.py:465
  25.6 0.4 collective-permute-start.9
  26.0 0.5 collective-permute-done.5.refs_1_.refs_2_
  26.5 0.0 collective-permute-done.7.refs_3_.refs_4_
  26.5 0.0 collective-permute-done.6.refs_2_.refs_3_
  26.5 1.2 %shard_map.94.mine = f32[136,384]{1,0:T(8,128)S(1)} custom-call(bf16[384,128]{1,0:T(8,128)(2,1)S(1)} %get-tuple-element.49.both_queries, bf16[1,2,192,128]{3,2,1,0:T(8,128)(2,1)S(1)} %collective-permute-done.3.refs_0_.refs_1_, bf16[2,2,192,128]{3,2,1,0:T(8,128)(2,1)S(1)} %collective-permute-done.5.refs_1_.refs_2_, ...), custom_call_target="tpu_custom_call" | custom-call | flops 5000000000 | bytes 1000000 | tf_op jit(solution)/shard_map/pallas_call | solution.py:465
  27.7 0.8 %collective-permute-start.8 = (f32[136,384]{1,0:T(8,128)S(1)}, f32[136,384]{1,0:T(8,128)S(1)}, u32[]{:S(2)}, u32[]{:S(2)}) collective-permute-start(f32[136,384]{1,0:T(8,128)S(1)} %shard_map.94.mine), channel_id=1, source_target_pairs={{0,8},{8,0},{16,24},{24,16},{1,9},{9,1},{17,25},{25,17},{2,10},{10... | collective-permute-start | bytes 626696 | tf_op jit(solution)/shard_map/ppermute | solution.py:106
  28.5 1.1 %collective-permute-done.8.theirs = f32[136,384]{1,0:T(8,128)S(1)} collective-permute-done((f32[136,384]{1,0:T(8,128)S(1)}, f32[136,384]{1,0:T(8,128)S(1)}, u32[]{:S(2)}, u32[]{:S(2)}) %collective-permute-start.8) | collective-permute-done | bytes 208928 | tf_op jit(solution)/shard_map/ppermute | solution.py:106
  29.6 0.0 collective-permute-done.9.payload
  29.6 1.1 %shard_map.95 = (f32[8,384]{1,0:T(8,128)S(1)}, bf16[192,128]{1,0:T(8,128)(2,1)S(1)}, bf16[32,1536]{1,0:T(8,128)(2,1)S(1)}, bf16[32,1536]{1,0:T(8,128)(2,1)S(1)},...) custom-call(s32[3]{0:T(128)S(1)} %pad_add_fusion.place, f32[136,384]{1,0:T(8,128)S(1)} %shard_map.94.mine, ...), custom_call_target="tpu_custom_call" | custom-call | flops 150994944 | bytes 2359296 | tf_op jit(solution)/shard_map/pallas_call | solution.py:351
  30.7 1.6 %collective-permute-start.10 = (bf16[32,1536]{1,0:T(8,128)(2,1)S(1)}, bf16[32,1536]{1,0:T(8,128)(2,1)S(1)}, u32[]{:S(2)}, u32[]{:S(2)}) collective-permute-start(bf16[32,1536]{1,0:T(8,128)(2,1)S(1)} %get-tuple-element.62), channel_id=1, source_target_pairs={{0,1},{1,0},{8,9},{9,8},{16,17},{17,16},{24,25},{25,24},{2,3},{3,2... | collective-permute-start | bytes 294920 | tf_op jit(solution)/shard_map/ppermute | solution.py:106
  32.3 0.4 collective-permute-start.11
  32.7 1.6 %collective-permute-start.12 = (bf16[32,1536]{1,0:T(8,128)(2,1)S(1)}, bf16[32,1536]{1,0:T(8,128)(2,1)S(1)}, u32[]{:S(2)}, u32[]{:S(2)}) collective-permute-start(bf16[32,1536]{1,0:T(8,128)(2,1)S(1)} %get-tuple-element.64), channel_id=1, source_target_pairs={{0,17},{1,16},{8,25},{9,24},{16,1},{17,0},{24,9},{25,8},{2,19},{3,... | collective-permute-start | bytes 294920 | tf_op jit(solution)/shard_map/ppermute | solution.py:106
  34.3 2.6 %shard_map.96 = (f32[3,2,192,128]{3,2,1,0:T(8,128)S(1)}, bf16[3,2,192,128]{3,2,1,0:T(8,128)(2,1)S(1)}, bf16[3,2,192,128]{3,2,1,0:T(8,128)(2,1)S(1)}, f32[128,384]{1,0:T(8,128)S(1)}) custom-call(s32[3]{0:T(128)S(1)} %pad_add_fusion.place, f32[8,384]{1,0:T(8,128)S(1)} %get-tuple-element.59.stats, bf16[384,128]{1,0:T(8,128)(2,1)S(1)} %get-tuple-element.49.both_queries, ...), custom_call_target="tpu_custom_call" | custom-call | flops 849346560 | bytes 2359296 | tf_op jit(solution)/shard_map/pallas_call | solution.py:351
  36.9 1.6 %collective-permute-start.19 = (bf16[3,2,192,128]{3,2,1,0:T(8,128)(2,1)S(1)}, bf16[3,2,192,128]{3,2,1,0:T(8,128)(2,1)S(1)}, u32[]{:S(2)}, u32[]{:S(2)}) collective-permute-start(bf16[3,2,192,128]{3,2,1,0:T(8,128)(2,1)S(1)} %get-tuple-element.82), channel_id=1, source_target_pairs={{0,1},{1,0},{2,3},{3,2},{4,5},{5,4},{6,7},{7,6},{8,9},{9,8},{10,11... | collective-permute-start | bytes 884744 | tf_op jit(solution)/shard_map/ppermute | solution.py:542
  38.5 0.0 collective-permute-done.10
  38.5 0.0 collective-permute-done.11
  38.5 0.6 collective-permute-done.12
  39.1 0.1 add_convert_fusion.2
  39.2 0.2 collective-permute-start.13
  39.4 0.7 %shard_map.97 = (f32[192,128]{1,0:T(8,128)S(1)}, bf16[16,1536]{1,0:T(8,128)(2,1)S(1)}) custom-call(s32[3]{0:T(128)S(1)} %pad_add_fusion.place, f32[128,384]{1,0:T(8,128)S(1)} %get-tuple-element.74.query_grad), custom_call_target="tpu_custom_call" | custom-call | flops 10000000000 | bytes 100000000 | tf_op jit(solution)/shard_map/pallas_call | solution.py:351
  40.1 3.2 %collective-permute-start.21 = (bf16[3,2,192,128]{3,2,1,0:T(8,128)(2,1)S(1)}, bf16[3,2,192,128]{3,2,1,0:T(8,128)(2,1)S(1)}, u32[]{:S(2)}, u32[]{:S(2)}) collective-permute-start(bf16[3,2,192,128]{3,2,1,0:T(8,128)(2,1)S(1)} %get-tuple-element.83), channel_id=1, source_target_pairs={{1,16},{0,17},{25,8},{24,9},{3,18},{2,19},{27,10},{26,11},{5,20},{... | collective-permute-start | bytes 884744 | tf_op jit(solution)/shard_map/ppermute | solution.py:544
  43.2 0.7 %collective-permute-start.20 = (bf16[3,2,192,128]{3,2,1,0:T(8,128)(2,1)S(1)}, bf16[3,2,192,128]{3,2,1,0:T(8,128)(2,1)S(1)}, u32[]{:S(2)}, u32[]{:S(2)}) collective-permute-start(bf16[3,2,192,128]{3,2,1,0:T(8,128)(2,1)S(1)} %get-tuple-element.83), channel_id=1, source_target_pairs={{8,16},{16,8},{9,17},{17,9},{10,18},{18,10},{11,19},{19,11},{12,20... | collective-permute-start | bytes 884744 | tf_op jit(solution)/shard_map/ppermute | solution.py:543
  43.9 0.0 collective-permute-done.13
  44.0 1.7 %collective-permute-start.14 = (bf16[32,1536]{1,0:T(8,128)(2,1)S(1)}, bf16[32,1536]{1,0:T(8,128)(2,1)S(1)}, u32[]{:S(2)}, u32[]{:S(2)}) collective-permute-start(bf16[32,1536]{1,0:T(8,128)(2,1)S(1)} %add_convert_fusion.1), channel_id=1, source_target_pairs={{0,4},{2,6},{4,0},{6,2},{1,5},{3,7},{5,1},{7,3},{8,12},{10,14},{12... | collective-permute-start | bytes 294920 | tf_op jit(solution)/shard_map/ppermute | solution.py:106
  45.6 1.5 %convolution_convert_fusion = bf16[192,3072]{1,0:T(8,128)(2,1)} fusion(bf16[192,128]{1,0:T(8,128)(2,1)S(1)} %get-tuple-element.69, bf16[128,3072]{1,0:T(8,128)(2,1)S(1)} %copy-done), kind=kOutput, calls=%fused_computation | convolution fusion | flops 151584768 | bytes 2015232 | tf_op jit(solution)/shard_map/dot_general | solution.py:535
  47.1 4.9 %collective-permute-done.14 = bf16[32,1536]{1,0:T(8,128)(2,1)S(1)} collective-permute-done((bf16[32,1536]{1,0:T(8,128)(2,1)S(1)}, bf16[32,1536]{1,0:T(8,128)(2,1)S(1)}, u32[]{:S(2)}, u32[]{:S(2)}) %collective-permute-start.14) | collective-permute-done | bytes 98336 | tf_op jit(solution)/shard_map/ppermute | solution.py:106
  52.0 0.5 collective-permute-start.17
  52.5 2.2 %collective-permute-start.16 = (bf16[32,1536]{1,0:T(8,128)(2,1)S(1)}, bf16[32,1536]{1,0:T(8,128)(2,1)S(1)}, u32[]{:S(2)}, u32[]{:S(2)}) collective-permute-start(bf16[32,1536]{1,0:T(8,128)(2,1)S(1)} %add_convert_fusion.refs_0_), channel_id=1, source_target_pairs={{0,16},{1,17},{8,24},{9,25},{16,0},{17,1},{24,8},{25,9},{2,18},{3,... | collective-permute-start | bytes 294920 | tf_op jit(solution)/shard_map/ppermute | solution.py:106
  54.7 0.0 collective-permute-done.19.refs_0_
  54.7 0.9 %collective-permute-start.15 = (bf16[32,1536]{1,0:T(8,128)(2,1)S(1)}, bf16[32,1536]{1,0:T(8,128)(2,1)S(1)}, u32[]{:S(2)}, u32[]{:S(2)}) collective-permute-start(bf16[32,1536]{1,0:T(8,128)(2,1)S(1)} %add_convert_fusion.refs_0_), channel_id=1, source_target_pairs={{0,1},{1,0},{8,9},{9,8},{16,17},{17,16},{24,25},{25,24},{2,3},{3,2... | collective-permute-start | bytes 294920 | tf_op jit(solution)/shard_map/ppermute | solution.py:106
  55.6 0.0 collective-permute-done.21.refs_2_
  55.6 0.0 collective-permute-done.20.refs_1_
  55.6 0.1 shard_map.101
  55.7 1.5 %collective-permute-start.24 = (bf16[2,192,128]{2,1,0:T(8,128)(2,1)S(1)}, bf16[2,192,128]{2,1,0:T(8,128)(2,1)S(1)}, u32[]{:S(2)}, u32[]{:S(2)}) collective-permute-start(bf16[2,192,128]{2,1,0:T(8,128)(2,1)S(1)} %get-tuple-element.87), channel_id=1, source_target_pairs={{6,2},{0,4},{7,3},{1,5},{14,10},{8,12},{15,11},{9,13},{22,18},{16,... | collective-permute-start | bytes 294920 | tf_op jit(solution)/shard_map/ppermute | solution.py:87
  57.2 0.7 %collective-permute-start.23 = (bf16[2,192,128]{2,1,0:T(8,128)(2,1)S(1)}, bf16[2,192,128]{2,1,0:T(8,128)(2,1)S(1)}, u32[]{:S(2)}, u32[]{:S(2)}) collective-permute-start(bf16[2,192,128]{2,1,0:T(8,128)(2,1)S(1)} %get-tuple-element.87), channel_id=1, source_target_pairs={{4,2},{2,4},{5,3},{3,5},{12,10},{10,12},{13,11},{11,13},{20,18},{1... | collective-permute-start | bytes 294920 | tf_op jit(solution)/shard_map/ppermute | solution.py:87
  57.9 0.0 collective-permute-done.17.refs_3_
  57.9 1.3 %collective-permute-start.22 = (bf16[2,192,128]{2,1,0:T(8,128)(2,1)S(1)}, bf16[2,192,128]{2,1,0:T(8,128)(2,1)S(1)}, u32[]{:S(2)}, u32[]{:S(2)}) collective-permute-start(bf16[2,192,128]{2,1,0:T(8,128)(2,1)S(1)} %get-tuple-element.86), channel_id=1, source_target_pairs={{0,2},{2,0},{4,6},{6,4},{1,3},{3,1},{5,7},{7,5},{8,10},{10,8},{12,... | collective-permute-start | bytes 294920 | tf_op jit(solution)/shard_map/ppermute | solution.py:87
  59.2 0.0 collective-permute-done.16.refs_2_
  59.2 0.1 collective-permute-done.15.refs_1_
  59.3 0.1 collective-permute-start.18
  59.4 1.5 %shard_map.99.refs_1_ = f32[128,3072]{1,0:T(8,128)} custom-call(s32[3]{0:T(128)S(1)} %pad_add_fusion.place, bf16[144,1536]{1,0:T(8,128)(2,1)S(1)} %shard_map.98.part), custom_call_target="tpu_custom_call" | custom-call | flops 10000000000 | bytes 100000000 | tf_op jit(solution)/shard_map/pallas_call | solution.py:309
  60.9 0.3 collective-permute-done.18.part
  61.2 1.5 %shard_map.100 = (f32[128,3072]{1,0:T(8,128)}, bf16[192,128]{1,0:T(8,128)(2,1)}) custom-call(s32[3]{0:T(128)S(1)} %pad_add_fusion.place, bf16[144,1536]{1,0:T(8,128)(2,1)S(1)} %collective-permute-done.18.part, f32[192,128]{1,0:T(8,128)S(1)} %get-tuple-element.78.refs_0_, f32[128,3072]{1,0:T(8,128)} %shard_map.99.refs_1_), custom_call_target="tpu_custom_call", output_to_operand_aliasing={{0}: (3, {})} | custom-call | flops 10000000000 | bytes 100000000 | tf_op jit(solution)/shard_map/pallas_call | solution.py:309
  62.7 0.0 collective-permute-done.24.refs_2_
  62.7 0.0 collective-permute-done.23.refs_1_
  62.7 0.7 %shard_map.102 = (bf16[192,128]{1,0:T(8,128)(2,1)}, bf16[192,128]{1,0:T(8,128)(2,1)}) custom-call(f32[2,192,128]{2,1,0:T(8,128)S(1)} %get-tuple-element.85.own_grad, bf16[2,192,128]{2,1,0:T(8,128)(2,1)S(1)} %collective-permute-done.22.refs_0_, bf16[2,192,128]{2,1,0:T(8,128)(2,1)S(1)} %collective-permute-done.23.refs_1_, ...), custom_call_target="tpu_custom_call" | custom-call | flops 10000000000 | bytes 100000000 | tf_op jit(solution)/shard_map/pallas_call | solution.py:581
  (12 shorter events, 0.2 us)
Async XLA Ops:
  0.6 17.4 %copy-start.2 = (bf16[4,6,8,128]{3,2,1,0:T(8,128)(2,1)S(1)}, bf16[4,6,8,128]{3,2,1,0:T(8,128)(2,1)}, u32[]{:S(2)}) copy-start(bf16[4,6,8,128]{3,2,1,0:T(8,128)(2,1)} %param.5) | copy-start | bytes 147460
  0.6 21.9 %copy-start = (bf16[128,3072]{1,0:T(8,128)(2,1)S(1)}, bf16[128,3072]{1,0:T(8,128)(2,1)}, u32[]{:S(2)}) copy-start(bf16[128,3072]{1,0:T(8,128)(2,1)} %weight.1) | copy-start | bytes 2359300
  1.6 9.8 %collective-permute-start.2 = (bf16[2,192,128]{2,1,0:T(8,128)(2,1)S(1)}, bf16[2,192,128]{2,1,0:T(8,128)(2,1)S(1)}, u32[]{:S(2)}, u32[]{:S(2)}) collective-permute-start(bf16[2,192,128]{2,1,0:T(8,128)(2,1)S(1)} %get-tuple-element.92), channel_id=1, source_target_pairs={{2,4},{4,2},{3,5},{5,3},{10,12},{12,10},{11,13},{13,11},{18,20},{2... | collective-permute-start | bytes 294920 | tf_op jit(solution)/shard_map/ppermute | solution.py:65
  2.2 10.5 %collective-permute-start.1 = (bf16[2,192,128]{2,1,0:T(8,128)(2,1)S(1)}, bf16[2,192,128]{2,1,0:T(8,128)(2,1)S(1)}, u32[]{:S(2)}, u32[]{:S(2)}) collective-permute-start(bf16[2,192,128]{2,1,0:T(8,128)(2,1)S(1)} %get-tuple-element.92), channel_id=1, source_target_pairs={{2,6},{4,0},{3,7},{5,1},{10,14},{12,8},{11,15},{13,9},{18,22},{20,... | collective-permute-start | bytes 294920 | tf_op jit(solution)/shard_map/ppermute | solution.py:65
  3.5 10.6 %collective-permute-start = (bf16[2,192,128]{2,1,0:T(8,128)(2,1)S(1)}, bf16[2,192,128]{2,1,0:T(8,128)(2,1)S(1)}, u32[]{:S(2)}, u32[]{:S(2)}) collective-permute-start(bf16[2,192,128]{2,1,0:T(8,128)(2,1)S(1)} %get-tuple-element.92), channel_id=1, source_target_pairs={{2,0},{0,2},{6,4},{4,6},{3,1},{1,3},{7,5},{5,7},{10,8},{8,10},{14,... | collective-permute-start | bytes 294920 | tf_op jit(solution)/shard_map/ppermute | solution.py:65
  9.8 4.6 %collective-permute-start.3 = (bf16[1,2,192,128]{3,2,1,0:T(8,128)(2,1)S(1)}, bf16[1,2,192,128]{3,2,1,0:T(8,128)(2,1)S(1)}, u32[]{:S(2)}, u32[]{:S(2)}) collective-permute-start(bf16[1,2,192,128]{3,2,1,0:T(8,128)(2,1)S(1)} %get-tuple-element.91), channel_id=1, source_target_pairs={{0,1},{1,0},{2,3},{3,2},{4,5},{5,4},{6,7},{7,6},{8,9},{9,8},{10,11... | collective-permute-start | bytes 294920 | tf_op jit(solution)/shard_map/ppermute | solution.py:414
  14.5 12.1 %collective-permute-start.7 = (bf16[3,2,192,128]{3,2,1,0:T(8,128)(2,1)S(1)}, bf16[3,2,192,128]{3,2,1,0:T(8,128)(2,1)S(1)}, u32[]{:S(2)}, u32[]{:S(2)}) collective-permute-start(bf16[3,2,192,128]{3,2,1,0:T(8,128)(2,1)S(1)} %pad_maximum_fusion.refs_0_), channel_id=1, source_target_pairs={{16,1},{17,0},{8,25},{9,24},{18,3},{19,2},{10,27},{11,26},{20,5},{... | collective-permute-start | bytes 884744 | tf_op jit(solution)/shard_map/ppermute | solution.py:423
  15.7 10.8 %collective-permute-start.6 = (bf16[3,2,192,128]{3,2,1,0:T(8,128)(2,1)S(1)}, bf16[3,2,192,128]{3,2,1,0:T(8,128)(2,1)S(1)}, u32[]{:S(2)}, u32[]{:S(2)}) collective-permute-start(bf16[3,2,192,128]{3,2,1,0:T(8,128)(2,1)S(1)} %pad_maximum_fusion.refs_0_), channel_id=1, source_target_pairs={{16,8},{8,16},{17,9},{9,17},{18,10},{10,18},{19,11},{11,19},{20,12... | collective-permute-start | bytes 884744 | tf_op jit(solution)/shard_map/ppermute | solution.py:422
  16.4 10.1 %collective-permute-start.5 = (bf16[2,2,192,128]{3,2,1,0:T(8,128)(2,1)S(1)}, bf16[2,2,192,128]{3,2,1,0:T(8,128)(2,1)S(1)}, u32[]{:S(2)}, u32[]{:S(2)}) collective-permute-start(bf16[2,2,192,128]{3,2,1,0:T(8,128)(2,1)S(1)} %pad_maximum_fusion.1), channel_id=1, source_target_pairs={{0,1},{1,0},{2,3},{3,2},{4,5},{5,4},{6,7},{7,6},{8,9},{9,8},{10,11... | collective-permute-start | bytes 589832 | tf_op jit(solution)/shard_map/ppermute | solution.py:420
  18.0 4.5 %collective-permute-start.4 = (bf16[192,128]{1,0:T(8,128)(2,1)S(1)}, bf16[192,128]{1,0:T(8,128)(2,1)S(1)}, u32[]{:S(2)}, u32[]{:S(2)}) collective-permute-start(bf16[192,128]{1,0:T(8,128)(2,1)S(1)} %bitcast.19), channel_id=1, source_target_pairs={{0,8},{8,0},{16,24},{24,16},{1,9},{9,1},{17,25},{25,17},{2,10},{10... | collective-permute-start | bytes 147464 | tf_op jit(solution)/shard_map/ppermute | solution.py:106
  22.6 1.3 %copy-start.1 = (bf16[4,6,8,3072]{3,2,1,0:T(8,128)(2,1)S(1)}, bf16[4,6,8,3072]{3,2,1,0:T(8,128)(2,1)}, u32[]{:S(2)}) copy-start(bf16[4,6,8,3072]{3,2,1,0:T(8,128)(2,1)} %param.9) | copy-start | bytes 3538948
  25.6 4.0 %collective-permute-start.9 = (bf16[192,1664]{1,0:T(8,128)(2,1)S(1)}, bf16[192,1664]{1,0:T(8,128)(2,1)S(1)}, u32[]{:S(2)}, u32[]{:S(2)}) collective-permute-start(bf16[192,1664]{1,0:T(8,128)(2,1)S(1)} %get-tuple-element.55), channel_id=1, source_target_pairs={{0,8},{8,0},{16,24},{24,16},{1,9},{9,1},{17,25},{25,17},{2,10},{10... | collective-permute-start | bytes 1916936 | tf_op jit(solution)/shard_map/ppermute | solution.py:106
  27.7 1.9 %collective-permute-start.8 = (f32[136,384]{1,0:T(8,128)S(1)}, f32[136,384]{1,0:T(8,128)S(1)}, u32[]{:S(2)}, u32[]{:S(2)}) collective-permute-start(f32[136,384]{1,0:T(8,128)S(1)} %shard_map.94.mine), channel_id=1, source_target_pairs={{0,8},{8,0},{16,24},{24,16},{1,9},{9,1},{17,25},{25,17},{2,10},{10... | collective-permute-start | bytes 626696 | tf_op jit(solution)/shard_map/ppermute | solution.py:106
  30.7 7.8 %collective-permute-start.10 = (bf16[32,1536]{1,0:T(8,128)(2,1)S(1)}, bf16[32,1536]{1,0:T(8,128)(2,1)S(1)}, u32[]{:S(2)}, u32[]{:S(2)}) collective-permute-start(bf16[32,1536]{1,0:T(8,128)(2,1)S(1)} %get-tuple-element.62), channel_id=1, source_target_pairs={{0,1},{1,0},{8,9},{9,8},{16,17},{17,16},{24,25},{25,24},{2,3},{3,2... | collective-permute-start | bytes 294920 | tf_op jit(solution)/shard_map/ppermute | solution.py:106
  32.3 6.2 %collective-permute-start.11 = (bf16[32,1536]{1,0:T(8,128)(2,1)S(1)}, bf16[32,1536]{1,0:T(8,128)(2,1)S(1)}, u32[]{:S(2)}, u32[]{:S(2)}) collective-permute-start(bf16[32,1536]{1,0:T(8,128)(2,1)S(1)} %get-tuple-element.63), channel_id=1, source_target_pairs={{0,16},{1,17},{8,24},{9,25},{16,0},{17,1},{24,8},{25,9},{2,18},{3,... | collective-permute-start | bytes 294920 | tf_op jit(solution)/shard_map/ppermute | solution.py:106
  32.7 6.4 %collective-permute-start.12 = (bf16[32,1536]{1,0:T(8,128)(2,1)S(1)}, bf16[32,1536]{1,0:T(8,128)(2,1)S(1)}, u32[]{:S(2)}, u32[]{:S(2)}) collective-permute-start(bf16[32,1536]{1,0:T(8,128)(2,1)S(1)} %get-tuple-element.64), channel_id=1, source_target_pairs={{0,17},{1,16},{8,25},{9,24},{16,1},{17,0},{24,9},{25,8},{2,19},{3,... | collective-permute-start | bytes 294920 | tf_op jit(solution)/shard_map/ppermute | solution.py:106
  36.9 17.8 %collective-permute-start.19 = (bf16[3,2,192,128]{3,2,1,0:T(8,128)(2,1)S(1)}, bf16[3,2,192,128]{3,2,1,0:T(8,128)(2,1)S(1)}, u32[]{:S(2)}, u32[]{:S(2)}) collective-permute-start(bf16[3,2,192,128]{3,2,1,0:T(8,128)(2,1)S(1)} %get-tuple-element.82), channel_id=1, source_target_pairs={{0,1},{1,0},{2,3},{3,2},{4,5},{5,4},{6,7},{7,6},{8,9},{9,8},{10,11... | collective-permute-start | bytes 884744 | tf_op jit(solution)/shard_map/ppermute | solution.py:542
  39.2 4.7 %collective-permute-start.13 = (bf16[32,1536]{1,0:T(8,128)(2,1)S(1)}, bf16[32,1536]{1,0:T(8,128)(2,1)S(1)}, u32[]{:S(2)}, u32[]{:S(2)}) collective-permute-start(bf16[32,1536]{1,0:T(8,128)(2,1)S(1)} %add_convert_fusion.2), channel_id=1, source_target_pairs={{0,2},{2,0},{4,6},{6,4},{1,3},{3,1},{5,7},{7,5},{8,10},{10,8},{12,... | collective-permute-start | bytes 294920 | tf_op jit(solution)/shard_map/ppermute | solution.py:106
  40.1 15.5 %collective-permute-start.21 = (bf16[3,2,192,128]{3,2,1,0:T(8,128)(2,1)S(1)}, bf16[3,2,192,128]{3,2,1,0:T(8,128)(2,1)S(1)}, u32[]{:S(2)}, u32[]{:S(2)}) collective-permute-start(bf16[3,2,192,128]{3,2,1,0:T(8,128)(2,1)S(1)} %get-tuple-element.83), channel_id=1, source_target_pairs={{1,16},{0,17},{25,8},{24,9},{3,18},{2,19},{27,10},{26,11},{5,20},{... | collective-permute-start | bytes 884744 | tf_op jit(solution)/shard_map/ppermute | solution.py:544
  43.2 12.3 %collective-permute-start.20 = (bf16[3,2,192,128]{3,2,1,0:T(8,128)(2,1)S(1)}, bf16[3,2,192,128]{3,2,1,0:T(8,128)(2,1)S(1)}, u32[]{:S(2)}, u32[]{:S(2)}) collective-permute-start(bf16[3,2,192,128]{3,2,1,0:T(8,128)(2,1)S(1)} %get-tuple-element.83), channel_id=1, source_target_pairs={{8,16},{16,8},{9,17},{17,9},{10,18},{18,10},{11,19},{19,11},{12,20... | collective-permute-start | bytes 884744 | tf_op jit(solution)/shard_map/ppermute | solution.py:543
  44.0 8.0 %collective-permute-start.14 = (bf16[32,1536]{1,0:T(8,128)(2,1)S(1)}, bf16[32,1536]{1,0:T(8,128)(2,1)S(1)}, u32[]{:S(2)}, u32[]{:S(2)}) collective-permute-start(bf16[32,1536]{1,0:T(8,128)(2,1)S(1)} %add_convert_fusion.1), channel_id=1, source_target_pairs={{0,4},{2,6},{4,0},{6,2},{1,5},{3,7},{5,1},{7,3},{8,12},{10,14},{12... | collective-permute-start | bytes 294920 | tf_op jit(solution)/shard_map/ppermute | solution.py:106
  52.0 5.9 %collective-permute-start.17 = (bf16[32,1536]{1,0:T(8,128)(2,1)S(1)}, bf16[32,1536]{1,0:T(8,128)(2,1)S(1)}, u32[]{:S(2)}, u32[]{:S(2)}) collective-permute-start(bf16[32,1536]{1,0:T(8,128)(2,1)S(1)} %add_convert_fusion.refs_0_), channel_id=1, source_target_pairs={{0,17},{1,16},{8,25},{9,24},{16,1},{17,0},{24,9},{25,8},{2,19},{3,... | collective-permute-start | bytes 294920 | tf_op jit(solution)/shard_map/ppermute | solution.py:106
  52.5 6.7 %collective-permute-start.16 = (bf16[32,1536]{1,0:T(8,128)(2,1)S(1)}, bf16[32,1536]{1,0:T(8,128)(2,1)S(1)}, u32[]{:S(2)}, u32[]{:S(2)}) collective-permute-start(bf16[32,1536]{1,0:T(8,128)(2,1)S(1)} %add_convert_fusion.refs_0_), channel_id=1, source_target_pairs={{0,16},{1,17},{8,24},{9,25},{16,0},{17,1},{24,8},{25,9},{2,18},{3,... | collective-permute-start | bytes 294920 | tf_op jit(solution)/shard_map/ppermute | solution.py:106
  54.7 4.6 %collective-permute-start.15 = (bf16[32,1536]{1,0:T(8,128)(2,1)S(1)}, bf16[32,1536]{1,0:T(8,128)(2,1)S(1)}, u32[]{:S(2)}, u32[]{:S(2)}) collective-permute-start(bf16[32,1536]{1,0:T(8,128)(2,1)S(1)} %add_convert_fusion.refs_0_), channel_id=1, source_target_pairs={{0,1},{1,0},{8,9},{9,8},{16,17},{17,16},{24,25},{25,24},{2,3},{3,2... | collective-permute-start | bytes 294920 | tf_op jit(solution)/shard_map/ppermute | solution.py:106
  55.7 7.0 %collective-permute-start.24 = (bf16[2,192,128]{2,1,0:T(8,128)(2,1)S(1)}, bf16[2,192,128]{2,1,0:T(8,128)(2,1)S(1)}, u32[]{:S(2)}, u32[]{:S(2)}) collective-permute-start(bf16[2,192,128]{2,1,0:T(8,128)(2,1)S(1)} %get-tuple-element.87), channel_id=1, source_target_pairs={{6,2},{0,4},{7,3},{1,5},{14,10},{8,12},{15,11},{9,13},{22,18},{16,... | collective-permute-start | bytes 294920 | tf_op jit(solution)/shard_map/ppermute | solution.py:87
  57.2 5.5 %collective-permute-start.23 = (bf16[2,192,128]{2,1,0:T(8,128)(2,1)S(1)}, bf16[2,192,128]{2,1,0:T(8,128)(2,1)S(1)}, u32[]{:S(2)}, u32[]{:S(2)}) collective-permute-start(bf16[2,192,128]{2,1,0:T(8,128)(2,1)S(1)} %get-tuple-element.87), channel_id=1, source_target_pairs={{4,2},{2,4},{5,3},{3,5},{12,10},{10,12},{13,11},{11,13},{20,18},{1... | collective-permute-start | bytes 294920 | tf_op jit(solution)/shard_map/ppermute | solution.py:87
  57.9 4.8 %collective-permute-start.22 = (bf16[2,192,128]{2,1,0:T(8,128)(2,1)S(1)}, bf16[2,192,128]{2,1,0:T(8,128)(2,1)S(1)}, u32[]{:S(2)}, u32[]{:S(2)}) collective-permute-start(bf16[2,192,128]{2,1,0:T(8,128)(2,1)S(1)} %get-tuple-element.86), channel_id=1, source_target_pairs={{0,2},{2,0},{4,6},{6,4},{1,3},{3,1},{5,7},{7,5},{8,10},{10,8},{12,... | collective-permute-start | bytes 294920 | tf_op jit(solution)/shard_map/ppermute | solution.py:87
  59.3 1.9 %collective-permute-start.18 = (bf16[144,1536]{1,0:T(8,128)(2,1)S(1)}, bf16[144,1536]{1,0:T(8,128)(2,1)S(1)}, u32[]{:S(2)}, u32[]{:S(2)}) collective-permute-start(bf16[144,1536]{1,0:T(8,128)(2,1)S(1)} %shard_map.98.part), channel_id=1, source_target_pairs={{0,8},{8,0},{16,24},{24,16},{1,9},{9,1},{17,25},{25,17},{2,10},{10... | collective-permute-start | bytes 1327112 | tf_op jit(solution)/shard_map/ppermute | solution.py:106

commit v14 on v13

--- a/solution.py
+++ b/solution.py
@@ -319,11 +319,17 @@
 
 
 def owner_kernel(own_grad, *refs):
-    for k, out in enumerate(refs[-2:]):
+    arrived, (key_out, value_out, sums, done) = refs[:-4], refs[-4:]
+    copies = []
+    for k, out in enumerate((key_out, value_out)):
         total = own_grad[k]
-        for block in refs[:-2]:
+        for block in arrived:
             total = total + block[k].astype(jnp.float32)
-        out[...] = total.astype(jnp.bfloat16)
+        sums[k] = total.astype(jnp.bfloat16)
+        copies.append(pltpu.make_async_copy(sums.at[k], out, done.at[k]))
+        copies[-1].start()
+    for copy in copies:
+        copy.wait()
 
 
 def pack_kernel(*refs):
@@ -582,7 +588,11 @@
         owner_kernel,
         out_shape=[shaped(tile, head_dim)] * 2,
         in_specs=[VMEM] * len(operands),
-        out_specs=[VMEM] * 2,
+        out_specs=[pl.BlockSpec(memory_space=pl.ANY)] * 2,
+        scratch_shapes=[
+            pltpu.VMEM((2, tile, head_dim), jnp.bfloat16),
+            pltpu.SemaphoreType.DMA((2,)),
+        ],
         compiler_params=PARAMS,
         cost_estimate=cost_of(10**10, 10**8),
     )(*operands)

time: 63.7 us -> 63.7 us (level)
  no operation moved by 1% of the time
where the time goes in v14:
time: 63.7 us; the launch traced here: 63.4 us
  starting transfers between devices  36.1 us (57%)
  waiting for transfers between devices  11.4 us (18%)
  Pallas kernels  11.1 us (17%)
  matrix products  1.47 us (2%)
  local copies, waits for them, and re-layouts  1.28 us (2%)
  other arithmetic  1.17 us (2%)
  between operations  0.88 us (1%)
    ppermute x12, starting transfers between devices, flip(): return lax.ppermute(block, axes, route)  13.9 us
    ppermute x3, starting transfers between devices, fetch(): arrived = [lax.ppermute(block, axis, route) for route in routes]  8.25 us
    ppermute x12, waiting for transfers between devices, flip(): return lax.ppermute(block, axes, route)  7.84 us
    pallas_call x4, Pallas kernels, kernel_call(): pl.pallas_call(kernel, out_shape=outs, in_specs=[SMEM] + [VMEM] * (len(op...  5.43 us
    ppermute x3, starting transfers between devices, returned(): arrived.append(lax.ppermute(outgoing, axis, [(p, s) for s, p in route]))  3.44 us
    ppermute x1, starting transfers between devices, body(): lax.ppermute(far_grad, ('frame', 'width'), [(p, s) for s, p in cross])  3.16 us
    pallas_call x2, Pallas kernels, assemble(): pl.pallas_call(functools.partial(assemble_kernel, flipped, rows), out_sha...  2.95 us
    ppermute x3, waiting for transfers between devices, fetch(): arrived = [lax.ppermute(block, axis, route) for route in routes]  2.79 us
  transfers between devices with their start and end apart: 25, of which 10 were waited for; matrix products, arithmetic and copies ran while one was open for 3% of the time, Pallas kernels for 15%

profile of v14, /device:TPU:0, one launch (start us, length us, event | category | flops | bytes accessed | tf_op | source)
XLA Modules:
  0.0 63.4 jit_solution(16380945870444202675)
XLA Ops:
  0.7 0.9 %fusion = (bf16[1,2,192,128]{3,2,1,0:T(8,128)(2,1)S(1)}, bf16[2,192,128]{2,1,0:T(8,128)(2,1)S(1)}) fusion(bf16[1,192,128]{2,1,0:T(8,128)(2,1)} %bitcast.24, bf16[1,192,128]{2,1,0:T(8,128)(2,1)} %bitcast.25), kind=kLoop, calls=%fused_computation.9 | loop fusion | flops 49152 | bytes 294912 | tf_op jit(solution)/shard_map/stack | solution.py:422
  1.6 0.7 %collective-permute-start.2 = (bf16[2,192,128]{2,1,0:T(8,128)(2,1)S(1)}, bf16[2,192,128]{2,1,0:T(8,128)(2,1)S(1)}, u32[]{:S(2)}, u32[]{:S(2)}) collective-permute-start(bf16[2,192,128]{2,1,0:T(8,128)(2,1)S(1)} %get-tuple-element.92), channel_id=1, source_target_pairs={{2,4},{4,2},{3,5},{5,3},{10,12},{12,10},{11,13},{13,11},{18,20},{2... | collective-permute-start | bytes 294920 | tf_op jit(solution)/shard_map/ppermute | solution.py:65
  2.2 1.3 %collective-permute-start.1 = (bf16[2,192,128]{2,1,0:T(8,128)(2,1)S(1)}, bf16[2,192,128]{2,1,0:T(8,128)(2,1)S(1)}, u32[]{:S(2)}, u32[]{:S(2)}) collective-permute-start(bf16[2,192,128]{2,1,0:T(8,128)(2,1)S(1)} %get-tuple-element.92), channel_id=1, source_target_pairs={{2,6},{4,0},{3,7},{5,1},{10,14},{12,8},{11,15},{13,9},{18,22},{20,... | collective-permute-start | bytes 294920 | tf_op jit(solution)/shard_map/ppermute | solution.py:65
  3.5 6.3 %collective-permute-start = (bf16[2,192,128]{2,1,0:T(8,128)(2,1)S(1)}, bf16[2,192,128]{2,1,0:T(8,128)(2,1)S(1)}, u32[]{:S(2)}, u32[]{:S(2)}) collective-permute-start(bf16[2,192,128]{2,1,0:T(8,128)(2,1)S(1)} %get-tuple-element.92), channel_id=1, source_target_pairs={{2,0},{0,2},{6,4},{4,6},{3,1},{1,3},{7,5},{5,7},{10,8},{8,10},{14,... | collective-permute-start | bytes 294920 | tf_op jit(solution)/shard_map/ppermute | solution.py:65
  9.8 1.5 %collective-permute-start.3 = (bf16[1,2,192,128]{3,2,1,0:T(8,128)(2,1)S(1)}, bf16[1,2,192,128]{3,2,1,0:T(8,128)(2,1)S(1)}, u32[]{:S(2)}, u32[]{:S(2)}) collective-permute-start(bf16[1,2,192,128]{3,2,1,0:T(8,128)(2,1)S(1)} %get-tuple-element.91), channel_id=1, source_target_pairs={{0,1},{1,0},{2,3},{3,2},{4,5},{5,4},{6,7},{7,6},{8,9},{9,8},{10,11... | collective-permute-start | bytes 294920 | tf_op jit(solution)/shard_map/ppermute | solution.py:420
  11.4 0.0 collective-permute-done.2
  11.4 1.4 %collective-permute-done.1 = bf16[2,192,128]{2,1,0:T(8,128)(2,1)S(1)} collective-permute-done((bf16[2,192,128]{2,1,0:T(8,128)(2,1)S(1)}, bf16[2,192,128]{2,1,0:T(8,128)(2,1)S(1)}, u32[]{:S(2)}, u32[]{:S(2)}) %collective-permute-start.1) | collective-permute-done | bytes 98336 | tf_op jit(solution)/shard_map/ppermute | solution.py:65
  12.8 1.4 %collective-permute-done = bf16[2,192,128]{2,1,0:T(8,128)(2,1)S(1)} collective-permute-done((bf16[2,192,128]{2,1,0:T(8,128)(2,1)S(1)}, bf16[2,192,128]{2,1,0:T(8,128)(2,1)S(1)}, u32[]{:S(2)}, u32[]{:S(2)}) %collective-permute-start) | collective-permute-done | bytes 98336 | tf_op jit(solution)/shard_map/ppermute | solution.py:65
  14.2 0.2 collective-permute-done.3.refs_0_.refs_1_
  14.5 1.3 %collective-permute-start.7 = (bf16[3,2,192,128]{3,2,1,0:T(8,128)(2,1)S(1)}, bf16[3,2,192,128]{3,2,1,0:T(8,128)(2,1)S(1)}, u32[]{:S(2)}, u32[]{:S(2)}) collective-permute-start(bf16[3,2,192,128]{3,2,1,0:T(8,128)(2,1)S(1)} %pad_maximum_fusion.refs_0_), channel_id=1, source_target_pairs={{16,1},{17,0},{8,25},{9,24},{18,3},{19,2},{10,27},{11,26},{20,5},{... | collective-permute-start | bytes 884744 | tf_op jit(solution)/shard_map/ppermute | solution.py:429
  15.7 0.7 %collective-permute-start.6 = (bf16[3,2,192,128]{3,2,1,0:T(8,128)(2,1)S(1)}, bf16[3,2,192,128]{3,2,1,0:T(8,128)(2,1)S(1)}, u32[]{:S(2)}, u32[]{:S(2)}) collective-permute-start(bf16[3,2,192,128]{3,2,1,0:T(8,128)(2,1)S(1)} %pad_maximum_fusion.refs_0_), channel_id=1, source_target_pairs={{16,8},{8,16},{17,9},{9,17},{18,10},{10,18},{19,11},{11,19},{20,12... | collective-permute-start | bytes 884744 | tf_op jit(solution)/shard_map/ppermute | solution.py:428
  16.4 1.6 %collective-permute-start.5 = (bf16[2,2,192,128]{3,2,1,0:T(8,128)(2,1)S(1)}, bf16[2,2,192,128]{3,2,1,0:T(8,128)(2,1)S(1)}, u32[]{:S(2)}, u32[]{:S(2)}) collective-permute-start(bf16[2,2,192,128]{3,2,1,0:T(8,128)(2,1)S(1)} %pad_maximum_fusion.1), channel_id=1, source_target_pairs={{0,1},{1,0},{2,3},{3,2},{4,5},{5,4},{6,7},{7,6},{8,9},{9,8},{10,11... | collective-permute-start | bytes 589832 | tf_op jit(solution)/shard_map/ppermute | solution.py:426
  18.0 3.7 %collective-permute-start.4 = (bf16[192,128]{1,0:T(8,128)(2,1)S(1)}, bf16[192,128]{1,0:T(8,128)(2,1)S(1)}, u32[]{:S(2)}, u32[]{:S(2)}) collective-permute-start(bf16[192,128]{1,0:T(8,128)(2,1)S(1)} %bitcast.19), channel_id=1, source_target_pairs={{0,8},{8,0},{16,24},{24,16},{1,9},{9,1},{17,25},{25,17},{2,10},{10... | collective-permute-start | bytes 147464 | tf_op jit(solution)/shard_map/ppermute | solution.py:106
  21.7 0.1 pad_add_fusion.place
  21.8 0.8 %collective-permute-done.4.queries_other = bf16[192,128]{1,0:T(8,128)(2,1)S(1)} collective-permute-done((bf16[192,128]{1,0:T(8,128)(2,1)S(1)}, bf16[192,128]{1,0:T(8,128)(2,1)S(1)}, u32[]{:S(2)}, u32[]{:S(2)}) %collective-permute-start.4) | collective-permute-done | bytes 49184 | tf_op jit(solution)/shard_map/ppermute | solution.py:106
  22.6 1.3 %copy-done.1 = bf16[4,6,8,3072]{3,2,1,0:T(8,128)(2,1)S(1)} copy-done((bf16[4,6,8,3072]{3,2,1,0:T(8,128)(2,1)S(1)}, bf16[4,6,8,3072]{3,2,1,0:T(8,128)(2,1)}, u32[]{:S(2)}) %copy-start.1) | copy-done | bytes 1179672
  23.8 1.0 %shard_map.92 = (bf16[192,1664]{1,0:T(8,128)(2,1)S(1)}, bf16[192,1536]{1,0:T(8,128)(2,1)S(1)}, bf16[192,128]{1,0:T(8,128)(2,1)S(1)}, bf16[384,128]{1,0:T(8,128)(2,1)S(1)}) custom-call(s32[3]{0:T(128)S(1)} %pad_add_fusion.place, bf16[192,128]{1,0:T(8,128)(2,1)S(1)} %bitcast.20, bf16[192,128]{1,0:T(8,128)(2,1)S(1)} %collective-permute-done.4.queries_other, ...), custom_call_target="tpu_custom_call" | custom-call | flops 150994944 | bytes 2359296 | tf_op jit(solution)/shard_map/pallas_call | solution.py:357
  24.9 0.7 %shard_map.93.refs_4_ = f32[136,384]{1,0:T(8,128)S(1)} custom-call(bf16[384,128]{1,0:T(8,128)(2,1)S(1)} %get-tuple-element.49.both_queries, bf16[3,2,192,128]{3,2,1,0:T(8,128)(2,1)S(1)} %pad_maximum_fusion.refs_0_), custom_call_target="tpu_custom_call" | custom-call | flops 100000000 | bytes 1000000 | tf_op jit(solution)/shard_map/pallas_call | solution.py:471
  25.6 0.4 collective-permute-start.9
  26.0 0.5 collective-permute-done.5.refs_1_.refs_2_
  26.5 0.0 collective-permute-done.7.refs_3_.refs_4_
  26.5 0.0 collective-permute-done.6.refs_2_.refs_3_
  26.5 1.2 %shard_map.94.mine = f32[136,384]{1,0:T(8,128)S(1)} custom-call(bf16[384,128]{1,0:T(8,128)(2,1)S(1)} %get-tuple-element.49.both_queries, bf16[1,2,192,128]{3,2,1,0:T(8,128)(2,1)S(1)} %collective-permute-done.3.refs_0_.refs_1_, bf16[2,2,192,128]{3,2,1,0:T(8,128)(2,1)S(1)} %collective-permute-done.5.refs_1_.refs_2_, ...), custom_call_target="tpu_custom_call" | custom-call | flops 5000000000 | bytes 1000000 | tf_op jit(solution)/shard_map/pallas_call | solution.py:471
  27.7 0.8 %collective-permute-start.8 = (f32[136,384]{1,0:T(8,128)S(1)}, f32[136,384]{1,0:T(8,128)S(1)}, u32[]{:S(2)}, u32[]{:S(2)}) collective-permute-start(f32[136,384]{1,0:T(8,128)S(1)} %shard_map.94.mine), channel_id=1, source_target_pairs={{0,8},{8,0},{16,24},{24,16},{1,9},{9,1},{17,25},{25,17},{2,10},{10... | collective-permute-start | bytes 626696 | tf_op jit(solution)/shard_map/ppermute | solution.py:106
  28.5 1.1 %collective-permute-done.8.theirs = f32[136,384]{1,0:T(8,128)S(1)} collective-permute-done((f32[136,384]{1,0:T(8,128)S(1)}, f32[136,384]{1,0:T(8,128)S(1)}, u32[]{:S(2)}, u32[]{:S(2)}) %collective-permute-start.8) | collective-permute-done | bytes 208928 | tf_op jit(solution)/shard_map/ppermute | solution.py:106
  29.6 0.0 collective-permute-done.9.payload
  29.6 1.1 %shard_map.95 = (f32[8,384]{1,0:T(8,128)S(1)}, bf16[192,128]{1,0:T(8,128)(2,1)S(1)}, bf16[32,1536]{1,0:T(8,128)(2,1)S(1)}, bf16[32,1536]{1,0:T(8,128)(2,1)S(1)},...) custom-call(s32[3]{0:T(128)S(1)} %pad_add_fusion.place, f32[136,384]{1,0:T(8,128)S(1)} %shard_map.94.mine, ...), custom_call_target="tpu_custom_call" | custom-call | flops 150994944 | bytes 2359296 | tf_op jit(solution)/shard_map/pallas_call | solution.py:357
  30.7 1.6 %collective-permute-start.10 = (bf16[32,1536]{1,0:T(8,128)(2,1)S(1)}, bf16[32,1536]{1,0:T(8,128)(2,1)S(1)}, u32[]{:S(2)}, u32[]{:S(2)}) collective-permute-start(bf16[32,1536]{1,0:T(8,128)(2,1)S(1)} %get-tuple-element.62), channel_id=1, source_target_pairs={{0,1},{1,0},{8,9},{9,8},{16,17},{17,16},{24,25},{25,24},{2,3},{3,2... | collective-permute-start | bytes 294920 | tf_op jit(solution)/shard_map/ppermute | solution.py:106
  32.3 0.4 collective-permute-start.11
  32.7 1.6 %collective-permute-start.12 = (bf16[32,1536]{1,0:T(8,128)(2,1)S(1)}, bf16[32,1536]{1,0:T(8,128)(2,1)S(1)}, u32[]{:S(2)}, u32[]{:S(2)}) collective-permute-start(bf16[32,1536]{1,0:T(8,128)(2,1)S(1)} %get-tuple-element.64), channel_id=1, source_target_pairs={{0,17},{1,16},{8,25},{9,24},{16,1},{17,0},{24,9},{25,8},{2,19},{3,... | collective-permute-start | bytes 294920 | tf_op jit(solution)/shard_map/ppermute | solution.py:106
  34.3 2.6 %shard_map.96 = (f32[3,2,192,128]{3,2,1,0:T(8,128)S(1)}, bf16[3,2,192,128]{3,2,1,0:T(8,128)(2,1)S(1)}, bf16[3,2,192,128]{3,2,1,0:T(8,128)(2,1)S(1)}, f32[128,384]{1,0:T(8,128)S(1)}) custom-call(s32[3]{0:T(128)S(1)} %pad_add_fusion.place, f32[8,384]{1,0:T(8,128)S(1)} %get-tuple-element.59.stats, bf16[384,128]{1,0:T(8,128)(2,1)S(1)} %get-tuple-element.49.both_queries, ...), custom_call_target="tpu_custom_call" | custom-call | flops 849346560 | bytes 2359296 | tf_op jit(solution)/shard_map/pallas_call | solution.py:357
  36.9 1.6 %collective-permute-start.19 = (bf16[3,2,192,128]{3,2,1,0:T(8,128)(2,1)S(1)}, bf16[3,2,192,128]{3,2,1,0:T(8,128)(2,1)S(1)}, u32[]{:S(2)}, u32[]{:S(2)}) collective-permute-start(bf16[3,2,192,128]{3,2,1,0:T(8,128)(2,1)S(1)} %get-tuple-element.82), channel_id=1, source_target_pairs={{0,1},{1,0},{2,3},{3,2},{4,5},{5,4},{6,7},{7,6},{8,9},{9,8},{10,11... | collective-permute-start | bytes 884744 | tf_op jit(solution)/shard_map/ppermute | solution.py:548
  38.5 0.0 collective-permute-done.10
  38.5 0.0 collective-permute-done.11
  38.5 0.6 collective-permute-done.12
  39.1 0.1 add_convert_fusion.2
  39.2 0.2 collective-permute-start.13
  39.4 0.7 %shard_map.97 = (f32[192,128]{1,0:T(8,128)S(1)}, bf16[16,1536]{1,0:T(8,128)(2,1)S(1)}) custom-call(s32[3]{0:T(128)S(1)} %pad_add_fusion.place, f32[128,384]{1,0:T(8,128)S(1)} %get-tuple-element.74.query_grad), custom_call_target="tpu_custom_call" | custom-call | flops 10000000000 | bytes 100000000 | tf_op jit(solution)/shard_map/pallas_call | solution.py:357
  40.1 3.2 %collective-permute-start.21 = (bf16[3,2,192,128]{3,2,1,0:T(8,128)(2,1)S(1)}, bf16[3,2,192,128]{3,2,1,0:T(8,128)(2,1)S(1)}, u32[]{:S(2)}, u32[]{:S(2)}) collective-permute-start(bf16[3,2,192,128]{3,2,1,0:T(8,128)(2,1)S(1)} %get-tuple-element.83), channel_id=1, source_target_pairs={{1,16},{0,17},{25,8},{24,9},{3,18},{2,19},{27,10},{26,11},{5,20},{... | collective-permute-start | bytes 884744 | tf_op jit(solution)/shard_map/ppermute | solution.py:550
  43.2 0.7 %collective-permute-start.20 = (bf16[3,2,192,128]{3,2,1,0:T(8,128)(2,1)S(1)}, bf16[3,2,192,128]{3,2,1,0:T(8,128)(2,1)S(1)}, u32[]{:S(2)}, u32[]{:S(2)}) collective-permute-start(bf16[3,2,192,128]{3,2,1,0:T(8,128)(2,1)S(1)} %get-tuple-element.83), channel_id=1, source_target_pairs={{8,16},{16,8},{9,17},{17,9},{10,18},{18,10},{11,19},{19,11},{12,20... | collective-permute-start | bytes 884744 | tf_op jit(solution)/shard_map/ppermute | solution.py:549
  43.9 0.0 collective-permute-done.13
  44.0 1.7 %collective-permute-start.14 = (bf16[32,1536]{1,0:T(8,128)(2,1)S(1)}, bf16[32,1536]{1,0:T(8,128)(2,1)S(1)}, u32[]{:S(2)}, u32[]{:S(2)}) collective-permute-start(bf16[32,1536]{1,0:T(8,128)(2,1)S(1)} %add_convert_fusion.1), channel_id=1, source_target_pairs={{0,4},{2,6},{4,0},{6,2},{1,5},{3,7},{5,1},{7,3},{8,12},{10,14},{12... | collective-permute-start | bytes 294920 | tf_op jit(solution)/shard_map/ppermute | solution.py:106
  45.6 1.5 %convolution_convert_fusion = bf16[192,3072]{1,0:T(8,128)(2,1)} fusion(bf16[192,128]{1,0:T(8,128)(2,1)S(1)} %get-tuple-element.69, bf16[128,3072]{1,0:T(8,128)(2,1)S(1)} %copy-done), kind=kOutput, calls=%fused_computation | convolution fusion | flops 151584768 | bytes 2015232 | tf_op jit(solution)/shard_map/dot_general | solution.py:541
  47.1 4.9 %collective-permute-done.14 = bf16[32,1536]{1,0:T(8,128)(2,1)S(1)} collective-permute-done((bf16[32,1536]{1,0:T(8,128)(2,1)S(1)}, bf16[32,1536]{1,0:T(8,128)(2,1)S(1)}, u32[]{:S(2)}, u32[]{:S(2)}) %collective-permute-start.14) | collective-permute-done | bytes 98336 | tf_op jit(solution)/shard_map/ppermute | solution.py:106
  52.0 0.5 collective-permute-start.17
  52.5 2.2 %collective-permute-start.16 = (bf16[32,1536]{1,0:T(8,128)(2,1)S(1)}, bf16[32,1536]{1,0:T(8,128)(2,1)S(1)}, u32[]{:S(2)}, u32[]{:S(2)}) collective-permute-start(bf16[32,1536]{1,0:T(8,128)(2,1)S(1)} %add_convert_fusion.refs_0_), channel_id=1, source_target_pairs={{0,16},{1,17},{8,24},{9,25},{16,0},{17,1},{24,8},{25,9},{2,18},{3,... | collective-permute-start | bytes 294920 | tf_op jit(solution)/shard_map/ppermute | solution.py:106
  54.7 0.0 collective-permute-done.19.refs_0_
  54.7 0.9 %collective-permute-start.15 = (bf16[32,1536]{1,0:T(8,128)(2,1)S(1)}, bf16[32,1536]{1,0:T(8,128)(2,1)S(1)}, u32[]{:S(2)}, u32[]{:S(2)}) collective-permute-start(bf16[32,1536]{1,0:T(8,128)(2,1)S(1)} %add_convert_fusion.refs_0_), channel_id=1, source_target_pairs={{0,1},{1,0},{8,9},{9,8},{16,17},{17,16},{24,25},{25,24},{2,3},{3,2... | collective-permute-start | bytes 294920 | tf_op jit(solution)/shard_map/ppermute | solution.py:106
  55.6 0.0 collective-permute-done.21.refs_2_
  55.6 0.0 collective-permute-done.20.refs_1_
  55.6 0.1 shard_map.101
  55.7 1.5 %collective-permute-start.24 = (bf16[2,192,128]{2,1,0:T(8,128)(2,1)S(1)}, bf16[2,192,128]{2,1,0:T(8,128)(2,1)S(1)}, u32[]{:S(2)}, u32[]{:S(2)}) collective-permute-start(bf16[2,192,128]{2,1,0:T(8,128)(2,1)S(1)} %get-tuple-element.87), channel_id=1, source_target_pairs={{6,2},{0,4},{7,3},{1,5},{14,10},{8,12},{15,11},{9,13},{22,18},{16,... | collective-permute-start | bytes 294920 | tf_op jit(solution)/shard_map/ppermute | solution.py:87
  57.2 0.7 %collective-permute-start.23 = (bf16[2,192,128]{2,1,0:T(8,128)(2,1)S(1)}, bf16[2,192,128]{2,1,0:T(8,128)(2,1)S(1)}, u32[]{:S(2)}, u32[]{:S(2)}) collective-permute-start(bf16[2,192,128]{2,1,0:T(8,128)(2,1)S(1)} %get-tuple-element.87), channel_id=1, source_target_pairs={{4,2},{2,4},{5,3},{3,5},{12,10},{10,12},{13,11},{11,13},{20,18},{1... | collective-permute-start | bytes 294920 | tf_op jit(solution)/shard_map/ppermute | solution.py:87
  57.9 0.0 collective-permute-done.17.refs_3_
  57.9 1.3 %collective-permute-start.22 = (bf16[2,192,128]{2,1,0:T(8,128)(2,1)S(1)}, bf16[2,192,128]{2,1,0:T(8,128)(2,1)S(1)}, u32[]{:S(2)}, u32[]{:S(2)}) collective-permute-start(bf16[2,192,128]{2,1,0:T(8,128)(2,1)S(1)} %get-tuple-element.86), channel_id=1, source_target_pairs={{0,2},{2,0},{4,6},{6,4},{1,3},{3,1},{5,7},{7,5},{8,10},{10,8},{12,... | collective-permute-start | bytes 294920 | tf_op jit(solution)/shard_map/ppermute | solution.py:87
  59.2 0.0 collective-permute-done.16.refs_2_
  59.2 0.1 collective-permute-done.15.refs_1_
  59.3 0.1 collective-permute-start.18
  59.4 1.5 %shard_map.99.refs_1_ = f32[128,3072]{1,0:T(8,128)} custom-call(s32[3]{0:T(128)S(1)} %pad_add_fusion.place, bf16[144,1536]{1,0:T(8,128)(2,1)S(1)} %shard_map.98.part), custom_call_target="tpu_custom_call" | custom-call | flops 10000000000 | bytes 100000000 | tf_op jit(solution)/shard_map/pallas_call | solution.py:309
  60.9 0.3 collective-permute-done.18.part
  61.2 1.5 %shard_map.100 = (f32[128,3072]{1,0:T(8,128)}, bf16[192,128]{1,0:T(8,128)(2,1)}) custom-call(s32[3]{0:T(128)S(1)} %pad_add_fusion.place, bf16[144,1536]{1,0:T(8,128)(2,1)S(1)} %collective-permute-done.18.part, f32[192,128]{1,0:T(8,128)S(1)} %get-tuple-element.78.refs_0_, f32[128,3072]{1,0:T(8,128)} %shard_map.99.refs_1_), custom_call_target="tpu_custom_call", output_to_operand_aliasing={{0}: (3, {})} | custom-call | flops 10000000000 | bytes 100000000 | tf_op jit(solution)/shard_map/pallas_call | solution.py:309
  62.7 0.0 collective-permute-done.22.refs_0_
  62.7 0.0 collective-permute-done.24.refs_2_
  62.7 0.7 %shard_map.102 = (bf16[192,128]{1,0:T(8,128)(2,1)}, bf16[192,128]{1,0:T(8,128)(2,1)}) custom-call(f32[2,192,128]{2,1,0:T(8,128)S(1)} %get-tuple-element.85.own_grad, bf16[2,192,128]{2,1,0:T(8,128)(2,1)S(1)} %collective-permute-done.22.refs_0_, bf16[2,192,128]{2,1,0:T(8,128)(2,1)S(1)} %collective-permute-done.23.refs_1_, ...), custom_call_target="tpu_custom_call" | custom-call | flops 10000000000 | bytes 100000000 | tf_op jit(solution)/shard_map/pallas_call | solution.py:587
  (12 shorter events, 0.2 us)
Async XLA Ops:
  0.6 17.4 %copy-start.2 = (bf16[4,6,8,128]{3,2,1,0:T(8,128)(2,1)S(1)}, bf16[4,6,8,128]{3,2,1,0:T(8,128)(2,1)}, u32[]{:S(2)}) copy-start(bf16[4,6,8,128]{3,2,1,0:T(8,128)(2,1)} %param.5) | copy-start | bytes 147460
  0.6 21.9 %copy-start = (bf16[128,3072]{1,0:T(8,128)(2,1)S(1)}, bf16[128,3072]{1,0:T(8,128)(2,1)}, u32[]{:S(2)}) copy-start(bf16[128,3072]{1,0:T(8,128)(2,1)} %weight.1) | copy-start | bytes 2359300
  1.6 9.8 %collective-permute-start.2 = (bf16[2,192,128]{2,1,0:T(8,128)(2,1)S(1)}, bf16[2,192,128]{2,1,0:T(8,128)(2,1)S(1)}, u32[]{:S(2)}, u32[]{:S(2)}) collective-permute-start(bf16[2,192,128]{2,1,0:T(8,128)(2,1)S(1)} %get-tuple-element.92), channel_id=1, source_target_pairs={{2,4},{4,2},{3,5},{5,3},{10,12},{12,10},{11,13},{13,11},{18,20},{2... | collective-permute-start | bytes 294920 | tf_op jit(solution)/shard_map/ppermute | solution.py:65
  2.2 10.5 %collective-permute-start.1 = (bf16[2,192,128]{2,1,0:T(8,128)(2,1)S(1)}, bf16[2,192,128]{2,1,0:T(8,128)(2,1)S(1)}, u32[]{:S(2)}, u32[]{:S(2)}) collective-permute-start(bf16[2,192,128]{2,1,0:T(8,128)(2,1)S(1)} %get-tuple-element.92), channel_id=1, source_target_pairs={{2,6},{4,0},{3,7},{5,1},{10,14},{12,8},{11,15},{13,9},{18,22},{20,... | collective-permute-start | bytes 294920 | tf_op jit(solution)/shard_map/ppermute | solution.py:65
  3.5 10.6 %collective-permute-start = (bf16[2,192,128]{2,1,0:T(8,128)(2,1)S(1)}, bf16[2,192,128]{2,1,0:T(8,128)(2,1)S(1)}, u32[]{:S(2)}, u32[]{:S(2)}) collective-permute-start(bf16[2,192,128]{2,1,0:T(8,128)(2,1)S(1)} %get-tuple-element.92), channel_id=1, source_target_pairs={{2,0},{0,2},{6,4},{4,6},{3,1},{1,3},{7,5},{5,7},{10,8},{8,10},{14,... | collective-permute-start | bytes 294920 | tf_op jit(solution)/shard_map/ppermute | solution.py:65
  9.8 4.6 %collective-permute-start.3 = (bf16[1,2,192,128]{3,2,1,0:T(8,128)(2,1)S(1)}, bf16[1,2,192,128]{3,2,1,0:T(8,128)(2,1)S(1)}, u32[]{:S(2)}, u32[]{:S(2)}) collective-permute-start(bf16[1,2,192,128]{3,2,1,0:T(8,128)(2,1)S(1)} %get-tuple-element.91), channel_id=1, source_target_pairs={{0,1},{1,0},{2,3},{3,2},{4,5},{5,4},{6,7},{7,6},{8,9},{9,8},{10,11... | collective-permute-start | bytes 294920 | tf_op jit(solution)/shard_map/ppermute | solution.py:420
  14.5 12.1 %collective-permute-start.7 = (bf16[3,2,192,128]{3,2,1,0:T(8,128)(2,1)S(1)}, bf16[3,2,192,128]{3,2,1,0:T(8,128)(2,1)S(1)}, u32[]{:S(2)}, u32[]{:S(2)}) collective-permute-start(bf16[3,2,192,128]{3,2,1,0:T(8,128)(2,1)S(1)} %pad_maximum_fusion.refs_0_), channel_id=1, source_target_pairs={{16,1},{17,0},{8,25},{9,24},{18,3},{19,2},{10,27},{11,26},{20,5},{... | collective-permute-start | bytes 884744 | tf_op jit(solution)/shard_map/ppermute | solution.py:429
  15.7 10.8 %collective-permute-start.6 = (bf16[3,2,192,128]{3,2,1,0:T(8,128)(2,1)S(1)}, bf16[3,2,192,128]{3,2,1,0:T(8,128)(2,1)S(1)}, u32[]{:S(2)}, u32[]{:S(2)}) collective-permute-start(bf16[3,2,192,128]{3,2,1,0:T(8,128)(2,1)S(1)} %pad_maximum_fusion.refs_0_), channel_id=1, source_target_pairs={{16,8},{8,16},{17,9},{9,17},{18,10},{10,18},{19,11},{11,19},{20,12... | collective-permute-start | bytes 884744 | tf_op jit(solution)/shard_map/ppermute | solution.py:428
  16.4 10.1 %collective-permute-start.5 = (bf16[2,2,192,128]{3,2,1,0:T(8,128)(2,1)S(1)}, bf16[2,2,192,128]{3,2,1,0:T(8,128)(2,1)S(1)}, u32[]{:S(2)}, u32[]{:S(2)}) collective-permute-start(bf16[2,2,192,128]{3,2,1,0:T(8,128)(2,1)S(1)} %pad_maximum_fusion.1), channel_id=1, source_target_pairs={{0,1},{1,0},{2,3},{3,2},{4,5},{5,4},{6,7},{7,6},{8,9},{9,8},{10,11... | collective-permute-start | bytes 589832 | tf_op jit(solution)/shard_map/ppermute | solution.py:426
  18.0 4.5 %collective-permute-start.4 = (bf16[192,128]{1,0:T(8,128)(2,1)S(1)}, bf16[192,128]{1,0:T(8,128)(2,1)S(1)}, u32[]{:S(2)}, u32[]{:S(2)}) collective-permute-start(bf16[192,128]{1,0:T(8,128)(2,1)S(1)} %bitcast.19), channel_id=1, source_target_pairs={{0,8},{8,0},{16,24},{24,16},{1,9},{9,1},{17,25},{25,17},{2,10},{10... | collective-permute-start | bytes 147464 | tf_op jit(solution)/shard_map/ppermute | solution.py:106
  22.6 1.3 %copy-start.1 = (bf16[4,6,8,3072]{3,2,1,0:T(8,128)(2,1)S(1)}, bf16[4,6,8,3072]{3,2,1,0:T(8,128)(2,1)}, u32[]{:S(2)}) copy-start(bf16[4,6,8,3072]{3,2,1,0:T(8,128)(2,1)} %param.9) | copy-start | bytes 3538948
  25.6 4.0 %collective-permute-start.9 = (bf16[192,1664]{1,0:T(8,128)(2,1)S(1)}, bf16[192,1664]{1,0:T(8,128)(2,1)S(1)}, u32[]{:S(2)}, u32[]{:S(2)}) collective-permute-start(bf16[192,1664]{1,0:T(8,128)(2,1)S(1)} %get-tuple-element.55), channel_id=1, source_target_pairs={{0,8},{8,0},{16,24},{24,16},{1,9},{9,1},{17,25},{25,17},{2,10},{10... | collective-permute-start | bytes 1916936 | tf_op jit(solution)/shard_map/ppermute | solution.py:106
  27.7 1.9 %collective-permute-start.8 = (f32[136,384]{1,0:T(8,128)S(1)}, f32[136,384]{1,0:T(8,128)S(1)}, u32[]{:S(2)}, u32[]{:S(2)}) collective-permute-start(f32[136,384]{1,0:T(8,128)S(1)} %shard_map.94.mine), channel_id=1, source_target_pairs={{0,8},{8,0},{16,24},{24,16},{1,9},{9,1},{17,25},{25,17},{2,10},{10... | collective-permute-start | bytes 626696 | tf_op jit(solution)/shard_map/ppermute | solution.py:106
  30.7 7.8 %collective-permute-start.10 = (bf16[32,1536]{1,0:T(8,128)(2,1)S(1)}, bf16[32,1536]{1,0:T(8,128)(2,1)S(1)}, u32[]{:S(2)}, u32[]{:S(2)}) collective-permute-start(bf16[32,1536]{1,0:T(8,128)(2,1)S(1)} %get-tuple-element.62), channel_id=1, source_target_pairs={{0,1},{1,0},{8,9},{9,8},{16,17},{17,16},{24,25},{25,24},{2,3},{3,2... | collective-permute-start | bytes 294920 | tf_op jit(solution)/shard_map/ppermute | solution.py:106
  32.3 6.2 %collective-permute-start.11 = (bf16[32,1536]{1,0:T(8,128)(2,1)S(1)}, bf16[32,1536]{1,0:T(8,128)(2,1)S(1)}, u32[]{:S(2)}, u32[]{:S(2)}) collective-permute-start(bf16[32,1536]{1,0:T(8,128)(2,1)S(1)} %get-tuple-element.63), channel_id=1, source_target_pairs={{0,16},{1,17},{8,24},{9,25},{16,0},{17,1},{24,8},{25,9},{2,18},{3,... | collective-permute-start | bytes 294920 | tf_op jit(solution)/shard_map/ppermute | solution.py:106
  32.7 6.4 %collective-permute-start.12 = (bf16[32,1536]{1,0:T(8,128)(2,1)S(1)}, bf16[32,1536]{1,0:T(8,128)(2,1)S(1)}, u32[]{:S(2)}, u32[]{:S(2)}) collective-permute-start(bf16[32,1536]{1,0:T(8,128)(2,1)S(1)} %get-tuple-element.64), channel_id=1, source_target_pairs={{0,17},{1,16},{8,25},{9,24},{16,1},{17,0},{24,9},{25,8},{2,19},{3,... | collective-permute-start | bytes 294920 | tf_op jit(solution)/shard_map/ppermute | solution.py:106
  36.9 17.8 %collective-permute-start.19 = (bf16[3,2,192,128]{3,2,1,0:T(8,128)(2,1)S(1)}, bf16[3,2,192,128]{3,2,1,0:T(8,128)(2,1)S(1)}, u32[]{:S(2)}, u32[]{:S(2)}) collective-permute-start(bf16[3,2,192,128]{3,2,1,0:T(8,128)(2,1)S(1)} %get-tuple-element.82), channel_id=1, source_target_pairs={{0,1},{1,0},{2,3},{3,2},{4,5},{5,4},{6,7},{7,6},{8,9},{9,8},{10,11... | collective-permute-start | bytes 884744 | tf_op jit(solution)/shard_map/ppermute | solution.py:548
  39.2 4.7 %collective-permute-start.13 = (bf16[32,1536]{1,0:T(8,128)(2,1)S(1)}, bf16[32,1536]{1,0:T(8,128)(2,1)S(1)}, u32[]{:S(2)}, u32[]{:S(2)}) collective-permute-start(bf16[32,1536]{1,0:T(8,128)(2,1)S(1)} %add_convert_fusion.2), channel_id=1, source_target_pairs={{0,2},{2,0},{4,6},{6,4},{1,3},{3,1},{5,7},{7,5},{8,10},{10,8},{12,... | collective-permute-start | bytes 294920 | tf_op jit(solution)/shard_map/ppermute | solution.py:106
  40.1 15.5 %collective-permute-start.21 = (bf16[3,2,192,128]{3,2,1,0:T(8,128)(2,1)S(1)}, bf16[3,2,192,128]{3,2,1,0:T(8,128)(2,1)S(1)}, u32[]{:S(2)}, u32[]{:S(2)}) collective-permute-start(bf16[3,2,192,128]{3,2,1,0:T(8,128)(2,1)S(1)} %get-tuple-element.83), channel_id=1, source_target_pairs={{1,16},{0,17},{25,8},{24,9},{3,18},{2,19},{27,10},{26,11},{5,20},{... | collective-permute-start | bytes 884744 | tf_op jit(solution)/shard_map/ppermute | solution.py:550
  43.2 12.3 %collective-permute-start.20 = (bf16[3,2,192,128]{3,2,1,0:T(8,128)(2,1)S(1)}, bf16[3,2,192,128]{3,2,1,0:T(8,128)(2,1)S(1)}, u32[]{:S(2)}, u32[]{:S(2)}) collective-permute-start(bf16[3,2,192,128]{3,2,1,0:T(8,128)(2,1)S(1)} %get-tuple-element.83), channel_id=1, source_target_pairs={{8,16},{16,8},{9,17},{17,9},{10,18},{18,10},{11,19},{19,11},{12,20... | collective-permute-start | bytes 884744 | tf_op jit(solution)/shard_map/ppermute | solution.py:549
  44.0 8.0 %collective-permute-start.14 = (bf16[32,1536]{1,0:T(8,128)(2,1)S(1)}, bf16[32,1536]{1,0:T(8,128)(2,1)S(1)}, u32[]{:S(2)}, u32[]{:S(2)}) collective-permute-start(bf16[32,1536]{1,0:T(8,128)(2,1)S(1)} %add_convert_fusion.1), channel_id=1, source_target_pairs={{0,4},{2,6},{4,0},{6,2},{1,5},{3,7},{5,1},{7,3},{8,12},{10,14},{12... | collective-permute-start | bytes 294920 | tf_op jit(solution)/shard_map/ppermute | solution.py:106
  52.0 5.9 %collective-permute-start.17 = (bf16[32,1536]{1,0:T(8,128)(2,1)S(1)}, bf16[32,1536]{1,0:T(8,128)(2,1)S(1)}, u32[]{:S(2)}, u32[]{:S(2)}) collective-permute-start(bf16[32,1536]{1,0:T(8,128)(2,1)S(1)} %add_convert_fusion.refs_0_), channel_id=1, source_target_pairs={{0,17},{1,16},{8,25},{9,24},{16,1},{17,0},{24,9},{25,8},{2,19},{3,... | collective-permute-start | bytes 294920 | tf_op jit(solution)/shard_map/ppermute | solution.py:106
  52.5 6.7 %collective-permute-start.16 = (bf16[32,1536]{1,0:T(8,128)(2,1)S(1)}, bf16[32,1536]{1,0:T(8,128)(2,1)S(1)}, u32[]{:S(2)}, u32[]{:S(2)}) collective-permute-start(bf16[32,1536]{1,0:T(8,128)(2,1)S(1)} %add_convert_fusion.refs_0_), channel_id=1, source_target_pairs={{0,16},{1,17},{8,24},{9,25},{16,0},{17,1},{24,8},{25,9},{2,18},{3,... | collective-permute-start | bytes 294920 | tf_op jit(solution)/shard_map/ppermute | solution.py:106
  54.7 4.6 %collective-permute-start.15 = (bf16[32,1536]{1,0:T(8,128)(2,1)S(1)}, bf16[32,1536]{1,0:T(8,128)(2,1)S(1)}, u32[]{:S(2)}, u32[]{:S(2)}) collective-permute-start(bf16[32,1536]{1,0:T(8,128)(2,1)S(1)} %add_convert_fusion.refs_0_), channel_id=1, source_target_pairs={{0,1},{1,0},{8,9},{9,8},{16,17},{17,16},{24,25},{25,24},{2,3},{3,2... | collective-permute-start | bytes 294920 | tf_op jit(solution)/shard_map/ppermute | solution.py:106
  55.7 7.0 %collective-permute-start.24 = (bf16[2,192,128]{2,1,0:T(8,128)(2,1)S(1)}, bf16[2,192,128]{2,1,0:T(8,128)(2,1)S(1)}, u32[]{:S(2)}, u32[]{:S(2)}) collective-permute-start(bf16[2,192,128]{2,1,0:T(8,128)(2,1)S(1)} %get-tuple-element.87), channel_id=1, source_target_pairs={{6,2},{0,4},{7,3},{1,5},{14,10},{8,12},{15,11},{9,13},{22,18},{16,... | collective-permute-start | bytes 294920 | tf_op jit(solution)/shard_map/ppermute | solution.py:87
  57.2 5.5 %collective-permute-start.23 = (bf16[2,192,128]{2,1,0:T(8,128)(2,1)S(1)}, bf16[2,192,128]{2,1,0:T(8,128)(2,1)S(1)}, u32[]{:S(2)}, u32[]{:S(2)}) collective-permute-start(bf16[2,192,128]{2,1,0:T(8,128)(2,1)S(1)} %get-tuple-element.87), channel_id=1, source_target_pairs={{4,2},{2,4},{5,3},{3,5},{12,10},{10,12},{13,11},{11,13},{20,18},{1... | collective-permute-start | bytes 294920 | tf_op jit(solution)/shard_map/ppermute | solution.py:87
  57.9 4.8 %collective-permute-start.22 = (bf16[2,192,128]{2,1,0:T(8,128)(2,1)S(1)}, bf16[2,192,128]{2,1,0:T(8,128)(2,1)S(1)}, u32[]{:S(2)}, u32[]{:S(2)}) collective-permute-start(bf16[2,192,128]{2,1,0:T(8,128)(2,1)S(1)} %get-tuple-element.86), channel_id=1, source_target_pairs={{0,2},{2,0},{4,6},{6,4},{1,3},{3,1},{5,7},{7,5},{8,10},{10,8},{12,... | collective-permute-start | bytes 294920 | tf_op jit(solution)/shard_map/ppermute | solution.py:87
  59.3 1.9 %collective-permute-start.18 = (bf16[144,1536]{1,0:T(8,128)(2,1)S(1)}, bf16[144,1536]{1,0:T(8,128)(2,1)S(1)}, u32[]{:S(2)}, u32[]{:S(2)}) collective-permute-start(bf16[144,1536]{1,0:T(8,128)(2,1)S(1)} %shard_map.98.part), channel_id=1, source_target_pairs={{0,8},{8,0},{16,24},{24,16},{1,9},{9,1},{17,25},{25,17},{2,10},{10... | collective-permute-start | bytes 1327112 | tf_op jit(solution)/shard_map/ppermute | solution.py:106
